TPU v7x, 32 devices: a whole 2x2x4 slice. The times are simulated.
32 devices in a mesh: pole: 4 (over y, core), snode: 8 (over z, x).
Axes of the slice: x: 2, y: 2, z: 4, core: 2. Of those that a mesh axis runs over, the one named last changes fastest.
Arguments:
- pivot_inverse: float32 [8, 16, 2, 256, 256], P('pole', 'snode'), as said below
- factor_block: float32 [8, 16, 2, 256, 256], P('pole', 'snode')
- live_width_array: int32 [16], P('snode'), may hold values from 128 to 256, as said below
- pole_weight: float32 [8, 2], P('pole'), may hold values from -4 to 4
Outputs:
- density_diag: float32 [16, 256, 256], P('snode')
- density_off: float32 [16, 256, 256], P('snode')
Inputs may be any that keep to these rules, and one draw needn't show every extreme that they name: `live_width_array`: live widths of the supernodes; at least one supernode is 256 wide and one is 128 wide. `pivot_inverse`: symmetric in its last two dimensions with a dominant real diagonal.
All inputs are finite; a program needn't handle non-finite values.
Results may differ from a plain program's by a relative error of at most 0.0003.
Values sent between devices are 32-bit elements; how exact they have to be, the bound alone decides.
No kernel may reach another device: no remote copies, remote signals or barrier semaphores. Data moves between devices by JAX's collectives and lax.ppermute only.
A program may use at most 192 MiB of HBM per device.

v0:
```python
import functools

import jax
import jax.numpy as jnp
from jax import lax
from jax.experimental import pallas as pl
from jax.experimental.pallas import tpu as pltpu
from jax.sharding import PartitionSpec as P

F32 = jnp.float32
BF16 = jnp.bfloat16
AXES = ("pole", "snode")
VMEM_LIMIT = 16 * 1024 * 1024


def halves(value):
    high = value.astype(BF16)
    return high, (value - high.astype(F32)).astype(BF16)


def split_pair(real, imag):
    (rh, rl), (ih, il) = halves(real), halves(imag)
    return rh, ih, rl, il


def dot(left, right):
    return jnp.dot(left, right, preferred_element_type=F32)


def dot3(lh, ll, rh, rl):
    return dot(lh, rh) + (dot(lh, rl) + dot(ll, rh))


def complex_dot(left, right):
    arh, aih, arl, ail = left
    brh, bih, brl, bil = right
    real = dot3(arh, arl, brh, brl) - dot3(aih, ail, bih, bil)
    imag = dot3(arh, arl, bih, bil) + dot3(aih, ail, brh, brl)
    return real, imag


def rows_columns(size):
    return (
        lax.broadcasted_iota(jnp.int32, (size, size), 0),
        lax.broadcasted_iota(jnp.int32, (size, size), 1),
    )


def packed(block):
    half = block.shape[0] // 2
    row, column = rows_columns(half)
    lower = block[half:, half:]
    mixed = jnp.where(row >= column, block[:half, :half], lower)
    diagonal = jnp.sum(jnp.where(row == column, lower, 0.0), axis=0, keepdims=True)
    return jnp.concatenate(
        [block[:half, half:], mixed, jnp.broadcast_to(diagonal, (8, half))], axis=0
    )


def unpacked(value):
    half = value.shape[1]
    row, column = rows_columns(half)
    right, mixed = value[:half], value[half : 2 * half]
    diagonal = value[2 * half : 2 * half + 1]
    turned = mixed.T
    first = jnp.where(row >= column, mixed, turned)
    last = jnp.where(row < column, mixed, jnp.where(row == column, diagonal, turned))
    return jnp.concatenate(
        [jnp.concatenate([first, right], axis=1), jnp.concatenate([right.T, last], axis=1)], axis=0
    )


def unpacked_split(ref):
    return split_pair(unpacked(ref[0]), unpacked(ref[1]))


def load4(ref):
    return tuple(ref[i] for i in range(4))


def store4(ref, parts):
    for i, part in enumerate(parts):
        ref[i] = part


def whereabouts():
    place = lax.axis_index("snode")
    return place, lax.rem(place, 2), lax.rem(lax.axis_index("pole"), 2)


def hosted_slot():
    place, odd, _ = whereabouts()
    return jnp.where(place < 2, 0, 1 - odd)


def slot_of(hosted):
    return hosted_slot() if hosted else 1 - hosted_slot()


def constant_kernel(hosted, fetch, live, pivot, factor, weight, *refs):
    width = pivot.shape[-1]
    slot = slot_of(hosted)
    if fetch:
        f1s, e, weighted, blocks, link, widths, weights, sems = refs
        copies = [
            pltpu.make_async_copy(live, widths, sems.at[0]),
            pltpu.make_async_copy(factor.at[slot, 1], link, sems.at[1]),
            pltpu.make_async_copy(pivot.at[slot, 0], blocks.at[0], sems.at[2]),
            pltpu.make_async_copy(pivot.at[slot, 1], blocks.at[1], sems.at[3]),
            pltpu.make_async_copy(weight, weights, sems.at[4]),
        ]
        for copy in copies:
            copy.start()
        copies[0].wait()
        copies[1].wait()
    else:
        _, f1s, e, weighted = refs
        blocks, link, widths, weights, copies = pivot.at[slot], factor.at[slot, 1], live, weight, []
    row, column = rows_columns(width)
    kept = [column < widths[k] for k in range(2)]
    both = [jnp.logical_and(row < widths[k], kept[k]) for k in range(2)]
    f1 = [jnp.where(kept[1], link[c], 0.0) for c in range(2)]
    s1, t1 = split_pair(*f1), split_pair(f1[0].T, f1[1].T)
    store4(f1s, s1)
    for copy in copies[2:]:
        copy.wait()
    d = [[jnp.where(both[k], blocks[k, c], 0.0) for c in range(2)] for k in range(2)]
    br, bi = complex_dot(split_pair(*d[0]), s1)
    tr, ti = complex_dot(t1, split_pair(br, bi))
    er, ei = d[1][0] + tr, d[1][1] + ti
    e[0], e[1] = packed(er), packed(ei)
    w0, w1 = weights[pl.ds(slot, 1), 0:1], weights[pl.ds(slot, 1), 1:2]
    weighted[0] = packed(w1 * d[0][0] + w0 * d[0][1])
    weighted[1] = packed(w1 * er + w0 * ei)
    weighted_b = flat(w1 * br + w0 * bi)
    weighted[2] = weighted_b[: width + 8]
    weighted[3, : width - 8] = weighted_b[width + 8 :]


def factor_kernel(hosted, live, factor, f1s, f0s, f0t, gs, gt, g):
    slot = slot_of(hosted)
    _, column = rows_columns(factor.shape[-1])
    f0 = [jnp.where(column < live[0], factor[slot, 0, c], 0.0) for c in range(2)]
    s0 = split_pair(*f0)
    gr, gi = complex_dot(s0, load4(f1s))
    g[0], g[1] = gr, gi
    store4(gs, split_pair(gr, gi))
    store4(gt, split_pair(gr.T, gi.T))
    store4(f0s, s0)
    store4(f0t, split_pair(f0[0].T, f0[1].T))


def fold(x, gs, gt, e, out):
    tr, ti = complex_dot(x, load4(gs))
    yr, yi = complex_dot(load4(gt), split_pair(tr, ti))
    out[0] = e[0] + packed(yr)
    out[1] = e[1] + packed(yi)


def step_kernel(active, gs, gt, e, *refs):
    *received, out = refs

    @pl.when(active(whereabouts()[0]))
    def _():
        value = received[0][...]
        for other in received[1:]:
            value = value + other[...]
        fold(split_pair(unpacked(value[0]), unpacked(value[1])), gs, gt, e, out)


def pair_kernel(g, e, g_in, e_in, e_second, fas, fat, ea, ps, pt, ep):
    upper = whereabouts()[0] > 1
    is_odd = whereabouts()[1] == 1
    ga = [jnp.where(is_odd, g_in[c], g[c]) for c in range(2)]
    gb = [jnp.where(is_odd, g[c], g_in[c]) for c in range(2)]
    theirs = [jnp.where(upper, e_in[c], e_second[c]) for c in range(2)]
    low = [jnp.where(is_odd, theirs[c], e[c]) for c in range(2)]
    high = [jnp.where(is_odd, e[c], theirs[c]) for c in range(2)]
    sa, sb = split_pair(*ga), split_pair(*gb)
    store4(fas, sa)
    store4(fat, split_pair(ga[0].T, ga[1].T))
    pr, pi = complex_dot(sa, sb)
    store4(ps, split_pair(pr, pi))
    store4(pt, split_pair(pr.T, pi.T))
    br, bi = complex_dot(split_pair(unpacked(low[0]), unpacked(low[1])), sb)
    tr, ti = complex_dot(split_pair(gb[0].T, gb[1].T), split_pair(br, bi))
    for c, term in enumerate((tr, ti)):
        ea[c] = low[c]
        ep[c] = high[c] + packed(term)


def share_kernel(fas, fat, ea, *refs):
    *received, own, sent, scratch = refs
    value = received[0][...]
    for other in received[1:]:
        value = value + other[...]
    value = jnp.where(whereabouts()[0] > 1, value, 0.0)
    fold(split_pair(unpacked(value[0]), unpacked(value[1])), fas, fat, ea, scratch)
    is_odd = whereabouts()[1] == 1
    own[...] = jnp.where(is_odd, scratch[...], value)
    sent[...] = jnp.where(is_odd, value, scratch[...])


def flat(block):
    half = block.shape[1] // 2
    return jnp.concatenate([block[:, :half], block[:, half:]], axis=0)


def real_dot(left, right):
    return dot3(left[0], left[2], right[0], right[2]) + dot3(left[1], left[3], right[1], right[3])


def off_values(slot, weight, xs, f0s, f0t, gs, weighted):
    width = f0s.shape[-1]
    w0, w1 = weight[pl.ds(slot, 1), 0:1], weight[pl.ds(slot, 1), 1:2]
    qr, qi = complex_dot(xs, load4(gs))
    ts = split_pair(w1 * qr + w0 * qi, w0 * qr - w1 * qi)
    second = real_dot(load4(f0t), ts)
    pr, pi = complex_dot(xs, load4(f0s))
    u = w1 * pr + w0 * pi
    us = split_pair(u, w0 * pr - w1 * pi)
    constant = jnp.concatenate([weighted[2], weighted[3, : width - 8]], axis=0)
    return -flat(u), -(flat(second) + constant), us, ts


def diag_values(us, ts, f0t, gt, weighted):
    return (
        weighted[0] + packed(real_dot(load4(f0t), us)),
        weighted[1] + packed(real_dot(load4(gt), ts)),
    )


def density_kernel(weight, x, f0s, f0t, gs, gt, weighted, off, diag):
    core = whereabouts()[2]
    first, second, us, ts = off_values(slot_of(True), weight, unpacked_split(x), f0s, f0t, gs, weighted)
    off[core], off[1 - core] = first, second
    diag[core], diag[1 - core] = diag_values(us, ts, f0t, gt, weighted)


def more_off_kernel(weight, x, x_first, f0s, f0t, gs, weighted, before, off, us_out, ts_out):
    core = whereabouts()[2]
    upper = whereabouts()[0] > 1
    x = [jnp.where(upper, x[c], x_first[c]) for c in range(2)]
    xs = split_pair(unpacked(x[0]), unpacked(x[1]))
    first, second, us, ts = off_values(slot_of(False), weight, xs, f0s, f0t, gs, weighted)
    off[core] = first + before[core]
    off[1 - core] = second + before[1 - core]
    store4(us_out, us)
    store4(ts_out, ts)


def more_diag_kernel(us, ts, f0t, gt, weighted, before, diag):
    core = whereabouts()[2]
    first, second = diag_values(load4(us), load4(ts), f0t, gt, weighted)
    diag[core] = first + before[core]
    diag[1 - core] = second + before[1 - core]


def unpack_off_kernel(mine, theirs, off, done):
    core = whereabouts()[2]
    width = off.shape[-1]
    half = width // 2
    for source, entry in ((mine, core), (theirs, 1 - core)):
        off[entry, :, :half] = source[:width]
        off[entry, :, half:] = source[width:]
    done[...] = jnp.zeros_like(done)


def unpack_diag_kernel(mine, theirs, _, diag):
    core = whereabouts()[2]
    for source, entry in ((mine, core), (theirs, 1 - core)):
        diag[entry] = unpacked(source[...])


SCALAR = pl.BlockSpec(memory_space=pltpu.SMEM)
WHOLE = pl.BlockSpec(memory_space=pltpu.VMEM)


COST = pl.CostEstimate(flops=1, bytes_accessed=1, transcendentals=0)


LONG = pl.CostEstimate(flops=10**11, bytes_accessed=1, transcendentals=0)


def run(kernel, scalars, arrays, shapes, scratch=(), cost=COST, far=()):
    return pl.pallas_call(
        kernel,
        out_shape=shapes,
        in_specs=[SCALAR] * len(scalars)
        + [pl.BlockSpec(memory_space=pltpu.HBM)] * len(far)
        + [WHOLE] * len(arrays),
        out_specs=[WHOLE] * len(shapes),
        scratch_shapes=list(scratch),
        compiler_params=pltpu.CompilerParams(vmem_limit_bytes=VMEM_LIMIT),
        cost_estimate=cost,
    )(*scalars, *far, *arrays)


def local(pivot, factor, live, weight):
    poles, turns = lax.axis_size("pole"), lax.axis_size("snode")
    rows = turns // 2
    width = pivot.shape[-1]
    quarter = (width + 8, width // 2)
    mirrored = jax.ShapeDtypeStruct((2,) + quarter, F32)
    parts = jax.ShapeDtypeStruct((4, width, width), BF16)

    def at(pole_index, snode_index):
        return pole_index * turns + snode_index

    def hosts(row, pole):
        return at(pole, 2 * row + 1), at(pole, 2 * row)

    swaps = [(at(p, s), at(p, s ^ 1)) for p in range(poles) for s in range(2, turns)]
    first = [(at(p, 0), at(p, 1)) for p in range(poles)]
    every = [(at(p, s), at(p, s ^ 1)) for p in range(poles) for s in range(turns)]
    constants = [parts, mirrored, jax.ShapeDtypeStruct((4,) + quarter, F32)]
    factors = [parts, parts, parts, parts, jax.ShapeDtypeStruct((2, width, width), F32)]

    o_f1s, o_e, o_w = run(
        functools.partial(constant_kernel, False, True),
        [],
        [],
        constants,
        [
            pltpu.VMEM(pivot.shape[1:], F32),
            pltpu.VMEM(factor.shape[2:], F32),
            pltpu.SMEM(live.shape, jnp.int32),
            pltpu.VMEM(weight.shape, F32),
            pltpu.SemaphoreType.DMA((5,)),
        ],
        far=[
            pltpu.with_memory_space_constraint(a, pltpu.HBM) for a in (live, pivot, factor, weight)
        ],
    )
    e_in = lax.ppermute(o_e, AXES, first + swaps)
    o_f0s, o_f0t, o_gs, o_gt, o_g = run(
        functools.partial(factor_kernel, False), [live], [factor, o_f1s], factors
    )
    g_in = lax.ppermute(o_g, AXES, swaps)
    m_f1s, m_e, m_w = run(
        functools.partial(constant_kernel, True, False),
        [live],
        [pivot, factor, weight, o_g],
        constants,
    )
    m_f0s, m_f0t, m_gs, m_gt, m_g = run(
        functools.partial(factor_kernel, True), [live], [factor, m_f1s], factors
    )
    e_second = lax.ppermute(m_e, AXES, first)

    starts = functools.partial(step_kernel, lambda place: place == 1)
    (wave_even,) = run(starts, [], [o_gs, o_gt, o_e, e_in], [mirrored])
    wave_even = lax.ppermute(wave_even, AXES, [(at(p, 1), at(p, 0)) for p in range(poles)])
    (wave_odd,) = run(starts, [], [m_gs, m_gt, m_e, e_second], [mirrored])
    received = []
    if rows > 1:
        received = [
            lax.ppermute(wave_odd, AXES, [(at(p, 1), at(p, 3)) for p in range(poles)]),
            lax.ppermute(wave_even, AXES, [(at(p, 0), at(p, 2)) for p in range(poles)]),
        ]
    else:
        received = [jnp.zeros(mirrored.shape, F32)]
    fas, fat, ea, ps, pt, ep = run(
        pair_kernel,
        [],
        [m_g, m_e, g_in, e_in, e_second],
        [parts, parts, mirrored, parts, parts, mirrored],
        cost=LONG,
    )
    arrived = list(received)
    for turn in range(1, rows - 1):
        active = functools.partial(step_kernel, lambda place, turn=turn: lax.div(place, 2) == turn)
        (wave,) = run(active, [], [ps, pt, ep] + arrived, [mirrored])
        up = [pair for p in range(poles) for pair in zip(hosts(turn, p), hosts(turn + 1, p))]
        arrived = [lax.ppermute(wave, AXES, up)]
        received += arrived
    own, sent = run(
        share_kernel,
        [],
        [fas, fat, ea] + received,
        [mirrored, mirrored],
        [pltpu.VMEM(mirrored.shape, F32)],
    )
    shared = lax.ppermute(sent, AXES, every)

    offs = jax.ShapeDtypeStruct((2, 2 * width, width // 2), F32)
    diags = jax.ShapeDtypeStruct((2,) + quarter, F32)
    off, diag = run(density_kernel, [], [weight, own, m_f0s, m_f0t, m_gs, m_gt, m_w], [offs, diags])
    off, us, ts = run(
        more_off_kernel,
        [],
        [weight, shared, e_in, o_f0s, o_f0t, o_gs, o_w, off],
        [offs, parts, parts],
    )

    def exchanged(value, distance):
        return lax.ppermute(value, "pole", [(p, p ^ distance) for p in range(poles)])

    def summed(parts):
        kept = parts[0] + exchanged(parts[1], 1)
        distance = 2
        while distance < poles:
            kept = kept + exchanged(kept, distance)
            distance *= 2
        return kept, exchanged(kept, 1)

    full = jax.ShapeDtypeStruct((2, width, width), F32)
    off_sums = summed(off)
    (diag,) = run(more_diag_kernel, [], [us, ts, o_f0t, o_gt, o_w, diag], [diags])
    diag_sums = summed(diag)
    done = jax.ShapeDtypeStruct((8, 128), F32)
    density_off, done = run(unpack_off_kernel, [], list(off_sums), [full, done])
    (density_diag,) = run(unpack_diag_kernel, [], [*diag_sums, done], [full])
    return density_diag, density_off


def solution(mesh):
    placed = (
        P("pole", "snode", None, None, None),
        P("pole", "snode", None, None, None),
        P("snode"),
        P("pole", None),
    )
    return jax.shard_map(
        local,
        mesh=mesh,
        in_specs=placed,
        out_specs=(P("snode", None, None), P("snode", None, None)),
        check_vma=False,
    )
```

profile of v0, /device:TPU:29, one launch (start us, length us, event | category | flops | bytes accessed | tf_op | source)
XLA Modules:
  0.0 69.3 jit_solution(14657300348646715638)
XLA Ops:
  0.6 0.0 copy-start
  0.6 0.0 copy-start.3
  0.6 2.7 %shard_map.59 = (bf16[4,256,256]{2,1,0:T(8,128)(2,1)S(1)}, f32[2,264,128]{2,1,0:T(8,128)S(1)}, f32[4,264,128]{2,1,0:T(8,128)S(1)}) custom-call(s32[2]{0:T(128)} %live.7, f32[2,2,2,256,256]{4,3,2,1,0:T(8,128)} %pivot.3, f32[2,2,2,256,256]{4,3,2,1,0:T(8,128)} %factor.7, f32[2,2]{1,0:T(2,128)} %weight.7), custom_call_target="tpu_custom_call" | custom-call | flops 1 | bytes 1 | tf_op jit(solution)/shard_map/pallas_call | solution.py:286
  3.4 0.0 copy-start.1
  3.4 0.0 copy-start.2
  3.4 3.2 %collective-permute-start.1 = (f32[2,264,128]{2,1,0:T(8,128)S(1)}, f32[2,264,128]{2,1,0:T(8,128)S(1)}, u32[]{:S(2)}, u32[]{:S(2)}) collective-permute-start(f32[2,264,128]{2,1,0:T(8,128)S(1)} %get-tuple-element.38.e), channel_id=1, source_target_pairs={{0,1},{8,9},{16,17},{24,25},{2,3},{3,2},{4,5},{5,4},{6,7},{7,6},{1... | collective-permute-start | bytes 811016 | tf_op jit(solution)/shard_map/ppermute | solution.py:335
  6.7 0.0 copy-done
  6.7 0.0 copy-done.3
  6.7 1.3 %shard_map.60 = (bf16[4,256,256]{2,1,0:T(8,128)(2,1)S(1)}, bf16[4,256,256]{2,1,0:T(8,128)(2,1)S(1)}, bf16[4,256,256]{2,1,0:T(8,128)(2,1)S(1)}, bf16[4,256,256]{2,1,0:T(8,128)(2,1)S(1)}, f32[2,256,256]{2,1,0:T(8,128)S(1)}) custom-call(s32[2]{0:T(128)S(1)} %copy-done.3, f32[2,2,2,256,256]{4,3,2,1,0:T(8,128)S(1)} %copy-done, ...), custom_call_target="tpu_custom_call" | custom-call | flops 1 | bytes 1 | tf_op jit(solution)/shard_map/pallas_call | solution.py:286
  8.0 2.2 %collective-permute-start = (f32[2,256,256]{2,1,0:T(8,128)S(1)}, f32[2,256,256]{2,1,0:T(8,128)S(1)}, u32[]{:S(2)}, u32[]{:S(2)}) collective-permute-start(f32[2,256,256]{2,1,0:T(8,128)S(1)} %get-tuple-element.34.refs_0_), channel_id=1, source_target_pairs={{2,3},{3,2},{4,5},{5,4},{6,7},{7,6},{10,11},{11,10},{12,13},{13,12... | collective-permute-start | bytes 1572872 | tf_op jit(solution)/shard_map/ppermute | solution.py:339
  10.2 0.0 copy-done.1
  10.2 1.8 %shard_map.61 = (bf16[4,256,256]{2,1,0:T(8,128)(2,1)S(1)}, f32[2,264,128]{2,1,0:T(8,128)S(1)}, f32[4,264,128]{2,1,0:T(8,128)S(1)}) custom-call(s32[2]{0:T(128)S(1)} %copy-done.3, f32[2,2,2,256,256]{4,3,2,1,0:T(8,128)S(1)} %copy-done.1, f32[2,2,2,256,256]{4,3,2,1,0:T(8,128)S(1)} %copy-done, f32[2,2]{1,0:T(2,128)S(1)} %copy-done.2, ...), custom_call_target="tpu_custom_call" | custom-call | flops 1 | bytes 1 | tf_op jit(solution)/shard_map/pallas_call | solution.py:286
  12.0 0.7 collective-permute-start.2
  12.7 0.1 collective-permute-done.1.e_in.refs_0_.x_first
  12.8 0.7 collective-permute-start.4
  13.5 1.3 %shard_map.62 = (bf16[4,256,256]{2,1,0:T(8,128)(2,1)S(1)}, bf16[4,256,256]{2,1,0:T(8,128)(2,1)S(1)}, bf16[4,256,256]{2,1,0:T(8,128)(2,1)S(1)}, bf16[4,256,256]{2,1,0:T(8,128)(2,1)S(1)}, f32[2,256,256]{2,1,0:T(8,128)S(1)}) custom-call(s32[2]{0:T(128)S(1)} %copy-done.3, f32[2,2,2,256,256]{4,3,2,1,0:T(8,128)S(1)} %copy-done, ...), custom_call_target="tpu_custom_call" | custom-call | flops 1 | bytes 1 | tf_op jit(solution)/shard_map/pallas_call | solution.py:286
  14.8 0.0 collective-permute-done.2.e_second.refs_0_
  14.8 0.7 collective-permute-start.3
  15.5 0.0 collective-permute-done.4
  15.5 0.7 collective-permute-start.5
  16.2 7.8 %collective-permute-done.g_in = f32[2,256,256]{2,1,0:T(8,128)S(1)} collective-permute-done((f32[2,256,256]{2,1,0:T(8,128)S(1)}, f32[2,256,256]{2,1,0:T(8,128)S(1)}, u32[]{:S(2)}, u32[]{:S(2)}) %collective-permute-start) | collective-permute-done | bytes 524320 | tf_op jit(solution)/shard_map/ppermute | solution.py:339
  24.0 1.7 %shard_map.63 = (bf16[4,256,256]{2,1,0:T(8,128)(2,1)S(1)}, bf16[4,256,256]{2,1,0:T(8,128)(2,1)S(1)}, f32[2,264,128]{2,1,0:T(8,128)S(1)}, bf16[4,256,256]{2,1,0:T...) custom-call(f32[2,256,256]{2,1,0:T(8,128)S(1)} %get-tuple-element.36.g, ...), custom_call_target="tpu_custom_call" | custom-call | flops 99999997952 | bytes 1 | tf_op jit(solution)/shard_map/pallas_call | solution.py:286
  25.7 0.0 collective-permute-done.3.refs_0_
  25.7 0.0 collective-permute-done.5.refs_1_
  25.8 0.7 collective-permute-start.6
  26.5 0.0 collective-permute-done.6.refs_0_.refs_2_
  26.5 1.5 %collective-permute-start.7 = (f32[2,264,128]{2,1,0:T(8,128)S(1)}, f32[2,264,128]{2,1,0:T(8,128)S(1)}, u32[]{:S(2)}, u32[]{:S(2)}) collective-permute-start(f32[2,264,128]{2,1,0:T(8,128)S(1)} %shard_map.67), channel_id=1, source_target_pairs={{5,7},{4,6},{13,15},{12,14},{21,23},{20,22},{29,31},{28,30}} | collective-permute-start | bytes 811016 | tf_op jit(solution)/shard_map/ppermute | solution.py:375
  28.0 11.5 %collective-permute-done.7.refs_3_ = f32[2,264,128]{2,1,0:T(8,128)S(1)} collective-permute-done((f32[2,264,128]{2,1,0:T(8,128)S(1)}, f32[2,264,128]{2,1,0:T(8,128)S(1)}, u32[]{:S(2)}, u32[]{:S(2)}) %collective-permute-start.7) | collective-permute-done | bytes 270368 | tf_op jit(solution)/shard_map/ppermute | solution.py:375
  39.5 1.2 %shard_map.68 = (f32[2,264,128]{2,1,0:T(8,128)S(1)}, f32[2,264,128]{2,1,0:T(8,128)S(1)}) custom-call(bf16[4,256,256]{2,1,0:T(8,128)(2,1)S(1)} %get-tuple-element.39.fas, bf16[4,256,256]{2,1,0:T(8,128)(2,1)S(1)} %get-tuple-element.40.fat, f32[2,264,128]{2,1,0:T(8,128)S(1)} %get-tuple-element.41.ea, f32[2,264,128]{2,1,0:T(8,128)S(1)} %collective-permute-done.3.refs_0_, ...), custom_call_target="tpu_custom_call" | custom-call | flops 1 | bytes 1 | tf_op jit(solution)/shard_map/pallas_call | solution.py:286
  40.7 4.6 %collective-permute-start.8 = (f32[2,264,128]{2,1,0:T(8,128)S(1)}, f32[2,264,128]{2,1,0:T(8,128)S(1)}, u32[]{:S(2)}, u32[]{:S(2)}) collective-permute-start(f32[2,264,128]{2,1,0:T(8,128)S(1)} %get-tuple-element.49), channel_id=1, source_target_pairs={{0,1},{1,0},{2,3},{3,2},{4,5},{5,4},{6,7},{7,6},{8,9},{9,8},{10,11... | collective-permute-start | bytes 811016 | tf_op jit(solution)/shard_map/ppermute | solution.py:384
  45.3 2.0 %shard_map.69 = (f32[2,512,128]{2,1,0:T(8,128)S(1)}, f32[2,264,128]{2,1,0:T(8,128)S(1)}) custom-call(f32[2,2]{1,0:T(2,128)S(1)} %copy-done.2, f32[2,264,128]{2,1,0:T(8,128)S(1)} %get-tuple-element.53.x, bf16[4,256,256]{2,1,0:T(8,128)(2,1)S(1)} %get-tuple-element.54.f0s, bf16[4,256,256]{2,1,0:T(8,128)(2,1)S(1)} %get-tuple-element.55.f0t, ...), custom_call_target="tpu_custom_call" | custom-call | flops 1 | bytes 1 | tf_op jit(solution)/shard_map/pallas_call | solution.py:286
  47.3 1.8 %collective-permute-done.8.x = f32[2,264,128]{2,1,0:T(8,128)S(1)} collective-permute-done((f32[2,264,128]{2,1,0:T(8,128)S(1)}, f32[2,264,128]{2,1,0:T(8,128)S(1)}, u32[]{:S(2)}, u32[]{:S(2)}) %collective-permute-start.8) | collective-permute-done | bytes 270368 | tf_op jit(solution)/shard_map/ppermute | solution.py:384
  49.1 1.5 %shard_map.70 = (f32[2,512,128]{2,1,0:T(8,128)S(1)}, bf16[4,256,256]{2,1,0:T(8,128)(2,1)S(1)}, bf16[4,256,256]{2,1,0:T(8,128)(2,1)S(1)}) custom-call(f32[2,2]{1,0:T(2,128)S(1)} %copy-done.2, f32[2,264,128]{2,1,0:T(8,128)S(1)} %collective-permute-done.8.x, f32[2,264,128]{2,1,0:T(8,128)S(1)} %collective-permute-done.1.e_in.refs_0_.x_first, ...), custom_call_target="tpu_custom_call" | custom-call | flops 1 | bytes 1 | tf_op jit(solution)/shard_map/pallas_call | solution.py:286
  50.7 3.8 %collective-permute-start.12 = (f32[512,128]{1,0:T(8,128)S(1)}, f32[512,128]{1,0:T(8,128)S(1)}, u32[]{:S(2)}, u32[]{:S(2)}) collective-permute-start(f32[512,128]{1,0:T(8,128)S(1)} %slice_bitcast_fusion), channel_id=1, source_target_pairs={{0,8},{8,0},{16,24},{24,16},{1,9},{9,1},{17,25},{25,17},{2,10},{10... | collective-permute-start | bytes 786440 | tf_op jit(solution)/shard_map/ppermute | solution.py:397
  54.5 0.6 shard_map.71
  55.1 0.1 collective-permute-start.9
  55.2 0.5 collective-permute-done.12
  55.7 0.3 collective-permute-start.13
  56.0 0.5 collective-permute-done.9
  56.5 0.8 %collective-permute-start.10 = (f32[264,128]{1,0:T(8,128)S(1)}, f32[264,128]{1,0:T(8,128)S(1)}, u32[]{:S(2)}, u32[]{:S(2)}) collective-permute-start(f32[264,128]{1,0:T(8,128)S(1)} %fusion), channel_id=1, source_target_pairs={{0,16},{8,24},{16,0},{24,8},{1,17},{9,25},{17,1},{25,9},{2,18},{10... | collective-permute-start | bytes 405512 | tf_op jit(solution)/shard_map/ppermute | solution.py:397
  57.3 6.0 %collective-permute-done.13 = f32[512,128]{1,0:T(8,128)S(1)} collective-permute-done((f32[512,128]{1,0:T(8,128)S(1)}, f32[512,128]{1,0:T(8,128)S(1)}, u32[]{:S(2)}, u32[]{:S(2)}) %collective-permute-start.13) | collective-permute-done | bytes 262176 | tf_op jit(solution)/shard_map/ppermute | solution.py:397
  63.3 2.1 %collective-permute-start.14 = (f32[512,128]{1,0:T(8,128)S(1)}, f32[512,128]{1,0:T(8,128)S(1)}, u32[]{:S(2)}, u32[]{:S(2)}) collective-permute-start(f32[512,128]{1,0:T(8,128)S(1)} %add.15.mine), channel_id=1, source_target_pairs={{0,8},{8,0},{16,24},{24,16},{1,9},{9,1},{17,25},{25,17},{2,10},{10... | collective-permute-start | bytes 786440 | tf_op jit(solution)/shard_map/ppermute | solution.py:397
  65.3 0.8 %collective-permute-done.10 = f32[264,128]{1,0:T(8,128)S(1)} collective-permute-done((f32[264,128]{1,0:T(8,128)S(1)}, f32[264,128]{1,0:T(8,128)S(1)}, u32[]{:S(2)}, u32[]{:S(2)}) %collective-permute-start.10) | collective-permute-done | bytes 135200 | tf_op jit(solution)/shard_map/ppermute | solution.py:397
  66.2 1.3 %collective-permute-start.11 = (f32[264,128]{1,0:T(8,128)S(1)}, f32[264,128]{1,0:T(8,128)S(1)}, u32[]{:S(2)}, u32[]{:S(2)}) collective-permute-start(f32[264,128]{1,0:T(8,128)S(1)} %add.13.mine), channel_id=1, source_target_pairs={{0,8},{8,0},{16,24},{24,16},{1,9},{9,1},{17,25},{25,17},{2,10},{10... | collective-permute-start | bytes 405512 | tf_op jit(solution)/shard_map/ppermute | solution.py:397
  67.4 0.0 collective-permute-done.14.theirs
  67.4 0.8 %shard_map.72 = (f32[2,256,256]{2,1,0:T(8,128)}, f32[8,128]{1,0:T(8,128)S(1)}) custom-call(f32[512,128]{1,0:T(8,128)S(1)} %add.15.mine, f32[512,128]{1,0:T(8,128)S(1)} %collective-permute-done.14.theirs), custom_call_target="tpu_custom_call" | custom-call | flops 1 | bytes 1 | tf_op jit(solution)/shard_map/pallas_call | solution.py:286
  68.3 0.1 collective-permute-done.11.theirs
  68.4 0.9 %shard_map.73 = f32[2,256,256]{2,1,0:T(8,128)} custom-call(f32[264,128]{1,0:T(8,128)S(1)} %add.13.mine, f32[264,128]{1,0:T(8,128)S(1)} %collective-permute-done.11.theirs, f32[8,128]{1,0:T(8,128)S(1)} %get-tuple-element.62._), custom_call_target="tpu_custom_call" | custom-call | flops 1 | bytes 1 | tf_op jit(solution)/shard_map/pallas_call | solution.py:286
  (11 shorter events, 0.2 us)
Async XLA Ops:
  0.6 6.0 %copy-start = (f32[2,2,2,256,256]{4,3,2,1,0:T(8,128)S(1)}, f32[2,2,2,256,256]{4,3,2,1,0:T(8,128)}, u32[]{:S(2)}) copy-start(f32[2,2,2,256,256]{4,3,2,1,0:T(8,128)} %factor.7) | copy-start | bytes 6291460
  0.6 6.0 %copy-start.3 = (s32[2]{0:T(128)S(1)}, s32[2]{0:T(128)}, u32[]{:S(2)}) copy-start(s32[2]{0:T(128)} %live.7) | copy-start | bytes 28
  3.4 6.8 %copy-start.1 = (f32[2,2,2,256,256]{4,3,2,1,0:T(8,128)S(1)}, f32[2,2,2,256,256]{4,3,2,1,0:T(8,128)}, u32[]{:S(2)}) copy-start(f32[2,2,2,256,256]{4,3,2,1,0:T(8,128)} %pivot.3) | copy-start | bytes 6291460
  3.4 6.8 %copy-start.2 = (f32[2,2]{1,0:T(2,128)S(1)}, f32[2,2]{1,0:T(2,128)}, u32[]{:S(2)}) copy-start(f32[2,2]{1,0:T(2,128)} %weight.7) | copy-start | bytes 52
  3.4 9.4 %collective-permute-start.1 = (f32[2,264,128]{2,1,0:T(8,128)S(1)}, f32[2,264,128]{2,1,0:T(8,128)S(1)}, u32[]{:S(2)}, u32[]{:S(2)}) collective-permute-start(f32[2,264,128]{2,1,0:T(8,128)S(1)} %get-tuple-element.38.e), channel_id=1, source_target_pairs={{0,1},{8,9},{16,17},{24,25},{2,3},{3,2},{4,5},{5,4},{6,7},{7,6},{1... | collective-permute-start | bytes 811016 | tf_op jit(solution)/shard_map/ppermute | solution.py:335
  8.0 16.0 %collective-permute-start = (f32[2,256,256]{2,1,0:T(8,128)S(1)}, f32[2,256,256]{2,1,0:T(8,128)S(1)}, u32[]{:S(2)}, u32[]{:S(2)}) collective-permute-start(f32[2,256,256]{2,1,0:T(8,128)S(1)} %get-tuple-element.34.refs_0_), channel_id=1, source_target_pairs={{2,3},{3,2},{4,5},{5,4},{6,7},{7,6},{10,11},{11,10},{12,13},{13,12... | collective-permute-start | bytes 1572872 | tf_op jit(solution)/shard_map/ppermute | solution.py:339
  12.0 2.8 %collective-permute-start.2 = (f32[2,264,128]{2,1,0:T(8,128)S(1)}, f32[2,264,128]{2,1,0:T(8,128)S(1)}, u32[]{:S(2)}, u32[]{:S(2)}) collective-permute-start(f32[2,264,128]{2,1,0:T(8,128)S(1)} %get-tuple-element.37.e), channel_id=1, source_target_pairs={{0,1},{8,9},{16,17},{24,25}} | collective-permute-start | bytes 811016 | tf_op jit(solution)/shard_map/ppermute | solution.py:349
  12.8 2.7 %collective-permute-start.4 = (f32[2,264,128]{2,1,0:T(8,128)S(1)}, f32[2,264,128]{2,1,0:T(8,128)S(1)}, u32[]{:S(2)}, u32[]{:S(2)}) collective-permute-start(f32[2,264,128]{2,1,0:T(8,128)S(1)} %shard_map.65), channel_id=1, source_target_pairs={{1,0},{9,8},{17,16},{25,24}} | collective-permute-start | bytes 811016 | tf_op jit(solution)/shard_map/ppermute | solution.py:353
  14.8 10.9 %collective-permute-start.3 = (f32[2,264,128]{2,1,0:T(8,128)S(1)}, f32[2,264,128]{2,1,0:T(8,128)S(1)}, u32[]{:S(2)}, u32[]{:S(2)}) collective-permute-start(f32[2,264,128]{2,1,0:T(8,128)S(1)} %shard_map.64), channel_id=1, source_target_pairs={{1,3},{9,11},{17,19},{25,27}} | collective-permute-start | bytes 811016 | tf_op jit(solution)/shard_map/ppermute | solution.py:358
  15.5 10.2 %collective-permute-start.5 = (f32[2,264,128]{2,1,0:T(8,128)S(1)}, f32[2,264,128]{2,1,0:T(8,128)S(1)}, u32[]{:S(2)}, u32[]{:S(2)}) collective-permute-start(f32[2,264,128]{2,1,0:T(8,128)S(1)} %collective-permute-done.4), channel_id=1, source_target_pairs={{0,2},{8,10},{16,18},{24,26}} | collective-permute-start | bytes 811016 | tf_op jit(solution)/shard_map/ppermute | solution.py:359
  25.8 0.7 collective-permute-start.6
  26.5 12.9 %collective-permute-start.7 = (f32[2,264,128]{2,1,0:T(8,128)S(1)}, f32[2,264,128]{2,1,0:T(8,128)S(1)}, u32[]{:S(2)}, u32[]{:S(2)}) collective-permute-start(f32[2,264,128]{2,1,0:T(8,128)S(1)} %shard_map.67), channel_id=1, source_target_pairs={{5,7},{4,6},{13,15},{12,14},{21,23},{20,22},{29,31},{28,30}} | collective-permute-start | bytes 811016 | tf_op jit(solution)/shard_map/ppermute | solution.py:375
  40.7 8.4 %collective-permute-start.8 = (f32[2,264,128]{2,1,0:T(8,128)S(1)}, f32[2,264,128]{2,1,0:T(8,128)S(1)}, u32[]{:S(2)}, u32[]{:S(2)}) collective-permute-start(f32[2,264,128]{2,1,0:T(8,128)S(1)} %get-tuple-element.49), channel_id=1, source_target_pairs={{0,1},{1,0},{2,3},{3,2},{4,5},{5,4},{6,7},{7,6},{8,9},{9,8},{10,11... | collective-permute-start | bytes 811016 | tf_op jit(solution)/shard_map/ppermute | solution.py:384
  50.7 5.0 %collective-permute-start.12 = (f32[512,128]{1,0:T(8,128)S(1)}, f32[512,128]{1,0:T(8,128)S(1)}, u32[]{:S(2)}, u32[]{:S(2)}) collective-permute-start(f32[512,128]{1,0:T(8,128)S(1)} %slice_bitcast_fusion), channel_id=1, source_target_pairs={{0,8},{8,0},{16,24},{24,16},{1,9},{9,1},{17,25},{25,17},{2,10},{10... | collective-permute-start | bytes 786440 | tf_op jit(solution)/shard_map/ppermute | solution.py:397
  55.1 1.4 %collective-permute-start.9 = (f32[264,128]{1,0:T(8,128)S(1)}, f32[264,128]{1,0:T(8,128)S(1)}, u32[]{:S(2)}, u32[]{:S(2)}) collective-permute-start(f32[264,128]{1,0:T(8,128)S(1)} %slice_bitcast_fusion.1), channel_id=1, source_target_pairs={{0,8},{8,0},{16,24},{24,16},{1,9},{9,1},{17,25},{25,17},{2,10},{10... | collective-permute-start | bytes 405512 | tf_op jit(solution)/shard_map/ppermute | solution.py:397
  55.7 7.6 %collective-permute-start.13 = (f32[512,128]{1,0:T(8,128)S(1)}, f32[512,128]{1,0:T(8,128)S(1)}, u32[]{:S(2)}, u32[]{:S(2)}) collective-permute-start(f32[512,128]{1,0:T(8,128)S(1)} %bitcast_add_fusion), channel_id=1, source_target_pairs={{0,16},{8,24},{16,0},{24,8},{1,17},{9,25},{17,1},{25,9},{2,18},{10... | collective-permute-start | bytes 786440 | tf_op jit(solution)/shard_map/ppermute | solution.py:397
  56.5 9.6 %collective-permute-start.10 = (f32[264,128]{1,0:T(8,128)S(1)}, f32[264,128]{1,0:T(8,128)S(1)}, u32[]{:S(2)}, u32[]{:S(2)}) collective-permute-start(f32[264,128]{1,0:T(8,128)S(1)} %fusion), channel_id=1, source_target_pairs={{0,16},{8,24},{16,0},{24,8},{1,17},{9,25},{17,1},{25,9},{2,18},{10... | collective-permute-start | bytes 405512 | tf_op jit(solution)/shard_map/ppermute | solution.py:397
  63.3 4.2 %collective-permute-start.14 = (f32[512,128]{1,0:T(8,128)S(1)}, f32[512,128]{1,0:T(8,128)S(1)}, u32[]{:S(2)}, u32[]{:S(2)}) collective-permute-start(f32[512,128]{1,0:T(8,128)S(1)} %add.15.mine), channel_id=1, source_target_pairs={{0,8},{8,0},{16,24},{24,16},{1,9},{9,1},{17,25},{25,17},{2,10},{10... | collective-permute-start | bytes 786440 | tf_op jit(solution)/shard_map/ppermute | solution.py:397
  66.2 2.3 %collective-permute-start.11 = (f32[264,128]{1,0:T(8,128)S(1)}, f32[264,128]{1,0:T(8,128)S(1)}, u32[]{:S(2)}, u32[]{:S(2)}) collective-permute-start(f32[264,128]{1,0:T(8,128)S(1)} %add.13.mine), channel_id=1, source_target_pairs={{0,8},{8,0},{16,24},{24,16},{1,9},{9,1},{17,25},{25,17},{2,10},{10... | collective-permute-start | bytes 405512 | tf_op jit(solution)/shard_map/ppermute | solution.py:397
where the time goes:
time: 70.2 us; the launch traced here: 69.3 us
  waiting for transfers between devices  29.1 us (41%)
  starting transfers between devices  23.1 us (33%)
  Pallas kernels  16 us (23%)
  between operations  0.91 us (1%)
    pallas_call x15, Pallas kernels, run(): pl.pallas_call(kernel, out_shape=shapes, in_specs=[SCALAR] * len(scalars)...  16 us
    ppermute x2, waiting for transfers between devices, local(): arrived = [lax.ppermute(wave, AXES, up)]  11.5 us
    ppermute x6, starting transfers between devices, exchanged(): lax.ppermute(value, 'pole', [(p, p ^ distance) for p in range(poles)])  8.29 us
    ppermute x6, waiting for transfers between devices, exchanged(): lax.ppermute(value, 'pole', [(p, p ^ distance) for p in range(poles)])  7.89 us
    ppermute x1, waiting for transfers between devices, local(): g_in = lax.ppermute(o_g, AXES, swaps)  7.82 us
    ppermute x1, starting transfers between devices, local(): shared = lax.ppermute(sent, AXES, every)  4.58 us
    ppermute x1, starting transfers between devices, local(): e_in = lax.ppermute(o_e, AXES, first + swaps)  3.25 us
    ppermute x1, starting transfers between devices, local(): g_in = lax.ppermute(o_g, AXES, swaps)  2.17 us
  transfers between devices with their start and end apart: 15, of which 9 were waited for; matrix products, arithmetic and copies ran while one was open for 0% of the time, Pallas kernels for 14%

commit v1 on v0

--- a/solution.py
+++ b/solution.py
@@ -137,7 +137,7 @@
     weighted[3, : width - 8] = weighted_b[width + 8 :]
 
 
-def factor_kernel(hosted, live, factor, f1s, f0s, f0t, gs, gt, g):
+def factor_kernel(hosted, live, factor, f1s, passed, f0s, f0t, gs, gt, g, handed):
     slot = slot_of(hosted)
     _, column = rows_columns(factor.shape[-1])
     f0 = [jnp.where(column < live[0], factor[slot, 0, c], 0.0) for c in range(2)]
@@ -148,6 +148,7 @@
     store4(gt, split_pair(gr.T, gi.T))
     store4(f0s, s0)
     store4(f0t, split_pair(f0[0].T, f0[1].T))
+    handed[...] = passed[...]
 
 
 def fold(x, gs, gt, e, out):
@@ -157,10 +158,19 @@
     out[1] = e[1] + packed(yi)
 
 
-def step_kernel(active, gs, gt, e, *refs):
+def start_kernel(gs, gt, e, x_core0, x_core1, out):
+    place, _, core = whereabouts()
+    for x, its_core in ((x_core0, 0), (x_core1, 1)):
+
+        @pl.when(jnp.logical_and(place == 1, core == its_core))
+        def _():
+            fold(unpacked_split(x), gs, gt, e, out)
+
+
+def step_kernel(turn, gs, gt, e, *refs):
     *received, out = refs
 
-    @pl.when(active(whereabouts()[0]))
+    @pl.when(lax.div(whereabouts()[0], 2) == turn)
     def _():
         value = received[0][...]
         for other in received[1:]:
@@ -168,12 +178,19 @@
         fold(split_pair(unpacked(value[0]), unpacked(value[1])), gs, gt, e, out)
 
 
-def pair_kernel(g, e, g_in, e_in, e_second, fas, fat, ea, ps, pt, ep):
-    upper = whereabouts()[0] > 1
-    is_odd = whereabouts()[1] == 1
+def pair_kernel(g, e, g_in, e_core0, e_core1, later_core0, later_core1, fas, fat, ea, ps, pt, ep):
+    place, odd, core = whereabouts()
+    is_odd, first_core, upper = odd == 1, core == 0, place > 1
     ga = [jnp.where(is_odd, g_in[c], g[c]) for c in range(2)]
     gb = [jnp.where(is_odd, g[c], g_in[c]) for c in range(2)]
-    theirs = [jnp.where(upper, e_in[c], e_second[c]) for c in range(2)]
+    theirs = [
+        jnp.where(
+            upper,
+            jnp.where(first_core, e_core0[c], e_core1[c]),
+            jnp.where(first_core, later_core0[c], later_core1[c]),
+        )
+        for c in range(2)
+    ]
     low = [jnp.where(is_odd, theirs[c], e[c]) for c in range(2)]
     high = [jnp.where(is_odd, e[c], theirs[c]) for c in range(2)]
     sa, sb = split_pair(*ga), split_pair(*gb)
@@ -237,10 +254,12 @@
     diag[core], diag[1 - core] = diag_values(us, ts, f0t, gt, weighted)
 
 
-def more_off_kernel(weight, x, x_first, f0s, f0t, gs, weighted, before, off, us_out, ts_out):
+def more_off_kernel(weight, x, x_core0, x_core1, f0s, f0t, gs, weighted, before, off, us_out, ts_out):
     core = whereabouts()[2]
     upper = whereabouts()[0] > 1
-    x = [jnp.where(upper, x[c], x_first[c]) for c in range(2)]
+    x = [
+        jnp.where(upper, x[c], jnp.where(core == 0, x_core0[c], x_core1[c])) for c in range(2)
+    ]
     xs = split_pair(unpacked(x[0]), unpacked(x[1]))
     first, second, us, ts = off_values(slot_of(False), weight, xs, f0s, f0t, gs, weighted)
     off[core] = first + before[core]
@@ -311,7 +330,13 @@
         return at(pole, 2 * row + 1), at(pole, 2 * row)
 
     swaps = [(at(p, s), at(p, s ^ 1)) for p in range(poles) for s in range(2, turns)]
-    first = [(at(p, 0), at(p, 1)) for p in range(poles)]
+
+    def first(core):
+        return [(at(p, 0), at(p, 1)) for p in range(core, poles, 2)]
+
+    def swaps_of(core):
+        return [(at(p, s), at(p, s ^ 1)) for p in range(core, poles, 2) for s in range(2, turns)]
+
     every = [(at(p, s), at(p, s ^ 1)) for p in range(poles) for s in range(turns)]
     constants = [parts, mirrored, jax.ShapeDtypeStruct((4,) + quarter, F32)]
     factors = [parts, parts, parts, parts, jax.ShapeDtypeStruct((2, width, width), F32)]
@@ -332,10 +357,11 @@
             pltpu.with_memory_space_constraint(a, pltpu.HBM) for a in (live, pivot, factor, weight)
         ],
     )
-    e_in = lax.ppermute(o_e, AXES, first + swaps)
-    o_f0s, o_f0t, o_gs, o_gt, o_g = run(
-        functools.partial(factor_kernel, False), [live], [factor, o_f1s], factors
-    )
+    e_core1 = lax.ppermute(o_e, AXES, first(1) + swaps_of(1))
+    o_f0s, o_f0t, o_gs, o_gt, o_g, e_late = run(
+        functools.partial(factor_kernel, False), [live], [factor, o_f1s, o_e], [*factors, mirrored]
+    )
+    e_core0 = lax.ppermute(e_late, AXES, first(0) + swaps_of(0))
     g_in = lax.ppermute(o_g, AXES, swaps)
     m_f1s, m_e, m_w = run(
         functools.partial(constant_kernel, True, False),
@@ -343,15 +369,15 @@
         [pivot, factor, weight, o_g],
         constants,
     )
-    m_f0s, m_f0t, m_gs, m_gt, m_g = run(
-        functools.partial(factor_kernel, True), [live], [factor, m_f1s], factors
-    )
-    e_second = lax.ppermute(m_e, AXES, first)
-
-    starts = functools.partial(step_kernel, lambda place: place == 1)
-    (wave_even,) = run(starts, [], [o_gs, o_gt, o_e, e_in], [mirrored])
+    later_core1 = lax.ppermute(m_e, AXES, first(1))
+    m_f0s, m_f0t, m_gs, m_gt, m_g, e_late = run(
+        functools.partial(factor_kernel, True), [live], [factor, m_f1s, m_e], [*factors, mirrored]
+    )
+    later_core0 = lax.ppermute(e_late, AXES, first(0))
+
+    (wave_even,) = run(start_kernel, [], [o_gs, o_gt, o_e, e_core0, e_core1], [mirrored])
     wave_even = lax.ppermute(wave_even, AXES, [(at(p, 1), at(p, 0)) for p in range(poles)])
-    (wave_odd,) = run(starts, [], [m_gs, m_gt, m_e, e_second], [mirrored])
+    (wave_odd,) = run(start_kernel, [], [m_gs, m_gt, m_e, later_core0, later_core1], [mirrored])
     received = []
     if rows > 1:
         received = [
@@ -363,14 +389,15 @@
     fas, fat, ea, ps, pt, ep = run(
         pair_kernel,
         [],
-        [m_g, m_e, g_in, e_in, e_second],
+        [m_g, m_e, g_in, e_core0, e_core1, later_core0, later_core1],
         [parts, parts, mirrored, parts, parts, mirrored],
         cost=LONG,
     )
     arrived = list(received)
     for turn in range(1, rows - 1):
-        active = functools.partial(step_kernel, lambda place, turn=turn: lax.div(place, 2) == turn)
-        (wave,) = run(active, [], [ps, pt, ep] + arrived, [mirrored])
+        (wave,) = run(
+            functools.partial(step_kernel, turn), [], [ps, pt, ep] + arrived, [mirrored]
+        )
         up = [pair for p in range(poles) for pair in zip(hosts(turn, p), hosts(turn + 1, p))]
         arrived = [lax.ppermute(wave, AXES, up)]
         received += arrived
@@ -389,7 +416,7 @@
     off, us, ts = run(
         more_off_kernel,
         [],
-        [weight, shared, e_in, o_f0s, o_f0t, o_gs, o_w, off],
+        [weight, shared, e_core0, e_core1, o_f0s, o_f0t, o_gs, o_w, off],
         [offs, parts, parts],
     )
 

time: 70.2 us -> 73.4 us (1.046)
  waiting for transfers between devices: 29.1 us -> 33.9 us
  starting transfers between devices: 23.1 us -> 22.1 us
    ppermute x1, starting transfers between devices: 4.58 us -> 1.22 us  [local(): shared = lax.ppermute(sent, AXES, every)]
    ppermute x2, waiting for transfers between devices: 11.5 us -> 14.4 us  [local(): arrived = [lax.ppermute(wave, AXES, up)]]
    ppermute x1, waiting for transfers between devices: 7.82 us -> 9.12 us  [local(): g_in = lax.ppermute(o_g, AXES, swaps)]
    ppermute x2 -> x4, starting transfers between devices: 3.93 us -> 5.15 us  [the longest x1 3.12 us: local(): e_core1 = lax.ppermute(o_e, AXES, first(1) + swaps_of(1))]
    ppermute x6, starting transfers between devices: 8.29 us -> 9.41 us  [exchanged(): lax.ppermute(value, 'pole', [(p, p ^ distance) for p in range(poles)])]
  transfers between devices with their start and end apart: 15 -> 17, of which waited for: 9 -> 9; matrix products, arithmetic and copies ran while one was open for 0% -> 0% of each run, Pallas kernels for 14% -> 11%
where the time goes in v1:
time: 73.4 us; the launch traced here: 73.2 us
  waiting for transfers between devices  33.9 us (46%)
  starting transfers between devices  22.1 us (30%)
  Pallas kernels  16.1 us (22%)
  between operations  0.94 us (1%)
    pallas_call x15, Pallas kernels, run(): pl.pallas_call(kernel, out_shape=shapes, in_specs=[SCALAR] * len(scalars)...  16.1 us
    ppermute x2, waiting for transfers between devices, local(): arrived = [lax.ppermute(wave, AXES, up)]  14.4 us
    ppermute x6, starting transfers between devices, exchanged(): lax.ppermute(value, 'pole', [(p, p ^ distance) for p in range(poles)])  9.41 us
    ppermute x1, waiting for transfers between devices, local(): g_in = lax.ppermute(o_g, AXES, swaps)  9.12 us
    ppermute x6, waiting for transfers between devices, exchanged(): lax.ppermute(value, 'pole', [(p, p ^ distance) for p in range(poles)])  8.05 us
    ppermute x1, starting transfers between devices, local(): e_core1 = lax.ppermute(o_e, AXES, first(1) + swaps_of(1))  3.12 us
    ppermute x1, starting transfers between devices, local(): g_in = lax.ppermute(o_g, AXES, swaps)  2.17 us
    ppermute x1, waiting for transfers between devices, local(): shared = lax.ppermute(sent, AXES, every)  2.16 us
  transfers between devices with their start and end apart: 17, of which 9 were waited for; matrix products, arithmetic and copies ran while one was open for 0% of the time, Pallas kernels for 11%

profile of v1, /device:TPU:29, one launch (start us, length us, event | category | flops | bytes accessed | tf_op | source)
XLA Modules:
  0.0 73.2 jit_solution(3086391913986918503)
XLA Ops:
  0.6 0.0 copy-start.3
  0.6 2.7 %shard_map.59 = (bf16[4,256,256]{2,1,0:T(8,128)(2,1)S(1)}, f32[2,264,128]{2,1,0:T(8,128)S(1)}, f32[4,264,128]{2,1,0:T(8,128)S(1)}) custom-call(s32[2]{0:T(128)} %live.7, f32[2,2,2,256,256]{4,3,2,1,0:T(8,128)} %pivot.3, f32[2,2,2,256,256]{4,3,2,1,0:T(8,128)} %factor.7, f32[2,2]{1,0:T(2,128)} %weight.7), custom_call_target="tpu_custom_call" | custom-call | flops 1 | bytes 1 | tf_op jit(solution)/shard_map/pallas_call | solution.py:305
  3.4 0.0 copy-start.1
  3.4 0.0 copy-start.2
  3.4 1.3 %shard_map.60 = (bf16[4,256,256]{2,1,0:T(8,128)(2,1)S(1)}, bf16[4,256,256]{2,1,0:T(8,128)(2,1)S(1)}, bf16[4,256,256]{2,1,0:T(8,128)(2,1)S(1)}, bf16[4,256,256]{2...) custom-call(s32[2]{0:T(128)S(1)} %copy-done.3, f32[2,2,2,256,256]{4,3,2,1,0:T(8,128)S(1)} %copy-done, ...), custom_call_target="tpu_custom_call" | custom-call | flops 1 | bytes 1 | tf_op jit(solution)/shard_map/pallas_call | solution.py:305
  4.8 0.7 collective-permute-start.1
  5.5 3.1 %collective-permute-start.2 = (f32[2,264,128]{2,1,0:T(8,128)S(1)}, f32[2,264,128]{2,1,0:T(8,128)S(1)}, u32[]{:S(2)}, u32[]{:S(2)}) collective-permute-start(f32[2,264,128]{2,1,0:T(8,128)S(1)} %get-tuple-element.36.passed.e), channel_id=1, source_target_pairs={{8,9},{24,25},{10,11},{11,10},{12,13},{13,12},{14,15},{15,14},{26,... | collective-permute-start | bytes 811016 | tf_op jit(solution)/shard_map/ppermute | solution.py:360
  8.6 2.2 %collective-permute-start = (f32[2,256,256]{2,1,0:T(8,128)S(1)}, f32[2,256,256]{2,1,0:T(8,128)S(1)}, u32[]{:S(2)}, u32[]{:S(2)}) collective-permute-start(f32[2,256,256]{2,1,0:T(8,128)S(1)} %get-tuple-element.37.refs_0_), channel_id=1, source_target_pairs={{2,3},{3,2},{4,5},{5,4},{6,7},{7,6},{10,11},{11,10},{12,13},{13,12... | collective-permute-start | bytes 1572872 | tf_op jit(solution)/shard_map/ppermute | solution.py:365
  10.8 1.8 %shard_map.61 = (bf16[4,256,256]{2,1,0:T(8,128)(2,1)S(1)}, f32[2,264,128]{2,1,0:T(8,128)S(1)}, f32[4,264,128]{2,1,0:T(8,128)S(1)}) custom-call(s32[2]{0:T(128)S(1)} %copy-done.3, f32[2,2,2,256,256]{4,3,2,1,0:T(8,128)S(1)} %copy-done.1, f32[2,2,2,256,256]{4,3,2,1,0:T(8,128)S(1)} %copy-done, f32[2,2]{1,0:T(2,128)S(1)} %copy-done.2, ...), custom_call_target="tpu_custom_call" | custom-call | flops 1 | bytes 1 | tf_op jit(solution)/shard_map/pallas_call | solution.py:305
  12.6 0.7 collective-permute-start.4
  13.3 1.3 %shard_map.62 = (bf16[4,256,256]{2,1,0:T(8,128)(2,1)S(1)}, bf16[4,256,256]{2,1,0:T(8,128)(2,1)S(1)}, bf16[4,256,256]{2,1,0:T(8,128)(2,1)S(1)}, bf16[4,256,256]{2...) custom-call(s32[2]{0:T(128)S(1)} %copy-done.3, f32[2,2,2,256,256]{4,3,2,1,0:T(8,128)S(1)} %copy-done, ...), custom_call_target="tpu_custom_call" | custom-call | flops 1 | bytes 1 | tf_op jit(solution)/shard_map/pallas_call | solution.py:305
  14.6 0.7 collective-permute-start.3
  15.3 0.0 collective-permute-done.1.e_core0.x_core0
  15.3 0.2 collective-permute-done.2.e_core1.x_core1
  15.5 0.7 collective-permute-start.6
  16.2 0.0 collective-permute-done.3.later_core0.x_core0
  16.2 0.0 collective-permute-done.4.later_core1.x_core1
  16.2 0.7 collective-permute-start.5
  16.9 0.0 collective-permute-done.6
  16.9 0.7 collective-permute-start.7
  17.6 9.1 %collective-permute-done.g_in = f32[2,256,256]{2,1,0:T(8,128)S(1)} collective-permute-done((f32[2,256,256]{2,1,0:T(8,128)S(1)}, f32[2,256,256]{2,1,0:T(8,128)S(1)}, u32[]{:S(2)}, u32[]{:S(2)}) %collective-permute-start) | collective-permute-done | bytes 524320 | tf_op jit(solution)/shard_map/ppermute | solution.py:365
  26.7 1.7 %shard_map.63 = (bf16[4,256,256]{2,1,0:T(8,128)(2,1)S(1)}, bf16[4,256,256]{2,1,0:T(8,128)(2,1)S(1)}, f32[2,264,128]{2,1,0:T(8,128)S(1)}, bf16[4,256,256]{2,1,0:T...) custom-call(f32[2,256,256]{2,1,0:T(8,128)S(1)} %get-tuple-element.40.g, ...), custom_call_target="tpu_custom_call" | custom-call | flops 99999997952 | bytes 1 | tf_op jit(solution)/shard_map/pallas_call | solution.py:305
  28.4 0.0 collective-permute-done.5.refs_0_
  28.4 0.0 collective-permute-done.7.refs_1_
  28.5 0.7 collective-permute-start.8
  29.2 0.0 collective-permute-done.8.refs_0_.refs_2_
  29.2 1.5 %collective-permute-start.9 = (f32[2,264,128]{2,1,0:T(8,128)S(1)}, f32[2,264,128]{2,1,0:T(8,128)S(1)}, u32[]{:S(2)}, u32[]{:S(2)}) collective-permute-start(f32[2,264,128]{2,1,0:T(8,128)S(1)} %shard_map.67), channel_id=1, source_target_pairs={{5,7},{4,6},{13,15},{12,14},{21,23},{20,22},{29,31},{28,30}} | collective-permute-start | bytes 811016 | tf_op jit(solution)/shard_map/ppermute | solution.py:402
  30.7 14.4 %collective-permute-done.9.refs_3_ = f32[2,264,128]{2,1,0:T(8,128)S(1)} collective-permute-done((f32[2,264,128]{2,1,0:T(8,128)S(1)}, f32[2,264,128]{2,1,0:T(8,128)S(1)}, u32[]{:S(2)}, u32[]{:S(2)}) %collective-permute-start.9) | collective-permute-done | bytes 270368 | tf_op jit(solution)/shard_map/ppermute | solution.py:402
  45.0 1.2 %shard_map.68 = (f32[2,264,128]{2,1,0:T(8,128)S(1)}, f32[2,264,128]{2,1,0:T(8,128)S(1)}) custom-call(bf16[4,256,256]{2,1,0:T(8,128)(2,1)S(1)} %get-tuple-element.43.fas, bf16[4,256,256]{2,1,0:T(8,128)(2,1)S(1)} %get-tuple-element.44.fat, f32[2,264,128]{2,1,0:T(8,128)S(1)} %get-tuple-element.45.ea, f32[2,264,128]{2,1,0:T(8,128)S(1)} %collective-permute-done.5.refs_0_, ...), custom_call_target="tpu_custom_call" | custom-call | flops 1 | bytes 1 | tf_op jit(solution)/shard_map/pallas_call | solution.py:305
  46.3 1.2 %collective-permute-start.10 = (f32[2,264,128]{2,1,0:T(8,128)S(1)}, f32[2,264,128]{2,1,0:T(8,128)S(1)}, u32[]{:S(2)}, u32[]{:S(2)}) collective-permute-start(f32[2,264,128]{2,1,0:T(8,128)S(1)} %get-tuple-element.53), channel_id=1, source_target_pairs={{0,1},{1,0},{2,3},{3,2},{4,5},{5,4},{6,7},{7,6},{8,9},{9,8},{10,11... | collective-permute-start | bytes 811016 | tf_op jit(solution)/shard_map/ppermute | solution.py:411
  47.5 2.0 %shard_map.69 = (f32[2,512,128]{2,1,0:T(8,128)S(1)}, f32[2,264,128]{2,1,0:T(8,128)S(1)}) custom-call(f32[2,2]{1,0:T(2,128)S(1)} %copy-done.2, f32[2,264,128]{2,1,0:T(8,128)S(1)} %get-tuple-element.57.x, bf16[4,256,256]{2,1,0:T(8,128)(2,1)S(1)} %get-tuple-element.58.f0s, bf16[4,256,256]{2,1,0:T(8,128)(2,1)S(1)} %get-tuple-element.59.f0t, ...), custom_call_target="tpu_custom_call" | custom-call | flops 1 | bytes 1 | tf_op jit(solution)/shard_map/pallas_call | solution.py:305
  49.5 2.2 %collective-permute-done.10.x = f32[2,264,128]{2,1,0:T(8,128)S(1)} collective-permute-done((f32[2,264,128]{2,1,0:T(8,128)S(1)}, f32[2,264,128]{2,1,0:T(8,128)S(1)}, u32[]{:S(2)}, u32[]{:S(2)}) %collective-permute-start.10) | collective-permute-done | bytes 270368 | tf_op jit(solution)/shard_map/ppermute | solution.py:411
  51.6 1.5 %shard_map.70 = (f32[2,512,128]{2,1,0:T(8,128)S(1)}, bf16[4,256,256]{2,1,0:T(8,128)(2,1)S(1)}, bf16[4,256,256]{2,1,0:T(8,128)(2,1)S(1)}) custom-call(f32[2,2]{1,0:T(2,128)S(1)} %copy-done.2, f32[2,264,128]{2,1,0:T(8,128)S(1)} %collective-permute-done.10.x, f32[2,264,128]{2,1,0:T(8,128)S(1)} %collective-permute-done.1.e_core0.x_core0, ...), custom_call_target="tpu_custom_call" | custom-call | flops 1 | bytes 1 | tf_op jit(solution)/shard_map/pallas_call | solution.py:305
  53.2 5.1 %collective-permute-start.14 = (f32[512,128]{1,0:T(8,128)S(1)}, f32[512,128]{1,0:T(8,128)S(1)}, u32[]{:S(2)}, u32[]{:S(2)}) collective-permute-start(f32[512,128]{1,0:T(8,128)S(1)} %slice_bitcast_fusion), channel_id=1, source_target_pairs={{0,8},{8,0},{16,24},{24,16},{1,9},{9,1},{17,25},{25,17},{2,10},{10... | collective-permute-start | bytes 786440 | tf_op jit(solution)/shard_map/ppermute | solution.py:424
  58.3 0.6 shard_map.71
  58.9 0.1 collective-permute-start.11
  59.0 0.5 collective-permute-done.14
  59.5 0.2 collective-permute-start.15
  59.6 0.7 collective-permute-done.11
  60.3 0.8 %collective-permute-start.12 = (f32[264,128]{1,0:T(8,128)S(1)}, f32[264,128]{1,0:T(8,128)S(1)}, u32[]{:S(2)}, u32[]{:S(2)}) collective-permute-start(f32[264,128]{1,0:T(8,128)S(1)} %fusion), channel_id=1, source_target_pairs={{0,16},{8,24},{16,0},{24,8},{1,17},{9,25},{17,1},{25,9},{2,18},{10... | collective-permute-start | bytes 405512 | tf_op jit(solution)/shard_map/ppermute | solution.py:424
  61.1 6.0 %collective-permute-done.15 = f32[512,128]{1,0:T(8,128)S(1)} collective-permute-done((f32[512,128]{1,0:T(8,128)S(1)}, f32[512,128]{1,0:T(8,128)S(1)}, u32[]{:S(2)}, u32[]{:S(2)}) %collective-permute-start.15) | collective-permute-done | bytes 262176 | tf_op jit(solution)/shard_map/ppermute | solution.py:424
  67.1 2.1 %collective-permute-start.16 = (f32[512,128]{1,0:T(8,128)S(1)}, f32[512,128]{1,0:T(8,128)S(1)}, u32[]{:S(2)}, u32[]{:S(2)}) collective-permute-start(f32[512,128]{1,0:T(8,128)S(1)} %add.15.mine), channel_id=1, source_target_pairs={{0,8},{8,0},{16,24},{24,16},{1,9},{9,1},{17,25},{25,17},{2,10},{10... | collective-permute-start | bytes 786440 | tf_op jit(solution)/shard_map/ppermute | solution.py:424
  69.2 0.8 %collective-permute-done.12 = f32[264,128]{1,0:T(8,128)S(1)} collective-permute-done((f32[264,128]{1,0:T(8,128)S(1)}, f32[264,128]{1,0:T(8,128)S(1)}, u32[]{:S(2)}, u32[]{:S(2)}) %collective-permute-start.12) | collective-permute-done | bytes 135200 | tf_op jit(solution)/shard_map/ppermute | solution.py:424
  70.0 1.3 %collective-permute-start.13 = (f32[264,128]{1,0:T(8,128)S(1)}, f32[264,128]{1,0:T(8,128)S(1)}, u32[]{:S(2)}, u32[]{:S(2)}) collective-permute-start(f32[264,128]{1,0:T(8,128)S(1)} %add.13.mine), channel_id=1, source_target_pairs={{0,8},{8,0},{16,24},{24,16},{1,9},{9,1},{17,25},{25,17},{2,10},{10... | collective-permute-start | bytes 405512 | tf_op jit(solution)/shard_map/ppermute | solution.py:424
  71.3 0.0 collective-permute-done.16.theirs
  71.3 0.8 %shard_map.72 = (f32[2,256,256]{2,1,0:T(8,128)}, f32[8,128]{1,0:T(8,128)S(1)}) custom-call(f32[512,128]{1,0:T(8,128)S(1)} %add.15.mine, f32[512,128]{1,0:T(8,128)S(1)} %collective-permute-done.16.theirs), custom_call_target="tpu_custom_call" | custom-call | flops 1 | bytes 1 | tf_op jit(solution)/shard_map/pallas_call | solution.py:305
  72.1 0.1 collective-permute-done.13.theirs
  72.2 0.9 %shard_map.73 = f32[2,256,256]{2,1,0:T(8,128)} custom-call(f32[264,128]{1,0:T(8,128)S(1)} %add.13.mine, f32[264,128]{1,0:T(8,128)S(1)} %collective-permute-done.13.theirs, f32[8,128]{1,0:T(8,128)S(1)} %get-tuple-element.66._), custom_call_target="tpu_custom_call" | custom-call | flops 1 | bytes 1 | tf_op jit(solution)/shard_map/pallas_call | solution.py:305
  (15 shorter events, 0.2 us)
Async XLA Ops:
  0.6 2.8 %copy-start.3 = (s32[2]{0:T(128)S(1)}, s32[2]{0:T(128)}, u32[]{:S(2)}) copy-start(s32[2]{0:T(128)} %live.7) | copy-start | bytes 28
  0.6 2.8 %copy-start = (f32[2,2,2,256,256]{4,3,2,1,0:T(8,128)S(1)}, f32[2,2,2,256,256]{4,3,2,1,0:T(8,128)}, u32[]{:S(2)}) copy-start(f32[2,2,2,256,256]{4,3,2,1,0:T(8,128)} %factor.7) | copy-start | bytes 6291460
  3.4 7.4 %copy-start.1 = (f32[2,2,2,256,256]{4,3,2,1,0:T(8,128)S(1)}, f32[2,2,2,256,256]{4,3,2,1,0:T(8,128)}, u32[]{:S(2)}) copy-start(f32[2,2,2,256,256]{4,3,2,1,0:T(8,128)} %pivot.3) | copy-start | bytes 6291460
  3.4 7.4 %copy-start.2 = (f32[2,2]{1,0:T(2,128)S(1)}, f32[2,2]{1,0:T(2,128)}, u32[]{:S(2)}) copy-start(f32[2,2]{1,0:T(2,128)} %weight.7) | copy-start | bytes 52
  4.8 10.5 %collective-permute-start.1 = (f32[2,264,128]{2,1,0:T(8,128)S(1)}, f32[2,264,128]{2,1,0:T(8,128)S(1)}, u32[]{:S(2)}, u32[]{:S(2)}) collective-permute-start(f32[2,264,128]{2,1,0:T(8,128)S(1)} %get-tuple-element.41), channel_id=1, source_target_pairs={{0,1},{16,17},{2,3},{3,2},{4,5},{5,4},{6,7},{7,6},{18,19},{19,18},... | collective-permute-start | bytes 811016 | tf_op jit(solution)/shard_map/ppermute | solution.py:364
  5.5 10.0 %collective-permute-start.2 = (f32[2,264,128]{2,1,0:T(8,128)S(1)}, f32[2,264,128]{2,1,0:T(8,128)S(1)}, u32[]{:S(2)}, u32[]{:S(2)}) collective-permute-start(f32[2,264,128]{2,1,0:T(8,128)S(1)} %get-tuple-element.36.passed.e), channel_id=1, source_target_pairs={{8,9},{24,25},{10,11},{11,10},{12,13},{13,12},{14,15},{15,14},{26,... | collective-permute-start | bytes 811016 | tf_op jit(solution)/shard_map/ppermute | solution.py:360
  8.6 18.1 %collective-permute-start = (f32[2,256,256]{2,1,0:T(8,128)S(1)}, f32[2,256,256]{2,1,0:T(8,128)S(1)}, u32[]{:S(2)}, u32[]{:S(2)}) collective-permute-start(f32[2,256,256]{2,1,0:T(8,128)S(1)} %get-tuple-element.37.refs_0_), channel_id=1, source_target_pairs={{2,3},{3,2},{4,5},{5,4},{6,7},{7,6},{10,11},{11,10},{12,13},{13,12... | collective-permute-start | bytes 1572872 | tf_op jit(solution)/shard_map/ppermute | solution.py:365
  12.6 3.6 %collective-permute-start.4 = (f32[2,264,128]{2,1,0:T(8,128)S(1)}, f32[2,264,128]{2,1,0:T(8,128)S(1)}, u32[]{:S(2)}, u32[]{:S(2)}) collective-permute-start(f32[2,264,128]{2,1,0:T(8,128)S(1)} %get-tuple-element.39.passed.e), channel_id=1, source_target_pairs={{8,9},{24,25}} | collective-permute-start | bytes 811016 | tf_op jit(solution)/shard_map/ppermute | solution.py:372
  14.6 1.5 %collective-permute-start.3 = (f32[2,264,128]{2,1,0:T(8,128)S(1)}, f32[2,264,128]{2,1,0:T(8,128)S(1)}, u32[]{:S(2)}, u32[]{:S(2)}) collective-permute-start(f32[2,264,128]{2,1,0:T(8,128)S(1)} %get-tuple-element.42), channel_id=1, source_target_pairs={{0,1},{16,17}} | collective-permute-start | bytes 811016 | tf_op jit(solution)/shard_map/ppermute | solution.py:376
  15.5 1.4 %collective-permute-start.6 = (f32[2,264,128]{2,1,0:T(8,128)S(1)}, f32[2,264,128]{2,1,0:T(8,128)S(1)}, u32[]{:S(2)}, u32[]{:S(2)}) collective-permute-start(f32[2,264,128]{2,1,0:T(8,128)S(1)} %shard_map.65), channel_id=1, source_target_pairs={{1,0},{9,8},{17,16},{25,24}} | collective-permute-start | bytes 811016 | tf_op jit(solution)/shard_map/ppermute | solution.py:379
  16.2 12.2 %collective-permute-start.5 = (f32[2,264,128]{2,1,0:T(8,128)S(1)}, f32[2,264,128]{2,1,0:T(8,128)S(1)}, u32[]{:S(2)}, u32[]{:S(2)}) collective-permute-start(f32[2,264,128]{2,1,0:T(8,128)S(1)} %shard_map.64), channel_id=1, source_target_pairs={{1,3},{9,11},{17,19},{25,27}} | collective-permute-start | bytes 811016 | tf_op jit(solution)/shard_map/ppermute | solution.py:384
  16.9 11.5 %collective-permute-start.7 = (f32[2,264,128]{2,1,0:T(8,128)S(1)}, f32[2,264,128]{2,1,0:T(8,128)S(1)}, u32[]{:S(2)}, u32[]{:S(2)}) collective-permute-start(f32[2,264,128]{2,1,0:T(8,128)S(1)} %collective-permute-done.6), channel_id=1, source_target_pairs={{0,2},{8,10},{16,18},{24,26}} | collective-permute-start | bytes 811016 | tf_op jit(solution)/shard_map/ppermute | solution.py:385
  28.5 0.7 collective-permute-start.8
  29.2 15.8 %collective-permute-start.9 = (f32[2,264,128]{2,1,0:T(8,128)S(1)}, f32[2,264,128]{2,1,0:T(8,128)S(1)}, u32[]{:S(2)}, u32[]{:S(2)}) collective-permute-start(f32[2,264,128]{2,1,0:T(8,128)S(1)} %shard_map.67), channel_id=1, source_target_pairs={{5,7},{4,6},{13,15},{12,14},{21,23},{20,22},{29,31},{28,30}} | collective-permute-start | bytes 811016 | tf_op jit(solution)/shard_map/ppermute | solution.py:402
  46.3 5.4 %collective-permute-start.10 = (f32[2,264,128]{2,1,0:T(8,128)S(1)}, f32[2,264,128]{2,1,0:T(8,128)S(1)}, u32[]{:S(2)}, u32[]{:S(2)}) collective-permute-start(f32[2,264,128]{2,1,0:T(8,128)S(1)} %get-tuple-element.53), channel_id=1, source_target_pairs={{0,1},{1,0},{2,3},{3,2},{4,5},{5,4},{6,7},{7,6},{8,9},{9,8},{10,11... | collective-permute-start | bytes 811016 | tf_op jit(solution)/shard_map/ppermute | solution.py:411
  53.2 6.2 %collective-permute-start.14 = (f32[512,128]{1,0:T(8,128)S(1)}, f32[512,128]{1,0:T(8,128)S(1)}, u32[]{:S(2)}, u32[]{:S(2)}) collective-permute-start(f32[512,128]{1,0:T(8,128)S(1)} %slice_bitcast_fusion), channel_id=1, source_target_pairs={{0,8},{8,0},{16,24},{24,16},{1,9},{9,1},{17,25},{25,17},{2,10},{10... | collective-permute-start | bytes 786440 | tf_op jit(solution)/shard_map/ppermute | solution.py:424
  58.9 1.4 %collective-permute-start.11 = (f32[264,128]{1,0:T(8,128)S(1)}, f32[264,128]{1,0:T(8,128)S(1)}, u32[]{:S(2)}, u32[]{:S(2)}) collective-permute-start(f32[264,128]{1,0:T(8,128)S(1)} %slice_bitcast_fusion.1), channel_id=1, source_target_pairs={{0,8},{8,0},{16,24},{24,16},{1,9},{9,1},{17,25},{25,17},{2,10},{10... | collective-permute-start | bytes 405512 | tf_op jit(solution)/shard_map/ppermute | solution.py:424
  59.5 7.6 %collective-permute-start.15 = (f32[512,128]{1,0:T(8,128)S(1)}, f32[512,128]{1,0:T(8,128)S(1)}, u32[]{:S(2)}, u32[]{:S(2)}) collective-permute-start(f32[512,128]{1,0:T(8,128)S(1)} %bitcast_add_fusion), channel_id=1, source_target_pairs={{0,16},{8,24},{16,0},{24,8},{1,17},{9,25},{17,1},{25,9},{2,18},{10... | collective-permute-start | bytes 786440 | tf_op jit(solution)/shard_map/ppermute | solution.py:424
  60.3 9.6 %collective-permute-start.12 = (f32[264,128]{1,0:T(8,128)S(1)}, f32[264,128]{1,0:T(8,128)S(1)}, u32[]{:S(2)}, u32[]{:S(2)}) collective-permute-start(f32[264,128]{1,0:T(8,128)S(1)} %fusion), channel_id=1, source_target_pairs={{0,16},{8,24},{16,0},{24,8},{1,17},{9,25},{17,1},{25,9},{2,18},{10... | collective-permute-start | bytes 405512 | tf_op jit(solution)/shard_map/ppermute | solution.py:424
  67.1 4.2 %collective-permute-start.16 = (f32[512,128]{1,0:T(8,128)S(1)}, f32[512,128]{1,0:T(8,128)S(1)}, u32[]{:S(2)}, u32[]{:S(2)}) collective-permute-start(f32[512,128]{1,0:T(8,128)S(1)} %add.15.mine), channel_id=1, source_target_pairs={{0,8},{8,0},{16,24},{24,16},{1,9},{9,1},{17,25},{25,17},{2,10},{10... | collective-permute-start | bytes 786440 | tf_op jit(solution)/shard_map/ppermute | solution.py:424
  70.0 2.3 %collective-permute-start.13 = (f32[264,128]{1,0:T(8,128)S(1)}, f32[264,128]{1,0:T(8,128)S(1)}, u32[]{:S(2)}, u32[]{:S(2)}) collective-permute-start(f32[264,128]{1,0:T(8,128)S(1)} %add.13.mine), channel_id=1, source_target_pairs={{0,8},{8,0},{16,24},{24,16},{1,9},{9,1},{17,25},{25,17},{2,10},{10... | collective-permute-start | bytes 405512 | tf_op jit(solution)/shard_map/ppermute | solution.py:424

commit v2 on v0

--- a/solution.py
+++ b/solution.py
@@ -97,33 +97,15 @@
     return hosted_slot() if hosted else 1 - hosted_slot()
 
 
-def constant_kernel(hosted, fetch, live, pivot, factor, weight, *refs):
-    width = pivot.shape[-1]
-    slot = slot_of(hosted)
-    if fetch:
-        f1s, e, weighted, blocks, link, widths, weights, sems = refs
-        copies = [
-            pltpu.make_async_copy(live, widths, sems.at[0]),
-            pltpu.make_async_copy(factor.at[slot, 1], link, sems.at[1]),
-            pltpu.make_async_copy(pivot.at[slot, 0], blocks.at[0], sems.at[2]),
-            pltpu.make_async_copy(pivot.at[slot, 1], blocks.at[1], sems.at[3]),
-            pltpu.make_async_copy(weight, weights, sems.at[4]),
-        ]
-        for copy in copies:
-            copy.start()
-        copies[0].wait()
-        copies[1].wait()
-    else:
-        _, f1s, e, weighted = refs
-        blocks, link, widths, weights, copies = pivot.at[slot], factor.at[slot, 1], live, weight, []
+def constants_of(slot, blocks, link, widths, weights, f1s, e, weighted, wait=lambda: None):
+    width = blocks.shape[-1]
     row, column = rows_columns(width)
     kept = [column < widths[k] for k in range(2)]
     both = [jnp.logical_and(row < widths[k], kept[k]) for k in range(2)]
     f1 = [jnp.where(kept[1], link[c], 0.0) for c in range(2)]
     s1, t1 = split_pair(*f1), split_pair(f1[0].T, f1[1].T)
     store4(f1s, s1)
-    for copy in copies[2:]:
-        copy.wait()
+    wait()
     d = [[jnp.where(both[k], blocks[k, c], 0.0) for c in range(2)] for k in range(2)]
     br, bi = complex_dot(split_pair(*d[0]), s1)
     tr, ti = complex_dot(t1, split_pair(br, bi))
@@ -135,6 +117,52 @@
     weighted_b = flat(w1 * br + w0 * bi)
     weighted[2] = weighted_b[: width + 8]
     weighted[3, : width - 8] = weighted_b[width + 8 :]
+
+
+def fetched_constants(slot, live, pivot, factor, weight, outs, scratch):
+    blocks, link, widths, weights, sems = scratch
+    copies = [
+        pltpu.make_async_copy(live, widths, sems.at[0]),
+        pltpu.make_async_copy(factor.at[slot, 1], link, sems.at[1]),
+        pltpu.make_async_copy(pivot.at[slot, 0], blocks.at[0], sems.at[2]),
+        pltpu.make_async_copy(pivot.at[slot, 1], blocks.at[1], sems.at[3]),
+        pltpu.make_async_copy(weight, weights, sems.at[4]),
+    ]
+    for copy in copies:
+        copy.start()
+    copies[0].wait()
+    copies[1].wait()
+
+    def wait():
+        for copy in copies[2:]:
+            copy.wait()
+
+    constants_of(slot, blocks, link, widths, weights, *outs, wait)
+
+
+def root_constant_kernel(live, pivot, factor, weight, *refs):
+    @pl.when(whereabouts()[0] == 0)
+    def _():
+        fetched_constants(slot_of(False), live, pivot, factor, weight, refs[:3], refs[3:])
+
+
+def first_constant_kernel(live, pivot, factor, weight, *refs):
+    made, outs, scratch = refs[:3], refs[3:6], refs[6:]
+    place = whereabouts()[0]
+
+    @pl.when(place == 0)
+    def _():
+        for source, target in zip(made, outs):
+            target[...] = source[...]
+
+    @pl.when(place > 0)
+    def _():
+        fetched_constants(slot_of(False), live, pivot, factor, weight, outs, scratch)
+
+
+def constant_kernel(live, pivot, factor, weight, _, f1s, e, weighted):
+    slot = slot_of(True)
+    constants_of(slot, pivot.at[slot], factor.at[slot, 1], live, weight, f1s, e, weighted)
 
 
 def factor_kernel(hosted, live, factor, f1s, f0s, f0t, gs, gt, g):
@@ -316,29 +344,24 @@
     constants = [parts, mirrored, jax.ShapeDtypeStruct((4,) + quarter, F32)]
     factors = [parts, parts, parts, parts, jax.ShapeDtypeStruct((2, width, width), F32)]
 
-    o_f1s, o_e, o_w = run(
-        functools.partial(constant_kernel, False, True),
-        [],
-        [],
-        constants,
-        [
-            pltpu.VMEM(pivot.shape[1:], F32),
-            pltpu.VMEM(factor.shape[2:], F32),
-            pltpu.SMEM(live.shape, jnp.int32),
-            pltpu.VMEM(weight.shape, F32),
-            pltpu.SemaphoreType.DMA((5,)),
-        ],
-        far=[
-            pltpu.with_memory_space_constraint(a, pltpu.HBM) for a in (live, pivot, factor, weight)
-        ],
-    )
-    e_in = lax.ppermute(o_e, AXES, first + swaps)
+    scratch = [
+        pltpu.VMEM(pivot.shape[1:], F32),
+        pltpu.VMEM(factor.shape[2:], F32),
+        pltpu.SMEM(live.shape, jnp.int32),
+        pltpu.VMEM(weight.shape, F32),
+        pltpu.SemaphoreType.DMA((5,)),
+    ]
+    far = [pltpu.with_memory_space_constraint(a, pltpu.HBM) for a in (live, pivot, factor, weight)]
+    made = run(root_constant_kernel, [], [], constants, scratch, far=far)
+    e_first = lax.ppermute(made[1], AXES, first)
+    o_f1s, o_e, o_w = run(first_constant_kernel, [], made, constants, scratch, far=far)
+    e_in = lax.ppermute(o_e, AXES, swaps)
     o_f0s, o_f0t, o_gs, o_gt, o_g = run(
         functools.partial(factor_kernel, False), [live], [factor, o_f1s], factors
     )
     g_in = lax.ppermute(o_g, AXES, swaps)
     m_f1s, m_e, m_w = run(
-        functools.partial(constant_kernel, True, False),
+        constant_kernel,
         [live],
         [pivot, factor, weight, o_g],
         constants,
@@ -349,7 +372,7 @@
     e_second = lax.ppermute(m_e, AXES, first)
 
     starts = functools.partial(step_kernel, lambda place: place == 1)
-    (wave_even,) = run(starts, [], [o_gs, o_gt, o_e, e_in], [mirrored])
+    (wave_even,) = run(starts, [], [o_gs, o_gt, o_e, e_first], [mirrored])
     wave_even = lax.ppermute(wave_even, AXES, [(at(p, 1), at(p, 0)) for p in range(poles)])
     (wave_odd,) = run(starts, [], [m_gs, m_gt, m_e, e_second], [mirrored])
     received = []
@@ -389,7 +412,7 @@
     off, us, ts = run(
         more_off_kernel,
         [],
-        [weight, shared, e_in, o_f0s, o_f0t, o_gs, o_w, off],
+        [weight, shared, e_first, o_f0s, o_f0t, o_gs, o_w, off],
         [offs, parts, parts],
     )
 

time: 70.2 us -> 70.7 us (level)
  waiting for transfers between devices: 29.1 us -> 32.3 us
  starting transfers between devices: 23.1 us -> 20.9 us
    ppermute x1 -> x2, waiting for transfers between devices: 0.07 us -> 9.18 us  [the longest x1 9.17 us: local(): e_in = lax.ppermute(o_e, AXES, swaps)]
    ppermute x1, waiting for transfers between devices: 7.82 us -> 0.01 us  [local(): g_in = lax.ppermute(o_g, AXES, swaps)]
    ppermute x1, starting transfers between devices: 4.58 us -> 1.27 us  [local(): shared = lax.ppermute(sent, AXES, every)]
    ppermute x2, waiting for transfers between devices: 11.5 us -> 13.1 us  [local(): arrived = [lax.ppermute(wave, AXES, up)]]
    ppermute x1, starting transfers between devices: 2.17 us -> 3.12 us  [local(): g_in = lax.ppermute(o_g, AXES, swaps)]
    ppermute x1 -> x2, starting transfers between devices: 3.25 us -> 2.84 us  [the longest x1 2.16 us: local(): e_in = lax.ppermute(o_e, AXES, swaps)]
    pallas_call x15 -> x16, Pallas kernels: 16 us -> 16.1 us  [run(): pl.pallas_call(kernel, out_shape=shapes, in_specs=[SCALAR] * len(scalars)...]
  transfers between devices with their start and end apart: 15 -> 16, of which waited for: 9 -> 8; matrix products, arithmetic and copies ran while one was open for 0% -> 0% of each run, Pallas kernels for 14% -> 18%
where the time goes in v2:
time: 70.7 us; the launch traced here: 70.4 us
  waiting for transfers between devices  32.3 us (46%)
  starting transfers between devices  20.9 us (30%)
  Pallas kernels  16.1 us (23%)
  between operations  0.94 us (1%)
    pallas_call x16, Pallas kernels, run(): pl.pallas_call(kernel, out_shape=shapes, in_specs=[SCALAR] * len(scalars)...  16.1 us
    ppermute x2, waiting for transfers between devices, local(): arrived = [lax.ppermute(wave, AXES, up)]  13.1 us
    ppermute x1, waiting for transfers between devices, local(): e_in = lax.ppermute(o_e, AXES, swaps)  9.17 us
    ppermute x6, starting transfers between devices, exchanged(): lax.ppermute(value, 'pole', [(p, p ^ distance) for p in range(poles)])  8.77 us
    ppermute x6, waiting for transfers between devices, exchanged(): lax.ppermute(value, 'pole', [(p, p ^ distance) for p in range(poles)])  7.94 us
    ppermute x1, starting transfers between devices, local(): g_in = lax.ppermute(o_g, AXES, swaps)  3.12 us
    ppermute x1, starting transfers between devices, local(): e_in = lax.ppermute(o_e, AXES, swaps)  2.16 us
    ppermute x2, starting transfers between devices, local(): arrived = [lax.ppermute(wave, AXES, up)]  2.15 us
  transfers between devices with their start and end apart: 16, of which 8 were waited for; matrix products, arithmetic and copies ran while one was open for 0% of the time, Pallas kernels for 18%

profile of v2, /device:TPU:29, one launch (start us, length us, event | category | flops | bytes accessed | tf_op | source)
XLA Modules:
  0.0 70.4 jit_solution(15367228110856758253)
XLA Ops:
  0.6 0.1 shard_map.59
  0.7 0.7 collective-permute-start.4
  1.4 0.0 copy-start
  1.4 0.0 copy-start.3
  1.4 2.7 %shard_map.60 = (bf16[4,256,256]{2,1,0:T(8,128)(2,1)S(1)}, f32[2,264,128]{2,1,0:T(8,128)S(1)}, f32[4,264,128]{2,1,0:T(8,128)S(1)}) custom-call(s32[2]{0:T(128)} %live.9, f32[2,2,2,256,256]{4,3,2,1,0:T(8,128)} %pivot.5, f32[2,2,2,256,256]{4,3,2,1,0:T(8,128)} %factor.9, f32[2,2]{1,0:T(2,128)} %weight.9, bf16[4,256,256]{2,1,0:T(8,128)(2,1)S(1)} %get-tuple-element.36.refs_0_, ...), custom_call_target="tpu_custom_call" | custom-call | flops 1 | bytes 1 | tf_op jit(solution)/shard_map/pallas_call | solution.py:314
  4.2 0.0 copy-start.1
  4.2 0.0 copy-start.2
  4.2 1.3 %shard_map.61 = (bf16[4,256,256]{2,1,0:T(8,128)(2,1)S(1)}, bf16[4,256,256]{2,1,0:T(8,128)(2,1)S(1)}, bf16[4,256,256]{2,1,0:T(8,128)(2,1)S(1)}, bf16[4,256,256]{2,1,0:T(8,128)(2,1)S(1)}, f32[2,256,256]{2,1,0:T(8,128)S(1)}) custom-call(s32[2]{0:T(128)S(1)} %copy-done.3, f32[2,2,2,256,256]{4,3,2,1,0:T(8,128)S(1)} %copy-done, ...), custom_call_target="tpu_custom_call" | custom-call | flops 1 | bytes 1 | tf_op jit(solution)/shard_map/pallas_call | solution.py:314
  5.5 3.1 %collective-permute-start = (f32[2,256,256]{2,1,0:T(8,128)S(1)}, f32[2,256,256]{2,1,0:T(8,128)S(1)}, u32[]{:S(2)}, u32[]{:S(2)}) collective-permute-start(f32[2,256,256]{2,1,0:T(8,128)S(1)} %get-tuple-element.40._), channel_id=1, source_target_pairs={{2,3},{3,2},{4,5},{5,4},{6,7},{7,6},{10,11},{11,10},{12,13},{13,12... | collective-permute-start | bytes 1572872 | tf_op jit(solution)/shard_map/ppermute | solution.py:362
  8.7 1.8 %shard_map.62 = (bf16[4,256,256]{2,1,0:T(8,128)(2,1)S(1)}, f32[2,264,128]{2,1,0:T(8,128)S(1)}, f32[4,264,128]{2,1,0:T(8,128)S(1)}) custom-call(s32[2]{0:T(128)S(1)} %copy-done.3, f32[2,2,2,256,256]{4,3,2,1,0:T(8,128)S(1)} %copy-done.1, f32[2,2,2,256,256]{4,3,2,1,0:T(8,128)S(1)} %copy-done, f32[2,2]{1,0:T(2,128)S(1)} %copy-done.2, ...), custom_call_target="tpu_custom_call" | custom-call | flops 1 | bytes 1 | tf_op jit(solution)/shard_map/pallas_call | solution.py:314
  10.5 0.7 collective-permute-start.2
  11.2 0.0 collective-permute-done.4.refs_0_.x_first
  11.2 0.7 collective-permute-start.5
  11.9 2.2 %collective-permute-start.1 = (f32[2,264,128]{2,1,0:T(8,128)S(1)}, f32[2,264,128]{2,1,0:T(8,128)S(1)}, u32[]{:S(2)}, u32[]{:S(2)}) collective-permute-start(f32[2,264,128]{2,1,0:T(8,128)S(1)} %get-tuple-element.44.e), channel_id=1, source_target_pairs={{2,3},{3,2},{4,5},{5,4},{6,7},{7,6},{10,11},{11,10},{12,13},{13,12... | collective-permute-start | bytes 811016 | tf_op jit(solution)/shard_map/ppermute | solution.py:358
  14.1 1.3 %shard_map.63 = (bf16[4,256,256]{2,1,0:T(8,128)(2,1)S(1)}, bf16[4,256,256]{2,1,0:T(8,128)(2,1)S(1)}, bf16[4,256,256]{2,1,0:T(8,128)(2,1)S(1)}, bf16[4,256,256]{2,1,0:T(8,128)(2,1)S(1)}, f32[2,256,256]{2,1,0:T(8,128)S(1)}) custom-call(s32[2]{0:T(128)S(1)} %copy-done.3, f32[2,2,2,256,256]{4,3,2,1,0:T(8,128)S(1)} %copy-done, ...), custom_call_target="tpu_custom_call" | custom-call | flops 1 | bytes 1 | tf_op jit(solution)/shard_map/pallas_call | solution.py:314
  15.4 0.0 collective-permute-done.2.e_second.refs_0_
  15.4 0.7 collective-permute-start.3
  16.1 0.0 collective-permute-done.5
  16.1 0.7 collective-permute-start.6
  16.8 9.2 %collective-permute-done.1.e_in = f32[2,264,128]{2,1,0:T(8,128)S(1)} collective-permute-done((f32[2,264,128]{2,1,0:T(8,128)S(1)}, f32[2,264,128]{2,1,0:T(8,128)S(1)}, u32[]{:S(2)}, u32[]{:S(2)}) %collective-permute-start.1) | collective-permute-done | bytes 270368 | tf_op jit(solution)/shard_map/ppermute | solution.py:358
  26.0 0.0 collective-permute-done.g_in
  26.0 1.7 %shard_map.64 = (bf16[4,256,256]{2,1,0:T(8,128)(2,1)S(1)}, bf16[4,256,256]{2,1,0:T(8,128)(2,1)S(1)}, f32[2,264,128]{2,1,0:T(8,128)S(1)}, bf16[4,256,256]{2,1,0:T...) custom-call(f32[2,256,256]{2,1,0:T(8,128)S(1)} %get-tuple-element.42.g, ...), custom_call_target="tpu_custom_call" | custom-call | flops 99999997952 | bytes 1 | tf_op jit(solution)/shard_map/pallas_call | solution.py:314
  27.7 0.0 collective-permute-done.3.refs_0_
  27.7 0.0 collective-permute-done.6.refs_1_
  27.8 0.7 collective-permute-start.7
  28.4 0.0 collective-permute-done.7.refs_0_.refs_2_
  28.5 1.5 %collective-permute-start.8 = (f32[2,264,128]{2,1,0:T(8,128)S(1)}, f32[2,264,128]{2,1,0:T(8,128)S(1)}, u32[]{:S(2)}, u32[]{:S(2)}) collective-permute-start(f32[2,264,128]{2,1,0:T(8,128)S(1)} %shard_map.68), channel_id=1, source_target_pairs={{5,7},{4,6},{13,15},{12,14},{21,23},{20,22},{29,31},{28,30}} | collective-permute-start | bytes 811016 | tf_op jit(solution)/shard_map/ppermute | solution.py:398
  30.0 13.1 %collective-permute-done.8.refs_3_ = f32[2,264,128]{2,1,0:T(8,128)S(1)} collective-permute-done((f32[2,264,128]{2,1,0:T(8,128)S(1)}, f32[2,264,128]{2,1,0:T(8,128)S(1)}, u32[]{:S(2)}, u32[]{:S(2)}) %collective-permute-start.8) | collective-permute-done | bytes 270368 | tf_op jit(solution)/shard_map/ppermute | solution.py:398
  43.0 1.2 %shard_map.69 = (f32[2,264,128]{2,1,0:T(8,128)S(1)}, f32[2,264,128]{2,1,0:T(8,128)S(1)}) custom-call(bf16[4,256,256]{2,1,0:T(8,128)(2,1)S(1)} %get-tuple-element.45.fas, bf16[4,256,256]{2,1,0:T(8,128)(2,1)S(1)} %get-tuple-element.46.fat, f32[2,264,128]{2,1,0:T(8,128)S(1)} %get-tuple-element.47.ea, f32[2,264,128]{2,1,0:T(8,128)S(1)} %collective-permute-done.3.refs_0_, ...), custom_call_target="tpu_custom_call" | custom-call | flops 1 | bytes 1 | tf_op jit(solution)/shard_map/pallas_call | solution.py:314
  44.3 1.3 %collective-permute-start.9 = (f32[2,264,128]{2,1,0:T(8,128)S(1)}, f32[2,264,128]{2,1,0:T(8,128)S(1)}, u32[]{:S(2)}, u32[]{:S(2)}) collective-permute-start(f32[2,264,128]{2,1,0:T(8,128)S(1)} %get-tuple-element.55), channel_id=1, source_target_pairs={{0,1},{1,0},{2,3},{3,2},{4,5},{5,4},{6,7},{7,6},{8,9},{9,8},{10,11... | collective-permute-start | bytes 811016 | tf_op jit(solution)/shard_map/ppermute | solution.py:407
  45.5 2.0 %shard_map.70 = (f32[2,512,128]{2,1,0:T(8,128)S(1)}, f32[2,264,128]{2,1,0:T(8,128)S(1)}) custom-call(f32[2,2]{1,0:T(2,128)S(1)} %copy-done.2, f32[2,264,128]{2,1,0:T(8,128)S(1)} %get-tuple-element.59.x, bf16[4,256,256]{2,1,0:T(8,128)(2,1)S(1)} %get-tuple-element.60.f0s, bf16[4,256,256]{2,1,0:T(8,128)(2,1)S(1)} %get-tuple-element.61.f0t, ...), custom_call_target="tpu_custom_call" | custom-call | flops 1 | bytes 1 | tf_op jit(solution)/shard_map/pallas_call | solution.py:314
  47.5 2.1 %collective-permute-done.9.x = f32[2,264,128]{2,1,0:T(8,128)S(1)} collective-permute-done((f32[2,264,128]{2,1,0:T(8,128)S(1)}, f32[2,264,128]{2,1,0:T(8,128)S(1)}, u32[]{:S(2)}, u32[]{:S(2)}) %collective-permute-start.9) | collective-permute-done | bytes 270368 | tf_op jit(solution)/shard_map/ppermute | solution.py:407
  49.6 1.5 %shard_map.71 = (f32[2,512,128]{2,1,0:T(8,128)S(1)}, bf16[4,256,256]{2,1,0:T(8,128)(2,1)S(1)}, bf16[4,256,256]{2,1,0:T(8,128)(2,1)S(1)}) custom-call(f32[2,2]{1,0:T(2,128)S(1)} %copy-done.2, f32[2,264,128]{2,1,0:T(8,128)S(1)} %collective-permute-done.9.x, f32[2,264,128]{2,1,0:T(8,128)S(1)} %collective-permute-done.4.refs_0_.x_first, ...), custom_call_target="tpu_custom_call" | custom-call | flops 1 | bytes 1 | tf_op jit(solution)/shard_map/pallas_call | solution.py:314
  51.2 4.3 %collective-permute-start.13 = (f32[512,128]{1,0:T(8,128)S(1)}, f32[512,128]{1,0:T(8,128)S(1)}, u32[]{:S(2)}, u32[]{:S(2)}) collective-permute-start(f32[512,128]{1,0:T(8,128)S(1)} %slice_bitcast_fusion), channel_id=1, source_target_pairs={{0,8},{8,0},{16,24},{24,16},{1,9},{9,1},{17,25},{25,17},{2,10},{10... | collective-permute-start | bytes 786440 | tf_op jit(solution)/shard_map/ppermute | solution.py:420
  55.5 0.6 shard_map.72
  56.1 0.1 collective-permute-start.10
  56.2 0.5 collective-permute-done.13
  56.7 0.3 collective-permute-start.14
  57.0 0.6 collective-permute-done.10
  57.6 0.8 %collective-permute-start.11 = (f32[264,128]{1,0:T(8,128)S(1)}, f32[264,128]{1,0:T(8,128)S(1)}, u32[]{:S(2)}, u32[]{:S(2)}) collective-permute-start(f32[264,128]{1,0:T(8,128)S(1)} %fusion), channel_id=1, source_target_pairs={{0,16},{8,24},{16,0},{24,8},{1,17},{9,25},{17,1},{25,9},{2,18},{10... | collective-permute-start | bytes 405512 | tf_op jit(solution)/shard_map/ppermute | solution.py:420
  58.3 6.0 %collective-permute-done.14 = f32[512,128]{1,0:T(8,128)S(1)} collective-permute-done((f32[512,128]{1,0:T(8,128)S(1)}, f32[512,128]{1,0:T(8,128)S(1)}, u32[]{:S(2)}, u32[]{:S(2)}) %collective-permute-start.14) | collective-permute-done | bytes 262176 | tf_op jit(solution)/shard_map/ppermute | solution.py:420
  64.3 2.1 %collective-permute-start.15 = (f32[512,128]{1,0:T(8,128)S(1)}, f32[512,128]{1,0:T(8,128)S(1)}, u32[]{:S(2)}, u32[]{:S(2)}) collective-permute-start(f32[512,128]{1,0:T(8,128)S(1)} %add.15.mine), channel_id=1, source_target_pairs={{0,8},{8,0},{16,24},{24,16},{1,9},{9,1},{17,25},{25,17},{2,10},{10... | collective-permute-start | bytes 786440 | tf_op jit(solution)/shard_map/ppermute | solution.py:420
  66.4 0.8 %collective-permute-done.11 = f32[264,128]{1,0:T(8,128)S(1)} collective-permute-done((f32[264,128]{1,0:T(8,128)S(1)}, f32[264,128]{1,0:T(8,128)S(1)}, u32[]{:S(2)}, u32[]{:S(2)}) %collective-permute-start.11) | collective-permute-done | bytes 135200 | tf_op jit(solution)/shard_map/ppermute | solution.py:420
  67.2 1.3 %collective-permute-start.12 = (f32[264,128]{1,0:T(8,128)S(1)}, f32[264,128]{1,0:T(8,128)S(1)}, u32[]{:S(2)}, u32[]{:S(2)}) collective-permute-start(f32[264,128]{1,0:T(8,128)S(1)} %add.13.mine), channel_id=1, source_target_pairs={{0,8},{8,0},{16,24},{24,16},{1,9},{9,1},{17,25},{25,17},{2,10},{10... | collective-permute-start | bytes 405512 | tf_op jit(solution)/shard_map/ppermute | solution.py:420
  68.5 0.0 collective-permute-done.15.theirs
  68.5 0.8 %shard_map.73 = (f32[2,256,256]{2,1,0:T(8,128)}, f32[8,128]{1,0:T(8,128)S(1)}) custom-call(f32[512,128]{1,0:T(8,128)S(1)} %add.15.mine, f32[512,128]{1,0:T(8,128)S(1)} %collective-permute-done.15.theirs), custom_call_target="tpu_custom_call" | custom-call | flops 1 | bytes 1 | tf_op jit(solution)/shard_map/pallas_call | solution.py:314
  69.3 0.1 collective-permute-done.12.theirs
  69.5 0.9 %shard_map.74 = f32[2,256,256]{2,1,0:T(8,128)} custom-call(f32[264,128]{1,0:T(8,128)S(1)} %add.13.mine, f32[264,128]{1,0:T(8,128)S(1)} %collective-permute-done.12.theirs, f32[8,128]{1,0:T(8,128)S(1)} %get-tuple-element.68._), custom_call_target="tpu_custom_call" | custom-call | flops 1 | bytes 1 | tf_op jit(solution)/shard_map/pallas_call | solution.py:314
  (14 shorter events, 0.2 us)
Async XLA Ops:
  0.7 10.5 %collective-permute-start.4 = (f32[2,264,128]{2,1,0:T(8,128)S(1)}, f32[2,264,128]{2,1,0:T(8,128)S(1)}, u32[]{:S(2)}, u32[]{:S(2)}) collective-permute-start(f32[2,264,128]{2,1,0:T(8,128)S(1)} %get-tuple-element.37.refs_1_), channel_id=1, source_target_pairs={{0,1},{8,9},{16,17},{24,25}} | collective-permute-start | bytes 811016 | tf_op jit(solution)/shard_map/ppermute | solution.py:356
  1.4 2.8 %copy-start = (f32[2,2,2,256,256]{4,3,2,1,0:T(8,128)S(1)}, f32[2,2,2,256,256]{4,3,2,1,0:T(8,128)}, u32[]{:S(2)}) copy-start(f32[2,2,2,256,256]{4,3,2,1,0:T(8,128)} %factor.9) | copy-start | bytes 6291460
  1.4 2.8 %copy-start.3 = (s32[2]{0:T(128)S(1)}, s32[2]{0:T(128)}, u32[]{:S(2)}) copy-start(s32[2]{0:T(128)} %live.9) | copy-start | bytes 28
  4.2 4.5 %copy-start.1 = (f32[2,2,2,256,256]{4,3,2,1,0:T(8,128)S(1)}, f32[2,2,2,256,256]{4,3,2,1,0:T(8,128)}, u32[]{:S(2)}) copy-start(f32[2,2,2,256,256]{4,3,2,1,0:T(8,128)} %pivot.5) | copy-start | bytes 6291460
  4.2 4.5 %copy-start.2 = (f32[2,2]{1,0:T(2,128)S(1)}, f32[2,2]{1,0:T(2,128)}, u32[]{:S(2)}) copy-start(f32[2,2]{1,0:T(2,128)} %weight.9) | copy-start | bytes 52
  5.5 20.5 %collective-permute-start = (f32[2,256,256]{2,1,0:T(8,128)S(1)}, f32[2,256,256]{2,1,0:T(8,128)S(1)}, u32[]{:S(2)}, u32[]{:S(2)}) collective-permute-start(f32[2,256,256]{2,1,0:T(8,128)S(1)} %get-tuple-element.40._), channel_id=1, source_target_pairs={{2,3},{3,2},{4,5},{5,4},{6,7},{7,6},{10,11},{11,10},{12,13},{13,12... | collective-permute-start | bytes 1572872 | tf_op jit(solution)/shard_map/ppermute | solution.py:362
  10.5 4.9 %collective-permute-start.2 = (f32[2,264,128]{2,1,0:T(8,128)S(1)}, f32[2,264,128]{2,1,0:T(8,128)S(1)}, u32[]{:S(2)}, u32[]{:S(2)}) collective-permute-start(f32[2,264,128]{2,1,0:T(8,128)S(1)} %get-tuple-element.43.e), channel_id=1, source_target_pairs={{0,1},{8,9},{16,17},{24,25}} | collective-permute-start | bytes 811016 | tf_op jit(solution)/shard_map/ppermute | solution.py:372
  11.2 4.9 %collective-permute-start.5 = (f32[2,264,128]{2,1,0:T(8,128)S(1)}, f32[2,264,128]{2,1,0:T(8,128)S(1)}, u32[]{:S(2)}, u32[]{:S(2)}) collective-permute-start(f32[2,264,128]{2,1,0:T(8,128)S(1)} %shard_map.66), channel_id=1, source_target_pairs={{1,0},{9,8},{17,16},{25,24}} | collective-permute-start | bytes 811016 | tf_op jit(solution)/shard_map/ppermute | solution.py:376
  11.9 14.1 %collective-permute-start.1 = (f32[2,264,128]{2,1,0:T(8,128)S(1)}, f32[2,264,128]{2,1,0:T(8,128)S(1)}, u32[]{:S(2)}, u32[]{:S(2)}) collective-permute-start(f32[2,264,128]{2,1,0:T(8,128)S(1)} %get-tuple-element.44.e), channel_id=1, source_target_pairs={{2,3},{3,2},{4,5},{5,4},{6,7},{7,6},{10,11},{11,10},{12,13},{13,12... | collective-permute-start | bytes 811016 | tf_op jit(solution)/shard_map/ppermute | solution.py:358
  15.4 12.3 %collective-permute-start.3 = (f32[2,264,128]{2,1,0:T(8,128)S(1)}, f32[2,264,128]{2,1,0:T(8,128)S(1)}, u32[]{:S(2)}, u32[]{:S(2)}) collective-permute-start(f32[2,264,128]{2,1,0:T(8,128)S(1)} %shard_map.65), channel_id=1, source_target_pairs={{1,3},{9,11},{17,19},{25,27}} | collective-permute-start | bytes 811016 | tf_op jit(solution)/shard_map/ppermute | solution.py:381
  16.1 11.6 %collective-permute-start.6 = (f32[2,264,128]{2,1,0:T(8,128)S(1)}, f32[2,264,128]{2,1,0:T(8,128)S(1)}, u32[]{:S(2)}, u32[]{:S(2)}) collective-permute-start(f32[2,264,128]{2,1,0:T(8,128)S(1)} %collective-permute-done.5), channel_id=1, source_target_pairs={{0,2},{8,10},{16,18},{24,26}} | collective-permute-start | bytes 811016 | tf_op jit(solution)/shard_map/ppermute | solution.py:382
  27.8 0.7 collective-permute-start.7
  28.5 14.6 %collective-permute-start.8 = (f32[2,264,128]{2,1,0:T(8,128)S(1)}, f32[2,264,128]{2,1,0:T(8,128)S(1)}, u32[]{:S(2)}, u32[]{:S(2)}) collective-permute-start(f32[2,264,128]{2,1,0:T(8,128)S(1)} %shard_map.68), channel_id=1, source_target_pairs={{5,7},{4,6},{13,15},{12,14},{21,23},{20,22},{29,31},{28,30}} | collective-permute-start | bytes 811016 | tf_op jit(solution)/shard_map/ppermute | solution.py:398
  44.3 5.4 %collective-permute-start.9 = (f32[2,264,128]{2,1,0:T(8,128)S(1)}, f32[2,264,128]{2,1,0:T(8,128)S(1)}, u32[]{:S(2)}, u32[]{:S(2)}) collective-permute-start(f32[2,264,128]{2,1,0:T(8,128)S(1)} %get-tuple-element.55), channel_id=1, source_target_pairs={{0,1},{1,0},{2,3},{3,2},{4,5},{5,4},{6,7},{7,6},{8,9},{9,8},{10,11... | collective-permute-start | bytes 811016 | tf_op jit(solution)/shard_map/ppermute | solution.py:407
  51.2 5.5 %collective-permute-start.13 = (f32[512,128]{1,0:T(8,128)S(1)}, f32[512,128]{1,0:T(8,128)S(1)}, u32[]{:S(2)}, u32[]{:S(2)}) collective-permute-start(f32[512,128]{1,0:T(8,128)S(1)} %slice_bitcast_fusion), channel_id=1, source_target_pairs={{0,8},{8,0},{16,24},{24,16},{1,9},{9,1},{17,25},{25,17},{2,10},{10... | collective-permute-start | bytes 786440 | tf_op jit(solution)/shard_map/ppermute | solution.py:420
  56.1 1.4 %collective-permute-start.10 = (f32[264,128]{1,0:T(8,128)S(1)}, f32[264,128]{1,0:T(8,128)S(1)}, u32[]{:S(2)}, u32[]{:S(2)}) collective-permute-start(f32[264,128]{1,0:T(8,128)S(1)} %slice_bitcast_fusion.1), channel_id=1, source_target_pairs={{0,8},{8,0},{16,24},{24,16},{1,9},{9,1},{17,25},{25,17},{2,10},{10... | collective-permute-start | bytes 405512 | tf_op jit(solution)/shard_map/ppermute | solution.py:420
  56.7 7.6 %collective-permute-start.14 = (f32[512,128]{1,0:T(8,128)S(1)}, f32[512,128]{1,0:T(8,128)S(1)}, u32[]{:S(2)}, u32[]{:S(2)}) collective-permute-start(f32[512,128]{1,0:T(8,128)S(1)} %bitcast_add_fusion), channel_id=1, source_target_pairs={{0,16},{8,24},{16,0},{24,8},{1,17},{9,25},{17,1},{25,9},{2,18},{10... | collective-permute-start | bytes 786440 | tf_op jit(solution)/shard_map/ppermute | solution.py:420
  57.6 9.6 %collective-permute-start.11 = (f32[264,128]{1,0:T(8,128)S(1)}, f32[264,128]{1,0:T(8,128)S(1)}, u32[]{:S(2)}, u32[]{:S(2)}) collective-permute-start(f32[264,128]{1,0:T(8,128)S(1)} %fusion), channel_id=1, source_target_pairs={{0,16},{8,24},{16,0},{24,8},{1,17},{9,25},{17,1},{25,9},{2,18},{10... | collective-permute-start | bytes 405512 | tf_op jit(solution)/shard_map/ppermute | solution.py:420
  64.3 4.2 %collective-permute-start.15 = (f32[512,128]{1,0:T(8,128)S(1)}, f32[512,128]{1,0:T(8,128)S(1)}, u32[]{:S(2)}, u32[]{:S(2)}) collective-permute-start(f32[512,128]{1,0:T(8,128)S(1)} %add.15.mine), channel_id=1, source_target_pairs={{0,8},{8,0},{16,24},{24,16},{1,9},{9,1},{17,25},{25,17},{2,10},{10... | collective-permute-start | bytes 786440 | tf_op jit(solution)/shard_map/ppermute | solution.py:420
  67.2 2.3 %collective-permute-start.12 = (f32[264,128]{1,0:T(8,128)S(1)}, f32[264,128]{1,0:T(8,128)S(1)}, u32[]{:S(2)}, u32[]{:S(2)}) collective-permute-start(f32[264,128]{1,0:T(8,128)S(1)} %add.13.mine), channel_id=1, source_target_pairs={{0,8},{8,0},{16,24},{24,16},{1,9},{9,1},{17,25},{25,17},{2,10},{10... | collective-permute-start | bytes 405512 | tf_op jit(solution)/shard_map/ppermute | solution.py:420

commit v3 on v2

--- a/solution.py
+++ b/solution.py
@@ -372,7 +372,7 @@
     e_second = lax.ppermute(m_e, AXES, first)
 
     starts = functools.partial(step_kernel, lambda place: place == 1)
-    (wave_even,) = run(starts, [], [o_gs, o_gt, o_e, e_first], [mirrored])
+    (wave_even,) = run(starts, [], [o_gs, o_gt, o_e, e_first, e_in], [mirrored])
     wave_even = lax.ppermute(wave_even, AXES, [(at(p, 1), at(p, 0)) for p in range(poles)])
     (wave_odd,) = run(starts, [], [m_gs, m_gt, m_e, e_second], [mirrored])
     received = []

time: 70.7 us -> 70.8 us (level)
  waiting for transfers between devices: 32.3 us -> 29.1 us
  starting transfers between devices: 20.9 us -> 23.7 us
    ppermute x1, waiting for transfers between devices: 9.17 us -> 0.01 us  [local(): e_in = lax.ppermute(o_e, AXES, swaps)]
    ppermute x1, waiting for transfers between devices: 0.01 us -> 7.49 us  [local(): g_in = lax.ppermute(o_g, AXES, swaps)]
    ppermute x1, starting transfers between devices: 1.27 us -> 4.51 us  [local(): shared = lax.ppermute(sent, AXES, every)]
    ppermute x2, waiting for transfers between devices: 13.1 us -> 11.8 us  [local(): arrived = [lax.ppermute(wave, AXES, up)]]
    ppermute x1, starting transfers between devices: 2.16 us -> 3.25 us  [local(): e_in = lax.ppermute(o_e, AXES, swaps)]
    ppermute x1, starting transfers between devices: 3.12 us -> 2.16 us  [local(): g_in = lax.ppermute(o_g, AXES, swaps)]
  transfers between devices with their start and end apart: 16 -> 16, of which waited for: 8 -> 8; matrix products, arithmetic and copies ran while one was open for 0% -> 0% of each run, Pallas kernels for 18% -> 14%
where the time goes in v3:
time: 70.8 us; the launch traced here: 70 us
  waiting for transfers between devices  29.1 us (41%)
  starting transfers between devices  23.7 us (33%)
  Pallas kernels  16.1 us (23%)
  between operations  0.95 us (1%)
    pallas_call x16, Pallas kernels, run(): pl.pallas_call(kernel, out_shape=shapes, in_specs=[SCALAR] * len(scalars)...  16.1 us
    ppermute x2, waiting for transfers between devices, local(): arrived = [lax.ppermute(wave, AXES, up)]  11.8 us
    ppermute x6, starting transfers between devices, exchanged(): lax.ppermute(value, 'pole', [(p, p ^ distance) for p in range(poles)])  8.28 us
    ppermute x6, waiting for transfers between devices, exchanged(): lax.ppermute(value, 'pole', [(p, p ^ distance) for p in range(poles)])  7.91 us
    ppermute x1, waiting for transfers between devices, local(): g_in = lax.ppermute(o_g, AXES, swaps)  7.49 us
    ppermute x1, starting transfers between devices, local(): shared = lax.ppermute(sent, AXES, every)  4.51 us
    ppermute x1, starting transfers between devices, local(): e_in = lax.ppermute(o_e, AXES, swaps)  3.25 us
    ppermute x1, starting transfers between devices, local(): g_in = lax.ppermute(o_g, AXES, swaps)  2.16 us
  transfers between devices with their start and end apart: 16, of which 8 were waited for; matrix products, arithmetic and copies ran while one was open for 0% of the time, Pallas kernels for 14%

profile of v3, /device:TPU:29, one launch (start us, length us, event | category | flops | bytes accessed | tf_op | source)
XLA Modules:
  0.0 70.0 jit_solution(3935296760308322025)
XLA Ops:
  0.6 0.1 shard_map.59
  0.7 0.0 copy-start
  0.7 0.0 copy-start.3
  0.7 2.7 %shard_map.60 = (bf16[4,256,256]{2,1,0:T(8,128)(2,1)S(1)}, f32[2,264,128]{2,1,0:T(8,128)S(1)}, f32[4,264,128]{2,1,0:T(8,128)S(1)}) custom-call(s32[2]{0:T(128)} %live.9, f32[2,2,2,256,256]{4,3,2,1,0:T(8,128)} %pivot.5, f32[2,2,2,256,256]{4,3,2,1,0:T(8,128)} %factor.9, f32[2,2]{1,0:T(2,128)} %weight.9, bf16[4,256,256]{2,1,0:T(8,128)(2,1)S(1)} %get-tuple-element.36.refs_0_, ...), custom_call_target="tpu_custom_call" | custom-call | flops 1 | bytes 1 | tf_op jit(solution)/shard_map/pallas_call | solution.py:314
  3.5 0.0 copy-start.1
  3.5 0.0 copy-start.2
  3.5 3.3 %collective-permute-start.1 = (f32[2,264,128]{2,1,0:T(8,128)S(1)}, f32[2,264,128]{2,1,0:T(8,128)S(1)}, u32[]{:S(2)}, u32[]{:S(2)}) collective-permute-start(f32[2,264,128]{2,1,0:T(8,128)S(1)} %get-tuple-element.44.e), channel_id=1, source_target_pairs={{2,3},{3,2},{4,5},{5,4},{6,7},{7,6},{10,11},{11,10},{12,13},{13,12... | collective-permute-start | bytes 811016 | tf_op jit(solution)/shard_map/ppermute | solution.py:358
  6.8 0.7 collective-permute-start.4
  7.5 1.3 %shard_map.61 = (bf16[4,256,256]{2,1,0:T(8,128)(2,1)S(1)}, bf16[4,256,256]{2,1,0:T(8,128)(2,1)S(1)}, bf16[4,256,256]{2,1,0:T(8,128)(2,1)S(1)}, bf16[4,256,256]{2,1,0:T(8,128)(2,1)S(1)}, f32[2,256,256]{2,1,0:T(8,128)S(1)}) custom-call(s32[2]{0:T(128)S(1)} %copy-done.3, f32[2,2,2,256,256]{4,3,2,1,0:T(8,128)S(1)} %copy-done, ...), custom_call_target="tpu_custom_call" | custom-call | flops 1 | bytes 1 | tf_op jit(solution)/shard_map/pallas_call | solution.py:314
  8.8 2.2 %collective-permute-start = (f32[2,256,256]{2,1,0:T(8,128)S(1)}, f32[2,256,256]{2,1,0:T(8,128)S(1)}, u32[]{:S(2)}, u32[]{:S(2)}) collective-permute-start(f32[2,256,256]{2,1,0:T(8,128)S(1)} %get-tuple-element.40._), channel_id=1, source_target_pairs={{2,3},{3,2},{4,5},{5,4},{6,7},{7,6},{10,11},{11,10},{12,13},{13,12... | collective-permute-start | bytes 1572872 | tf_op jit(solution)/shard_map/ppermute | solution.py:362
  11.0 1.8 %shard_map.62 = (bf16[4,256,256]{2,1,0:T(8,128)(2,1)S(1)}, f32[2,264,128]{2,1,0:T(8,128)S(1)}, f32[4,264,128]{2,1,0:T(8,128)S(1)}) custom-call(s32[2]{0:T(128)S(1)} %copy-done.3, f32[2,2,2,256,256]{4,3,2,1,0:T(8,128)S(1)} %copy-done.1, f32[2,2,2,256,256]{4,3,2,1,0:T(8,128)S(1)} %copy-done, f32[2,2]{1,0:T(2,128)S(1)} %copy-done.2, ...), custom_call_target="tpu_custom_call" | custom-call | flops 1 | bytes 1 | tf_op jit(solution)/shard_map/pallas_call | solution.py:314
  12.8 0.7 collective-permute-start.2
  13.5 0.0 collective-permute-done.1.e_in.refs_1_
  13.5 0.0 collective-permute-done.4.refs_0_.x_first
  13.5 0.7 collective-permute-start.5
  14.2 1.3 %shard_map.63 = (bf16[4,256,256]{2,1,0:T(8,128)(2,1)S(1)}, bf16[4,256,256]{2,1,0:T(8,128)(2,1)S(1)}, bf16[4,256,256]{2,1,0:T(8,128)(2,1)S(1)}, bf16[4,256,256]{2,1,0:T(8,128)(2,1)S(1)}, f32[2,256,256]{2,1,0:T(8,128)S(1)}) custom-call(s32[2]{0:T(128)S(1)} %copy-done.3, f32[2,2,2,256,256]{4,3,2,1,0:T(8,128)S(1)} %copy-done, ...), custom_call_target="tpu_custom_call" | custom-call | flops 1 | bytes 1 | tf_op jit(solution)/shard_map/pallas_call | solution.py:314
  15.5 0.0 collective-permute-done.2.e_second.refs_0_
  15.6 0.7 collective-permute-start.3
  16.2 0.0 collective-permute-done.5
  16.3 0.7 collective-permute-start.6
  16.9 7.5 %collective-permute-done.g_in = f32[2,256,256]{2,1,0:T(8,128)S(1)} collective-permute-done((f32[2,256,256]{2,1,0:T(8,128)S(1)}, f32[2,256,256]{2,1,0:T(8,128)S(1)}, u32[]{:S(2)}, u32[]{:S(2)}) %collective-permute-start) | collective-permute-done | bytes 524320 | tf_op jit(solution)/shard_map/ppermute | solution.py:362
  24.4 1.7 %shard_map.64 = (bf16[4,256,256]{2,1,0:T(8,128)(2,1)S(1)}, bf16[4,256,256]{2,1,0:T(8,128)(2,1)S(1)}, f32[2,264,128]{2,1,0:T(8,128)S(1)}, bf16[4,256,256]{2,1,0:T...) custom-call(f32[2,256,256]{2,1,0:T(8,128)S(1)} %get-tuple-element.42.g, ...), custom_call_target="tpu_custom_call" | custom-call | flops 99999997952 | bytes 1 | tf_op jit(solution)/shard_map/pallas_call | solution.py:314
  26.1 0.0 collective-permute-done.3.refs_0_
  26.1 0.0 collective-permute-done.6.refs_1_
  26.2 0.7 collective-permute-start.7
  26.9 0.0 collective-permute-done.7.refs_0_.refs_2_
  26.9 1.5 %collective-permute-start.8 = (f32[2,264,128]{2,1,0:T(8,128)S(1)}, f32[2,264,128]{2,1,0:T(8,128)S(1)}, u32[]{:S(2)}, u32[]{:S(2)}) collective-permute-start(f32[2,264,128]{2,1,0:T(8,128)S(1)} %shard_map.68), channel_id=1, source_target_pairs={{5,7},{4,6},{13,15},{12,14},{21,23},{20,22},{29,31},{28,30}} | collective-permute-start | bytes 811016 | tf_op jit(solution)/shard_map/ppermute | solution.py:398
  28.4 11.8 %collective-permute-done.8.refs_3_ = f32[2,264,128]{2,1,0:T(8,128)S(1)} collective-permute-done((f32[2,264,128]{2,1,0:T(8,128)S(1)}, f32[2,264,128]{2,1,0:T(8,128)S(1)}, u32[]{:S(2)}, u32[]{:S(2)}) %collective-permute-start.8) | collective-permute-done | bytes 270368 | tf_op jit(solution)/shard_map/ppermute | solution.py:398
  40.2 1.2 %shard_map.69 = (f32[2,264,128]{2,1,0:T(8,128)S(1)}, f32[2,264,128]{2,1,0:T(8,128)S(1)}) custom-call(bf16[4,256,256]{2,1,0:T(8,128)(2,1)S(1)} %get-tuple-element.45.fas, bf16[4,256,256]{2,1,0:T(8,128)(2,1)S(1)} %get-tuple-element.46.fat, f32[2,264,128]{2,1,0:T(8,128)S(1)} %get-tuple-element.47.ea, f32[2,264,128]{2,1,0:T(8,128)S(1)} %collective-permute-done.3.refs_0_, ...), custom_call_target="tpu_custom_call" | custom-call | flops 1 | bytes 1 | tf_op jit(solution)/shard_map/pallas_call | solution.py:314
  41.4 4.5 %collective-permute-start.9 = (f32[2,264,128]{2,1,0:T(8,128)S(1)}, f32[2,264,128]{2,1,0:T(8,128)S(1)}, u32[]{:S(2)}, u32[]{:S(2)}) collective-permute-start(f32[2,264,128]{2,1,0:T(8,128)S(1)} %get-tuple-element.55), channel_id=1, source_target_pairs={{0,1},{1,0},{2,3},{3,2},{4,5},{5,4},{6,7},{7,6},{8,9},{9,8},{10,11... | collective-permute-start | bytes 811016 | tf_op jit(solution)/shard_map/ppermute | solution.py:407
  46.0 2.0 %shard_map.70 = (f32[2,512,128]{2,1,0:T(8,128)S(1)}, f32[2,264,128]{2,1,0:T(8,128)S(1)}) custom-call(f32[2,2]{1,0:T(2,128)S(1)} %copy-done.2, f32[2,264,128]{2,1,0:T(8,128)S(1)} %get-tuple-element.59.x, bf16[4,256,256]{2,1,0:T(8,128)(2,1)S(1)} %get-tuple-element.60.f0s, bf16[4,256,256]{2,1,0:T(8,128)(2,1)S(1)} %get-tuple-element.61.f0t, ...), custom_call_target="tpu_custom_call" | custom-call | flops 1 | bytes 1 | tf_op jit(solution)/shard_map/pallas_call | solution.py:314
  48.0 1.8 %collective-permute-done.9.x = f32[2,264,128]{2,1,0:T(8,128)S(1)} collective-permute-done((f32[2,264,128]{2,1,0:T(8,128)S(1)}, f32[2,264,128]{2,1,0:T(8,128)S(1)}, u32[]{:S(2)}, u32[]{:S(2)}) %collective-permute-start.9) | collective-permute-done | bytes 270368 | tf_op jit(solution)/shard_map/ppermute | solution.py:407
  49.8 1.5 %shard_map.71 = (f32[2,512,128]{2,1,0:T(8,128)S(1)}, bf16[4,256,256]{2,1,0:T(8,128)(2,1)S(1)}, bf16[4,256,256]{2,1,0:T(8,128)(2,1)S(1)}) custom-call(f32[2,2]{1,0:T(2,128)S(1)} %copy-done.2, f32[2,264,128]{2,1,0:T(8,128)S(1)} %collective-permute-done.9.x, f32[2,264,128]{2,1,0:T(8,128)S(1)} %collective-permute-done.4.refs_0_.x_first, ...), custom_call_target="tpu_custom_call" | custom-call | flops 1 | bytes 1 | tf_op jit(solution)/shard_map/pallas_call | solution.py:314
  51.4 3.8 %collective-permute-start.13 = (f32[512,128]{1,0:T(8,128)S(1)}, f32[512,128]{1,0:T(8,128)S(1)}, u32[]{:S(2)}, u32[]{:S(2)}) collective-permute-start(f32[512,128]{1,0:T(8,128)S(1)} %slice_bitcast_fusion), channel_id=1, source_target_pairs={{0,8},{8,0},{16,24},{24,16},{1,9},{9,1},{17,25},{25,17},{2,10},{10... | collective-permute-start | bytes 786440 | tf_op jit(solution)/shard_map/ppermute | solution.py:420
  55.2 0.6 shard_map.72
  55.8 0.1 collective-permute-start.10
  55.9 0.5 collective-permute-done.13
  56.4 0.3 collective-permute-start.14
  56.7 0.5 collective-permute-done.10
  57.2 0.8 %collective-permute-start.11 = (f32[264,128]{1,0:T(8,128)S(1)}, f32[264,128]{1,0:T(8,128)S(1)}, u32[]{:S(2)}, u32[]{:S(2)}) collective-permute-start(f32[264,128]{1,0:T(8,128)S(1)} %fusion), channel_id=1, source_target_pairs={{0,16},{8,24},{16,0},{24,8},{1,17},{9,25},{17,1},{25,9},{2,18},{10... | collective-permute-start | bytes 405512 | tf_op jit(solution)/shard_map/ppermute | solution.py:420
  58.0 6.0 %collective-permute-done.14 = f32[512,128]{1,0:T(8,128)S(1)} collective-permute-done((f32[512,128]{1,0:T(8,128)S(1)}, f32[512,128]{1,0:T(8,128)S(1)}, u32[]{:S(2)}, u32[]{:S(2)}) %collective-permute-start.14) | collective-permute-done | bytes 262176 | tf_op jit(solution)/shard_map/ppermute | solution.py:420
  64.0 2.1 %collective-permute-start.15 = (f32[512,128]{1,0:T(8,128)S(1)}, f32[512,128]{1,0:T(8,128)S(1)}, u32[]{:S(2)}, u32[]{:S(2)}) collective-permute-start(f32[512,128]{1,0:T(8,128)S(1)} %add.15.mine), channel_id=1, source_target_pairs={{0,8},{8,0},{16,24},{24,16},{1,9},{9,1},{17,25},{25,17},{2,10},{10... | collective-permute-start | bytes 786440 | tf_op jit(solution)/shard_map/ppermute | solution.py:420
  66.0 0.8 %collective-permute-done.11 = f32[264,128]{1,0:T(8,128)S(1)} collective-permute-done((f32[264,128]{1,0:T(8,128)S(1)}, f32[264,128]{1,0:T(8,128)S(1)}, u32[]{:S(2)}, u32[]{:S(2)}) %collective-permute-start.11) | collective-permute-done | bytes 135200 | tf_op jit(solution)/shard_map/ppermute | solution.py:420
  66.9 1.3 %collective-permute-start.12 = (f32[264,128]{1,0:T(8,128)S(1)}, f32[264,128]{1,0:T(8,128)S(1)}, u32[]{:S(2)}, u32[]{:S(2)}) collective-permute-start(f32[264,128]{1,0:T(8,128)S(1)} %add.13.mine), channel_id=1, source_target_pairs={{0,8},{8,0},{16,24},{24,16},{1,9},{9,1},{17,25},{25,17},{2,10},{10... | collective-permute-start | bytes 405512 | tf_op jit(solution)/shard_map/ppermute | solution.py:420
  68.1 0.0 collective-permute-done.15.theirs
  68.1 0.8 %shard_map.73 = (f32[2,256,256]{2,1,0:T(8,128)}, f32[8,128]{1,0:T(8,128)S(1)}) custom-call(f32[512,128]{1,0:T(8,128)S(1)} %add.15.mine, f32[512,128]{1,0:T(8,128)S(1)} %collective-permute-done.15.theirs), custom_call_target="tpu_custom_call" | custom-call | flops 1 | bytes 1 | tf_op jit(solution)/shard_map/pallas_call | solution.py:314
  69.0 0.1 collective-permute-done.12.theirs
  69.1 0.9 %shard_map.74 = f32[2,256,256]{2,1,0:T(8,128)} custom-call(f32[264,128]{1,0:T(8,128)S(1)} %add.13.mine, f32[264,128]{1,0:T(8,128)S(1)} %collective-permute-done.12.theirs, f32[8,128]{1,0:T(8,128)S(1)} %get-tuple-element.68._), custom_call_target="tpu_custom_call" | custom-call | flops 1 | bytes 1 | tf_op jit(solution)/shard_map/pallas_call | solution.py:314
  (14 shorter events, 0.2 us)
Async XLA Ops:
  0.7 6.7 %copy-start = (f32[2,2,2,256,256]{4,3,2,1,0:T(8,128)S(1)}, f32[2,2,2,256,256]{4,3,2,1,0:T(8,128)}, u32[]{:S(2)}) copy-start(f32[2,2,2,256,256]{4,3,2,1,0:T(8,128)} %factor.9) | copy-start | bytes 6291460
  0.7 6.7 %copy-start.3 = (s32[2]{0:T(128)S(1)}, s32[2]{0:T(128)}, u32[]{:S(2)}) copy-start(s32[2]{0:T(128)} %live.9) | copy-start | bytes 28
  3.5 7.5 %copy-start.1 = (f32[2,2,2,256,256]{4,3,2,1,0:T(8,128)S(1)}, f32[2,2,2,256,256]{4,3,2,1,0:T(8,128)}, u32[]{:S(2)}) copy-start(f32[2,2,2,256,256]{4,3,2,1,0:T(8,128)} %pivot.5) | copy-start | bytes 6291460
  3.5 7.5 %copy-start.2 = (f32[2,2]{1,0:T(2,128)S(1)}, f32[2,2]{1,0:T(2,128)}, u32[]{:S(2)}) copy-start(f32[2,2]{1,0:T(2,128)} %weight.9) | copy-start | bytes 52
  3.5 10.0 %collective-permute-start.1 = (f32[2,264,128]{2,1,0:T(8,128)S(1)}, f32[2,264,128]{2,1,0:T(8,128)S(1)}, u32[]{:S(2)}, u32[]{:S(2)}) collective-permute-start(f32[2,264,128]{2,1,0:T(8,128)S(1)} %get-tuple-element.44.e), channel_id=1, source_target_pairs={{2,3},{3,2},{4,5},{5,4},{6,7},{7,6},{10,11},{11,10},{12,13},{13,12... | collective-permute-start | bytes 811016 | tf_op jit(solution)/shard_map/ppermute | solution.py:358
  6.8 6.7 %collective-permute-start.4 = (f32[2,264,128]{2,1,0:T(8,128)S(1)}, f32[2,264,128]{2,1,0:T(8,128)S(1)}, u32[]{:S(2)}, u32[]{:S(2)}) collective-permute-start(f32[2,264,128]{2,1,0:T(8,128)S(1)} %get-tuple-element.37.refs_1_), channel_id=1, source_target_pairs={{0,1},{8,9},{16,17},{24,25}} | collective-permute-start | bytes 811016 | tf_op jit(solution)/shard_map/ppermute | solution.py:356
  8.8 15.7 %collective-permute-start = (f32[2,256,256]{2,1,0:T(8,128)S(1)}, f32[2,256,256]{2,1,0:T(8,128)S(1)}, u32[]{:S(2)}, u32[]{:S(2)}) collective-permute-start(f32[2,256,256]{2,1,0:T(8,128)S(1)} %get-tuple-element.40._), channel_id=1, source_target_pairs={{2,3},{3,2},{4,5},{5,4},{6,7},{7,6},{10,11},{11,10},{12,13},{13,12... | collective-permute-start | bytes 1572872 | tf_op jit(solution)/shard_map/ppermute | solution.py:362
  12.8 2.7 %collective-permute-start.2 = (f32[2,264,128]{2,1,0:T(8,128)S(1)}, f32[2,264,128]{2,1,0:T(8,128)S(1)}, u32[]{:S(2)}, u32[]{:S(2)}) collective-permute-start(f32[2,264,128]{2,1,0:T(8,128)S(1)} %get-tuple-element.43.e), channel_id=1, source_target_pairs={{0,1},{8,9},{16,17},{24,25}} | collective-permute-start | bytes 811016 | tf_op jit(solution)/shard_map/ppermute | solution.py:372
  13.5 2.7 %collective-permute-start.5 = (f32[2,264,128]{2,1,0:T(8,128)S(1)}, f32[2,264,128]{2,1,0:T(8,128)S(1)}, u32[]{:S(2)}, u32[]{:S(2)}) collective-permute-start(f32[2,264,128]{2,1,0:T(8,128)S(1)} %shard_map.66), channel_id=1, source_target_pairs={{1,0},{9,8},{17,16},{25,24}} | collective-permute-start | bytes 811016 | tf_op jit(solution)/shard_map/ppermute | solution.py:376
  15.6 10.6 %collective-permute-start.3 = (f32[2,264,128]{2,1,0:T(8,128)S(1)}, f32[2,264,128]{2,1,0:T(8,128)S(1)}, u32[]{:S(2)}, u32[]{:S(2)}) collective-permute-start(f32[2,264,128]{2,1,0:T(8,128)S(1)} %shard_map.65), channel_id=1, source_target_pairs={{1,3},{9,11},{17,19},{25,27}} | collective-permute-start | bytes 811016 | tf_op jit(solution)/shard_map/ppermute | solution.py:381
  16.3 9.9 %collective-permute-start.6 = (f32[2,264,128]{2,1,0:T(8,128)S(1)}, f32[2,264,128]{2,1,0:T(8,128)S(1)}, u32[]{:S(2)}, u32[]{:S(2)}) collective-permute-start(f32[2,264,128]{2,1,0:T(8,128)S(1)} %collective-permute-done.5), channel_id=1, source_target_pairs={{0,2},{8,10},{16,18},{24,26}} | collective-permute-start | bytes 811016 | tf_op jit(solution)/shard_map/ppermute | solution.py:382
  26.2 0.7 collective-permute-start.7
  26.9 13.3 %collective-permute-start.8 = (f32[2,264,128]{2,1,0:T(8,128)S(1)}, f32[2,264,128]{2,1,0:T(8,128)S(1)}, u32[]{:S(2)}, u32[]{:S(2)}) collective-permute-start(f32[2,264,128]{2,1,0:T(8,128)S(1)} %shard_map.68), channel_id=1, source_target_pairs={{5,7},{4,6},{13,15},{12,14},{21,23},{20,22},{29,31},{28,30}} | collective-permute-start | bytes 811016 | tf_op jit(solution)/shard_map/ppermute | solution.py:398
  41.4 8.4 %collective-permute-start.9 = (f32[2,264,128]{2,1,0:T(8,128)S(1)}, f32[2,264,128]{2,1,0:T(8,128)S(1)}, u32[]{:S(2)}, u32[]{:S(2)}) collective-permute-start(f32[2,264,128]{2,1,0:T(8,128)S(1)} %get-tuple-element.55), channel_id=1, source_target_pairs={{0,1},{1,0},{2,3},{3,2},{4,5},{5,4},{6,7},{7,6},{8,9},{9,8},{10,11... | collective-permute-start | bytes 811016 | tf_op jit(solution)/shard_map/ppermute | solution.py:407
  51.4 5.0 %collective-permute-start.13 = (f32[512,128]{1,0:T(8,128)S(1)}, f32[512,128]{1,0:T(8,128)S(1)}, u32[]{:S(2)}, u32[]{:S(2)}) collective-permute-start(f32[512,128]{1,0:T(8,128)S(1)} %slice_bitcast_fusion), channel_id=1, source_target_pairs={{0,8},{8,0},{16,24},{24,16},{1,9},{9,1},{17,25},{25,17},{2,10},{10... | collective-permute-start | bytes 786440 | tf_op jit(solution)/shard_map/ppermute | solution.py:420
  55.8 1.4 %collective-permute-start.10 = (f32[264,128]{1,0:T(8,128)S(1)}, f32[264,128]{1,0:T(8,128)S(1)}, u32[]{:S(2)}, u32[]{:S(2)}) collective-permute-start(f32[264,128]{1,0:T(8,128)S(1)} %slice_bitcast_fusion.1), channel_id=1, source_target_pairs={{0,8},{8,0},{16,24},{24,16},{1,9},{9,1},{17,25},{25,17},{2,10},{10... | collective-permute-start | bytes 405512 | tf_op jit(solution)/shard_map/ppermute | solution.py:420
  56.4 7.6 %collective-permute-start.14 = (f32[512,128]{1,0:T(8,128)S(1)}, f32[512,128]{1,0:T(8,128)S(1)}, u32[]{:S(2)}, u32[]{:S(2)}) collective-permute-start(f32[512,128]{1,0:T(8,128)S(1)} %bitcast_add_fusion), channel_id=1, source_target_pairs={{0,16},{8,24},{16,0},{24,8},{1,17},{9,25},{17,1},{25,9},{2,18},{10... | collective-permute-start | bytes 786440 | tf_op jit(solution)/shard_map/ppermute | solution.py:420
  57.2 9.6 %collective-permute-start.11 = (f32[264,128]{1,0:T(8,128)S(1)}, f32[264,128]{1,0:T(8,128)S(1)}, u32[]{:S(2)}, u32[]{:S(2)}) collective-permute-start(f32[264,128]{1,0:T(8,128)S(1)} %fusion), channel_id=1, source_target_pairs={{0,16},{8,24},{16,0},{24,8},{1,17},{9,25},{17,1},{25,9},{2,18},{10... | collective-permute-start | bytes 405512 | tf_op jit(solution)/shard_map/ppermute | solution.py:420
  64.0 4.2 %collective-permute-start.15 = (f32[512,128]{1,0:T(8,128)S(1)}, f32[512,128]{1,0:T(8,128)S(1)}, u32[]{:S(2)}, u32[]{:S(2)}) collective-permute-start(f32[512,128]{1,0:T(8,128)S(1)} %add.15.mine), channel_id=1, source_target_pairs={{0,8},{8,0},{16,24},{24,16},{1,9},{9,1},{17,25},{25,17},{2,10},{10... | collective-permute-start | bytes 786440 | tf_op jit(solution)/shard_map/ppermute | solution.py:420
  66.9 2.3 %collective-permute-start.12 = (f32[264,128]{1,0:T(8,128)S(1)}, f32[264,128]{1,0:T(8,128)S(1)}, u32[]{:S(2)}, u32[]{:S(2)}) collective-permute-start(f32[264,128]{1,0:T(8,128)S(1)} %add.13.mine), channel_id=1, source_target_pairs={{0,8},{8,0},{16,24},{24,16},{1,9},{9,1},{17,25},{25,17},{2,10},{10... | collective-permute-start | bytes 405512 | tf_op jit(solution)/shard_map/ppermute | solution.py:420

commit v4 on v3

--- a/solution.py
+++ b/solution.py
@@ -140,8 +140,8 @@
     constants_of(slot, blocks, link, widths, weights, *outs, wait)
 
 
-def root_constant_kernel(live, pivot, factor, weight, *refs):
-    @pl.when(whereabouts()[0] == 0)
+def sent_constant_kernel(live, pivot, factor, weight, *refs):
+    @pl.when(whereabouts()[0] != 1)
     def _():
         fetched_constants(slot_of(False), live, pivot, factor, weight, refs[:3], refs[3:])
 
@@ -150,12 +150,12 @@
     made, outs, scratch = refs[:3], refs[3:6], refs[6:]
     place = whereabouts()[0]
 
-    @pl.when(place == 0)
+    @pl.when(place != 1)
     def _():
         for source, target in zip(made, outs):
             target[...] = source[...]
 
-    @pl.when(place > 0)
+    @pl.when(place == 1)
     def _():
         fetched_constants(slot_of(False), live, pivot, factor, weight, outs, scratch)
 
@@ -352,10 +352,9 @@
         pltpu.SemaphoreType.DMA((5,)),
     ]
     far = [pltpu.with_memory_space_constraint(a, pltpu.HBM) for a in (live, pivot, factor, weight)]
-    made = run(root_constant_kernel, [], [], constants, scratch, far=far)
-    e_first = lax.ppermute(made[1], AXES, first)
+    made = run(sent_constant_kernel, [], [], constants, scratch, far=far)
+    e_in = lax.ppermute(made[1], AXES, first + swaps)
     o_f1s, o_e, o_w = run(first_constant_kernel, [], made, constants, scratch, far=far)
-    e_in = lax.ppermute(o_e, AXES, swaps)
     o_f0s, o_f0t, o_gs, o_gt, o_g = run(
         functools.partial(factor_kernel, False), [live], [factor, o_f1s], factors
     )
@@ -372,7 +371,7 @@
     e_second = lax.ppermute(m_e, AXES, first)
 
     starts = functools.partial(step_kernel, lambda place: place == 1)
-    (wave_even,) = run(starts, [], [o_gs, o_gt, o_e, e_first, e_in], [mirrored])
+    (wave_even,) = run(starts, [], [o_gs, o_gt, o_e, e_in], [mirrored])
     wave_even = lax.ppermute(wave_even, AXES, [(at(p, 1), at(p, 0)) for p in range(poles)])
     (wave_odd,) = run(starts, [], [m_gs, m_gt, m_e, e_second], [mirrored])
     received = []
@@ -412,7 +411,7 @@
     off, us, ts = run(
         more_off_kernel,
         [],
-        [weight, shared, e_first, o_f0s, o_f0t, o_gs, o_w, off],
+        [weight, shared, e_in, o_f0s, o_f0t, o_gs, o_w, off],
         [offs, parts, parts],
     )
 

time: 70.8 us -> 69.1 us (0.976)
  starting transfers between devices: 23.7 us -> 21.4 us
  local copies, waits for them, and re-layouts: 0.06 us -> 1.44 us
    ppermute x1, starting transfers between devices: 4.51 us -> 2.67 us  [local(): shared = lax.ppermute(sent, AXES, every)]
    unnamed x8, local copies, waits for them, and re-layouts: 0.03 us -> 1.41 us
    ppermute x1, waiting for transfers between devices: 7.49 us -> 6.19 us  [local(): g_in = lax.ppermute(o_g, AXES, swaps)]
    ppermute x2, waiting for transfers between devices: 11.8 us -> 12.9 us  [local(): arrived = [lax.ppermute(wave, AXES, up)]]
    ppermute x2 -> x1, starting transfers between devices: 3.93 us -> 3.12 us  [local(): e_in = lax.ppermute(made[1], AXES, first + swaps)]
  transfers between devices with their start and end apart: 16 -> 15, of which waited for: 8 -> 8; matrix products, arithmetic and copies ran while one was open for 0% -> 0% of each run, Pallas kernels for 14% -> 14%
where the time goes in v4:
time: 69.1 us; the launch traced here: 68.8 us
  waiting for transfers between devices  28.9 us (42%)
  starting transfers between devices  21.4 us (31%)
  Pallas kernels  16.1 us (23%)
  local copies, waits for them, and re-layouts  1.44 us (2%)
  between operations  0.92 us (1%)
    pallas_call x16, Pallas kernels, run(): pl.pallas_call(kernel, out_shape=shapes, in_specs=[SCALAR] * len(scalars)...  16.1 us
    ppermute x2, waiting for transfers between devices, local(): arrived = [lax.ppermute(wave, AXES, up)]  12.9 us
    ppermute x6, starting transfers between devices, exchanged(): lax.ppermute(value, 'pole', [(p, p ^ distance) for p in range(poles)])  8.61 us
    ppermute x6, waiting for transfers between devices, exchanged(): lax.ppermute(value, 'pole', [(p, p ^ distance) for p in range(poles)])  7.89 us
    ppermute x1, waiting for transfers between devices, local(): g_in = lax.ppermute(o_g, AXES, swaps)  6.19 us
    ppermute x1, starting transfers between devices, local(): e_in = lax.ppermute(made[1], AXES, first + swaps)  3.12 us
    ppermute x1, starting transfers between devices, local(): shared = lax.ppermute(sent, AXES, every)  2.67 us
    ppermute x1, starting transfers between devices, local(): g_in = lax.ppermute(o_g, AXES, swaps)  2.16 us
  transfers between devices with their start and end apart: 15, of which 8 were waited for; matrix products, arithmetic and copies ran while one was open for 0% of the time, Pallas kernels for 14%

profile of v4, /device:TPU:29, one launch (start us, length us, event | category | flops | bytes accessed | tf_op | source)
XLA Modules:
  0.0 68.8 jit_solution(9848562553388656412)
XLA Ops:
  0.6 2.6 %shard_map.59 = (bf16[4,256,256]{2,1,0:T(8,128)(2,1)S(1)}, f32[2,264,128]{2,1,0:T(8,128)S(1)}, f32[4,264,128]{2,1,0:T(8,128)S(1)}) custom-call(s32[2]{0:T(128)} %live.9, f32[2,2,2,256,256]{4,3,2,1,0:T(8,128)} %pivot.5, f32[2,2,2,256,256]{4,3,2,1,0:T(8,128)} %factor.9, f32[2,2]{1,0:T(2,128)} %weight.9), custom_call_target="tpu_custom_call" | custom-call | flops 1 | bytes 1 | tf_op jit(solution)/shard_map/pallas_call | solution.py:314
  3.2 3.1 %collective-permute-start.1 = (f32[2,264,128]{2,1,0:T(8,128)S(1)}, f32[2,264,128]{2,1,0:T(8,128)S(1)}, u32[]{:S(2)}, u32[]{:S(2)}) collective-permute-start(f32[2,264,128]{2,1,0:T(8,128)S(1)} %get-tuple-element.37.refs_1_), channel_id=1, source_target_pairs={{0,1},{8,9},{16,17},{24,25},{2,3},{3,2},{4,5},{5,4},{6,7},{7,6},{1... | collective-permute-start | bytes 811016 | tf_op jit(solution)/shard_map/ppermute | solution.py:356
  6.4 0.0 copy-start
  6.4 0.0 copy-start.3
  6.4 0.1 shard_map.60
  6.5 0.0 copy-start.1
  6.6 0.0 copy-start.2
  6.6 1.4 %copy-done = f32[2,2,2,256,256]{4,3,2,1,0:T(8,128)S(1)} copy-done((f32[2,2,2,256,256]{4,3,2,1,0:T(8,128)S(1)}, f32[2,2,2,256,256]{4,3,2,1,0:T(8,128)}, u32[]{:S(2)}) %copy-start) | copy-done | bytes 2097176
  8.0 0.0 copy-done.3
  8.0 1.3 %shard_map.61 = (bf16[4,256,256]{2,1,0:T(8,128)(2,1)S(1)}, bf16[4,256,256]{2,1,0:T(8,128)(2,1)S(1)}, bf16[4,256,256]{2,1,0:T(8,128)(2,1)S(1)}, bf16[4,256,256]{2,1,0:T(8,128)(2,1)S(1)}, f32[2,256,256]{2,1,0:T(8,128)S(1)}) custom-call(s32[2]{0:T(128)S(1)} %copy-done.3, f32[2,2,2,256,256]{4,3,2,1,0:T(8,128)S(1)} %copy-done, ...), custom_call_target="tpu_custom_call" | custom-call | flops 1 | bytes 1 | tf_op jit(solution)/shard_map/pallas_call | solution.py:314
  9.3 2.2 %collective-permute-start = (f32[2,256,256]{2,1,0:T(8,128)S(1)}, f32[2,256,256]{2,1,0:T(8,128)S(1)}, u32[]{:S(2)}, u32[]{:S(2)}) collective-permute-start(f32[2,256,256]{2,1,0:T(8,128)S(1)} %get-tuple-element.40._), channel_id=1, source_target_pairs={{2,3},{3,2},{4,5},{5,4},{6,7},{7,6},{10,11},{11,10},{12,13},{13,12... | collective-permute-start | bytes 1572872 | tf_op jit(solution)/shard_map/ppermute | solution.py:361
  11.5 1.8 %shard_map.62 = (bf16[4,256,256]{2,1,0:T(8,128)(2,1)S(1)}, f32[2,264,128]{2,1,0:T(8,128)S(1)}, f32[4,264,128]{2,1,0:T(8,128)S(1)}) custom-call(s32[2]{0:T(128)S(1)} %copy-done.3, f32[2,2,2,256,256]{4,3,2,1,0:T(8,128)S(1)} %copy-done.1, f32[2,2,2,256,256]{4,3,2,1,0:T(8,128)S(1)} %copy-done, f32[2,2]{1,0:T(2,128)S(1)} %copy-done.2, ...), custom_call_target="tpu_custom_call" | custom-call | flops 1 | bytes 1 | tf_op jit(solution)/shard_map/pallas_call | solution.py:314
  13.3 0.7 collective-permute-start.2
  14.0 0.0 collective-permute-done.1.e_in.refs_0_.x_first
  14.0 0.7 collective-permute-start.4
  14.7 1.3 %shard_map.63 = (bf16[4,256,256]{2,1,0:T(8,128)(2,1)S(1)}, bf16[4,256,256]{2,1,0:T(8,128)(2,1)S(1)}, bf16[4,256,256]{2,1,0:T(8,128)(2,1)S(1)}, bf16[4,256,256]{2,1,0:T(8,128)(2,1)S(1)}, f32[2,256,256]{2,1,0:T(8,128)S(1)}) custom-call(s32[2]{0:T(128)S(1)} %copy-done.3, f32[2,2,2,256,256]{4,3,2,1,0:T(8,128)S(1)} %copy-done, ...), custom_call_target="tpu_custom_call" | custom-call | flops 1 | bytes 1 | tf_op jit(solution)/shard_map/pallas_call | solution.py:314
  16.0 0.0 collective-permute-done.2.e_second.refs_0_
  16.1 0.7 collective-permute-start.3
  16.7 0.0 collective-permute-done.4
  16.8 0.7 collective-permute-start.5
  17.4 6.2 %collective-permute-done.g_in = f32[2,256,256]{2,1,0:T(8,128)S(1)} collective-permute-done((f32[2,256,256]{2,1,0:T(8,128)S(1)}, f32[2,256,256]{2,1,0:T(8,128)S(1)}, u32[]{:S(2)}, u32[]{:S(2)}) %collective-permute-start) | collective-permute-done | bytes 524320 | tf_op jit(solution)/shard_map/ppermute | solution.py:361
  23.6 1.7 %shard_map.64 = (bf16[4,256,256]{2,1,0:T(8,128)(2,1)S(1)}, bf16[4,256,256]{2,1,0:T(8,128)(2,1)S(1)}, f32[2,264,128]{2,1,0:T(8,128)S(1)}, bf16[4,256,256]{2,1,0:T...) custom-call(f32[2,256,256]{2,1,0:T(8,128)S(1)} %get-tuple-element.42.g, ...), custom_call_target="tpu_custom_call" | custom-call | flops 99999997952 | bytes 1 | tf_op jit(solution)/shard_map/pallas_call | solution.py:314
  25.3 0.0 collective-permute-done.3.refs_0_
  25.3 0.0 collective-permute-done.5.refs_1_
  25.4 0.7 collective-permute-start.6
  26.1 0.0 collective-permute-done.6.refs_0_.refs_2_
  26.1 1.5 %collective-permute-start.7 = (f32[2,264,128]{2,1,0:T(8,128)S(1)}, f32[2,264,128]{2,1,0:T(8,128)S(1)}, u32[]{:S(2)}, u32[]{:S(2)}) collective-permute-start(f32[2,264,128]{2,1,0:T(8,128)S(1)} %shard_map.68), channel_id=1, source_target_pairs={{5,7},{4,6},{13,15},{12,14},{21,23},{20,22},{29,31},{28,30}} | collective-permute-start | bytes 811016 | tf_op jit(solution)/shard_map/ppermute | solution.py:397
  27.6 12.9 %collective-permute-done.7.refs_3_ = f32[2,264,128]{2,1,0:T(8,128)S(1)} collective-permute-done((f32[2,264,128]{2,1,0:T(8,128)S(1)}, f32[2,264,128]{2,1,0:T(8,128)S(1)}, u32[]{:S(2)}, u32[]{:S(2)}) %collective-permute-start.7) | collective-permute-done | bytes 270368 | tf_op jit(solution)/shard_map/ppermute | solution.py:397
  40.5 1.2 %shard_map.69 = (f32[2,264,128]{2,1,0:T(8,128)S(1)}, f32[2,264,128]{2,1,0:T(8,128)S(1)}) custom-call(bf16[4,256,256]{2,1,0:T(8,128)(2,1)S(1)} %get-tuple-element.44.fas, bf16[4,256,256]{2,1,0:T(8,128)(2,1)S(1)} %get-tuple-element.45.fat, f32[2,264,128]{2,1,0:T(8,128)S(1)} %get-tuple-element.46.ea, f32[2,264,128]{2,1,0:T(8,128)S(1)} %collective-permute-done.3.refs_0_, ...), custom_call_target="tpu_custom_call" | custom-call | flops 1 | bytes 1 | tf_op jit(solution)/shard_map/pallas_call | solution.py:314
  41.7 2.7 %collective-permute-start.8 = (f32[2,264,128]{2,1,0:T(8,128)S(1)}, f32[2,264,128]{2,1,0:T(8,128)S(1)}, u32[]{:S(2)}, u32[]{:S(2)}) collective-permute-start(f32[2,264,128]{2,1,0:T(8,128)S(1)} %get-tuple-element.55), channel_id=1, source_target_pairs={{0,1},{1,0},{2,3},{3,2},{4,5},{5,4},{6,7},{7,6},{8,9},{9,8},{10,11... | collective-permute-start | bytes 811016 | tf_op jit(solution)/shard_map/ppermute | solution.py:406
  44.4 2.0 %shard_map.70 = (f32[2,512,128]{2,1,0:T(8,128)S(1)}, f32[2,264,128]{2,1,0:T(8,128)S(1)}) custom-call(f32[2,2]{1,0:T(2,128)S(1)} %copy-done.2, f32[2,264,128]{2,1,0:T(8,128)S(1)} %get-tuple-element.59.x, bf16[4,256,256]{2,1,0:T(8,128)(2,1)S(1)} %get-tuple-element.60.f0s, bf16[4,256,256]{2,1,0:T(8,128)(2,1)S(1)} %get-tuple-element.61.f0t, ...), custom_call_target="tpu_custom_call" | custom-call | flops 1 | bytes 1 | tf_op jit(solution)/shard_map/pallas_call | solution.py:314
  46.4 1.8 %collective-permute-done.8.x = f32[2,264,128]{2,1,0:T(8,128)S(1)} collective-permute-done((f32[2,264,128]{2,1,0:T(8,128)S(1)}, f32[2,264,128]{2,1,0:T(8,128)S(1)}, u32[]{:S(2)}, u32[]{:S(2)}) %collective-permute-start.8) | collective-permute-done | bytes 270368 | tf_op jit(solution)/shard_map/ppermute | solution.py:406
  48.3 1.5 %shard_map.71 = (f32[2,512,128]{2,1,0:T(8,128)S(1)}, bf16[4,256,256]{2,1,0:T(8,128)(2,1)S(1)}, bf16[4,256,256]{2,1,0:T(8,128)(2,1)S(1)}) custom-call(f32[2,2]{1,0:T(2,128)S(1)} %copy-done.2, f32[2,264,128]{2,1,0:T(8,128)S(1)} %collective-permute-done.8.x, f32[2,264,128]{2,1,0:T(8,128)S(1)} %collective-permute-done.1.e_in.refs_0_.x_first, ...), custom_call_target="tpu_custom_call" | custom-call | flops 1 | bytes 1 | tf_op jit(solution)/shard_map/pallas_call | solution.py:314
  49.8 4.1 %collective-permute-start.12 = (f32[512,128]{1,0:T(8,128)S(1)}, f32[512,128]{1,0:T(8,128)S(1)}, u32[]{:S(2)}, u32[]{:S(2)}) collective-permute-start(f32[512,128]{1,0:T(8,128)S(1)} %slice_bitcast_fusion), channel_id=1, source_target_pairs={{0,8},{8,0},{16,24},{24,16},{1,9},{9,1},{17,25},{25,17},{2,10},{10... | collective-permute-start | bytes 786440 | tf_op jit(solution)/shard_map/ppermute | solution.py:419
  53.9 0.6 shard_map.72
  54.5 0.1 collective-permute-start.9
  54.6 0.5 collective-permute-done.12
  55.1 0.3 collective-permute-start.13
  55.4 0.5 collective-permute-done.9
  56.0 0.8 %collective-permute-start.10 = (f32[264,128]{1,0:T(8,128)S(1)}, f32[264,128]{1,0:T(8,128)S(1)}, u32[]{:S(2)}, u32[]{:S(2)}) collective-permute-start(f32[264,128]{1,0:T(8,128)S(1)} %fusion), channel_id=1, source_target_pairs={{0,16},{8,24},{16,0},{24,8},{1,17},{9,25},{17,1},{25,9},{2,18},{10... | collective-permute-start | bytes 405512 | tf_op jit(solution)/shard_map/ppermute | solution.py:419
  56.8 6.0 %collective-permute-done.13 = f32[512,128]{1,0:T(8,128)S(1)} collective-permute-done((f32[512,128]{1,0:T(8,128)S(1)}, f32[512,128]{1,0:T(8,128)S(1)}, u32[]{:S(2)}, u32[]{:S(2)}) %collective-permute-start.13) | collective-permute-done | bytes 262176 | tf_op jit(solution)/shard_map/ppermute | solution.py:419
  62.8 2.1 %collective-permute-start.14 = (f32[512,128]{1,0:T(8,128)S(1)}, f32[512,128]{1,0:T(8,128)S(1)}, u32[]{:S(2)}, u32[]{:S(2)}) collective-permute-start(f32[512,128]{1,0:T(8,128)S(1)} %add.15.mine), channel_id=1, source_target_pairs={{0,8},{8,0},{16,24},{24,16},{1,9},{9,1},{17,25},{25,17},{2,10},{10... | collective-permute-start | bytes 786440 | tf_op jit(solution)/shard_map/ppermute | solution.py:419
  64.8 0.8 %collective-permute-done.10 = f32[264,128]{1,0:T(8,128)S(1)} collective-permute-done((f32[264,128]{1,0:T(8,128)S(1)}, f32[264,128]{1,0:T(8,128)S(1)}, u32[]{:S(2)}, u32[]{:S(2)}) %collective-permute-start.10) | collective-permute-done | bytes 135200 | tf_op jit(solution)/shard_map/ppermute | solution.py:419
  65.6 1.3 %collective-permute-start.11 = (f32[264,128]{1,0:T(8,128)S(1)}, f32[264,128]{1,0:T(8,128)S(1)}, u32[]{:S(2)}, u32[]{:S(2)}) collective-permute-start(f32[264,128]{1,0:T(8,128)S(1)} %add.13.mine), channel_id=1, source_target_pairs={{0,8},{8,0},{16,24},{24,16},{1,9},{9,1},{17,25},{25,17},{2,10},{10... | collective-permute-start | bytes 405512 | tf_op jit(solution)/shard_map/ppermute | solution.py:419
  66.9 0.0 collective-permute-done.14.theirs
  66.9 0.8 %shard_map.73 = (f32[2,256,256]{2,1,0:T(8,128)}, f32[8,128]{1,0:T(8,128)S(1)}) custom-call(f32[512,128]{1,0:T(8,128)S(1)} %add.15.mine, f32[512,128]{1,0:T(8,128)S(1)} %collective-permute-done.14.theirs), custom_call_target="tpu_custom_call" | custom-call | flops 1 | bytes 1 | tf_op jit(solution)/shard_map/pallas_call | solution.py:314
  67.7 0.1 collective-permute-done.11.theirs
  67.9 0.9 %shard_map.74 = f32[2,256,256]{2,1,0:T(8,128)} custom-call(f32[264,128]{1,0:T(8,128)S(1)} %add.13.mine, f32[264,128]{1,0:T(8,128)S(1)} %collective-permute-done.11.theirs, f32[8,128]{1,0:T(8,128)S(1)} %get-tuple-element.68._), custom_call_target="tpu_custom_call" | custom-call | flops 1 | bytes 1 | tf_op jit(solution)/shard_map/pallas_call | solution.py:314
  (12 shorter events, 0.2 us)
Async XLA Ops:
  3.2 10.8 %collective-permute-start.1 = (f32[2,264,128]{2,1,0:T(8,128)S(1)}, f32[2,264,128]{2,1,0:T(8,128)S(1)}, u32[]{:S(2)}, u32[]{:S(2)}) collective-permute-start(f32[2,264,128]{2,1,0:T(8,128)S(1)} %get-tuple-element.37.refs_1_), channel_id=1, source_target_pairs={{0,1},{8,9},{16,17},{24,25},{2,3},{3,2},{4,5},{5,4},{6,7},{7,6},{1... | collective-permute-start | bytes 811016 | tf_op jit(solution)/shard_map/ppermute | solution.py:356
  6.4 1.6 %copy-start = (f32[2,2,2,256,256]{4,3,2,1,0:T(8,128)S(1)}, f32[2,2,2,256,256]{4,3,2,1,0:T(8,128)}, u32[]{:S(2)}) copy-start(f32[2,2,2,256,256]{4,3,2,1,0:T(8,128)} %factor.9) | copy-start | bytes 6291460
  6.4 1.6 %copy-start.3 = (s32[2]{0:T(128)S(1)}, s32[2]{0:T(128)}, u32[]{:S(2)}) copy-start(s32[2]{0:T(128)} %live.9) | copy-start | bytes 28
  6.5 4.9 %copy-start.1 = (f32[2,2,2,256,256]{4,3,2,1,0:T(8,128)S(1)}, f32[2,2,2,256,256]{4,3,2,1,0:T(8,128)}, u32[]{:S(2)}) copy-start(f32[2,2,2,256,256]{4,3,2,1,0:T(8,128)} %pivot.5) | copy-start | bytes 6291460
  6.6 4.9 %copy-start.2 = (f32[2,2]{1,0:T(2,128)S(1)}, f32[2,2]{1,0:T(2,128)}, u32[]{:S(2)}) copy-start(f32[2,2]{1,0:T(2,128)} %weight.9) | copy-start | bytes 52
  9.3 14.4 %collective-permute-start = (f32[2,256,256]{2,1,0:T(8,128)S(1)}, f32[2,256,256]{2,1,0:T(8,128)S(1)}, u32[]{:S(2)}, u32[]{:S(2)}) collective-permute-start(f32[2,256,256]{2,1,0:T(8,128)S(1)} %get-tuple-element.40._), channel_id=1, source_target_pairs={{2,3},{3,2},{4,5},{5,4},{6,7},{7,6},{10,11},{11,10},{12,13},{13,12... | collective-permute-start | bytes 1572872 | tf_op jit(solution)/shard_map/ppermute | solution.py:361
  13.3 2.7 %collective-permute-start.2 = (f32[2,264,128]{2,1,0:T(8,128)S(1)}, f32[2,264,128]{2,1,0:T(8,128)S(1)}, u32[]{:S(2)}, u32[]{:S(2)}) collective-permute-start(f32[2,264,128]{2,1,0:T(8,128)S(1)} %get-tuple-element.43.e), channel_id=1, source_target_pairs={{0,1},{8,9},{16,17},{24,25}} | collective-permute-start | bytes 811016 | tf_op jit(solution)/shard_map/ppermute | solution.py:371
  14.0 2.7 %collective-permute-start.4 = (f32[2,264,128]{2,1,0:T(8,128)S(1)}, f32[2,264,128]{2,1,0:T(8,128)S(1)}, u32[]{:S(2)}, u32[]{:S(2)}) collective-permute-start(f32[2,264,128]{2,1,0:T(8,128)S(1)} %shard_map.66), channel_id=1, source_target_pairs={{1,0},{9,8},{17,16},{25,24}} | collective-permute-start | bytes 811016 | tf_op jit(solution)/shard_map/ppermute | solution.py:375
  16.1 9.3 %collective-permute-start.3 = (f32[2,264,128]{2,1,0:T(8,128)S(1)}, f32[2,264,128]{2,1,0:T(8,128)S(1)}, u32[]{:S(2)}, u32[]{:S(2)}) collective-permute-start(f32[2,264,128]{2,1,0:T(8,128)S(1)} %shard_map.65), channel_id=1, source_target_pairs={{1,3},{9,11},{17,19},{25,27}} | collective-permute-start | bytes 811016 | tf_op jit(solution)/shard_map/ppermute | solution.py:380
  16.8 8.6 %collective-permute-start.5 = (f32[2,264,128]{2,1,0:T(8,128)S(1)}, f32[2,264,128]{2,1,0:T(8,128)S(1)}, u32[]{:S(2)}, u32[]{:S(2)}) collective-permute-start(f32[2,264,128]{2,1,0:T(8,128)S(1)} %collective-permute-done.4), channel_id=1, source_target_pairs={{0,2},{8,10},{16,18},{24,26}} | collective-permute-start | bytes 811016 | tf_op jit(solution)/shard_map/ppermute | solution.py:381
  25.4 0.7 %collective-permute-start.6 = (f32[2,264,128]{2,1,0:T(8,128)S(1)}, f32[2,264,128]{2,1,0:T(8,128)S(1)}, u32[]{:S(2)}, u32[]{:S(2)}) collective-permute-start(f32[2,264,128]{2,1,0:T(8,128)S(1)} %shard_map.67), channel_id=1, source_target_pairs={{3,5},{2,4},{11,13},{10,12},{19,21},{18,20},{27,29},{26,28}} | collective-permute-start | bytes 811016 | tf_op jit(solution)/shard_map/ppermute | solution.py:397
  26.1 14.4 %collective-permute-start.7 = (f32[2,264,128]{2,1,0:T(8,128)S(1)}, f32[2,264,128]{2,1,0:T(8,128)S(1)}, u32[]{:S(2)}, u32[]{:S(2)}) collective-permute-start(f32[2,264,128]{2,1,0:T(8,128)S(1)} %shard_map.68), channel_id=1, source_target_pairs={{5,7},{4,6},{13,15},{12,14},{21,23},{20,22},{29,31},{28,30}} | collective-permute-start | bytes 811016 | tf_op jit(solution)/shard_map/ppermute | solution.py:397
  41.7 6.5 %collective-permute-start.8 = (f32[2,264,128]{2,1,0:T(8,128)S(1)}, f32[2,264,128]{2,1,0:T(8,128)S(1)}, u32[]{:S(2)}, u32[]{:S(2)}) collective-permute-start(f32[2,264,128]{2,1,0:T(8,128)S(1)} %get-tuple-element.55), channel_id=1, source_target_pairs={{0,1},{1,0},{2,3},{3,2},{4,5},{5,4},{6,7},{7,6},{8,9},{9,8},{10,11... | collective-permute-start | bytes 811016 | tf_op jit(solution)/shard_map/ppermute | solution.py:406
  49.8 5.3 %collective-permute-start.12 = (f32[512,128]{1,0:T(8,128)S(1)}, f32[512,128]{1,0:T(8,128)S(1)}, u32[]{:S(2)}, u32[]{:S(2)}) collective-permute-start(f32[512,128]{1,0:T(8,128)S(1)} %slice_bitcast_fusion), channel_id=1, source_target_pairs={{0,8},{8,0},{16,24},{24,16},{1,9},{9,1},{17,25},{25,17},{2,10},{10... | collective-permute-start | bytes 786440 | tf_op jit(solution)/shard_map/ppermute | solution.py:419
  54.5 1.4 %collective-permute-start.9 = (f32[264,128]{1,0:T(8,128)S(1)}, f32[264,128]{1,0:T(8,128)S(1)}, u32[]{:S(2)}, u32[]{:S(2)}) collective-permute-start(f32[264,128]{1,0:T(8,128)S(1)} %slice_bitcast_fusion.1), channel_id=1, source_target_pairs={{0,8},{8,0},{16,24},{24,16},{1,9},{9,1},{17,25},{25,17},{2,10},{10... | collective-permute-start | bytes 405512 | tf_op jit(solution)/shard_map/ppermute | solution.py:419
  55.1 7.6 %collective-permute-start.13 = (f32[512,128]{1,0:T(8,128)S(1)}, f32[512,128]{1,0:T(8,128)S(1)}, u32[]{:S(2)}, u32[]{:S(2)}) collective-permute-start(f32[512,128]{1,0:T(8,128)S(1)} %bitcast_add_fusion), channel_id=1, source_target_pairs={{0,16},{8,24},{16,0},{24,8},{1,17},{9,25},{17,1},{25,9},{2,18},{10... | collective-permute-start | bytes 786440 | tf_op jit(solution)/shard_map/ppermute | solution.py:419
  56.0 9.6 %collective-permute-start.10 = (f32[264,128]{1,0:T(8,128)S(1)}, f32[264,128]{1,0:T(8,128)S(1)}, u32[]{:S(2)}, u32[]{:S(2)}) collective-permute-start(f32[264,128]{1,0:T(8,128)S(1)} %fusion), channel_id=1, source_target_pairs={{0,16},{8,24},{16,0},{24,8},{1,17},{9,25},{17,1},{25,9},{2,18},{10... | collective-permute-start | bytes 405512 | tf_op jit(solution)/shard_map/ppermute | solution.py:419
  62.8 4.2 %collective-permute-start.14 = (f32[512,128]{1,0:T(8,128)S(1)}, f32[512,128]{1,0:T(8,128)S(1)}, u32[]{:S(2)}, u32[]{:S(2)}) collective-permute-start(f32[512,128]{1,0:T(8,128)S(1)} %add.15.mine), channel_id=1, source_target_pairs={{0,8},{8,0},{16,24},{24,16},{1,9},{9,1},{17,25},{25,17},{2,10},{10... | collective-permute-start | bytes 786440 | tf_op jit(solution)/shard_map/ppermute | solution.py:419
  65.6 2.3 %collective-permute-start.11 = (f32[264,128]{1,0:T(8,128)S(1)}, f32[264,128]{1,0:T(8,128)S(1)}, u32[]{:S(2)}, u32[]{:S(2)}) collective-permute-start(f32[264,128]{1,0:T(8,128)S(1)} %add.13.mine), channel_id=1, source_target_pairs={{0,8},{8,0},{16,24},{24,16},{1,9},{9,1},{17,25},{25,17},{2,10},{10... | collective-permute-start | bytes 405512 | tf_op jit(solution)/shard_map/ppermute | solution.py:419

commit v5 on v4

--- a/solution.py
+++ b/solution.py
@@ -23,19 +23,18 @@
     return rh, ih, rl, il
 
 
-def dot(left, right):
-    return jnp.dot(left, right, preferred_element_type=F32)
-
-
-def dot3(lh, ll, rh, rl):
-    return dot(lh, rh) + (dot(lh, rl) + dot(ll, rh))
+def deep_dot(left, right):
+    return jnp.dot(
+        jnp.concatenate(left, axis=1), jnp.concatenate(right, axis=0), preferred_element_type=F32
+    )
 
 
 def complex_dot(left, right):
     arh, aih, arl, ail = left
     brh, bih, brl, bil = right
-    real = dot3(arh, arl, brh, brl) - dot3(aih, ail, bih, bil)
-    imag = dot3(arh, arl, bih, bil) + dot3(aih, ail, brh, brl)
+    blocks = [arh, arh, arl, aih, aih, ail]
+    real = deep_dot(blocks, [brh, brl, brh, -bih, -bil, -bih])
+    imag = deep_dot(blocks, [bih, bil, bih, brh, brl, brh])
     return real, imag
 
 
@@ -97,7 +96,7 @@
     return hosted_slot() if hosted else 1 - hosted_slot()
 
 
-def constants_of(slot, blocks, link, widths, weights, f1s, e, weighted, wait=lambda: None):
+def constants_of(slot, blocks, link, widths, weights, f1s, e, weighted, *_, wait=lambda: None):
     width = blocks.shape[-1]
     row, column = rows_columns(width)
     kept = [column < widths[k] for k in range(2)]
@@ -121,6 +120,7 @@
 
 def fetched_constants(slot, live, pivot, factor, weight, outs, scratch):
     blocks, link, widths, weights, sems = scratch
+    first_factor = pltpu.make_async_copy(factor.at[slot, 0], outs[3], sems.at[5])
     copies = [
         pltpu.make_async_copy(live, widths, sems.at[0]),
         pltpu.make_async_copy(factor.at[slot, 1], link, sems.at[1]),
@@ -130,6 +130,7 @@
     ]
     for copy in copies:
         copy.start()
+    first_factor.start()
     copies[0].wait()
     copies[1].wait()
 
@@ -137,17 +138,18 @@
         for copy in copies[2:]:
             copy.wait()
 
-    constants_of(slot, blocks, link, widths, weights, *outs, wait)
+    constants_of(slot, blocks, link, widths, weights, *outs, wait=wait)
+    first_factor.wait()
 
 
 def sent_constant_kernel(live, pivot, factor, weight, *refs):
     @pl.when(whereabouts()[0] != 1)
     def _():
-        fetched_constants(slot_of(False), live, pivot, factor, weight, refs[:3], refs[3:])
+        fetched_constants(slot_of(False), live, pivot, factor, weight, refs[:4], refs[4:])
 
 
 def first_constant_kernel(live, pivot, factor, weight, *refs):
-    made, outs, scratch = refs[:3], refs[3:6], refs[6:]
+    made, outs, scratch = refs[:4], refs[4:8], refs[8:]
     place = whereabouts()[0]
 
     @pl.when(place != 1)
@@ -160,15 +162,15 @@
         fetched_constants(slot_of(False), live, pivot, factor, weight, outs, scratch)
 
 
-def constant_kernel(live, pivot, factor, weight, _, f1s, e, weighted):
+def constant_kernel(live, pivot, factor, weight, _, f1s, e, weighted, first_factor):
     slot = slot_of(True)
+    first_factor[...] = factor[slot, 0]
     constants_of(slot, pivot.at[slot], factor.at[slot, 1], live, weight, f1s, e, weighted)
 
 
-def factor_kernel(hosted, live, factor, f1s, f0s, f0t, gs, gt, g):
-    slot = slot_of(hosted)
+def factor_kernel(live, factor, f1s, f0s, f0t, gs, gt, g):
     _, column = rows_columns(factor.shape[-1])
-    f0 = [jnp.where(column < live[0], factor[slot, 0, c], 0.0) for c in range(2)]
+    f0 = [jnp.where(column < live[0], factor[c], 0.0) for c in range(2)]
     s0 = split_pair(*f0)
     gr, gi = complex_dot(s0, load4(f1s))
     g[0], g[1] = gr, gi
@@ -235,7 +237,9 @@
 
 
 def real_dot(left, right):
-    return dot3(left[0], left[2], right[0], right[2]) + dot3(left[1], left[3], right[1], right[3])
+    arh, aih, arl, ail = left
+    brh, bih, brl, bil = right
+    return deep_dot([arh, arh, arl, aih, aih, ail], [brh, brl, brh, bih, bil, bih])
 
 
 def off_values(slot, weight, xs, f0s, f0t, gs, weighted):
@@ -341,32 +345,33 @@
     swaps = [(at(p, s), at(p, s ^ 1)) for p in range(poles) for s in range(2, turns)]
     first = [(at(p, 0), at(p, 1)) for p in range(poles)]
     every = [(at(p, s), at(p, s ^ 1)) for p in range(poles) for s in range(turns)]
-    constants = [parts, mirrored, jax.ShapeDtypeStruct((4,) + quarter, F32)]
-    factors = [parts, parts, parts, parts, jax.ShapeDtypeStruct((2, width, width), F32)]
+    raw = jax.ShapeDtypeStruct((2, width, width), F32)
+    constants = [parts, mirrored, jax.ShapeDtypeStruct((4,) + quarter, F32), raw]
+    factors = [parts, parts, parts, parts, raw]
 
     scratch = [
         pltpu.VMEM(pivot.shape[1:], F32),
         pltpu.VMEM(factor.shape[2:], F32),
         pltpu.SMEM(live.shape, jnp.int32),
         pltpu.VMEM(weight.shape, F32),
-        pltpu.SemaphoreType.DMA((5,)),
+        pltpu.SemaphoreType.DMA((6,)),
     ]
     far = [pltpu.with_memory_space_constraint(a, pltpu.HBM) for a in (live, pivot, factor, weight)]
     made = run(sent_constant_kernel, [], [], constants, scratch, far=far)
     e_in = lax.ppermute(made[1], AXES, first + swaps)
-    o_f1s, o_e, o_w = run(first_constant_kernel, [], made, constants, scratch, far=far)
+    o_f1s, o_e, o_w, o_f0 = run(first_constant_kernel, [], made, constants, scratch, far=far)
     o_f0s, o_f0t, o_gs, o_gt, o_g = run(
-        functools.partial(factor_kernel, False), [live], [factor, o_f1s], factors
+        factor_kernel, [live], [o_f0, o_f1s], factors
     )
     g_in = lax.ppermute(o_g, AXES, swaps)
-    m_f1s, m_e, m_w = run(
+    m_f1s, m_e, m_w, m_f0 = run(
         constant_kernel,
         [live],
         [pivot, factor, weight, o_g],
         constants,
     )
     m_f0s, m_f0t, m_gs, m_gt, m_g = run(
-        functools.partial(factor_kernel, True), [live], [factor, m_f1s], factors
+        factor_kernel, [live], [m_f0, m_f1s], factors
     )
     e_second = lax.ppermute(m_e, AXES, first)
 

time: 69.1 us -> 69.5 us (level)
  local copies, waits for them, and re-layouts: 1.44 us -> 0.47 us
  waiting for transfers between devices: 28.9 us -> 29.7 us
  Pallas kernels: 16.1 us -> 16.8 us
    ppermute x1, waiting for transfers between devices: 6.19 us -> 7.57 us  [local(): g_in = lax.ppermute(o_g, AXES, swaps)]
    ppermute x1, starting transfers between devices: 2.67 us -> 1.33 us  [local(): shared = lax.ppermute(sent, AXES, every)]
    ppermute x6, starting transfers between devices: 8.61 us -> 9.71 us  [exchanged(): lax.ppermute(value, 'pole', [(p, p ^ distance) for p in range(poles)])]
    unnamed x8, local copies, waits for them, and re-layouts: 1.41 us -> 0.44 us
    pallas_call x16, Pallas kernels: 16.1 us -> 16.8 us  [run(): pl.pallas_call(kernel, out_shape=shapes, in_specs=[SCALAR] * len(scalars)...]
  transfers between devices with their start and end apart: 15 -> 15, of which waited for: 8 -> 8; matrix products, arithmetic and copies ran while one was open for 0% -> 0% of each run, Pallas kernels for 14% -> 15%
where the time goes in v5:
time: 69.5 us; the launch traced here: 69.2 us
  waiting for transfers between devices  29.7 us (43%)
  starting transfers between devices  21.2 us (31%)
  Pallas kernels  16.8 us (24%)
  between operations  0.93 us (1%)
    pallas_call x16, Pallas kernels, run(): pl.pallas_call(kernel, out_shape=shapes, in_specs=[SCALAR] * len(scalars)...  16.8 us
    ppermute x2, waiting for transfers between devices, local(): arrived = [lax.ppermute(wave, AXES, up)]  12.6 us
    ppermute x6, starting transfers between devices, exchanged(): lax.ppermute(value, 'pole', [(p, p ^ distance) for p in range(poles)])  9.71 us
    ppermute x6, waiting for transfers between devices, exchanged(): lax.ppermute(value, 'pole', [(p, p ^ distance) for p in range(poles)])  7.91 us
    ppermute x1, waiting for transfers between devices, local(): g_in = lax.ppermute(o_g, AXES, swaps)  7.57 us
    ppermute x1, starting transfers between devices, local(): e_in = lax.ppermute(made[1], AXES, first + swaps)  3.12 us
    ppermute x1, starting transfers between devices, local(): g_in = lax.ppermute(o_g, AXES, swaps)  2.16 us
    ppermute x2, starting transfers between devices, local(): arrived = [lax.ppermute(wave, AXES, up)]  2.15 us
  transfers between devices with their start and end apart: 15, of which 8 were waited for; matrix products, arithmetic and copies ran while one was open for 0% of the time, Pallas kernels for 15%

profile of v5, /device:TPU:29, one launch (start us, length us, event | category | flops | bytes accessed | tf_op | source)
XLA Modules:
  0.0 69.2 jit_solution(14374090198932715154)
XLA Ops:
  0.6 2.6 %shard_map.59 = (bf16[4,256,256]{2,1,0:T(8,128)(2,1)S(1)}, f32[2,264,128]{2,1,0:T(8,128)S(1)}, f32[4,264,128]{2,1,0:T(8,128)S(1)}, f32[2,256,256]{2,1,0:T(8,128)S(1)}) custom-call(s32[2]{0:T(128)} %live.9, f32[2,2,2,256,256]{4,3,2,1,0:T(8,128)} %pivot.5, f32[2,2,2,256,256]{4,3,2,1,0:T(8,128)} %factor.5, f32[2,2]{1,0:T(2,128)} %weight.9), custom_call_target="tpu_custom_call" | custom-call | flops 1 | bytes 1 | tf_op jit(solution)/shard_map/pallas_call | solution.py:318
  3.2 3.1 %collective-permute-start.1 = (f32[2,264,128]{2,1,0:T(8,128)S(1)}, f32[2,264,128]{2,1,0:T(8,128)S(1)}, u32[]{:S(2)}, u32[]{:S(2)}) collective-permute-start(f32[2,264,128]{2,1,0:T(8,128)S(1)} %get-tuple-element.40.refs_1_), channel_id=1, source_target_pairs={{0,1},{8,9},{16,17},{24,25},{2,3},{3,2},{4,5},{5,4},{6,7},{7,6},{1... | collective-permute-start | bytes 811016 | tf_op jit(solution)/shard_map/ppermute | solution.py:361
  6.4 0.0 copy-start.3
  6.4 0.0 copy-start
  6.4 0.0 copy-start.1
  6.4 0.0 copy-start.2
  6.4 0.2 shard_map.60
  6.6 0.4 copy-done.3
  7.0 1.3 %shard_map.61 = (bf16[4,256,256]{2,1,0:T(8,128)(2,1)S(1)}, bf16[4,256,256]{2,1,0:T(8,128)(2,1)S(1)}, bf16[4,256,256]{2,1,0:T(8,128)(2,1)S(1)}, bf16[4,256,256]{2,1,0:T(8,128)(2,1)S(1)}, f32[2,256,256]{2,1,0:T(8,128)S(1)}) custom-call(s32[2]{0:T(128)S(1)} %copy-done.3, f32[2,256,256]{2,1,0:T(8,128)S(1)} %get-tuple-element.43.factor, ...), custom_call_target="tpu_custom_call" | custom-call | flops 1 | bytes 1 | tf_op jit(solution)/shard_map/pallas_call | solution.py:318
  8.3 2.2 %collective-permute-start = (f32[2,256,256]{2,1,0:T(8,128)S(1)}, f32[2,256,256]{2,1,0:T(8,128)S(1)}, u32[]{:S(2)}, u32[]{:S(2)}) collective-permute-start(f32[2,256,256]{2,1,0:T(8,128)S(1)} %get-tuple-element.45._), channel_id=1, source_target_pairs={{2,3},{3,2},{4,5},{5,4},{6,7},{7,6},{10,11},{11,10},{12,13},{13,12... | collective-permute-start | bytes 1572872 | tf_op jit(solution)/shard_map/ppermute | solution.py:366
  10.5 0.0 copy-done
  10.5 1.8 %shard_map.62 = (bf16[4,256,256]{2,1,0:T(8,128)(2,1)S(1)}, f32[2,264,128]{2,1,0:T(8,128)S(1)}, f32[4,264,128]{2,1,0:T(8,128)S(1)}, f32[2,256,256]{2,1,0:T(8,128)S(1)}) custom-call(s32[2]{0:T(128)S(1)} %copy-done.3, f32[2,2,2,256,256]{4,3,2,1,0:T(8,128)S(1)} %copy-done, f32[2,2,2,256,256]{4,3,2,1,0:T(8,128)S(1)} %copy-done.1, f32[2,2]{1,0:T(2,128)S(1)} %copy-done.2, ...), custom_call_target="tpu_custom_call" | custom-call | flops 1 | bytes 1 | tf_op jit(solution)/shard_map/pallas_call | solution.py:318
  12.4 0.7 collective-permute-start.2
  13.1 0.0 collective-permute-done.1.e_in.refs_0_.x_first
  13.1 0.7 collective-permute-start.4
  13.8 1.3 %shard_map.63 = (bf16[4,256,256]{2,1,0:T(8,128)(2,1)S(1)}, bf16[4,256,256]{2,1,0:T(8,128)(2,1)S(1)}, bf16[4,256,256]{2,1,0:T(8,128)(2,1)S(1)}, bf16[4,256,256]{2,1,0:T(8,128)(2,1)S(1)}, f32[2,256,256]{2,1,0:T(8,128)S(1)}) custom-call(s32[2]{0:T(128)S(1)} %copy-done.3, f32[2,256,256]{2,1,0:T(8,128)S(1)} %get-tuple-element.46.factor, ...), custom_call_target="tpu_custom_call" | custom-call | flops 1 | bytes 1 | tf_op jit(solution)/shard_map/pallas_call | solution.py:318
  15.1 0.0 collective-permute-done.2.e_second.refs_0_
  15.1 0.7 collective-permute-start.3
  15.8 0.0 collective-permute-done.4
  15.8 0.7 collective-permute-start.5
  16.5 7.6 %collective-permute-done.g_in = f32[2,256,256]{2,1,0:T(8,128)S(1)} collective-permute-done((f32[2,256,256]{2,1,0:T(8,128)S(1)}, f32[2,256,256]{2,1,0:T(8,128)S(1)}, u32[]{:S(2)}, u32[]{:S(2)}) %collective-permute-start) | collective-permute-done | bytes 524320 | tf_op jit(solution)/shard_map/ppermute | solution.py:366
  24.1 1.7 %shard_map.64 = (bf16[4,256,256]{2,1,0:T(8,128)(2,1)S(1)}, bf16[4,256,256]{2,1,0:T(8,128)(2,1)S(1)}, f32[2,264,128]{2,1,0:T(8,128)S(1)}, bf16[4,256,256]{2,1,0:T...) custom-call(f32[2,256,256]{2,1,0:T(8,128)S(1)} %get-tuple-element.48.g, ...), custom_call_target="tpu_custom_call" | custom-call | flops 99999997952 | bytes 1 | tf_op jit(solution)/shard_map/pallas_call | solution.py:318
  25.8 0.0 collective-permute-done.3.refs_0_
  25.8 0.0 collective-permute-done.5.refs_1_
  25.8 0.7 collective-permute-start.6
  26.5 0.0 collective-permute-done.6.refs_0_.refs_2_
  26.5 1.5 %collective-permute-start.7 = (f32[2,264,128]{2,1,0:T(8,128)S(1)}, f32[2,264,128]{2,1,0:T(8,128)S(1)}, u32[]{:S(2)}, u32[]{:S(2)}) collective-permute-start(f32[2,264,128]{2,1,0:T(8,128)S(1)} %shard_map.68), channel_id=1, source_target_pairs={{5,7},{4,6},{13,15},{12,14},{21,23},{20,22},{29,31},{28,30}} | collective-permute-start | bytes 811016 | tf_op jit(solution)/shard_map/ppermute | solution.py:402
  28.0 12.6 %collective-permute-done.7.refs_3_ = f32[2,264,128]{2,1,0:T(8,128)S(1)} collective-permute-done((f32[2,264,128]{2,1,0:T(8,128)S(1)}, f32[2,264,128]{2,1,0:T(8,128)S(1)}, u32[]{:S(2)}, u32[]{:S(2)}) %collective-permute-start.7) | collective-permute-done | bytes 270368 | tf_op jit(solution)/shard_map/ppermute | solution.py:402
  40.6 1.2 %shard_map.69 = (f32[2,264,128]{2,1,0:T(8,128)S(1)}, f32[2,264,128]{2,1,0:T(8,128)S(1)}) custom-call(bf16[4,256,256]{2,1,0:T(8,128)(2,1)S(1)} %get-tuple-element.50.fas, bf16[4,256,256]{2,1,0:T(8,128)(2,1)S(1)} %get-tuple-element.51.fat, f32[2,264,128]{2,1,0:T(8,128)S(1)} %get-tuple-element.52.ea, f32[2,264,128]{2,1,0:T(8,128)S(1)} %collective-permute-done.3.refs_0_, ...), custom_call_target="tpu_custom_call" | custom-call | flops 1 | bytes 1 | tf_op jit(solution)/shard_map/pallas_call | solution.py:318
  41.8 1.3 %collective-permute-start.8 = (f32[2,264,128]{2,1,0:T(8,128)S(1)}, f32[2,264,128]{2,1,0:T(8,128)S(1)}, u32[]{:S(2)}, u32[]{:S(2)}) collective-permute-start(f32[2,264,128]{2,1,0:T(8,128)S(1)} %get-tuple-element.61), channel_id=1, source_target_pairs={{0,1},{1,0},{2,3},{3,2},{4,5},{5,4},{6,7},{7,6},{8,9},{9,8},{10,11... | collective-permute-start | bytes 811016 | tf_op jit(solution)/shard_map/ppermute | solution.py:411
  43.1 2.4 %shard_map.70 = (f32[2,512,128]{2,1,0:T(8,128)S(1)}, f32[2,264,128]{2,1,0:T(8,128)S(1)}) custom-call(f32[2,2]{1,0:T(2,128)S(1)} %copy-done.2, f32[2,264,128]{2,1,0:T(8,128)S(1)} %get-tuple-element.65.x, bf16[4,256,256]{2,1,0:T(8,128)(2,1)S(1)} %get-tuple-element.66.f0s, bf16[4,256,256]{2,1,0:T(8,128)(2,1)S(1)} %get-tuple-element.67.f0t, ...), custom_call_target="tpu_custom_call" | custom-call | flops 1 | bytes 1 | tf_op jit(solution)/shard_map/pallas_call | solution.py:318
  45.5 1.7 %collective-permute-done.8.x = f32[2,264,128]{2,1,0:T(8,128)S(1)} collective-permute-done((f32[2,264,128]{2,1,0:T(8,128)S(1)}, f32[2,264,128]{2,1,0:T(8,128)S(1)}, u32[]{:S(2)}, u32[]{:S(2)}) %collective-permute-start.8) | collective-permute-done | bytes 270368 | tf_op jit(solution)/shard_map/ppermute | solution.py:411
  47.2 1.9 %shard_map.71 = (f32[2,512,128]{2,1,0:T(8,128)S(1)}, bf16[4,256,256]{2,1,0:T(8,128)(2,1)S(1)}, bf16[4,256,256]{2,1,0:T(8,128)(2,1)S(1)}) custom-call(f32[2,2]{1,0:T(2,128)S(1)} %copy-done.2, f32[2,264,128]{2,1,0:T(8,128)S(1)} %collective-permute-done.8.x, f32[2,264,128]{2,1,0:T(8,128)S(1)} %collective-permute-done.1.e_in.refs_0_.x_first, ...), custom_call_target="tpu_custom_call" | custom-call | flops 1 | bytes 1 | tf_op jit(solution)/shard_map/pallas_call | solution.py:318
  49.1 5.2 %collective-permute-start.12 = (f32[512,128]{1,0:T(8,128)S(1)}, f32[512,128]{1,0:T(8,128)S(1)}, u32[]{:S(2)}, u32[]{:S(2)}) collective-permute-start(f32[512,128]{1,0:T(8,128)S(1)} %slice_bitcast_fusion), channel_id=1, source_target_pairs={{0,8},{8,0},{16,24},{24,16},{1,9},{9,1},{17,25},{25,17},{2,10},{10... | collective-permute-start | bytes 786440 | tf_op jit(solution)/shard_map/ppermute | solution.py:424
  54.3 0.6 shard_map.72
  54.9 0.1 collective-permute-start.9
  55.0 0.5 collective-permute-done.12
  55.5 0.3 collective-permute-start.13
  55.8 0.5 collective-permute-done.9
  56.4 0.8 %collective-permute-start.10 = (f32[264,128]{1,0:T(8,128)S(1)}, f32[264,128]{1,0:T(8,128)S(1)}, u32[]{:S(2)}, u32[]{:S(2)}) collective-permute-start(f32[264,128]{1,0:T(8,128)S(1)} %fusion), channel_id=1, source_target_pairs={{0,16},{8,24},{16,0},{24,8},{1,17},{9,25},{17,1},{25,9},{2,18},{10... | collective-permute-start | bytes 405512 | tf_op jit(solution)/shard_map/ppermute | solution.py:424
  57.1 6.0 %collective-permute-done.13 = f32[512,128]{1,0:T(8,128)S(1)} collective-permute-done((f32[512,128]{1,0:T(8,128)S(1)}, f32[512,128]{1,0:T(8,128)S(1)}, u32[]{:S(2)}, u32[]{:S(2)}) %collective-permute-start.13) | collective-permute-done | bytes 262176 | tf_op jit(solution)/shard_map/ppermute | solution.py:424
  63.1 2.1 %collective-permute-start.14 = (f32[512,128]{1,0:T(8,128)S(1)}, f32[512,128]{1,0:T(8,128)S(1)}, u32[]{:S(2)}, u32[]{:S(2)}) collective-permute-start(f32[512,128]{1,0:T(8,128)S(1)} %add.15.mine), channel_id=1, source_target_pairs={{0,8},{8,0},{16,24},{24,16},{1,9},{9,1},{17,25},{25,17},{2,10},{10... | collective-permute-start | bytes 786440 | tf_op jit(solution)/shard_map/ppermute | solution.py:424
  65.2 0.8 %collective-permute-done.10 = f32[264,128]{1,0:T(8,128)S(1)} collective-permute-done((f32[264,128]{1,0:T(8,128)S(1)}, f32[264,128]{1,0:T(8,128)S(1)}, u32[]{:S(2)}, u32[]{:S(2)}) %collective-permute-start.10) | collective-permute-done | bytes 135200 | tf_op jit(solution)/shard_map/ppermute | solution.py:424
  66.0 1.3 %collective-permute-start.11 = (f32[264,128]{1,0:T(8,128)S(1)}, f32[264,128]{1,0:T(8,128)S(1)}, u32[]{:S(2)}, u32[]{:S(2)}) collective-permute-start(f32[264,128]{1,0:T(8,128)S(1)} %add.13.mine), channel_id=1, source_target_pairs={{0,8},{8,0},{16,24},{24,16},{1,9},{9,1},{17,25},{25,17},{2,10},{10... | collective-permute-start | bytes 405512 | tf_op jit(solution)/shard_map/ppermute | solution.py:424
  67.3 0.0 collective-permute-done.14.theirs
  67.3 0.8 %shard_map.73 = (f32[2,256,256]{2,1,0:T(8,128)}, f32[8,128]{1,0:T(8,128)S(1)}) custom-call(f32[512,128]{1,0:T(8,128)S(1)} %add.15.mine, f32[512,128]{1,0:T(8,128)S(1)} %collective-permute-done.14.theirs), custom_call_target="tpu_custom_call" | custom-call | flops 1 | bytes 1 | tf_op jit(solution)/shard_map/pallas_call | solution.py:318
  68.1 0.1 collective-permute-done.11.theirs
  68.3 0.9 %shard_map.74 = f32[2,256,256]{2,1,0:T(8,128)} custom-call(f32[264,128]{1,0:T(8,128)S(1)} %add.13.mine, f32[264,128]{1,0:T(8,128)S(1)} %collective-permute-done.11.theirs, f32[8,128]{1,0:T(8,128)S(1)} %get-tuple-element.74._), custom_call_target="tpu_custom_call" | custom-call | flops 1 | bytes 1 | tf_op jit(solution)/shard_map/pallas_call | solution.py:318
  (12 shorter events, 0.2 us)
Async XLA Ops:
  3.2 9.8 %collective-permute-start.1 = (f32[2,264,128]{2,1,0:T(8,128)S(1)}, f32[2,264,128]{2,1,0:T(8,128)S(1)}, u32[]{:S(2)}, u32[]{:S(2)}) collective-permute-start(f32[2,264,128]{2,1,0:T(8,128)S(1)} %get-tuple-element.40.refs_1_), channel_id=1, source_target_pairs={{0,1},{8,9},{16,17},{24,25},{2,3},{3,2},{4,5},{5,4},{6,7},{7,6},{1... | collective-permute-start | bytes 811016 | tf_op jit(solution)/shard_map/ppermute | solution.py:361
  6.4 0.7 copy-start.3
  6.4 4.1 %copy-start = (f32[2,2,2,256,256]{4,3,2,1,0:T(8,128)S(1)}, f32[2,2,2,256,256]{4,3,2,1,0:T(8,128)}, u32[]{:S(2)}) copy-start(f32[2,2,2,256,256]{4,3,2,1,0:T(8,128)} %pivot.5) | copy-start | bytes 6291460
  6.4 4.1 %copy-start.1 = (f32[2,2,2,256,256]{4,3,2,1,0:T(8,128)S(1)}, f32[2,2,2,256,256]{4,3,2,1,0:T(8,128)}, u32[]{:S(2)}) copy-start(f32[2,2,2,256,256]{4,3,2,1,0:T(8,128)} %factor.5) | copy-start | bytes 6291460
  6.4 4.1 %copy-start.2 = (f32[2,2]{1,0:T(2,128)S(1)}, f32[2,2]{1,0:T(2,128)}, u32[]{:S(2)}) copy-start(f32[2,2]{1,0:T(2,128)} %weight.9) | copy-start | bytes 52
  8.3 15.7 %collective-permute-start = (f32[2,256,256]{2,1,0:T(8,128)S(1)}, f32[2,256,256]{2,1,0:T(8,128)S(1)}, u32[]{:S(2)}, u32[]{:S(2)}) collective-permute-start(f32[2,256,256]{2,1,0:T(8,128)S(1)} %get-tuple-element.45._), channel_id=1, source_target_pairs={{2,3},{3,2},{4,5},{5,4},{6,7},{7,6},{10,11},{11,10},{12,13},{13,12... | collective-permute-start | bytes 1572872 | tf_op jit(solution)/shard_map/ppermute | solution.py:366
  12.4 2.7 %collective-permute-start.2 = (f32[2,264,128]{2,1,0:T(8,128)S(1)}, f32[2,264,128]{2,1,0:T(8,128)S(1)}, u32[]{:S(2)}, u32[]{:S(2)}) collective-permute-start(f32[2,264,128]{2,1,0:T(8,128)S(1)} %get-tuple-element.49.e), channel_id=1, source_target_pairs={{0,1},{8,9},{16,17},{24,25}} | collective-permute-start | bytes 811016 | tf_op jit(solution)/shard_map/ppermute | solution.py:376
  13.1 2.7 %collective-permute-start.4 = (f32[2,264,128]{2,1,0:T(8,128)S(1)}, f32[2,264,128]{2,1,0:T(8,128)S(1)}, u32[]{:S(2)}, u32[]{:S(2)}) collective-permute-start(f32[2,264,128]{2,1,0:T(8,128)S(1)} %shard_map.66), channel_id=1, source_target_pairs={{1,0},{9,8},{17,16},{25,24}} | collective-permute-start | bytes 811016 | tf_op jit(solution)/shard_map/ppermute | solution.py:380
  15.1 10.6 %collective-permute-start.3 = (f32[2,264,128]{2,1,0:T(8,128)S(1)}, f32[2,264,128]{2,1,0:T(8,128)S(1)}, u32[]{:S(2)}, u32[]{:S(2)}) collective-permute-start(f32[2,264,128]{2,1,0:T(8,128)S(1)} %shard_map.65), channel_id=1, source_target_pairs={{1,3},{9,11},{17,19},{25,27}} | collective-permute-start | bytes 811016 | tf_op jit(solution)/shard_map/ppermute | solution.py:385
  15.8 9.9 %collective-permute-start.5 = (f32[2,264,128]{2,1,0:T(8,128)S(1)}, f32[2,264,128]{2,1,0:T(8,128)S(1)}, u32[]{:S(2)}, u32[]{:S(2)}) collective-permute-start(f32[2,264,128]{2,1,0:T(8,128)S(1)} %collective-permute-done.4), channel_id=1, source_target_pairs={{0,2},{8,10},{16,18},{24,26}} | collective-permute-start | bytes 811016 | tf_op jit(solution)/shard_map/ppermute | solution.py:386
  25.8 0.7 collective-permute-start.6
  26.5 14.0 %collective-permute-start.7 = (f32[2,264,128]{2,1,0:T(8,128)S(1)}, f32[2,264,128]{2,1,0:T(8,128)S(1)}, u32[]{:S(2)}, u32[]{:S(2)}) collective-permute-start(f32[2,264,128]{2,1,0:T(8,128)S(1)} %shard_map.68), channel_id=1, source_target_pairs={{5,7},{4,6},{13,15},{12,14},{21,23},{20,22},{29,31},{28,30}} | collective-permute-start | bytes 811016 | tf_op jit(solution)/shard_map/ppermute | solution.py:402
  41.8 5.4 %collective-permute-start.8 = (f32[2,264,128]{2,1,0:T(8,128)S(1)}, f32[2,264,128]{2,1,0:T(8,128)S(1)}, u32[]{:S(2)}, u32[]{:S(2)}) collective-permute-start(f32[2,264,128]{2,1,0:T(8,128)S(1)} %get-tuple-element.61), channel_id=1, source_target_pairs={{0,1},{1,0},{2,3},{3,2},{4,5},{5,4},{6,7},{7,6},{8,9},{9,8},{10,11... | collective-permute-start | bytes 811016 | tf_op jit(solution)/shard_map/ppermute | solution.py:411
  49.1 6.4 %collective-permute-start.12 = (f32[512,128]{1,0:T(8,128)S(1)}, f32[512,128]{1,0:T(8,128)S(1)}, u32[]{:S(2)}, u32[]{:S(2)}) collective-permute-start(f32[512,128]{1,0:T(8,128)S(1)} %slice_bitcast_fusion), channel_id=1, source_target_pairs={{0,8},{8,0},{16,24},{24,16},{1,9},{9,1},{17,25},{25,17},{2,10},{10... | collective-permute-start | bytes 786440 | tf_op jit(solution)/shard_map/ppermute | solution.py:424
  54.9 1.4 %collective-permute-start.9 = (f32[264,128]{1,0:T(8,128)S(1)}, f32[264,128]{1,0:T(8,128)S(1)}, u32[]{:S(2)}, u32[]{:S(2)}) collective-permute-start(f32[264,128]{1,0:T(8,128)S(1)} %slice_bitcast_fusion.1), channel_id=1, source_target_pairs={{0,8},{8,0},{16,24},{24,16},{1,9},{9,1},{17,25},{25,17},{2,10},{10... | collective-permute-start | bytes 405512 | tf_op jit(solution)/shard_map/ppermute | solution.py:424
  55.5 7.6 %collective-permute-start.13 = (f32[512,128]{1,0:T(8,128)S(1)}, f32[512,128]{1,0:T(8,128)S(1)}, u32[]{:S(2)}, u32[]{:S(2)}) collective-permute-start(f32[512,128]{1,0:T(8,128)S(1)} %bitcast_add_fusion), channel_id=1, source_target_pairs={{0,16},{8,24},{16,0},{24,8},{1,17},{9,25},{17,1},{25,9},{2,18},{10... | collective-permute-start | bytes 786440 | tf_op jit(solution)/shard_map/ppermute | solution.py:424
  56.4 9.6 %collective-permute-start.10 = (f32[264,128]{1,0:T(8,128)S(1)}, f32[264,128]{1,0:T(8,128)S(1)}, u32[]{:S(2)}, u32[]{:S(2)}) collective-permute-start(f32[264,128]{1,0:T(8,128)S(1)} %fusion), channel_id=1, source_target_pairs={{0,16},{8,24},{16,0},{24,8},{1,17},{9,25},{17,1},{25,9},{2,18},{10... | collective-permute-start | bytes 405512 | tf_op jit(solution)/shard_map/ppermute | solution.py:424
  63.1 4.2 %collective-permute-start.14 = (f32[512,128]{1,0:T(8,128)S(1)}, f32[512,128]{1,0:T(8,128)S(1)}, u32[]{:S(2)}, u32[]{:S(2)}) collective-permute-start(f32[512,128]{1,0:T(8,128)S(1)} %add.15.mine), channel_id=1, source_target_pairs={{0,8},{8,0},{16,24},{24,16},{1,9},{9,1},{17,25},{25,17},{2,10},{10... | collective-permute-start | bytes 786440 | tf_op jit(solution)/shard_map/ppermute | solution.py:424
  66.0 2.3 %collective-permute-start.11 = (f32[264,128]{1,0:T(8,128)S(1)}, f32[264,128]{1,0:T(8,128)S(1)}, u32[]{:S(2)}, u32[]{:S(2)}) collective-permute-start(f32[264,128]{1,0:T(8,128)S(1)} %add.13.mine), channel_id=1, source_target_pairs={{0,8},{8,0},{16,24},{24,16},{1,9},{9,1},{17,25},{25,17},{2,10},{10... | collective-permute-start | bytes 405512 | tf_op jit(solution)/shard_map/ppermute | solution.py:424

commit v6 on v5

--- a/solution.py
+++ b/solution.py
@@ -27,6 +27,22 @@
     return jnp.dot(
         jnp.concatenate(left, axis=1), jnp.concatenate(right, axis=0), preferred_element_type=F32
     )
+
+
+def dot(left, right):
+    return jnp.dot(left, right, preferred_element_type=F32)
+
+
+def dot3(lh, ll, rh, rl):
+    return dot(lh, rh) + (dot(lh, rl) + dot(ll, rh))
+
+
+def wide_dot(left, right):
+    arh, aih, arl, ail = left
+    brh, bih, brl, bil = right
+    real = dot3(arh, arl, brh, brl) - dot3(aih, ail, bih, bil)
+    imag = dot3(arh, arl, bih, bil) + dot3(aih, ail, brh, brl)
+    return real, imag
 
 
 def complex_dot(left, right):
@@ -162,10 +178,30 @@
         fetched_constants(slot_of(False), live, pivot, factor, weight, outs, scratch)
 
 
-def constant_kernel(live, pivot, factor, weight, _, f1s, e, weighted, first_factor):
+def second_constants(live, pivot, factor, weight, f1s, e, weighted, first_factor):
     slot = slot_of(True)
     first_factor[...] = factor[slot, 0]
     constants_of(slot, pivot.at[slot], factor.at[slot, 1], live, weight, f1s, e, weighted)
+
+
+def sent_second_kernel(live, pivot, factor, weight, _, *outs):
+    @pl.when(whereabouts()[0] != 1)
+    def _():
+        second_constants(live, pivot, factor, weight, *outs)
+
+
+def second_constant_kernel(live, pivot, factor, weight, *refs):
+    made, outs = refs[:4], refs[4:]
+    place = whereabouts()[0]
+
+    @pl.when(place != 1)
+    def _():
+        for source, target in zip(made, outs):
+            target[...] = source[...]
+
+    @pl.when(place == 1)
+    def _():
+        second_constants(live, pivot, factor, weight, *outs)
 
 
 def factor_kernel(live, factor, f1s, f0s, f0t, gs, gt, g):
@@ -237,18 +273,16 @@
 
 
 def real_dot(left, right):
-    arh, aih, arl, ail = left
-    brh, bih, brl, bil = right
-    return deep_dot([arh, arh, arl, aih, aih, ail], [brh, brl, brh, bih, bil, bih])
+    return dot3(left[0], left[2], right[0], right[2]) + dot3(left[1], left[3], right[1], right[3])
 
 
 def off_values(slot, weight, xs, f0s, f0t, gs, weighted):
     width = f0s.shape[-1]
     w0, w1 = weight[pl.ds(slot, 1), 0:1], weight[pl.ds(slot, 1), 1:2]
-    qr, qi = complex_dot(xs, load4(gs))
+    qr, qi = wide_dot(xs, load4(gs))
     ts = split_pair(w1 * qr + w0 * qi, w0 * qr - w1 * qi)
     second = real_dot(load4(f0t), ts)
-    pr, pi = complex_dot(xs, load4(f0s))
+    pr, pi = wide_dot(xs, load4(f0s))
     u = w1 * pr + w0 * pi
     us = split_pair(u, w0 * pr - w1 * pi)
     constant = jnp.concatenate([weighted[2], weighted[3, : width - 8]], axis=0)
@@ -364,17 +398,14 @@
         factor_kernel, [live], [o_f0, o_f1s], factors
     )
     g_in = lax.ppermute(o_g, AXES, swaps)
+    made = run(sent_second_kernel, [live], [pivot, factor, weight, o_g], constants)
+    e_second = lax.ppermute(made[1], AXES, first)
     m_f1s, m_e, m_w, m_f0 = run(
-        constant_kernel,
-        [live],
-        [pivot, factor, weight, o_g],
-        constants,
+        second_constant_kernel, [live], [pivot, factor, weight, *made], constants
     )
     m_f0s, m_f0t, m_gs, m_gt, m_g = run(
         factor_kernel, [live], [m_f0, m_f1s], factors
     )
-    e_second = lax.ppermute(m_e, AXES, first)
-
     starts = functools.partial(step_kernel, lambda place: place == 1)
     (wave_even,) = run(starts, [], [o_gs, o_gt, o_e, e_in], [mirrored])
     wave_even = lax.ppermute(wave_even, AXES, [(at(p, 1), at(p, 0)) for p in range(poles)])

time: 69.5 us -> 68.7 us (0.988)
  waiting for transfers between devices: 29.7 us -> 28.5 us
    pallas_call x16 -> x17, Pallas kernels: 16.8 us -> 16.8 us  [run(): pl.pallas_call(kernel, out_shape=shapes, in_specs=[SCALAR] * len(scalars)...]
where the time goes in v6:
time: 68.7 us; the launch traced here: 68.3 us
  waiting for transfers between devices  28.5 us (41%)
  starting transfers between devices  21.5 us (31%)
  Pallas kernels  16.8 us (24%)
  between operations  0.94 us (1%)
    pallas_call x17, Pallas kernels, run(): pl.pallas_call(kernel, out_shape=shapes, in_specs=[SCALAR] * len(scalars)...  16.8 us
    ppermute x2, waiting for transfers between devices, local(): arrived = [lax.ppermute(wave, AXES, up)]  12 us
    ppermute x6, starting transfers between devices, exchanged(): lax.ppermute(value, 'pole', [(p, p ^ distance) for p in range(poles)])  9.34 us
    ppermute x6, waiting for transfers between devices, exchanged(): lax.ppermute(value, 'pole', [(p, p ^ distance) for p in range(poles)])  7.79 us
    ppermute x1, waiting for transfers between devices, local(): g_in = lax.ppermute(o_g, AXES, swaps)  6.89 us
    ppermute x1, starting transfers between devices, local(): e_in = lax.ppermute(made[1], AXES, first + swaps)  3.12 us
    ppermute x1, starting transfers between devices, local(): g_in = lax.ppermute(o_g, AXES, swaps)  2.16 us
    ppermute x2, starting transfers between devices, local(): arrived = [lax.ppermute(wave, AXES, up)]  2.15 us
  transfers between devices with their start and end apart: 15, of which 8 were waited for; matrix products, arithmetic and copies ran while one was open for 0% of the time, Pallas kernels for 15%

profile of v6, /device:TPU:29, one launch (start us, length us, event | category | flops | bytes accessed | tf_op | source)
XLA Modules:
  0.0 68.3 jit_solution(15287624607384868795)
XLA Ops:
  0.6 2.6 %shard_map.59 = (bf16[4,256,256]{2,1,0:T(8,128)(2,1)S(1)}, f32[2,264,128]{2,1,0:T(8,128)S(1)}, f32[4,264,128]{2,1,0:T(8,128)S(1)}, f32[2,256,256]{2,1,0:T(8,128)S(1)}) custom-call(s32[2]{0:T(128)} %live.11, f32[2,2,2,256,256]{4,3,2,1,0:T(8,128)} %pivot.7, f32[2,2,2,256,256]{4,3,2,1,0:T(8,128)} %factor.7, f32[2,2]{1,0:T(2,128)} %weight.11), custom_call_target="tpu_custom_call" | custom-call | flops 1 | bytes 1 | tf_op jit(solution)/shard_map/pallas_call | solution.py:352
  3.2 3.1 %collective-permute-start.1 = (f32[2,264,128]{2,1,0:T(8,128)S(1)}, f32[2,264,128]{2,1,0:T(8,128)S(1)}, u32[]{:S(2)}, u32[]{:S(2)}) collective-permute-start(f32[2,264,128]{2,1,0:T(8,128)S(1)} %get-tuple-element.44.refs_1_), channel_id=1, source_target_pairs={{0,1},{8,9},{16,17},{24,25},{2,3},{3,2},{4,5},{5,4},{6,7},{7,6},{1... | collective-permute-start | bytes 811016 | tf_op jit(solution)/shard_map/ppermute | solution.py:395
  6.4 0.0 copy-start.3
  6.4 0.0 copy-start
  6.4 0.0 copy-start.1
  6.4 0.0 copy-start.2
  6.4 0.2 shard_map.60
  6.6 0.4 copy-done.3
  7.0 1.3 %shard_map.61 = (bf16[4,256,256]{2,1,0:T(8,128)(2,1)S(1)}, bf16[4,256,256]{2,1,0:T(8,128)(2,1)S(1)}, bf16[4,256,256]{2,1,0:T(8,128)(2,1)S(1)}, bf16[4,256,256]{2,1,0:T(8,128)(2,1)S(1)}, f32[2,256,256]{2,1,0:T(8,128)S(1)}) custom-call(s32[2]{0:T(128)S(1)} %copy-done.3, f32[2,256,256]{2,1,0:T(8,128)S(1)} %get-tuple-element.47.factor, ...), custom_call_target="tpu_custom_call" | custom-call | flops 1 | bytes 1 | tf_op jit(solution)/shard_map/pallas_call | solution.py:352
  8.3 2.2 %collective-permute-start = (f32[2,256,256]{2,1,0:T(8,128)S(1)}, f32[2,256,256]{2,1,0:T(8,128)S(1)}, u32[]{:S(2)}, u32[]{:S(2)}) collective-permute-start(f32[2,256,256]{2,1,0:T(8,128)S(1)} %get-tuple-element.49._), channel_id=1, source_target_pairs={{2,3},{3,2},{4,5},{5,4},{6,7},{7,6},{10,11},{11,10},{12,13},{13,12... | collective-permute-start | bytes 1572872 | tf_op jit(solution)/shard_map/ppermute | solution.py:400
  10.5 1.8 %shard_map.62 = (bf16[4,256,256]{2,1,0:T(8,128)(2,1)S(1)}, f32[2,264,128]{2,1,0:T(8,128)S(1)}, f32[4,264,128]{2,1,0:T(8,128)S(1)}, f32[2,256,256]{2,1,0:T(8,128)S(1)}) custom-call(s32[2]{0:T(128)S(1)} %copy-done.3, f32[2,2,2,256,256]{4,3,2,1,0:T(8,128)S(1)} %copy-done, f32[2,2,2,256,256]{4,3,2,1,0:T(8,128)S(1)} %copy-done.1, f32[2,2]{1,0:T(2,128)S(1)} %copy-done.2, ...), custom_call_target="tpu_custom_call" | custom-call | flops 1 | bytes 1 | tf_op jit(solution)/shard_map/pallas_call | solution.py:352
  12.4 0.7 collective-permute-start.2
  13.1 0.0 collective-permute-done.1.e_in.refs_0_.x_first
  13.1 0.7 collective-permute-start.4
  13.8 0.7 shard_map.63
  14.5 1.3 %shard_map.64 = (bf16[4,256,256]{2,1,0:T(8,128)(2,1)S(1)}, bf16[4,256,256]{2,1,0:T(8,128)(2,1)S(1)}, bf16[4,256,256]{2,1,0:T(8,128)(2,1)S(1)}, bf16[4,256,256]{2,1,0:T(8,128)(2,1)S(1)}, f32[2,256,256]{2,1,0:T(8,128)S(1)}) custom-call(s32[2]{0:T(128)S(1)} %copy-done.3, f32[2,256,256]{2,1,0:T(8,128)S(1)} %get-tuple-element.54.factor, ...), custom_call_target="tpu_custom_call" | custom-call | flops 1 | bytes 1 | tf_op jit(solution)/shard_map/pallas_call | solution.py:352
  15.8 0.0 collective-permute-done.2.e_second.refs_0_
  15.8 0.7 collective-permute-start.3
  16.5 0.0 collective-permute-done.4
  16.5 0.7 collective-permute-start.5
  17.2 6.9 %collective-permute-done.g_in = f32[2,256,256]{2,1,0:T(8,128)S(1)} collective-permute-done((f32[2,256,256]{2,1,0:T(8,128)S(1)}, f32[2,256,256]{2,1,0:T(8,128)S(1)}, u32[]{:S(2)}, u32[]{:S(2)}) %collective-permute-start) | collective-permute-done | bytes 524320 | tf_op jit(solution)/shard_map/ppermute | solution.py:400
  24.1 1.7 %shard_map.65 = (bf16[4,256,256]{2,1,0:T(8,128)(2,1)S(1)}, bf16[4,256,256]{2,1,0:T(8,128)(2,1)S(1)}, f32[2,264,128]{2,1,0:T(8,128)S(1)}, bf16[4,256,256]{2,1,0:T...) custom-call(f32[2,256,256]{2,1,0:T(8,128)S(1)} %get-tuple-element.56.g, ...), custom_call_target="tpu_custom_call" | custom-call | flops 99999997952 | bytes 1 | tf_op jit(solution)/shard_map/pallas_call | solution.py:352
  25.8 0.0 collective-permute-done.3.refs_0_
  25.8 0.0 collective-permute-done.5.refs_1_
  25.8 0.7 collective-permute-start.6
  26.5 0.0 collective-permute-done.6.refs_0_.refs_2_
  26.5 1.5 %collective-permute-start.7 = (f32[2,264,128]{2,1,0:T(8,128)S(1)}, f32[2,264,128]{2,1,0:T(8,128)S(1)}, u32[]{:S(2)}, u32[]{:S(2)}) collective-permute-start(f32[2,264,128]{2,1,0:T(8,128)S(1)} %shard_map.69), channel_id=1, source_target_pairs={{5,7},{4,6},{13,15},{12,14},{21,23},{20,22},{29,31},{28,30}} | collective-permute-start | bytes 811016 | tf_op jit(solution)/shard_map/ppermute | solution.py:433
  28.0 12.0 %collective-permute-done.7.refs_3_ = f32[2,264,128]{2,1,0:T(8,128)S(1)} collective-permute-done((f32[2,264,128]{2,1,0:T(8,128)S(1)}, f32[2,264,128]{2,1,0:T(8,128)S(1)}, u32[]{:S(2)}, u32[]{:S(2)}) %collective-permute-start.7) | collective-permute-done | bytes 270368 | tf_op jit(solution)/shard_map/ppermute | solution.py:433
  40.0 1.2 %shard_map.70 = (f32[2,264,128]{2,1,0:T(8,128)S(1)}, f32[2,264,128]{2,1,0:T(8,128)S(1)}) custom-call(bf16[4,256,256]{2,1,0:T(8,128)(2,1)S(1)} %get-tuple-element.58.fas, bf16[4,256,256]{2,1,0:T(8,128)(2,1)S(1)} %get-tuple-element.59.fat, f32[2,264,128]{2,1,0:T(8,128)S(1)} %get-tuple-element.60.ea, f32[2,264,128]{2,1,0:T(8,128)S(1)} %collective-permute-done.3.refs_0_, ...), custom_call_target="tpu_custom_call" | custom-call | flops 1 | bytes 1 | tf_op jit(solution)/shard_map/pallas_call | solution.py:352
  41.2 2.0 %collective-permute-start.8 = (f32[2,264,128]{2,1,0:T(8,128)S(1)}, f32[2,264,128]{2,1,0:T(8,128)S(1)}, u32[]{:S(2)}, u32[]{:S(2)}) collective-permute-start(f32[2,264,128]{2,1,0:T(8,128)S(1)} %get-tuple-element.69), channel_id=1, source_target_pairs={{0,1},{1,0},{2,3},{3,2},{4,5},{5,4},{6,7},{7,6},{8,9},{9,8},{10,11... | collective-permute-start | bytes 811016 | tf_op jit(solution)/shard_map/ppermute | solution.py:442
  43.2 2.0 %shard_map.71 = (f32[2,512,128]{2,1,0:T(8,128)S(1)}, f32[2,264,128]{2,1,0:T(8,128)S(1)}) custom-call(f32[2,2]{1,0:T(2,128)S(1)} %copy-done.2, f32[2,264,128]{2,1,0:T(8,128)S(1)} %get-tuple-element.73.x, bf16[4,256,256]{2,1,0:T(8,128)(2,1)S(1)} %get-tuple-element.74.f0s, bf16[4,256,256]{2,1,0:T(8,128)(2,1)S(1)} %get-tuple-element.75.f0t, ...), custom_call_target="tpu_custom_call" | custom-call | flops 1 | bytes 1 | tf_op jit(solution)/shard_map/pallas_call | solution.py:352
  45.2 1.8 %collective-permute-done.8.x = f32[2,264,128]{2,1,0:T(8,128)S(1)} collective-permute-done((f32[2,264,128]{2,1,0:T(8,128)S(1)}, f32[2,264,128]{2,1,0:T(8,128)S(1)}, u32[]{:S(2)}, u32[]{:S(2)}) %collective-permute-start.8) | collective-permute-done | bytes 270368 | tf_op jit(solution)/shard_map/ppermute | solution.py:442
  47.1 1.5 %shard_map.72 = (f32[2,512,128]{2,1,0:T(8,128)S(1)}, bf16[4,256,256]{2,1,0:T(8,128)(2,1)S(1)}, bf16[4,256,256]{2,1,0:T(8,128)(2,1)S(1)}) custom-call(f32[2,2]{1,0:T(2,128)S(1)} %copy-done.2, f32[2,264,128]{2,1,0:T(8,128)S(1)} %collective-permute-done.8.x, f32[2,264,128]{2,1,0:T(8,128)S(1)} %collective-permute-done.1.e_in.refs_0_.x_first, ...), custom_call_target="tpu_custom_call" | custom-call | flops 1 | bytes 1 | tf_op jit(solution)/shard_map/pallas_call | solution.py:352
  48.7 4.7 %collective-permute-start.12 = (f32[512,128]{1,0:T(8,128)S(1)}, f32[512,128]{1,0:T(8,128)S(1)}, u32[]{:S(2)}, u32[]{:S(2)}) collective-permute-start(f32[512,128]{1,0:T(8,128)S(1)} %slice_bitcast_fusion), channel_id=1, source_target_pairs={{0,8},{8,0},{16,24},{24,16},{1,9},{9,1},{17,25},{25,17},{2,10},{10... | collective-permute-start | bytes 786440 | tf_op jit(solution)/shard_map/ppermute | solution.py:455
  53.4 0.6 shard_map.73
  54.0 0.1 collective-permute-start.9
  54.1 0.5 collective-permute-done.12
  54.6 0.4 collective-permute-start.13
  55.0 0.4 collective-permute-done.9
  55.4 0.8 %collective-permute-start.10 = (f32[264,128]{1,0:T(8,128)S(1)}, f32[264,128]{1,0:T(8,128)S(1)}, u32[]{:S(2)}, u32[]{:S(2)}) collective-permute-start(f32[264,128]{1,0:T(8,128)S(1)} %fusion), channel_id=1, source_target_pairs={{0,16},{8,24},{16,0},{24,8},{1,17},{9,25},{17,1},{25,9},{2,18},{10... | collective-permute-start | bytes 405512 | tf_op jit(solution)/shard_map/ppermute | solution.py:455
  56.2 6.0 %collective-permute-done.13 = f32[512,128]{1,0:T(8,128)S(1)} collective-permute-done((f32[512,128]{1,0:T(8,128)S(1)}, f32[512,128]{1,0:T(8,128)S(1)}, u32[]{:S(2)}, u32[]{:S(2)}) %collective-permute-start.13) | collective-permute-done | bytes 262176 | tf_op jit(solution)/shard_map/ppermute | solution.py:455
  62.2 2.1 %collective-permute-start.14 = (f32[512,128]{1,0:T(8,128)S(1)}, f32[512,128]{1,0:T(8,128)S(1)}, u32[]{:S(2)}, u32[]{:S(2)}) collective-permute-start(f32[512,128]{1,0:T(8,128)S(1)} %add.15.mine), channel_id=1, source_target_pairs={{0,8},{8,0},{16,24},{24,16},{1,9},{9,1},{17,25},{25,17},{2,10},{10... | collective-permute-start | bytes 786440 | tf_op jit(solution)/shard_map/ppermute | solution.py:455
  64.3 0.8 %collective-permute-done.10 = f32[264,128]{1,0:T(8,128)S(1)} collective-permute-done((f32[264,128]{1,0:T(8,128)S(1)}, f32[264,128]{1,0:T(8,128)S(1)}, u32[]{:S(2)}, u32[]{:S(2)}) %collective-permute-start.10) | collective-permute-done | bytes 135200 | tf_op jit(solution)/shard_map/ppermute | solution.py:455
  65.1 1.3 %collective-permute-start.11 = (f32[264,128]{1,0:T(8,128)S(1)}, f32[264,128]{1,0:T(8,128)S(1)}, u32[]{:S(2)}, u32[]{:S(2)}) collective-permute-start(f32[264,128]{1,0:T(8,128)S(1)} %add.13.mine), channel_id=1, source_target_pairs={{0,8},{8,0},{16,24},{24,16},{1,9},{9,1},{17,25},{25,17},{2,10},{10... | collective-permute-start | bytes 405512 | tf_op jit(solution)/shard_map/ppermute | solution.py:455
  66.4 0.0 collective-permute-done.14.theirs
  66.4 0.8 %shard_map.74 = (f32[2,256,256]{2,1,0:T(8,128)}, f32[8,128]{1,0:T(8,128)S(1)}) custom-call(f32[512,128]{1,0:T(8,128)S(1)} %add.15.mine, f32[512,128]{1,0:T(8,128)S(1)} %collective-permute-done.14.theirs), custom_call_target="tpu_custom_call" | custom-call | flops 1 | bytes 1 | tf_op jit(solution)/shard_map/pallas_call | solution.py:352
  67.2 0.1 collective-permute-done.11.theirs
  67.4 0.9 %shard_map.75 = f32[2,256,256]{2,1,0:T(8,128)} custom-call(f32[264,128]{1,0:T(8,128)S(1)} %add.13.mine, f32[264,128]{1,0:T(8,128)S(1)} %collective-permute-done.11.theirs, f32[8,128]{1,0:T(8,128)S(1)} %get-tuple-element.82._), custom_call_target="tpu_custom_call" | custom-call | flops 1 | bytes 1 | tf_op jit(solution)/shard_map/pallas_call | solution.py:352
  (13 shorter events, 0.2 us)
Async XLA Ops:
  3.2 9.8 %collective-permute-start.1 = (f32[2,264,128]{2,1,0:T(8,128)S(1)}, f32[2,264,128]{2,1,0:T(8,128)S(1)}, u32[]{:S(2)}, u32[]{:S(2)}) collective-permute-start(f32[2,264,128]{2,1,0:T(8,128)S(1)} %get-tuple-element.44.refs_1_), channel_id=1, source_target_pairs={{0,1},{8,9},{16,17},{24,25},{2,3},{3,2},{4,5},{5,4},{6,7},{7,6},{1... | collective-permute-start | bytes 811016 | tf_op jit(solution)/shard_map/ppermute | solution.py:395
  6.4 0.7 copy-start.3
  6.4 4.1 %copy-start = (f32[2,2,2,256,256]{4,3,2,1,0:T(8,128)S(1)}, f32[2,2,2,256,256]{4,3,2,1,0:T(8,128)}, u32[]{:S(2)}) copy-start(f32[2,2,2,256,256]{4,3,2,1,0:T(8,128)} %pivot.7) | copy-start | bytes 6291460
  6.4 4.1 %copy-start.1 = (f32[2,2,2,256,256]{4,3,2,1,0:T(8,128)S(1)}, f32[2,2,2,256,256]{4,3,2,1,0:T(8,128)}, u32[]{:S(2)}) copy-start(f32[2,2,2,256,256]{4,3,2,1,0:T(8,128)} %factor.7) | copy-start | bytes 6291460
  6.4 4.1 %copy-start.2 = (f32[2,2]{1,0:T(2,128)S(1)}, f32[2,2]{1,0:T(2,128)}, u32[]{:S(2)}) copy-start(f32[2,2]{1,0:T(2,128)} %weight.11) | copy-start | bytes 52
  8.3 15.7 %collective-permute-start = (f32[2,256,256]{2,1,0:T(8,128)S(1)}, f32[2,256,256]{2,1,0:T(8,128)S(1)}, u32[]{:S(2)}, u32[]{:S(2)}) collective-permute-start(f32[2,256,256]{2,1,0:T(8,128)S(1)} %get-tuple-element.49._), channel_id=1, source_target_pairs={{2,3},{3,2},{4,5},{5,4},{6,7},{7,6},{10,11},{11,10},{12,13},{13,12... | collective-permute-start | bytes 1572872 | tf_op jit(solution)/shard_map/ppermute | solution.py:400
  12.4 3.4 %collective-permute-start.2 = (f32[2,264,128]{2,1,0:T(8,128)S(1)}, f32[2,264,128]{2,1,0:T(8,128)S(1)}, u32[]{:S(2)}, u32[]{:S(2)}) collective-permute-start(f32[2,264,128]{2,1,0:T(8,128)S(1)} %get-tuple-element.51.refs_1_), channel_id=1, source_target_pairs={{0,1},{8,9},{16,17},{24,25}} | collective-permute-start | bytes 811016 | tf_op jit(solution)/shard_map/ppermute | solution.py:402
  13.1 3.4 %collective-permute-start.4 = (f32[2,264,128]{2,1,0:T(8,128)S(1)}, f32[2,264,128]{2,1,0:T(8,128)S(1)}, u32[]{:S(2)}, u32[]{:S(2)}) collective-permute-start(f32[2,264,128]{2,1,0:T(8,128)S(1)} %shard_map.67), channel_id=1, source_target_pairs={{1,0},{9,8},{17,16},{25,24}} | collective-permute-start | bytes 811016 | tf_op jit(solution)/shard_map/ppermute | solution.py:411
  15.8 10.0 %collective-permute-start.3 = (f32[2,264,128]{2,1,0:T(8,128)S(1)}, f32[2,264,128]{2,1,0:T(8,128)S(1)}, u32[]{:S(2)}, u32[]{:S(2)}) collective-permute-start(f32[2,264,128]{2,1,0:T(8,128)S(1)} %shard_map.66), channel_id=1, source_target_pairs={{1,3},{9,11},{17,19},{25,27}} | collective-permute-start | bytes 811016 | tf_op jit(solution)/shard_map/ppermute | solution.py:416
  16.5 9.3 %collective-permute-start.5 = (f32[2,264,128]{2,1,0:T(8,128)S(1)}, f32[2,264,128]{2,1,0:T(8,128)S(1)}, u32[]{:S(2)}, u32[]{:S(2)}) collective-permute-start(f32[2,264,128]{2,1,0:T(8,128)S(1)} %collective-permute-done.4), channel_id=1, source_target_pairs={{0,2},{8,10},{16,18},{24,26}} | collective-permute-start | bytes 811016 | tf_op jit(solution)/shard_map/ppermute | solution.py:417
  25.8 0.7 %collective-permute-start.6 = (f32[2,264,128]{2,1,0:T(8,128)S(1)}, f32[2,264,128]{2,1,0:T(8,128)S(1)}, u32[]{:S(2)}, u32[]{:S(2)}) collective-permute-start(f32[2,264,128]{2,1,0:T(8,128)S(1)} %shard_map.68), channel_id=1, source_target_pairs={{3,5},{2,4},{11,13},{10,12},{19,21},{18,20},{27,29},{26,28}} | collective-permute-start | bytes 811016 | tf_op jit(solution)/shard_map/ppermute | solution.py:433
  26.5 13.5 %collective-permute-start.7 = (f32[2,264,128]{2,1,0:T(8,128)S(1)}, f32[2,264,128]{2,1,0:T(8,128)S(1)}, u32[]{:S(2)}, u32[]{:S(2)}) collective-permute-start(f32[2,264,128]{2,1,0:T(8,128)S(1)} %shard_map.69), channel_id=1, source_target_pairs={{5,7},{4,6},{13,15},{12,14},{21,23},{20,22},{29,31},{28,30}} | collective-permute-start | bytes 811016 | tf_op jit(solution)/shard_map/ppermute | solution.py:433
  41.2 5.9 %collective-permute-start.8 = (f32[2,264,128]{2,1,0:T(8,128)S(1)}, f32[2,264,128]{2,1,0:T(8,128)S(1)}, u32[]{:S(2)}, u32[]{:S(2)}) collective-permute-start(f32[2,264,128]{2,1,0:T(8,128)S(1)} %get-tuple-element.69), channel_id=1, source_target_pairs={{0,1},{1,0},{2,3},{3,2},{4,5},{5,4},{6,7},{7,6},{8,9},{9,8},{10,11... | collective-permute-start | bytes 811016 | tf_op jit(solution)/shard_map/ppermute | solution.py:442
  48.7 5.9 %collective-permute-start.12 = (f32[512,128]{1,0:T(8,128)S(1)}, f32[512,128]{1,0:T(8,128)S(1)}, u32[]{:S(2)}, u32[]{:S(2)}) collective-permute-start(f32[512,128]{1,0:T(8,128)S(1)} %slice_bitcast_fusion), channel_id=1, source_target_pairs={{0,8},{8,0},{16,24},{24,16},{1,9},{9,1},{17,25},{25,17},{2,10},{10... | collective-permute-start | bytes 786440 | tf_op jit(solution)/shard_map/ppermute | solution.py:455
  54.0 1.4 %collective-permute-start.9 = (f32[264,128]{1,0:T(8,128)S(1)}, f32[264,128]{1,0:T(8,128)S(1)}, u32[]{:S(2)}, u32[]{:S(2)}) collective-permute-start(f32[264,128]{1,0:T(8,128)S(1)} %slice_bitcast_fusion.1), channel_id=1, source_target_pairs={{0,8},{8,0},{16,24},{24,16},{1,9},{9,1},{17,25},{25,17},{2,10},{10... | collective-permute-start | bytes 405512 | tf_op jit(solution)/shard_map/ppermute | solution.py:455
  54.6 7.6 %collective-permute-start.13 = (f32[512,128]{1,0:T(8,128)S(1)}, f32[512,128]{1,0:T(8,128)S(1)}, u32[]{:S(2)}, u32[]{:S(2)}) collective-permute-start(f32[512,128]{1,0:T(8,128)S(1)} %bitcast_add_fusion), channel_id=1, source_target_pairs={{0,16},{8,24},{16,0},{24,8},{1,17},{9,25},{17,1},{25,9},{2,18},{10... | collective-permute-start | bytes 786440 | tf_op jit(solution)/shard_map/ppermute | solution.py:455
  55.4 9.6 %collective-permute-start.10 = (f32[264,128]{1,0:T(8,128)S(1)}, f32[264,128]{1,0:T(8,128)S(1)}, u32[]{:S(2)}, u32[]{:S(2)}) collective-permute-start(f32[264,128]{1,0:T(8,128)S(1)} %fusion), channel_id=1, source_target_pairs={{0,16},{8,24},{16,0},{24,8},{1,17},{9,25},{17,1},{25,9},{2,18},{10... | collective-permute-start | bytes 405512 | tf_op jit(solution)/shard_map/ppermute | solution.py:455
  62.2 4.2 %collective-permute-start.14 = (f32[512,128]{1,0:T(8,128)S(1)}, f32[512,128]{1,0:T(8,128)S(1)}, u32[]{:S(2)}, u32[]{:S(2)}) collective-permute-start(f32[512,128]{1,0:T(8,128)S(1)} %add.15.mine), channel_id=1, source_target_pairs={{0,8},{8,0},{16,24},{24,16},{1,9},{9,1},{17,25},{25,17},{2,10},{10... | collective-permute-start | bytes 786440 | tf_op jit(solution)/shard_map/ppermute | solution.py:455
  65.1 2.3 %collective-permute-start.11 = (f32[264,128]{1,0:T(8,128)S(1)}, f32[264,128]{1,0:T(8,128)S(1)}, u32[]{:S(2)}, u32[]{:S(2)}) collective-permute-start(f32[264,128]{1,0:T(8,128)S(1)} %add.13.mine), channel_id=1, source_target_pairs={{0,8},{8,0},{16,24},{24,16},{1,9},{9,1},{17,25},{25,17},{2,10},{10... | collective-permute-start | bytes 405512 | tf_op jit(solution)/shard_map/ppermute | solution.py:455

commit v7 on v6

--- a/solution.py
+++ b/solution.py
@@ -159,9 +159,16 @@
 
 
 def sent_constant_kernel(live, pivot, factor, weight, *refs):
-    @pl.when(whereabouts()[0] != 1)
-    def _():
-        fetched_constants(slot_of(False), live, pivot, factor, weight, refs[:4], refs[4:])
+    outs, second, scratch = refs[:4], refs[4:8], refs[8:]
+    place, _, core = whereabouts()
+
+    @pl.when(jnp.logical_and(place != 1, core == 0))
+    def _():
+        fetched_constants(slot_of(True), live, pivot, factor, weight, second, scratch)
+
+    @pl.when(place != 1)
+    def _():
+        fetched_constants(slot_of(False), live, pivot, factor, weight, outs, scratch)
 
 
 def first_constant_kernel(live, pivot, factor, weight, *refs):
@@ -184,8 +191,16 @@
     constants_of(slot, pivot.at[slot], factor.at[slot, 1], live, weight, f1s, e, weighted)
 
 
-def sent_second_kernel(live, pivot, factor, weight, _, *outs):
-    @pl.when(whereabouts()[0] != 1)
+def sent_second_kernel(live, pivot, factor, weight, _, *refs):
+    made, outs = refs[:4], refs[4:]
+    place, _, core = whereabouts()
+
+    @pl.when(core == 0)
+    def _():
+        for source, target in zip(made, outs):
+            target[...] = source[...]
+
+    @pl.when(jnp.logical_and(place != 1, core == 1))
     def _():
         second_constants(live, pivot, factor, weight, *outs)
 
@@ -391,14 +406,15 @@
         pltpu.SemaphoreType.DMA((6,)),
     ]
     far = [pltpu.with_memory_space_constraint(a, pltpu.HBM) for a in (live, pivot, factor, weight)]
-    made = run(sent_constant_kernel, [], [], constants, scratch, far=far)
+    made = run(sent_constant_kernel, [], [], constants * 2, scratch, far=far)
+    made, second = made[:4], made[4:]
     e_in = lax.ppermute(made[1], AXES, first + swaps)
     o_f1s, o_e, o_w, o_f0 = run(first_constant_kernel, [], made, constants, scratch, far=far)
     o_f0s, o_f0t, o_gs, o_gt, o_g = run(
         factor_kernel, [live], [o_f0, o_f1s], factors
     )
     g_in = lax.ppermute(o_g, AXES, swaps)
-    made = run(sent_second_kernel, [live], [pivot, factor, weight, o_g], constants)
+    made = run(sent_second_kernel, [live], [pivot, factor, weight, o_g, *second], constants)
     e_second = lax.ppermute(made[1], AXES, first)
     m_f1s, m_e, m_w, m_f0 = run(
         second_constant_kernel, [live], [pivot, factor, weight, *made], constants

time: 68.7 us -> 68 us (0.990)
  waiting for transfers between devices: 28.5 us -> 27.3 us
  starting transfers between devices: 21.5 us -> 22.2 us
    ppermute x6, starting transfers between devices: 9.34 us -> 10.7 us  [exchanged(): lax.ppermute(value, 'pole', [(p, p ^ distance) for p in range(poles)])]
    ppermute x1, waiting for transfers between devices: 6.89 us -> 5.87 us  [local(): g_in = lax.ppermute(o_g, AXES, swaps)]
where the time goes in v7:
time: 68 us; the launch traced here: 67.7 us
  waiting for transfers between devices  27.3 us (40%)
  starting transfers between devices  22.2 us (33%)
  Pallas kernels  16.8 us (25%)
  between operations  0.94 us (1%)
    pallas_call x17, Pallas kernels, run(): pl.pallas_call(kernel, out_shape=shapes, in_specs=[SCALAR] * len(scalars)...  16.8 us
    ppermute x2, waiting for transfers between devices, local(): arrived = [lax.ppermute(wave, AXES, up)]  11.5 us
    ppermute x6, starting transfers between devices, exchanged(): lax.ppermute(value, 'pole', [(p, p ^ distance) for p in range(poles)])  10.7 us
    ppermute x6, waiting for transfers between devices, exchanged(): lax.ppermute(value, 'pole', [(p, p ^ distance) for p in range(poles)])  7.9 us
    ppermute x1, waiting for transfers between devices, local(): g_in = lax.ppermute(o_g, AXES, swaps)  5.87 us
    ppermute x1, starting transfers between devices, local(): e_in = lax.ppermute(made[1], AXES, first + swaps)  3.12 us
    ppermute x1, starting transfers between devices, local(): g_in = lax.ppermute(o_g, AXES, swaps)  2.16 us
    ppermute x2, starting transfers between devices, local(): arrived = [lax.ppermute(wave, AXES, up)]  2.15 us
  transfers between devices with their start and end apart: 15, of which 8 were waited for; matrix products, arithmetic and copies ran while one was open for 0% of the time, Pallas kernels for 15%

profile of v7, /device:TPU:29, one launch (start us, length us, event | category | flops | bytes accessed | tf_op | source)
XLA Modules:
  0.0 67.7 jit_solution(1004222690292443168)
XLA Ops:
  0.6 2.6 %shard_map.59 = (bf16[4,256,256]{2,1,0:T(8,128)(2,1)S(1)}, f32[2,264,128]{2,1,0:T(8,128)S(1)}, f32[4,264,128]{2,1,0:T(8,128)S(1)}, f32[2,256,256]{2,1,0:T(8,128)...) custom-call(s32[2]{0:T(128)} %live.11, ...), custom_call_target="tpu_custom_call" | custom-call | flops 1 | bytes 1 | tf_op jit(solution)/shard_map/pallas_call | solution.py:367
  3.3 3.1 %collective-permute-start.1 = (f32[2,264,128]{2,1,0:T(8,128)S(1)}, f32[2,264,128]{2,1,0:T(8,128)S(1)}, u32[]{:S(2)}, u32[]{:S(2)}) collective-permute-start(f32[2,264,128]{2,1,0:T(8,128)S(1)} %get-tuple-element.48.refs_1_), channel_id=1, source_target_pairs={{0,1},{8,9},{16,17},{24,25},{2,3},{3,2},{4,5},{5,4},{6,7},{7,6},{1... | collective-permute-start | bytes 811016 | tf_op jit(solution)/shard_map/ppermute | solution.py:411
  6.4 0.0 copy-start.3
  6.4 0.0 copy-start
  6.4 0.0 copy-start.1
  6.4 0.0 copy-start.2
  6.4 0.2 shard_map.60
  6.6 0.4 copy-done.3
  7.0 1.3 %shard_map.61 = (bf16[4,256,256]{2,1,0:T(8,128)(2,1)S(1)}, bf16[4,256,256]{2,1,0:T(8,128)(2,1)S(1)}, bf16[4,256,256]{2,1,0:T(8,128)(2,1)S(1)}, bf16[4,256,256]{2,1,0:T(8,128)(2,1)S(1)}, f32[2,256,256]{2,1,0:T(8,128)S(1)}) custom-call(s32[2]{0:T(128)S(1)} %copy-done.3, f32[2,256,256]{2,1,0:T(8,128)S(1)} %get-tuple-element.51.factor, ...), custom_call_target="tpu_custom_call" | custom-call | flops 1 | bytes 1 | tf_op jit(solution)/shard_map/pallas_call | solution.py:367
  8.4 2.2 %collective-permute-start = (f32[2,256,256]{2,1,0:T(8,128)S(1)}, f32[2,256,256]{2,1,0:T(8,128)S(1)}, u32[]{:S(2)}, u32[]{:S(2)}) collective-permute-start(f32[2,256,256]{2,1,0:T(8,128)S(1)} %get-tuple-element.53._), channel_id=1, source_target_pairs={{2,3},{3,2},{4,5},{5,4},{6,7},{7,6},{10,11},{11,10},{12,13},{13,12... | collective-permute-start | bytes 1572872 | tf_op jit(solution)/shard_map/ppermute | solution.py:416
  10.6 1.8 %shard_map.62 = (bf16[4,256,256]{2,1,0:T(8,128)(2,1)S(1)}, f32[2,264,128]{2,1,0:T(8,128)S(1)}, f32[4,264,128]{2,1,0:T(8,128)S(1)}, f32[2,256,256]{2,1,0:T(8,128)S(1)}) custom-call(s32[2]{0:T(128)S(1)} %copy-done.3, f32[2,2,2,256,256]{4,3,2,1,0:T(8,128)S(1)} %copy-done, f32[2,2,2,256,256]{4,3,2,1,0:T(8,128)S(1)} %copy-done.1, f32[2,2]{1,0:T(2,128)S(1)} %copy-done.2, ...), custom_call_target="tpu_custom_call" | custom-call | flops 1 | bytes 1 | tf_op jit(solution)/shard_map/pallas_call | solution.py:367
  12.4 0.7 %collective-permute-start.2 = (f32[2,264,128]{2,1,0:T(8,128)S(1)}, f32[2,264,128]{2,1,0:T(8,128)S(1)}, u32[]{:S(2)}, u32[]{:S(2)}) collective-permute-start(f32[2,264,128]{2,1,0:T(8,128)S(1)} %get-tuple-element.59.refs_1_), channel_id=1, source_target_pairs={{0,1},{8,9},{16,17},{24,25}} | collective-permute-start | bytes 811016 | tf_op jit(solution)/shard_map/ppermute | solution.py:418
  13.1 0.0 collective-permute-done.1.e_in.refs_0_.x_first
  13.1 0.7 %collective-permute-start.4 = (f32[2,264,128]{2,1,0:T(8,128)S(1)}, f32[2,264,128]{2,1,0:T(8,128)S(1)}, u32[]{:S(2)}, u32[]{:S(2)}) collective-permute-start(f32[2,264,128]{2,1,0:T(8,128)S(1)} %shard_map.67), channel_id=1, source_target_pairs={{1,0},{9,8},{17,16},{25,24}} | collective-permute-start | bytes 811016 | tf_op jit(solution)/shard_map/ppermute | solution.py:427
  13.8 0.7 shard_map.63
  14.5 1.3 %shard_map.64 = (bf16[4,256,256]{2,1,0:T(8,128)(2,1)S(1)}, bf16[4,256,256]{2,1,0:T(8,128)(2,1)S(1)}, bf16[4,256,256]{2,1,0:T(8,128)(2,1)S(1)}, bf16[4,256,256]{2,1,0:T(8,128)(2,1)S(1)}, f32[2,256,256]{2,1,0:T(8,128)S(1)}) custom-call(s32[2]{0:T(128)S(1)} %copy-done.3, f32[2,256,256]{2,1,0:T(8,128)S(1)} %get-tuple-element.62.factor, ...), custom_call_target="tpu_custom_call" | custom-call | flops 1 | bytes 1 | tf_op jit(solution)/shard_map/pallas_call | solution.py:367
  15.8 0.0 collective-permute-done.2.e_second.refs_0_
  15.8 0.7 %collective-permute-start.3 = (f32[2,264,128]{2,1,0:T(8,128)S(1)}, f32[2,264,128]{2,1,0:T(8,128)S(1)}, u32[]{:S(2)}, u32[]{:S(2)}) collective-permute-start(f32[2,264,128]{2,1,0:T(8,128)S(1)} %shard_map.66), channel_id=1, source_target_pairs={{1,3},{9,11},{17,19},{25,27}} | collective-permute-start | bytes 811016 | tf_op jit(solution)/shard_map/ppermute | solution.py:432
  16.5 0.0 collective-permute-done.4
  16.5 0.7 %collective-permute-start.5 = (f32[2,264,128]{2,1,0:T(8,128)S(1)}, f32[2,264,128]{2,1,0:T(8,128)S(1)}, u32[]{:S(2)}, u32[]{:S(2)}) collective-permute-start(f32[2,264,128]{2,1,0:T(8,128)S(1)} %collective-permute-done.4), channel_id=1, source_target_pairs={{0,2},{8,10},{16,18},{24,26}} | collective-permute-start | bytes 811016 | tf_op jit(solution)/shard_map/ppermute | solution.py:433
  17.2 5.9 %collective-permute-done.g_in = f32[2,256,256]{2,1,0:T(8,128)S(1)} collective-permute-done((f32[2,256,256]{2,1,0:T(8,128)S(1)}, f32[2,256,256]{2,1,0:T(8,128)S(1)}, u32[]{:S(2)}, u32[]{:S(2)}) %collective-permute-start) | collective-permute-done | bytes 524320 | tf_op jit(solution)/shard_map/ppermute | solution.py:416
  23.1 1.7 %shard_map.65 = (bf16[4,256,256]{2,1,0:T(8,128)(2,1)S(1)}, bf16[4,256,256]{2,1,0:T(8,128)(2,1)S(1)}, f32[2,264,128]{2,1,0:T(8,128)S(1)}, bf16[4,256,256]{2,1,0:T...) custom-call(f32[2,256,256]{2,1,0:T(8,128)S(1)} %get-tuple-element.64.g, ...), custom_call_target="tpu_custom_call" | custom-call | flops 99999997952 | bytes 1 | tf_op jit(solution)/shard_map/pallas_call | solution.py:367
  24.8 0.0 collective-permute-done.3.refs_0_
  24.8 0.0 collective-permute-done.5.refs_1_
  24.8 0.9 %collective-permute-start.6 = (f32[2,264,128]{2,1,0:T(8,128)S(1)}, f32[2,264,128]{2,1,0:T(8,128)S(1)}, u32[]{:S(2)}, u32[]{:S(2)}) collective-permute-start(f32[2,264,128]{2,1,0:T(8,128)S(1)} %shard_map.68), channel_id=1, source_target_pairs={{3,5},{2,4},{11,13},{10,12},{19,21},{18,20},{27,29},{26,28}} | collective-permute-start | bytes 811016 | tf_op jit(solution)/shard_map/ppermute | solution.py:449
  25.7 0.0 collective-permute-done.6.refs_0_.refs_2_
  25.7 1.3 %collective-permute-start.7 = (f32[2,264,128]{2,1,0:T(8,128)S(1)}, f32[2,264,128]{2,1,0:T(8,128)S(1)}, u32[]{:S(2)}, u32[]{:S(2)}) collective-permute-start(f32[2,264,128]{2,1,0:T(8,128)S(1)} %shard_map.69), channel_id=1, source_target_pairs={{5,7},{4,6},{13,15},{12,14},{21,23},{20,22},{29,31},{28,30}} | collective-permute-start | bytes 811016 | tf_op jit(solution)/shard_map/ppermute | solution.py:449
  27.0 11.5 %collective-permute-done.7.refs_3_ = f32[2,264,128]{2,1,0:T(8,128)S(1)} collective-permute-done((f32[2,264,128]{2,1,0:T(8,128)S(1)}, f32[2,264,128]{2,1,0:T(8,128)S(1)}, u32[]{:S(2)}, u32[]{:S(2)}) %collective-permute-start.7) | collective-permute-done | bytes 270368 | tf_op jit(solution)/shard_map/ppermute | solution.py:449
  38.5 1.2 %shard_map.70 = (f32[2,264,128]{2,1,0:T(8,128)S(1)}, f32[2,264,128]{2,1,0:T(8,128)S(1)}) custom-call(bf16[4,256,256]{2,1,0:T(8,128)(2,1)S(1)} %get-tuple-element.66.fas, bf16[4,256,256]{2,1,0:T(8,128)(2,1)S(1)} %get-tuple-element.67.fat, f32[2,264,128]{2,1,0:T(8,128)S(1)} %get-tuple-element.68.ea, f32[2,264,128]{2,1,0:T(8,128)S(1)} %collective-permute-done.3.refs_0_, ...), custom_call_target="tpu_custom_call" | custom-call | flops 1 | bytes 1 | tf_op jit(solution)/shard_map/pallas_call | solution.py:367
  39.7 1.4 %collective-permute-start.8 = (f32[2,264,128]{2,1,0:T(8,128)S(1)}, f32[2,264,128]{2,1,0:T(8,128)S(1)}, u32[]{:S(2)}, u32[]{:S(2)}) collective-permute-start(f32[2,264,128]{2,1,0:T(8,128)S(1)} %get-tuple-element.77), channel_id=1, source_target_pairs={{0,1},{1,0},{2,3},{3,2},{4,5},{5,4},{6,7},{7,6},{8,9},{9,8},{10,11... | collective-permute-start | bytes 811016 | tf_op jit(solution)/shard_map/ppermute | solution.py:458
  41.1 2.0 %shard_map.71 = (f32[2,512,128]{2,1,0:T(8,128)S(1)}, f32[2,264,128]{2,1,0:T(8,128)S(1)}) custom-call(f32[2,2]{1,0:T(2,128)S(1)} %copy-done.2, f32[2,264,128]{2,1,0:T(8,128)S(1)} %get-tuple-element.81.x, bf16[4,256,256]{2,1,0:T(8,128)(2,1)S(1)} %get-tuple-element.82.f0s, bf16[4,256,256]{2,1,0:T(8,128)(2,1)S(1)} %get-tuple-element.83.f0t, ...), custom_call_target="tpu_custom_call" | custom-call | flops 1 | bytes 1 | tf_op jit(solution)/shard_map/pallas_call | solution.py:367
  43.1 2.0 %collective-permute-done.8.x = f32[2,264,128]{2,1,0:T(8,128)S(1)} collective-permute-done((f32[2,264,128]{2,1,0:T(8,128)S(1)}, f32[2,264,128]{2,1,0:T(8,128)S(1)}, u32[]{:S(2)}, u32[]{:S(2)}) %collective-permute-start.8) | collective-permute-done | bytes 270368 | tf_op jit(solution)/shard_map/ppermute | solution.py:458
  45.1 1.5 %shard_map.72 = (f32[2,512,128]{2,1,0:T(8,128)S(1)}, bf16[4,256,256]{2,1,0:T(8,128)(2,1)S(1)}, bf16[4,256,256]{2,1,0:T(8,128)(2,1)S(1)}) custom-call(f32[2,2]{1,0:T(2,128)S(1)} %copy-done.2, f32[2,264,128]{2,1,0:T(8,128)S(1)} %collective-permute-done.8.x, f32[2,264,128]{2,1,0:T(8,128)S(1)} %collective-permute-done.1.e_in.refs_0_.x_first, ...), custom_call_target="tpu_custom_call" | custom-call | flops 1 | bytes 1 | tf_op jit(solution)/shard_map/pallas_call | solution.py:367
  46.7 6.2 %collective-permute-start.12 = (f32[512,128]{1,0:T(8,128)S(1)}, f32[512,128]{1,0:T(8,128)S(1)}, u32[]{:S(2)}, u32[]{:S(2)}) collective-permute-start(f32[512,128]{1,0:T(8,128)S(1)} %slice_bitcast_fusion), channel_id=1, source_target_pairs={{0,8},{8,0},{16,24},{24,16},{1,9},{9,1},{17,25},{25,17},{2,10},{10... | collective-permute-start | bytes 786440 | tf_op jit(solution)/shard_map/ppermute | solution.py:471
  52.9 0.6 shard_map.73
  53.5 0.1 collective-permute-start.9
  53.5 0.5 collective-permute-done.12
  54.1 0.3 collective-permute-start.13
  54.4 0.5 collective-permute-done.9
  54.9 0.8 %collective-permute-start.10 = (f32[264,128]{1,0:T(8,128)S(1)}, f32[264,128]{1,0:T(8,128)S(1)}, u32[]{:S(2)}, u32[]{:S(2)}) collective-permute-start(f32[264,128]{1,0:T(8,128)S(1)} %fusion), channel_id=1, source_target_pairs={{0,16},{8,24},{16,0},{24,8},{1,17},{9,25},{17,1},{25,9},{2,18},{10... | collective-permute-start | bytes 405512 | tf_op jit(solution)/shard_map/ppermute | solution.py:471
  55.7 6.0 %collective-permute-done.13 = f32[512,128]{1,0:T(8,128)S(1)} collective-permute-done((f32[512,128]{1,0:T(8,128)S(1)}, f32[512,128]{1,0:T(8,128)S(1)}, u32[]{:S(2)}, u32[]{:S(2)}) %collective-permute-start.13) | collective-permute-done | bytes 262176 | tf_op jit(solution)/shard_map/ppermute | solution.py:471
  61.7 2.1 %collective-permute-start.14 = (f32[512,128]{1,0:T(8,128)S(1)}, f32[512,128]{1,0:T(8,128)S(1)}, u32[]{:S(2)}, u32[]{:S(2)}) collective-permute-start(f32[512,128]{1,0:T(8,128)S(1)} %add.15.mine), channel_id=1, source_target_pairs={{0,8},{8,0},{16,24},{24,16},{1,9},{9,1},{17,25},{25,17},{2,10},{10... | collective-permute-start | bytes 786440 | tf_op jit(solution)/shard_map/ppermute | solution.py:471
  63.7 0.8 %collective-permute-done.10 = f32[264,128]{1,0:T(8,128)S(1)} collective-permute-done((f32[264,128]{1,0:T(8,128)S(1)}, f32[264,128]{1,0:T(8,128)S(1)}, u32[]{:S(2)}, u32[]{:S(2)}) %collective-permute-start.10) | collective-permute-done | bytes 135200 | tf_op jit(solution)/shard_map/ppermute | solution.py:471
  64.6 1.3 %collective-permute-start.11 = (f32[264,128]{1,0:T(8,128)S(1)}, f32[264,128]{1,0:T(8,128)S(1)}, u32[]{:S(2)}, u32[]{:S(2)}) collective-permute-start(f32[264,128]{1,0:T(8,128)S(1)} %add.13.mine), channel_id=1, source_target_pairs={{0,8},{8,0},{16,24},{24,16},{1,9},{9,1},{17,25},{25,17},{2,10},{10... | collective-permute-start | bytes 405512 | tf_op jit(solution)/shard_map/ppermute | solution.py:471
  65.8 0.0 collective-permute-done.14.theirs
  65.8 0.8 %shard_map.74 = (f32[2,256,256]{2,1,0:T(8,128)}, f32[8,128]{1,0:T(8,128)S(1)}) custom-call(f32[512,128]{1,0:T(8,128)S(1)} %add.15.mine, f32[512,128]{1,0:T(8,128)S(1)} %collective-permute-done.14.theirs), custom_call_target="tpu_custom_call" | custom-call | flops 1 | bytes 1 | tf_op jit(solution)/shard_map/pallas_call | solution.py:367
  66.7 0.1 collective-permute-done.11.theirs
  66.8 0.9 %shard_map.75 = f32[2,256,256]{2,1,0:T(8,128)} custom-call(f32[264,128]{1,0:T(8,128)S(1)} %add.13.mine, f32[264,128]{1,0:T(8,128)S(1)} %collective-permute-done.11.theirs, f32[8,128]{1,0:T(8,128)S(1)} %get-tuple-element.90._), custom_call_target="tpu_custom_call" | custom-call | flops 1 | bytes 1 | tf_op jit(solution)/shard_map/pallas_call | solution.py:367
  (13 shorter events, 0.2 us)
Async XLA Ops:
  3.3 9.8 %collective-permute-start.1 = (f32[2,264,128]{2,1,0:T(8,128)S(1)}, f32[2,264,128]{2,1,0:T(8,128)S(1)}, u32[]{:S(2)}, u32[]{:S(2)}) collective-permute-start(f32[2,264,128]{2,1,0:T(8,128)S(1)} %get-tuple-element.48.refs_1_), channel_id=1, source_target_pairs={{0,1},{8,9},{16,17},{24,25},{2,3},{3,2},{4,5},{5,4},{6,7},{7,6},{1... | collective-permute-start | bytes 811016 | tf_op jit(solution)/shard_map/ppermute | solution.py:411
  6.4 0.7 copy-start.3
  6.4 4.1 %copy-start = (f32[2,2,2,256,256]{4,3,2,1,0:T(8,128)S(1)}, f32[2,2,2,256,256]{4,3,2,1,0:T(8,128)}, u32[]{:S(2)}) copy-start(f32[2,2,2,256,256]{4,3,2,1,0:T(8,128)} %pivot.7) | copy-start | bytes 6291460
  6.4 4.1 %copy-start.1 = (f32[2,2,2,256,256]{4,3,2,1,0:T(8,128)S(1)}, f32[2,2,2,256,256]{4,3,2,1,0:T(8,128)}, u32[]{:S(2)}) copy-start(f32[2,2,2,256,256]{4,3,2,1,0:T(8,128)} %factor.7) | copy-start | bytes 6291460
  6.4 4.1 %copy-start.2 = (f32[2,2]{1,0:T(2,128)S(1)}, f32[2,2]{1,0:T(2,128)}, u32[]{:S(2)}) copy-start(f32[2,2]{1,0:T(2,128)} %weight.11) | copy-start | bytes 52
  8.4 14.7 %collective-permute-start = (f32[2,256,256]{2,1,0:T(8,128)S(1)}, f32[2,256,256]{2,1,0:T(8,128)S(1)}, u32[]{:S(2)}, u32[]{:S(2)}) collective-permute-start(f32[2,256,256]{2,1,0:T(8,128)S(1)} %get-tuple-element.53._), channel_id=1, source_target_pairs={{2,3},{3,2},{4,5},{5,4},{6,7},{7,6},{10,11},{11,10},{12,13},{13,12... | collective-permute-start | bytes 1572872 | tf_op jit(solution)/shard_map/ppermute | solution.py:416
  12.4 3.4 %collective-permute-start.2 = (f32[2,264,128]{2,1,0:T(8,128)S(1)}, f32[2,264,128]{2,1,0:T(8,128)S(1)}, u32[]{:S(2)}, u32[]{:S(2)}) collective-permute-start(f32[2,264,128]{2,1,0:T(8,128)S(1)} %get-tuple-element.59.refs_1_), channel_id=1, source_target_pairs={{0,1},{8,9},{16,17},{24,25}} | collective-permute-start | bytes 811016 | tf_op jit(solution)/shard_map/ppermute | solution.py:418
  13.1 3.4 %collective-permute-start.4 = (f32[2,264,128]{2,1,0:T(8,128)S(1)}, f32[2,264,128]{2,1,0:T(8,128)S(1)}, u32[]{:S(2)}, u32[]{:S(2)}) collective-permute-start(f32[2,264,128]{2,1,0:T(8,128)S(1)} %shard_map.67), channel_id=1, source_target_pairs={{1,0},{9,8},{17,16},{25,24}} | collective-permute-start | bytes 811016 | tf_op jit(solution)/shard_map/ppermute | solution.py:427
  15.8 8.9 %collective-permute-start.3 = (f32[2,264,128]{2,1,0:T(8,128)S(1)}, f32[2,264,128]{2,1,0:T(8,128)S(1)}, u32[]{:S(2)}, u32[]{:S(2)}) collective-permute-start(f32[2,264,128]{2,1,0:T(8,128)S(1)} %shard_map.66), channel_id=1, source_target_pairs={{1,3},{9,11},{17,19},{25,27}} | collective-permute-start | bytes 811016 | tf_op jit(solution)/shard_map/ppermute | solution.py:432
  16.5 8.3 %collective-permute-start.5 = (f32[2,264,128]{2,1,0:T(8,128)S(1)}, f32[2,264,128]{2,1,0:T(8,128)S(1)}, u32[]{:S(2)}, u32[]{:S(2)}) collective-permute-start(f32[2,264,128]{2,1,0:T(8,128)S(1)} %collective-permute-done.4), channel_id=1, source_target_pairs={{0,2},{8,10},{16,18},{24,26}} | collective-permute-start | bytes 811016 | tf_op jit(solution)/shard_map/ppermute | solution.py:433
  24.8 0.9 %collective-permute-start.6 = (f32[2,264,128]{2,1,0:T(8,128)S(1)}, f32[2,264,128]{2,1,0:T(8,128)S(1)}, u32[]{:S(2)}, u32[]{:S(2)}) collective-permute-start(f32[2,264,128]{2,1,0:T(8,128)S(1)} %shard_map.68), channel_id=1, source_target_pairs={{3,5},{2,4},{11,13},{10,12},{19,21},{18,20},{27,29},{26,28}} | collective-permute-start | bytes 811016 | tf_op jit(solution)/shard_map/ppermute | solution.py:449
  25.7 12.8 %collective-permute-start.7 = (f32[2,264,128]{2,1,0:T(8,128)S(1)}, f32[2,264,128]{2,1,0:T(8,128)S(1)}, u32[]{:S(2)}, u32[]{:S(2)}) collective-permute-start(f32[2,264,128]{2,1,0:T(8,128)S(1)} %shard_map.69), channel_id=1, source_target_pairs={{5,7},{4,6},{13,15},{12,14},{21,23},{20,22},{29,31},{28,30}} | collective-permute-start | bytes 811016 | tf_op jit(solution)/shard_map/ppermute | solution.py:449
  39.7 5.4 %collective-permute-start.8 = (f32[2,264,128]{2,1,0:T(8,128)S(1)}, f32[2,264,128]{2,1,0:T(8,128)S(1)}, u32[]{:S(2)}, u32[]{:S(2)}) collective-permute-start(f32[2,264,128]{2,1,0:T(8,128)S(1)} %get-tuple-element.77), channel_id=1, source_target_pairs={{0,1},{1,0},{2,3},{3,2},{4,5},{5,4},{6,7},{7,6},{8,9},{9,8},{10,11... | collective-permute-start | bytes 811016 | tf_op jit(solution)/shard_map/ppermute | solution.py:458
  46.7 7.3 %collective-permute-start.12 = (f32[512,128]{1,0:T(8,128)S(1)}, f32[512,128]{1,0:T(8,128)S(1)}, u32[]{:S(2)}, u32[]{:S(2)}) collective-permute-start(f32[512,128]{1,0:T(8,128)S(1)} %slice_bitcast_fusion), channel_id=1, source_target_pairs={{0,8},{8,0},{16,24},{24,16},{1,9},{9,1},{17,25},{25,17},{2,10},{10... | collective-permute-start | bytes 786440 | tf_op jit(solution)/shard_map/ppermute | solution.py:471
  53.5 1.4 %collective-permute-start.9 = (f32[264,128]{1,0:T(8,128)S(1)}, f32[264,128]{1,0:T(8,128)S(1)}, u32[]{:S(2)}, u32[]{:S(2)}) collective-permute-start(f32[264,128]{1,0:T(8,128)S(1)} %slice_bitcast_fusion.1), channel_id=1, source_target_pairs={{0,8},{8,0},{16,24},{24,16},{1,9},{9,1},{17,25},{25,17},{2,10},{10... | collective-permute-start | bytes 405512 | tf_op jit(solution)/shard_map/ppermute | solution.py:471
  54.1 7.6 %collective-permute-start.13 = (f32[512,128]{1,0:T(8,128)S(1)}, f32[512,128]{1,0:T(8,128)S(1)}, u32[]{:S(2)}, u32[]{:S(2)}) collective-permute-start(f32[512,128]{1,0:T(8,128)S(1)} %bitcast_add_fusion), channel_id=1, source_target_pairs={{0,16},{8,24},{16,0},{24,8},{1,17},{9,25},{17,1},{25,9},{2,18},{10... | collective-permute-start | bytes 786440 | tf_op jit(solution)/shard_map/ppermute | solution.py:471
  54.9 9.6 %collective-permute-start.10 = (f32[264,128]{1,0:T(8,128)S(1)}, f32[264,128]{1,0:T(8,128)S(1)}, u32[]{:S(2)}, u32[]{:S(2)}) collective-permute-start(f32[264,128]{1,0:T(8,128)S(1)} %fusion), channel_id=1, source_target_pairs={{0,16},{8,24},{16,0},{24,8},{1,17},{9,25},{17,1},{25,9},{2,18},{10... | collective-permute-start | bytes 405512 | tf_op jit(solution)/shard_map/ppermute | solution.py:471
  61.7 4.2 %collective-permute-start.14 = (f32[512,128]{1,0:T(8,128)S(1)}, f32[512,128]{1,0:T(8,128)S(1)}, u32[]{:S(2)}, u32[]{:S(2)}) collective-permute-start(f32[512,128]{1,0:T(8,128)S(1)} %add.15.mine), channel_id=1, source_target_pairs={{0,8},{8,0},{16,24},{24,16},{1,9},{9,1},{17,25},{25,17},{2,10},{10... | collective-permute-start | bytes 786440 | tf_op jit(solution)/shard_map/ppermute | solution.py:471
  64.6 2.3 %collective-permute-start.11 = (f32[264,128]{1,0:T(8,128)S(1)}, f32[264,128]{1,0:T(8,128)S(1)}, u32[]{:S(2)}, u32[]{:S(2)}) collective-permute-start(f32[264,128]{1,0:T(8,128)S(1)} %add.13.mine), channel_id=1, source_target_pairs={{0,8},{8,0},{16,24},{24,16},{1,9},{9,1},{17,25},{25,17},{2,10},{10... | collective-permute-start | bytes 405512 | tf_op jit(solution)/shard_map/ppermute | solution.py:471

commit v8 on v7

--- a/solution.py
+++ b/solution.py
@@ -320,8 +320,10 @@
 
 def more_off_kernel(weight, x, x_first, f0s, f0t, gs, weighted, before, off, us_out, ts_out):
     core = whereabouts()[2]
-    upper = whereabouts()[0] > 1
-    x = [jnp.where(upper, x[c], x_first[c]) for c in range(2)]
+    place = whereabouts()[0]
+    x = [
+        jnp.where(place > 1, x[c], jnp.where(place == 1, x_first[c], 0.0)) for c in range(2)
+    ]
     xs = split_pair(unpacked(x[0]), unpacked(x[1]))
     first, second, us, ts = off_values(slot_of(False), weight, xs, f0s, f0t, gs, weighted)
     off[core] = first + before[core]
@@ -408,7 +410,7 @@
     far = [pltpu.with_memory_space_constraint(a, pltpu.HBM) for a in (live, pivot, factor, weight)]
     made = run(sent_constant_kernel, [], [], constants * 2, scratch, far=far)
     made, second = made[:4], made[4:]
-    e_in = lax.ppermute(made[1], AXES, first + swaps)
+    e_in = lax.ppermute(made[1], AXES, every)
     o_f1s, o_e, o_w, o_f0 = run(first_constant_kernel, [], made, constants, scratch, far=far)
     o_f0s, o_f0t, o_gs, o_gt, o_g = run(
         factor_kernel, [live], [o_f0, o_f1s], factors

time: 68 us -> 69.8 us (1.026)
  waiting for transfers between devices: 27.3 us -> 29.5 us
    ppermute x6, starting transfers between devices: 10.7 us -> 12.8 us  [exchanged(): lax.ppermute(value, 'pole', [(p, p ^ distance) for p in range(poles)])]
    ppermute x1, starting transfers between devices: 3.12 us -> 1.27 us  [local(): e_in = lax.ppermute(made[1], AXES, every)]
    ppermute x1, waiting for transfers between devices: 2.01 us -> 3.03 us  [local(): shared = lax.ppermute(sent, AXES, every)]
    ppermute x2, waiting for transfers between devices: 11.5 us -> 12.4 us  [local(): arrived = [lax.ppermute(wave, AXES, up)]]
    ppermute x1, starting transfers between devices: 1.36 us -> 0.63 us  [local(): shared = lax.ppermute(sent, AXES, every)]
where the time goes in v8:
time: 69.8 us; the launch traced here: 69.5 us
  waiting for transfers between devices  29.5 us (42%)
  starting transfers between devices  21.7 us (31%)
  Pallas kernels  16.8 us (24%)
  between operations  0.91 us (1%)
    pallas_call x17, Pallas kernels, run(): pl.pallas_call(kernel, out_shape=shapes, in_specs=[SCALAR] * len(scalars)...  16.8 us
    ppermute x6, starting transfers between devices, exchanged(): lax.ppermute(value, 'pole', [(p, p ^ distance) for p in range(poles)])  12.8 us
    ppermute x2, waiting for transfers between devices, local(): arrived = [lax.ppermute(wave, AXES, up)]  12.4 us
    ppermute x6, waiting for transfers between devices, exchanged(): lax.ppermute(value, 'pole', [(p, p ^ distance) for p in range(poles)])  8.13 us
    ppermute x1, waiting for transfers between devices, local(): g_in = lax.ppermute(o_g, AXES, swaps)  5.92 us
    ppermute x1, waiting for transfers between devices, local(): shared = lax.ppermute(sent, AXES, every)  3.03 us
    ppermute x1, starting transfers between devices, local(): g_in = lax.ppermute(o_g, AXES, swaps)  2.16 us
    ppermute x2, starting transfers between devices, local(): arrived = [lax.ppermute(wave, AXES, up)]  2.15 us
  transfers between devices with their start and end apart: 15, of which 8 were waited for; matrix products, arithmetic and copies ran while one was open for 0% of the time, Pallas kernels for 15%

profile of v8, /device:TPU:29, one launch (start us, length us, event | category | flops | bytes accessed | tf_op | source)
XLA Modules:
  0.0 69.5 jit_solution(15729898283570528613)
XLA Ops:
  0.6 2.6 %shard_map.59 = (bf16[4,256,256]{2,1,0:T(8,128)(2,1)S(1)}, f32[2,264,128]{2,1,0:T(8,128)S(1)}, f32[4,264,128]{2,1,0:T(8,128)S(1)}, f32[2,256,256]{2,1,0:T(8,128)...) custom-call(s32[2]{0:T(128)} %live.11, ...), custom_call_target="tpu_custom_call" | custom-call | flops 1 | bytes 1 | tf_op jit(solution)/shard_map/pallas_call | solution.py:369
  3.3 1.3 %collective-permute-start.1 = (f32[2,264,128]{2,1,0:T(8,128)S(1)}, f32[2,264,128]{2,1,0:T(8,128)S(1)}, u32[]{:S(2)}, u32[]{:S(2)}) collective-permute-start(f32[2,264,128]{2,1,0:T(8,128)S(1)} %get-tuple-element.48.refs_1_), channel_id=1, source_target_pairs={{0,1},{1,0},{2,3},{3,2},{4,5},{5,4},{6,7},{7,6},{8,9},{9,8},{10,11... | collective-permute-start | bytes 811016 | tf_op jit(solution)/shard_map/ppermute | solution.py:413
  4.5 0.0 copy-start.3
  4.5 0.2 shard_map.60
  4.7 0.4 copy-done.3
  5.2 1.3 %shard_map.61 = (bf16[4,256,256]{2,1,0:T(8,128)(2,1)S(1)}, bf16[4,256,256]{2,1,0:T(8,128)(2,1)S(1)}, bf16[4,256,256]{2,1,0:T(8,128)(2,1)S(1)}, bf16[4,256,256]{2,1,0:T(8,128)(2,1)S(1)}, f32[2,256,256]{2,1,0:T(8,128)S(1)}) custom-call(s32[2]{0:T(128)S(1)} %copy-done.3, f32[2,256,256]{2,1,0:T(8,128)S(1)} %get-tuple-element.51.factor, ...), custom_call_target="tpu_custom_call" | custom-call | flops 1 | bytes 1 | tf_op jit(solution)/shard_map/pallas_call | solution.py:369
  6.5 2.2 %collective-permute-start = (f32[2,256,256]{2,1,0:T(8,128)S(1)}, f32[2,256,256]{2,1,0:T(8,128)S(1)}, u32[]{:S(2)}, u32[]{:S(2)}) collective-permute-start(f32[2,256,256]{2,1,0:T(8,128)S(1)} %get-tuple-element.53._), channel_id=1, source_target_pairs={{2,3},{3,2},{4,5},{5,4},{6,7},{7,6},{10,11},{11,10},{12,13},{13,12... | collective-permute-start | bytes 1572872 | tf_op jit(solution)/shard_map/ppermute | solution.py:418
  8.7 0.0 copy-done
  8.7 0.0 copy-done.1
  8.7 0.0 copy-done.2
  8.7 1.8 %shard_map.62 = (bf16[4,256,256]{2,1,0:T(8,128)(2,1)S(1)}, f32[2,264,128]{2,1,0:T(8,128)S(1)}, f32[4,264,128]{2,1,0:T(8,128)S(1)}, f32[2,256,256]{2,1,0:T(8,128)S(1)}) custom-call(s32[2]{0:T(128)S(1)} %copy-done.3, f32[2,2,2,256,256]{4,3,2,1,0:T(8,128)S(1)} %copy-done, f32[2,2,2,256,256]{4,3,2,1,0:T(8,128)S(1)} %copy-done.1, f32[2,2]{1,0:T(2,128)S(1)} %copy-done.2, ...), custom_call_target="tpu_custom_call" | custom-call | flops 1 | bytes 1 | tf_op jit(solution)/shard_map/pallas_call | solution.py:369
  10.6 0.7 collective-permute-start.2
  11.2 0.0 collective-permute-done.1.e_in.refs_0_.x_first
  11.3 0.7 collective-permute-start.4
  12.0 0.7 shard_map.63
  12.6 1.3 %shard_map.64 = (bf16[4,256,256]{2,1,0:T(8,128)(2,1)S(1)}, bf16[4,256,256]{2,1,0:T(8,128)(2,1)S(1)}, bf16[4,256,256]{2,1,0:T(8,128)(2,1)S(1)}, bf16[4,256,256]{2,1,0:T(8,128)(2,1)S(1)}, f32[2,256,256]{2,1,0:T(8,128)S(1)}) custom-call(s32[2]{0:T(128)S(1)} %copy-done.3, f32[2,256,256]{2,1,0:T(8,128)S(1)} %get-tuple-element.62.factor, ...), custom_call_target="tpu_custom_call" | custom-call | flops 1 | bytes 1 | tf_op jit(solution)/shard_map/pallas_call | solution.py:369
  13.9 0.0 collective-permute-done.2.e_second.refs_0_
  14.0 0.7 collective-permute-start.3
  14.7 0.0 collective-permute-done.4
  14.7 0.7 collective-permute-start.5
  15.4 5.9 %collective-permute-done.g_in = f32[2,256,256]{2,1,0:T(8,128)S(1)} collective-permute-done((f32[2,256,256]{2,1,0:T(8,128)S(1)}, f32[2,256,256]{2,1,0:T(8,128)S(1)}, u32[]{:S(2)}, u32[]{:S(2)}) %collective-permute-start) | collective-permute-done | bytes 524320 | tf_op jit(solution)/shard_map/ppermute | solution.py:418
  21.3 1.7 %shard_map.65 = (bf16[4,256,256]{2,1,0:T(8,128)(2,1)S(1)}, bf16[4,256,256]{2,1,0:T(8,128)(2,1)S(1)}, f32[2,264,128]{2,1,0:T(8,128)S(1)}, bf16[4,256,256]{2,1,0:T...) custom-call(f32[2,256,256]{2,1,0:T(8,128)S(1)} %get-tuple-element.64.g, ...), custom_call_target="tpu_custom_call" | custom-call | flops 99999997952 | bytes 1 | tf_op jit(solution)/shard_map/pallas_call | solution.py:369
  23.0 0.0 collective-permute-done.3.refs_0_
  23.0 0.0 collective-permute-done.5.refs_1_
  23.0 0.9 %collective-permute-start.6 = (f32[2,264,128]{2,1,0:T(8,128)S(1)}, f32[2,264,128]{2,1,0:T(8,128)S(1)}, u32[]{:S(2)}, u32[]{:S(2)}) collective-permute-start(f32[2,264,128]{2,1,0:T(8,128)S(1)} %shard_map.68), channel_id=1, source_target_pairs={{3,5},{2,4},{11,13},{10,12},{19,21},{18,20},{27,29},{26,28}} | collective-permute-start | bytes 811016 | tf_op jit(solution)/shard_map/ppermute | solution.py:451
  23.9 0.0 collective-permute-done.6.refs_0_.refs_2_
  23.9 1.3 %collective-permute-start.7 = (f32[2,264,128]{2,1,0:T(8,128)S(1)}, f32[2,264,128]{2,1,0:T(8,128)S(1)}, u32[]{:S(2)}, u32[]{:S(2)}) collective-permute-start(f32[2,264,128]{2,1,0:T(8,128)S(1)} %shard_map.69), channel_id=1, source_target_pairs={{5,7},{4,6},{13,15},{12,14},{21,23},{20,22},{29,31},{28,30}} | collective-permute-start | bytes 811016 | tf_op jit(solution)/shard_map/ppermute | solution.py:451
  25.2 12.4 %collective-permute-done.7.refs_3_ = f32[2,264,128]{2,1,0:T(8,128)S(1)} collective-permute-done((f32[2,264,128]{2,1,0:T(8,128)S(1)}, f32[2,264,128]{2,1,0:T(8,128)S(1)}, u32[]{:S(2)}, u32[]{:S(2)}) %collective-permute-start.7) | collective-permute-done | bytes 270368 | tf_op jit(solution)/shard_map/ppermute | solution.py:451
  37.6 1.2 %shard_map.70 = (f32[2,264,128]{2,1,0:T(8,128)S(1)}, f32[2,264,128]{2,1,0:T(8,128)S(1)}) custom-call(bf16[4,256,256]{2,1,0:T(8,128)(2,1)S(1)} %get-tuple-element.66.fas, bf16[4,256,256]{2,1,0:T(8,128)(2,1)S(1)} %get-tuple-element.67.fat, f32[2,264,128]{2,1,0:T(8,128)S(1)} %get-tuple-element.68.ea, f32[2,264,128]{2,1,0:T(8,128)S(1)} %collective-permute-done.3.refs_0_, ...), custom_call_target="tpu_custom_call" | custom-call | flops 1 | bytes 1 | tf_op jit(solution)/shard_map/pallas_call | solution.py:369
  38.8 0.6 collective-permute-start.8
  39.5 2.0 %shard_map.71 = (f32[2,512,128]{2,1,0:T(8,128)S(1)}, f32[2,264,128]{2,1,0:T(8,128)S(1)}) custom-call(f32[2,2]{1,0:T(2,128)S(1)} %copy-done.2, f32[2,264,128]{2,1,0:T(8,128)S(1)} %get-tuple-element.81.x, bf16[4,256,256]{2,1,0:T(8,128)(2,1)S(1)} %get-tuple-element.82.f0s, bf16[4,256,256]{2,1,0:T(8,128)(2,1)S(1)} %get-tuple-element.83.f0t, ...), custom_call_target="tpu_custom_call" | custom-call | flops 1 | bytes 1 | tf_op jit(solution)/shard_map/pallas_call | solution.py:369
  41.5 3.0 %collective-permute-done.8.x = f32[2,264,128]{2,1,0:T(8,128)S(1)} collective-permute-done((f32[2,264,128]{2,1,0:T(8,128)S(1)}, f32[2,264,128]{2,1,0:T(8,128)S(1)}, u32[]{:S(2)}, u32[]{:S(2)}) %collective-permute-start.8) | collective-permute-done | bytes 270368 | tf_op jit(solution)/shard_map/ppermute | solution.py:460
  44.5 1.6 %shard_map.72 = (f32[2,512,128]{2,1,0:T(8,128)S(1)}, bf16[4,256,256]{2,1,0:T(8,128)(2,1)S(1)}, bf16[4,256,256]{2,1,0:T(8,128)(2,1)S(1)}) custom-call(f32[2,2]{1,0:T(2,128)S(1)} %copy-done.2, f32[2,264,128]{2,1,0:T(8,128)S(1)} %collective-permute-done.8.x, f32[2,264,128]{2,1,0:T(8,128)S(1)} %collective-permute-done.1.e_in.refs_0_.x_first, ...), custom_call_target="tpu_custom_call" | custom-call | flops 1 | bytes 1 | tf_op jit(solution)/shard_map/pallas_call | solution.py:369
  46.1 8.5 %collective-permute-start.12 = (f32[512,128]{1,0:T(8,128)S(1)}, f32[512,128]{1,0:T(8,128)S(1)}, u32[]{:S(2)}, u32[]{:S(2)}) collective-permute-start(f32[512,128]{1,0:T(8,128)S(1)} %slice_bitcast_fusion), channel_id=1, source_target_pairs={{0,8},{8,0},{16,24},{24,16},{1,9},{9,1},{17,25},{25,17},{2,10},{10... | collective-permute-start | bytes 786440 | tf_op jit(solution)/shard_map/ppermute | solution.py:473
  54.6 0.6 shard_map.73
  55.3 0.1 collective-permute-start.9
  55.3 0.5 collective-permute-done.12
  55.8 0.1 collective-permute-start.13
  55.9 0.8 %collective-permute-done.9 = f32[264,128]{1,0:T(8,128)S(1)} collective-permute-done((f32[264,128]{1,0:T(8,128)S(1)}, f32[264,128]{1,0:T(8,128)S(1)}, u32[]{:S(2)}, u32[]{:S(2)}) %collective-permute-start.9) | collective-permute-done | bytes 135200 | tf_op jit(solution)/shard_map/ppermute | solution.py:473
  56.7 0.8 %collective-permute-start.10 = (f32[264,128]{1,0:T(8,128)S(1)}, f32[264,128]{1,0:T(8,128)S(1)}, u32[]{:S(2)}, u32[]{:S(2)}) collective-permute-start(f32[264,128]{1,0:T(8,128)S(1)} %fusion), channel_id=1, source_target_pairs={{0,16},{8,24},{16,0},{24,8},{1,17},{9,25},{17,1},{25,9},{2,18},{10... | collective-permute-start | bytes 405512 | tf_op jit(solution)/shard_map/ppermute | solution.py:473
  57.5 6.0 %collective-permute-done.13 = f32[512,128]{1,0:T(8,128)S(1)} collective-permute-done((f32[512,128]{1,0:T(8,128)S(1)}, f32[512,128]{1,0:T(8,128)S(1)}, u32[]{:S(2)}, u32[]{:S(2)}) %collective-permute-start.13) | collective-permute-done | bytes 262176 | tf_op jit(solution)/shard_map/ppermute | solution.py:473
  63.5 2.1 %collective-permute-start.14 = (f32[512,128]{1,0:T(8,128)S(1)}, f32[512,128]{1,0:T(8,128)S(1)}, u32[]{:S(2)}, u32[]{:S(2)}) collective-permute-start(f32[512,128]{1,0:T(8,128)S(1)} %add.15.mine), channel_id=1, source_target_pairs={{0,8},{8,0},{16,24},{24,16},{1,9},{9,1},{17,25},{25,17},{2,10},{10... | collective-permute-start | bytes 786440 | tf_op jit(solution)/shard_map/ppermute | solution.py:473
  65.5 0.8 %collective-permute-done.10 = f32[264,128]{1,0:T(8,128)S(1)} collective-permute-done((f32[264,128]{1,0:T(8,128)S(1)}, f32[264,128]{1,0:T(8,128)S(1)}, u32[]{:S(2)}, u32[]{:S(2)}) %collective-permute-start.10) | collective-permute-done | bytes 135200 | tf_op jit(solution)/shard_map/ppermute | solution.py:473
  66.3 1.3 %collective-permute-start.11 = (f32[264,128]{1,0:T(8,128)S(1)}, f32[264,128]{1,0:T(8,128)S(1)}, u32[]{:S(2)}, u32[]{:S(2)}) collective-permute-start(f32[264,128]{1,0:T(8,128)S(1)} %add.13.mine), channel_id=1, source_target_pairs={{0,8},{8,0},{16,24},{24,16},{1,9},{9,1},{17,25},{25,17},{2,10},{10... | collective-permute-start | bytes 405512 | tf_op jit(solution)/shard_map/ppermute | solution.py:473
  67.6 0.0 collective-permute-done.14.theirs
  67.6 0.8 %shard_map.74 = (f32[2,256,256]{2,1,0:T(8,128)}, f32[8,128]{1,0:T(8,128)S(1)}) custom-call(f32[512,128]{1,0:T(8,128)S(1)} %add.15.mine, f32[512,128]{1,0:T(8,128)S(1)} %collective-permute-done.14.theirs), custom_call_target="tpu_custom_call" | custom-call | flops 1 | bytes 1 | tf_op jit(solution)/shard_map/pallas_call | solution.py:369
  68.5 0.1 collective-permute-done.11.theirs
  68.6 0.9 %shard_map.75 = f32[2,256,256]{2,1,0:T(8,128)} custom-call(f32[264,128]{1,0:T(8,128)S(1)} %add.13.mine, f32[264,128]{1,0:T(8,128)S(1)} %collective-permute-done.11.theirs, f32[8,128]{1,0:T(8,128)S(1)} %get-tuple-element.90._), custom_call_target="tpu_custom_call" | custom-call | flops 1 | bytes 1 | tf_op jit(solution)/shard_map/pallas_call | solution.py:369
  (13 shorter events, 0.2 us)
Async XLA Ops:
  3.3 8.0 %collective-permute-start.1 = (f32[2,264,128]{2,1,0:T(8,128)S(1)}, f32[2,264,128]{2,1,0:T(8,128)S(1)}, u32[]{:S(2)}, u32[]{:S(2)}) collective-permute-start(f32[2,264,128]{2,1,0:T(8,128)S(1)} %get-tuple-element.48.refs_1_), channel_id=1, source_target_pairs={{0,1},{1,0},{2,3},{3,2},{4,5},{5,4},{6,7},{7,6},{8,9},{9,8},{10,11... | collective-permute-start | bytes 811016 | tf_op jit(solution)/shard_map/ppermute | solution.py:413
  4.5 0.7 copy-start.3
  4.5 4.2 %copy-start = (f32[2,2,2,256,256]{4,3,2,1,0:T(8,128)S(1)}, f32[2,2,2,256,256]{4,3,2,1,0:T(8,128)}, u32[]{:S(2)}) copy-start(f32[2,2,2,256,256]{4,3,2,1,0:T(8,128)} %pivot.7) | copy-start | bytes 6291460
  4.5 4.2 %copy-start.1 = (f32[2,2,2,256,256]{4,3,2,1,0:T(8,128)S(1)}, f32[2,2,2,256,256]{4,3,2,1,0:T(8,128)}, u32[]{:S(2)}) copy-start(f32[2,2,2,256,256]{4,3,2,1,0:T(8,128)} %factor.7) | copy-start | bytes 6291460
  4.5 4.2 %copy-start.2 = (f32[2,2]{1,0:T(2,128)S(1)}, f32[2,2]{1,0:T(2,128)}, u32[]{:S(2)}) copy-start(f32[2,2]{1,0:T(2,128)} %weight.11) | copy-start | bytes 52
  6.5 14.8 %collective-permute-start = (f32[2,256,256]{2,1,0:T(8,128)S(1)}, f32[2,256,256]{2,1,0:T(8,128)S(1)}, u32[]{:S(2)}, u32[]{:S(2)}) collective-permute-start(f32[2,256,256]{2,1,0:T(8,128)S(1)} %get-tuple-element.53._), channel_id=1, source_target_pairs={{2,3},{3,2},{4,5},{5,4},{6,7},{7,6},{10,11},{11,10},{12,13},{13,12... | collective-permute-start | bytes 1572872 | tf_op jit(solution)/shard_map/ppermute | solution.py:418
  10.6 3.4 %collective-permute-start.2 = (f32[2,264,128]{2,1,0:T(8,128)S(1)}, f32[2,264,128]{2,1,0:T(8,128)S(1)}, u32[]{:S(2)}, u32[]{:S(2)}) collective-permute-start(f32[2,264,128]{2,1,0:T(8,128)S(1)} %get-tuple-element.59.refs_1_), channel_id=1, source_target_pairs={{0,1},{8,9},{16,17},{24,25}} | collective-permute-start | bytes 811016 | tf_op jit(solution)/shard_map/ppermute | solution.py:420
  11.3 3.4 %collective-permute-start.4 = (f32[2,264,128]{2,1,0:T(8,128)S(1)}, f32[2,264,128]{2,1,0:T(8,128)S(1)}, u32[]{:S(2)}, u32[]{:S(2)}) collective-permute-start(f32[2,264,128]{2,1,0:T(8,128)S(1)} %shard_map.67), channel_id=1, source_target_pairs={{1,0},{9,8},{17,16},{25,24}} | collective-permute-start | bytes 811016 | tf_op jit(solution)/shard_map/ppermute | solution.py:429
  14.0 9.0 %collective-permute-start.3 = (f32[2,264,128]{2,1,0:T(8,128)S(1)}, f32[2,264,128]{2,1,0:T(8,128)S(1)}, u32[]{:S(2)}, u32[]{:S(2)}) collective-permute-start(f32[2,264,128]{2,1,0:T(8,128)S(1)} %shard_map.66), channel_id=1, source_target_pairs={{1,3},{9,11},{17,19},{25,27}} | collective-permute-start | bytes 811016 | tf_op jit(solution)/shard_map/ppermute | solution.py:434
  14.7 8.3 %collective-permute-start.5 = (f32[2,264,128]{2,1,0:T(8,128)S(1)}, f32[2,264,128]{2,1,0:T(8,128)S(1)}, u32[]{:S(2)}, u32[]{:S(2)}) collective-permute-start(f32[2,264,128]{2,1,0:T(8,128)S(1)} %collective-permute-done.4), channel_id=1, source_target_pairs={{0,2},{8,10},{16,18},{24,26}} | collective-permute-start | bytes 811016 | tf_op jit(solution)/shard_map/ppermute | solution.py:435
  23.0 0.9 %collective-permute-start.6 = (f32[2,264,128]{2,1,0:T(8,128)S(1)}, f32[2,264,128]{2,1,0:T(8,128)S(1)}, u32[]{:S(2)}, u32[]{:S(2)}) collective-permute-start(f32[2,264,128]{2,1,0:T(8,128)S(1)} %shard_map.68), channel_id=1, source_target_pairs={{3,5},{2,4},{11,13},{10,12},{19,21},{18,20},{27,29},{26,28}} | collective-permute-start | bytes 811016 | tf_op jit(solution)/shard_map/ppermute | solution.py:451
  23.9 13.7 %collective-permute-start.7 = (f32[2,264,128]{2,1,0:T(8,128)S(1)}, f32[2,264,128]{2,1,0:T(8,128)S(1)}, u32[]{:S(2)}, u32[]{:S(2)}) collective-permute-start(f32[2,264,128]{2,1,0:T(8,128)S(1)} %shard_map.69), channel_id=1, source_target_pairs={{5,7},{4,6},{13,15},{12,14},{21,23},{20,22},{29,31},{28,30}} | collective-permute-start | bytes 811016 | tf_op jit(solution)/shard_map/ppermute | solution.py:451
  38.8 5.7 %collective-permute-start.8 = (f32[2,264,128]{2,1,0:T(8,128)S(1)}, f32[2,264,128]{2,1,0:T(8,128)S(1)}, u32[]{:S(2)}, u32[]{:S(2)}) collective-permute-start(f32[2,264,128]{2,1,0:T(8,128)S(1)} %get-tuple-element.77), channel_id=1, source_target_pairs={{0,1},{1,0},{2,3},{3,2},{4,5},{5,4},{6,7},{7,6},{8,9},{9,8},{10,11... | collective-permute-start | bytes 811016 | tf_op jit(solution)/shard_map/ppermute | solution.py:460
  46.1 9.7 %collective-permute-start.12 = (f32[512,128]{1,0:T(8,128)S(1)}, f32[512,128]{1,0:T(8,128)S(1)}, u32[]{:S(2)}, u32[]{:S(2)}) collective-permute-start(f32[512,128]{1,0:T(8,128)S(1)} %slice_bitcast_fusion), channel_id=1, source_target_pairs={{0,8},{8,0},{16,24},{24,16},{1,9},{9,1},{17,25},{25,17},{2,10},{10... | collective-permute-start | bytes 786440 | tf_op jit(solution)/shard_map/ppermute | solution.py:473
  55.3 1.4 %collective-permute-start.9 = (f32[264,128]{1,0:T(8,128)S(1)}, f32[264,128]{1,0:T(8,128)S(1)}, u32[]{:S(2)}, u32[]{:S(2)}) collective-permute-start(f32[264,128]{1,0:T(8,128)S(1)} %slice_bitcast_fusion.1), channel_id=1, source_target_pairs={{0,8},{8,0},{16,24},{24,16},{1,9},{9,1},{17,25},{25,17},{2,10},{10... | collective-permute-start | bytes 405512 | tf_op jit(solution)/shard_map/ppermute | solution.py:473
  55.8 7.6 %collective-permute-start.13 = (f32[512,128]{1,0:T(8,128)S(1)}, f32[512,128]{1,0:T(8,128)S(1)}, u32[]{:S(2)}, u32[]{:S(2)}) collective-permute-start(f32[512,128]{1,0:T(8,128)S(1)} %bitcast_add_fusion), channel_id=1, source_target_pairs={{0,16},{8,24},{16,0},{24,8},{1,17},{9,25},{17,1},{25,9},{2,18},{10... | collective-permute-start | bytes 786440 | tf_op jit(solution)/shard_map/ppermute | solution.py:473
  56.7 9.6 %collective-permute-start.10 = (f32[264,128]{1,0:T(8,128)S(1)}, f32[264,128]{1,0:T(8,128)S(1)}, u32[]{:S(2)}, u32[]{:S(2)}) collective-permute-start(f32[264,128]{1,0:T(8,128)S(1)} %fusion), channel_id=1, source_target_pairs={{0,16},{8,24},{16,0},{24,8},{1,17},{9,25},{17,1},{25,9},{2,18},{10... | collective-permute-start | bytes 405512 | tf_op jit(solution)/shard_map/ppermute | solution.py:473
  63.5 4.2 %collective-permute-start.14 = (f32[512,128]{1,0:T(8,128)S(1)}, f32[512,128]{1,0:T(8,128)S(1)}, u32[]{:S(2)}, u32[]{:S(2)}) collective-permute-start(f32[512,128]{1,0:T(8,128)S(1)} %add.15.mine), channel_id=1, source_target_pairs={{0,8},{8,0},{16,24},{24,16},{1,9},{9,1},{17,25},{25,17},{2,10},{10... | collective-permute-start | bytes 786440 | tf_op jit(solution)/shard_map/ppermute | solution.py:473
  66.3 2.3 %collective-permute-start.11 = (f32[264,128]{1,0:T(8,128)S(1)}, f32[264,128]{1,0:T(8,128)S(1)}, u32[]{:S(2)}, u32[]{:S(2)}) collective-permute-start(f32[264,128]{1,0:T(8,128)S(1)} %add.13.mine), channel_id=1, source_target_pairs={{0,8},{8,0},{16,24},{24,16},{1,9},{9,1},{17,25},{25,17},{2,10},{10... | collective-permute-start | bytes 405512 | tf_op jit(solution)/shard_map/ppermute | solution.py:473

commit v9 on v8

--- a/solution.py
+++ b/solution.py
@@ -166,21 +166,22 @@
     def _():
         fetched_constants(slot_of(True), live, pivot, factor, weight, second, scratch)
 
-    @pl.when(place != 1)
+    @pl.when(jnp.logical_or(place != 1, core == 0))
     def _():
         fetched_constants(slot_of(False), live, pivot, factor, weight, outs, scratch)
 
 
 def first_constant_kernel(live, pivot, factor, weight, *refs):
     made, outs, scratch = refs[:4], refs[4:8], refs[8:]
-    place = whereabouts()[0]
-
-    @pl.when(place != 1)
+    place, _, core = whereabouts()
+    late = jnp.logical_and(place == 1, core == 1)
+
+    @pl.when(jnp.logical_not(late))
     def _():
         for source, target in zip(made, outs):
             target[...] = source[...]
 
-    @pl.when(place == 1)
+    @pl.when(late)
     def _():
         fetched_constants(slot_of(False), live, pivot, factor, weight, outs, scratch)
 

time: 69.8 us -> 68.4 us (0.980)
  starting transfers between devices: 21.7 us -> 19.5 us
  waiting for transfers between devices: 29.5 us -> 30.3 us
    ppermute x6, starting transfers between devices: 12.8 us -> 10.9 us  [exchanged(): lax.ppermute(value, 'pole', [(p, p ^ distance) for p in range(poles)])]
    ppermute x2, waiting for transfers between devices: 12.4 us -> 13.3 us  [local(): arrived = [lax.ppermute(wave, AXES, up)]]
where the time goes in v9:
time: 68.4 us; the launch traced here: 68.2 us
  waiting for transfers between devices  30.3 us (44%)
  starting transfers between devices  19.5 us (29%)
  Pallas kernels  16.8 us (25%)
  between operations  0.91 us (1%)
    pallas_call x17, Pallas kernels, run(): pl.pallas_call(kernel, out_shape=shapes, in_specs=[SCALAR] * len(scalars)...  16.8 us
    ppermute x2, waiting for transfers between devices, local(): arrived = [lax.ppermute(wave, AXES, up)]  13.3 us
    ppermute x6, starting transfers between devices, exchanged(): lax.ppermute(value, 'pole', [(p, p ^ distance) for p in range(poles)])  10.9 us
    ppermute x6, waiting for transfers between devices, exchanged(): lax.ppermute(value, 'pole', [(p, p ^ distance) for p in range(poles)])  8.09 us
    ppermute x1, waiting for transfers between devices, local(): g_in = lax.ppermute(o_g, AXES, swaps)  5.92 us
    ppermute x1, waiting for transfers between devices, local(): shared = lax.ppermute(sent, AXES, every)  2.98 us
    ppermute x1, starting transfers between devices, local(): g_in = lax.ppermute(o_g, AXES, swaps)  2.16 us
    ppermute x2, starting transfers between devices, local(): arrived = [lax.ppermute(wave, AXES, up)]  2.15 us
  transfers between devices with their start and end apart: 15, of which 8 were waited for; matrix products, arithmetic and copies ran while one was open for 0% of the time, Pallas kernels for 15%

profile of v9, /device:TPU:29, one launch (start us, length us, event | category | flops | bytes accessed | tf_op | source)
XLA Modules:
  0.0 68.2 jit_solution(8774695601476688755)
XLA Ops:
  0.6 2.6 %shard_map.59 = (bf16[4,256,256]{2,1,0:T(8,128)(2,1)S(1)}, f32[2,264,128]{2,1,0:T(8,128)S(1)}, f32[4,264,128]{2,1,0:T(8,128)S(1)}, f32[2,256,256]{2,1,0:T(8,128)...) custom-call(s32[2]{0:T(128)} %live.11, ...), custom_call_target="tpu_custom_call" | custom-call | flops 1 | bytes 1 | tf_op jit(solution)/shard_map/pallas_call | solution.py:370
  3.3 1.3 %collective-permute-start.1 = (f32[2,264,128]{2,1,0:T(8,128)S(1)}, f32[2,264,128]{2,1,0:T(8,128)S(1)}, u32[]{:S(2)}, u32[]{:S(2)}) collective-permute-start(f32[2,264,128]{2,1,0:T(8,128)S(1)} %get-tuple-element.48.refs_1_), channel_id=1, source_target_pairs={{0,1},{1,0},{2,3},{3,2},{4,5},{5,4},{6,7},{7,6},{8,9},{9,8},{10,11... | collective-permute-start | bytes 811016 | tf_op jit(solution)/shard_map/ppermute | solution.py:414
  4.5 0.0 copy-start.3
  4.5 0.2 shard_map.60
  4.7 0.4 copy-done.3
  5.2 1.3 %shard_map.61 = (bf16[4,256,256]{2,1,0:T(8,128)(2,1)S(1)}, bf16[4,256,256]{2,1,0:T(8,128)(2,1)S(1)}, bf16[4,256,256]{2,1,0:T(8,128)(2,1)S(1)}, bf16[4,256,256]{2,1,0:T(8,128)(2,1)S(1)}, f32[2,256,256]{2,1,0:T(8,128)S(1)}) custom-call(s32[2]{0:T(128)S(1)} %copy-done.3, f32[2,256,256]{2,1,0:T(8,128)S(1)} %get-tuple-element.51.factor, ...), custom_call_target="tpu_custom_call" | custom-call | flops 1 | bytes 1 | tf_op jit(solution)/shard_map/pallas_call | solution.py:370
  6.5 2.2 %collective-permute-start = (f32[2,256,256]{2,1,0:T(8,128)S(1)}, f32[2,256,256]{2,1,0:T(8,128)S(1)}, u32[]{:S(2)}, u32[]{:S(2)}) collective-permute-start(f32[2,256,256]{2,1,0:T(8,128)S(1)} %get-tuple-element.53._), channel_id=1, source_target_pairs={{2,3},{3,2},{4,5},{5,4},{6,7},{7,6},{10,11},{11,10},{12,13},{13,12... | collective-permute-start | bytes 1572872 | tf_op jit(solution)/shard_map/ppermute | solution.py:419
  8.7 0.0 copy-done
  8.7 0.0 copy-done.1
  8.7 0.0 copy-done.2
  8.7 1.8 %shard_map.62 = (bf16[4,256,256]{2,1,0:T(8,128)(2,1)S(1)}, f32[2,264,128]{2,1,0:T(8,128)S(1)}, f32[4,264,128]{2,1,0:T(8,128)S(1)}, f32[2,256,256]{2,1,0:T(8,128)S(1)}) custom-call(s32[2]{0:T(128)S(1)} %copy-done.3, f32[2,2,2,256,256]{4,3,2,1,0:T(8,128)S(1)} %copy-done, f32[2,2,2,256,256]{4,3,2,1,0:T(8,128)S(1)} %copy-done.1, f32[2,2]{1,0:T(2,128)S(1)} %copy-done.2, ...), custom_call_target="tpu_custom_call" | custom-call | flops 1 | bytes 1 | tf_op jit(solution)/shard_map/pallas_call | solution.py:370
  10.6 0.7 collective-permute-start.2
  11.2 0.0 collective-permute-done.1.e_in.refs_0_.x_first
  11.3 0.7 collective-permute-start.4
  12.0 0.7 shard_map.63
  12.6 1.3 %shard_map.64 = (bf16[4,256,256]{2,1,0:T(8,128)(2,1)S(1)}, bf16[4,256,256]{2,1,0:T(8,128)(2,1)S(1)}, bf16[4,256,256]{2,1,0:T(8,128)(2,1)S(1)}, bf16[4,256,256]{2,1,0:T(8,128)(2,1)S(1)}, f32[2,256,256]{2,1,0:T(8,128)S(1)}) custom-call(s32[2]{0:T(128)S(1)} %copy-done.3, f32[2,256,256]{2,1,0:T(8,128)S(1)} %get-tuple-element.62.factor, ...), custom_call_target="tpu_custom_call" | custom-call | flops 1 | bytes 1 | tf_op jit(solution)/shard_map/pallas_call | solution.py:370
  13.9 0.0 collective-permute-done.2.e_second.refs_0_
  14.0 0.7 collective-permute-start.3
  14.7 0.0 collective-permute-done.4
  14.7 0.7 collective-permute-start.5
  15.4 5.9 %collective-permute-done.g_in = f32[2,256,256]{2,1,0:T(8,128)S(1)} collective-permute-done((f32[2,256,256]{2,1,0:T(8,128)S(1)}, f32[2,256,256]{2,1,0:T(8,128)S(1)}, u32[]{:S(2)}, u32[]{:S(2)}) %collective-permute-start) | collective-permute-done | bytes 524320 | tf_op jit(solution)/shard_map/ppermute | solution.py:419
  21.3 1.7 %shard_map.65 = (bf16[4,256,256]{2,1,0:T(8,128)(2,1)S(1)}, bf16[4,256,256]{2,1,0:T(8,128)(2,1)S(1)}, f32[2,264,128]{2,1,0:T(8,128)S(1)}, bf16[4,256,256]{2,1,0:T...) custom-call(f32[2,256,256]{2,1,0:T(8,128)S(1)} %get-tuple-element.64.g, ...), custom_call_target="tpu_custom_call" | custom-call | flops 99999997952 | bytes 1 | tf_op jit(solution)/shard_map/pallas_call | solution.py:370
  23.0 0.0 collective-permute-done.3.refs_0_
  23.0 0.0 collective-permute-done.5.refs_1_
  23.0 0.9 %collective-permute-start.6 = (f32[2,264,128]{2,1,0:T(8,128)S(1)}, f32[2,264,128]{2,1,0:T(8,128)S(1)}, u32[]{:S(2)}, u32[]{:S(2)}) collective-permute-start(f32[2,264,128]{2,1,0:T(8,128)S(1)} %shard_map.68), channel_id=1, source_target_pairs={{3,5},{2,4},{11,13},{10,12},{19,21},{18,20},{27,29},{26,28}} | collective-permute-start | bytes 811016 | tf_op jit(solution)/shard_map/ppermute | solution.py:452
  23.9 0.0 collective-permute-done.6.refs_0_.refs_2_
  23.9 1.3 %collective-permute-start.7 = (f32[2,264,128]{2,1,0:T(8,128)S(1)}, f32[2,264,128]{2,1,0:T(8,128)S(1)}, u32[]{:S(2)}, u32[]{:S(2)}) collective-permute-start(f32[2,264,128]{2,1,0:T(8,128)S(1)} %shard_map.69), channel_id=1, source_target_pairs={{5,7},{4,6},{13,15},{12,14},{21,23},{20,22},{29,31},{28,30}} | collective-permute-start | bytes 811016 | tf_op jit(solution)/shard_map/ppermute | solution.py:452
  25.2 13.3 %collective-permute-done.7.refs_3_ = f32[2,264,128]{2,1,0:T(8,128)S(1)} collective-permute-done((f32[2,264,128]{2,1,0:T(8,128)S(1)}, f32[2,264,128]{2,1,0:T(8,128)S(1)}, u32[]{:S(2)}, u32[]{:S(2)}) %collective-permute-start.7) | collective-permute-done | bytes 270368 | tf_op jit(solution)/shard_map/ppermute | solution.py:452
  38.5 1.2 %shard_map.70 = (f32[2,264,128]{2,1,0:T(8,128)S(1)}, f32[2,264,128]{2,1,0:T(8,128)S(1)}) custom-call(bf16[4,256,256]{2,1,0:T(8,128)(2,1)S(1)} %get-tuple-element.66.fas, bf16[4,256,256]{2,1,0:T(8,128)(2,1)S(1)} %get-tuple-element.67.fat, f32[2,264,128]{2,1,0:T(8,128)S(1)} %get-tuple-element.68.ea, f32[2,264,128]{2,1,0:T(8,128)S(1)} %collective-permute-done.3.refs_0_, ...), custom_call_target="tpu_custom_call" | custom-call | flops 1 | bytes 1 | tf_op jit(solution)/shard_map/pallas_call | solution.py:370
  39.8 0.4 collective-permute-start.8
  40.1 2.0 %shard_map.71 = (f32[2,512,128]{2,1,0:T(8,128)S(1)}, f32[2,264,128]{2,1,0:T(8,128)S(1)}) custom-call(f32[2,2]{1,0:T(2,128)S(1)} %copy-done.2, f32[2,264,128]{2,1,0:T(8,128)S(1)} %get-tuple-element.81.x, bf16[4,256,256]{2,1,0:T(8,128)(2,1)S(1)} %get-tuple-element.82.f0s, bf16[4,256,256]{2,1,0:T(8,128)(2,1)S(1)} %get-tuple-element.83.f0t, ...), custom_call_target="tpu_custom_call" | custom-call | flops 1 | bytes 1 | tf_op jit(solution)/shard_map/pallas_call | solution.py:370
  42.2 3.0 %collective-permute-done.8.x = f32[2,264,128]{2,1,0:T(8,128)S(1)} collective-permute-done((f32[2,264,128]{2,1,0:T(8,128)S(1)}, f32[2,264,128]{2,1,0:T(8,128)S(1)}, u32[]{:S(2)}, u32[]{:S(2)}) %collective-permute-start.8) | collective-permute-done | bytes 270368 | tf_op jit(solution)/shard_map/ppermute | solution.py:461
  45.1 1.6 %shard_map.72 = (f32[2,512,128]{2,1,0:T(8,128)S(1)}, bf16[4,256,256]{2,1,0:T(8,128)(2,1)S(1)}, bf16[4,256,256]{2,1,0:T(8,128)(2,1)S(1)}) custom-call(f32[2,2]{1,0:T(2,128)S(1)} %copy-done.2, f32[2,264,128]{2,1,0:T(8,128)S(1)} %collective-permute-done.8.x, f32[2,264,128]{2,1,0:T(8,128)S(1)} %collective-permute-done.1.e_in.refs_0_.x_first, ...), custom_call_target="tpu_custom_call" | custom-call | flops 1 | bytes 1 | tf_op jit(solution)/shard_map/pallas_call | solution.py:370
  46.7 6.6 %collective-permute-start.12 = (f32[512,128]{1,0:T(8,128)S(1)}, f32[512,128]{1,0:T(8,128)S(1)}, u32[]{:S(2)}, u32[]{:S(2)}) collective-permute-start(f32[512,128]{1,0:T(8,128)S(1)} %slice_bitcast_fusion), channel_id=1, source_target_pairs={{0,8},{8,0},{16,24},{24,16},{1,9},{9,1},{17,25},{25,17},{2,10},{10... | collective-permute-start | bytes 786440 | tf_op jit(solution)/shard_map/ppermute | solution.py:474
  53.3 0.6 shard_map.73
  53.9 0.1 collective-permute-start.9
  54.0 0.5 collective-permute-done.12
  54.5 0.1 collective-permute-start.13
  54.6 0.7 %collective-permute-done.9 = f32[264,128]{1,0:T(8,128)S(1)} collective-permute-done((f32[264,128]{1,0:T(8,128)S(1)}, f32[264,128]{1,0:T(8,128)S(1)}, u32[]{:S(2)}, u32[]{:S(2)}) %collective-permute-start.9) | collective-permute-done | bytes 135200 | tf_op jit(solution)/shard_map/ppermute | solution.py:474
  55.3 0.8 %collective-permute-start.10 = (f32[264,128]{1,0:T(8,128)S(1)}, f32[264,128]{1,0:T(8,128)S(1)}, u32[]{:S(2)}, u32[]{:S(2)}) collective-permute-start(f32[264,128]{1,0:T(8,128)S(1)} %fusion), channel_id=1, source_target_pairs={{0,16},{8,24},{16,0},{24,8},{1,17},{9,25},{17,1},{25,9},{2,18},{10... | collective-permute-start | bytes 405512 | tf_op jit(solution)/shard_map/ppermute | solution.py:474
  56.1 6.0 %collective-permute-done.13 = f32[512,128]{1,0:T(8,128)S(1)} collective-permute-done((f32[512,128]{1,0:T(8,128)S(1)}, f32[512,128]{1,0:T(8,128)S(1)}, u32[]{:S(2)}, u32[]{:S(2)}) %collective-permute-start.13) | collective-permute-done | bytes 262176 | tf_op jit(solution)/shard_map/ppermute | solution.py:474
  62.1 2.1 %collective-permute-start.14 = (f32[512,128]{1,0:T(8,128)S(1)}, f32[512,128]{1,0:T(8,128)S(1)}, u32[]{:S(2)}, u32[]{:S(2)}) collective-permute-start(f32[512,128]{1,0:T(8,128)S(1)} %add.15.mine), channel_id=1, source_target_pairs={{0,8},{8,0},{16,24},{24,16},{1,9},{9,1},{17,25},{25,17},{2,10},{10... | collective-permute-start | bytes 786440 | tf_op jit(solution)/shard_map/ppermute | solution.py:474
  64.2 0.8 %collective-permute-done.10 = f32[264,128]{1,0:T(8,128)S(1)} collective-permute-done((f32[264,128]{1,0:T(8,128)S(1)}, f32[264,128]{1,0:T(8,128)S(1)}, u32[]{:S(2)}, u32[]{:S(2)}) %collective-permute-start.10) | collective-permute-done | bytes 135200 | tf_op jit(solution)/shard_map/ppermute | solution.py:474
  65.0 1.3 %collective-permute-start.11 = (f32[264,128]{1,0:T(8,128)S(1)}, f32[264,128]{1,0:T(8,128)S(1)}, u32[]{:S(2)}, u32[]{:S(2)}) collective-permute-start(f32[264,128]{1,0:T(8,128)S(1)} %add.13.mine), channel_id=1, source_target_pairs={{0,8},{8,0},{16,24},{24,16},{1,9},{9,1},{17,25},{25,17},{2,10},{10... | collective-permute-start | bytes 405512 | tf_op jit(solution)/shard_map/ppermute | solution.py:474
  66.2 0.0 collective-permute-done.14.theirs
  66.2 0.8 %shard_map.74 = (f32[2,256,256]{2,1,0:T(8,128)}, f32[8,128]{1,0:T(8,128)S(1)}) custom-call(f32[512,128]{1,0:T(8,128)S(1)} %add.15.mine, f32[512,128]{1,0:T(8,128)S(1)} %collective-permute-done.14.theirs), custom_call_target="tpu_custom_call" | custom-call | flops 1 | bytes 1 | tf_op jit(solution)/shard_map/pallas_call | solution.py:370
  67.1 0.1 collective-permute-done.11.theirs
  67.2 0.9 %shard_map.75 = f32[2,256,256]{2,1,0:T(8,128)} custom-call(f32[264,128]{1,0:T(8,128)S(1)} %add.13.mine, f32[264,128]{1,0:T(8,128)S(1)} %collective-permute-done.11.theirs, f32[8,128]{1,0:T(8,128)S(1)} %get-tuple-element.90._), custom_call_target="tpu_custom_call" | custom-call | flops 1 | bytes 1 | tf_op jit(solution)/shard_map/pallas_call | solution.py:370
  (13 shorter events, 0.2 us)
Async XLA Ops:
  3.3 8.0 %collective-permute-start.1 = (f32[2,264,128]{2,1,0:T(8,128)S(1)}, f32[2,264,128]{2,1,0:T(8,128)S(1)}, u32[]{:S(2)}, u32[]{:S(2)}) collective-permute-start(f32[2,264,128]{2,1,0:T(8,128)S(1)} %get-tuple-element.48.refs_1_), channel_id=1, source_target_pairs={{0,1},{1,0},{2,3},{3,2},{4,5},{5,4},{6,7},{7,6},{8,9},{9,8},{10,11... | collective-permute-start | bytes 811016 | tf_op jit(solution)/shard_map/ppermute | solution.py:414
  4.5 0.7 copy-start.3
  4.5 4.2 %copy-start = (f32[2,2,2,256,256]{4,3,2,1,0:T(8,128)S(1)}, f32[2,2,2,256,256]{4,3,2,1,0:T(8,128)}, u32[]{:S(2)}) copy-start(f32[2,2,2,256,256]{4,3,2,1,0:T(8,128)} %pivot.7) | copy-start | bytes 6291460
  4.5 4.2 %copy-start.1 = (f32[2,2,2,256,256]{4,3,2,1,0:T(8,128)S(1)}, f32[2,2,2,256,256]{4,3,2,1,0:T(8,128)}, u32[]{:S(2)}) copy-start(f32[2,2,2,256,256]{4,3,2,1,0:T(8,128)} %factor.7) | copy-start | bytes 6291460
  4.5 4.2 %copy-start.2 = (f32[2,2]{1,0:T(2,128)S(1)}, f32[2,2]{1,0:T(2,128)}, u32[]{:S(2)}) copy-start(f32[2,2]{1,0:T(2,128)} %weight.11) | copy-start | bytes 52
  6.5 14.8 %collective-permute-start = (f32[2,256,256]{2,1,0:T(8,128)S(1)}, f32[2,256,256]{2,1,0:T(8,128)S(1)}, u32[]{:S(2)}, u32[]{:S(2)}) collective-permute-start(f32[2,256,256]{2,1,0:T(8,128)S(1)} %get-tuple-element.53._), channel_id=1, source_target_pairs={{2,3},{3,2},{4,5},{5,4},{6,7},{7,6},{10,11},{11,10},{12,13},{13,12... | collective-permute-start | bytes 1572872 | tf_op jit(solution)/shard_map/ppermute | solution.py:419
  10.6 3.4 %collective-permute-start.2 = (f32[2,264,128]{2,1,0:T(8,128)S(1)}, f32[2,264,128]{2,1,0:T(8,128)S(1)}, u32[]{:S(2)}, u32[]{:S(2)}) collective-permute-start(f32[2,264,128]{2,1,0:T(8,128)S(1)} %get-tuple-element.59.refs_1_), channel_id=1, source_target_pairs={{0,1},{8,9},{16,17},{24,25}} | collective-permute-start | bytes 811016 | tf_op jit(solution)/shard_map/ppermute | solution.py:421
  11.3 3.4 %collective-permute-start.4 = (f32[2,264,128]{2,1,0:T(8,128)S(1)}, f32[2,264,128]{2,1,0:T(8,128)S(1)}, u32[]{:S(2)}, u32[]{:S(2)}) collective-permute-start(f32[2,264,128]{2,1,0:T(8,128)S(1)} %shard_map.67), channel_id=1, source_target_pairs={{1,0},{9,8},{17,16},{25,24}} | collective-permute-start | bytes 811016 | tf_op jit(solution)/shard_map/ppermute | solution.py:430
  14.0 9.0 %collective-permute-start.3 = (f32[2,264,128]{2,1,0:T(8,128)S(1)}, f32[2,264,128]{2,1,0:T(8,128)S(1)}, u32[]{:S(2)}, u32[]{:S(2)}) collective-permute-start(f32[2,264,128]{2,1,0:T(8,128)S(1)} %shard_map.66), channel_id=1, source_target_pairs={{1,3},{9,11},{17,19},{25,27}} | collective-permute-start | bytes 811016 | tf_op jit(solution)/shard_map/ppermute | solution.py:435
  14.7 8.3 %collective-permute-start.5 = (f32[2,264,128]{2,1,0:T(8,128)S(1)}, f32[2,264,128]{2,1,0:T(8,128)S(1)}, u32[]{:S(2)}, u32[]{:S(2)}) collective-permute-start(f32[2,264,128]{2,1,0:T(8,128)S(1)} %collective-permute-done.4), channel_id=1, source_target_pairs={{0,2},{8,10},{16,18},{24,26}} | collective-permute-start | bytes 811016 | tf_op jit(solution)/shard_map/ppermute | solution.py:436
  23.0 0.9 %collective-permute-start.6 = (f32[2,264,128]{2,1,0:T(8,128)S(1)}, f32[2,264,128]{2,1,0:T(8,128)S(1)}, u32[]{:S(2)}, u32[]{:S(2)}) collective-permute-start(f32[2,264,128]{2,1,0:T(8,128)S(1)} %shard_map.68), channel_id=1, source_target_pairs={{3,5},{2,4},{11,13},{10,12},{19,21},{18,20},{27,29},{26,28}} | collective-permute-start | bytes 811016 | tf_op jit(solution)/shard_map/ppermute | solution.py:452
  23.9 14.6 %collective-permute-start.7 = (f32[2,264,128]{2,1,0:T(8,128)S(1)}, f32[2,264,128]{2,1,0:T(8,128)S(1)}, u32[]{:S(2)}, u32[]{:S(2)}) collective-permute-start(f32[2,264,128]{2,1,0:T(8,128)S(1)} %shard_map.69), channel_id=1, source_target_pairs={{5,7},{4,6},{13,15},{12,14},{21,23},{20,22},{29,31},{28,30}} | collective-permute-start | bytes 811016 | tf_op jit(solution)/shard_map/ppermute | solution.py:452
  39.8 5.4 %collective-permute-start.8 = (f32[2,264,128]{2,1,0:T(8,128)S(1)}, f32[2,264,128]{2,1,0:T(8,128)S(1)}, u32[]{:S(2)}, u32[]{:S(2)}) collective-permute-start(f32[2,264,128]{2,1,0:T(8,128)S(1)} %get-tuple-element.77), channel_id=1, source_target_pairs={{0,1},{1,0},{2,3},{3,2},{4,5},{5,4},{6,7},{7,6},{8,9},{9,8},{10,11... | collective-permute-start | bytes 811016 | tf_op jit(solution)/shard_map/ppermute | solution.py:461
  46.7 7.7 %collective-permute-start.12 = (f32[512,128]{1,0:T(8,128)S(1)}, f32[512,128]{1,0:T(8,128)S(1)}, u32[]{:S(2)}, u32[]{:S(2)}) collective-permute-start(f32[512,128]{1,0:T(8,128)S(1)} %slice_bitcast_fusion), channel_id=1, source_target_pairs={{0,8},{8,0},{16,24},{24,16},{1,9},{9,1},{17,25},{25,17},{2,10},{10... | collective-permute-start | bytes 786440 | tf_op jit(solution)/shard_map/ppermute | solution.py:474
  53.9 1.4 %collective-permute-start.9 = (f32[264,128]{1,0:T(8,128)S(1)}, f32[264,128]{1,0:T(8,128)S(1)}, u32[]{:S(2)}, u32[]{:S(2)}) collective-permute-start(f32[264,128]{1,0:T(8,128)S(1)} %slice_bitcast_fusion.1), channel_id=1, source_target_pairs={{0,8},{8,0},{16,24},{24,16},{1,9},{9,1},{17,25},{25,17},{2,10},{10... | collective-permute-start | bytes 405512 | tf_op jit(solution)/shard_map/ppermute | solution.py:474
  54.5 7.6 %collective-permute-start.13 = (f32[512,128]{1,0:T(8,128)S(1)}, f32[512,128]{1,0:T(8,128)S(1)}, u32[]{:S(2)}, u32[]{:S(2)}) collective-permute-start(f32[512,128]{1,0:T(8,128)S(1)} %bitcast_add_fusion), channel_id=1, source_target_pairs={{0,16},{8,24},{16,0},{24,8},{1,17},{9,25},{17,1},{25,9},{2,18},{10... | collective-permute-start | bytes 786440 | tf_op jit(solution)/shard_map/ppermute | solution.py:474
  55.3 9.6 %collective-permute-start.10 = (f32[264,128]{1,0:T(8,128)S(1)}, f32[264,128]{1,0:T(8,128)S(1)}, u32[]{:S(2)}, u32[]{:S(2)}) collective-permute-start(f32[264,128]{1,0:T(8,128)S(1)} %fusion), channel_id=1, source_target_pairs={{0,16},{8,24},{16,0},{24,8},{1,17},{9,25},{17,1},{25,9},{2,18},{10... | collective-permute-start | bytes 405512 | tf_op jit(solution)/shard_map/ppermute | solution.py:474
  62.1 4.2 %collective-permute-start.14 = (f32[512,128]{1,0:T(8,128)S(1)}, f32[512,128]{1,0:T(8,128)S(1)}, u32[]{:S(2)}, u32[]{:S(2)}) collective-permute-start(f32[512,128]{1,0:T(8,128)S(1)} %add.15.mine), channel_id=1, source_target_pairs={{0,8},{8,0},{16,24},{24,16},{1,9},{9,1},{17,25},{25,17},{2,10},{10... | collective-permute-start | bytes 786440 | tf_op jit(solution)/shard_map/ppermute | solution.py:474
  65.0 2.3 %collective-permute-start.11 = (f32[264,128]{1,0:T(8,128)S(1)}, f32[264,128]{1,0:T(8,128)S(1)}, u32[]{:S(2)}, u32[]{:S(2)}) collective-permute-start(f32[264,128]{1,0:T(8,128)S(1)} %add.13.mine), channel_id=1, source_target_pairs={{0,8},{8,0},{16,24},{24,16},{1,9},{9,1},{17,25},{25,17},{2,10},{10... | collective-permute-start | bytes 405512 | tf_op jit(solution)/shard_map/ppermute | solution.py:474

commit v10 on v9

--- a/solution.py
+++ b/solution.py
@@ -271,6 +271,14 @@
         ep[c] = high[c] + packed(term)
 
 
+def sum_kernel(*refs):
+    *parts, out = refs
+    value = parts[0][...]
+    for part in parts[1:]:
+        value = value + part[...]
+    out[...] = value
+
+
 def share_kernel(fas, fat, ea, *refs):
     *received, own, sent, scratch = refs
     value = received[0][...]
@@ -312,18 +320,19 @@
     )
 
 
-def density_kernel(weight, x, f0s, f0t, gs, gt, weighted, off, diag):
+def density_kernel(weight, x, f0s, f0t, gs, gt, weighted, _, off, diag):
     core = whereabouts()[2]
     first, second, us, ts = off_values(slot_of(True), weight, unpacked_split(x), f0s, f0t, gs, weighted)
     off[core], off[1 - core] = first, second
     diag[core], diag[1 - core] = diag_values(us, ts, f0t, gt, weighted)
 
 
-def more_off_kernel(weight, x, x_first, f0s, f0t, gs, weighted, before, off, us_out, ts_out):
+def more_off_kernel(weight, x_even, x_odd, x_first, f0s, f0t, gs, weighted, before, off, us_out, ts_out):
     core = whereabouts()[2]
     place = whereabouts()[0]
     x = [
-        jnp.where(place > 1, x[c], jnp.where(place == 1, x_first[c], 0.0)) for c in range(2)
+        jnp.where(place > 1, x_even[c] + x_odd[c], jnp.where(place == 1, x_first[c], 0.0))
+        for c in range(2)
     ]
     xs = split_pair(unpacked(x[0]), unpacked(x[1]))
     first, second, us, ts = off_values(slot_of(False), weight, xs, f0s, f0t, gs, weighted)
@@ -446,11 +455,24 @@
     )
     arrived = list(received)
     for turn in range(1, rows - 1):
-        active = functools.partial(step_kernel, lambda place, turn=turn: lax.div(place, 2) == turn)
-        (wave,) = run(active, [], [ps, pt, ep] + arrived, [mirrored])
-        up = [pair for p in range(poles) for pair in zip(hosts(turn, p), hosts(turn + 1, p))]
-        arrived = [lax.ppermute(wave, AXES, up)]
+        (wave,) = run(
+            functools.partial(step_kernel, lambda place, turn=turn: lax.div(place, 2) == turn),
+            [],
+            [ps, pt, ep] + arrived,
+            [mirrored],
+        )
+        odd, even = (
+            [pair for p in range(poles) for pair in [(hosts(turn, p)[c], hosts(turn + 1, p)[c])]]
+            for c in range(2)
+        )
+        if turn < rows - 2:
+            arrived = [lax.ppermute(wave, AXES, odd + even)]
+        else:
+            arrived = [lax.ppermute(wave, AXES, odd), lax.ppermute(wave, AXES, even)]
         received += arrived
+    pairs_in_rows = [(at(p, s), at(p, s + 1)) for p in range(poles) for s in range(2, turns, 2)]
+    (entered_odd,) = run(sum_kernel, [], received[:1] + received[2:-1], [mirrored])
+    shared_even = lax.ppermute(entered_odd, AXES, [(t, s) for s, t in pairs_in_rows])
     own, sent = run(
         share_kernel,
         [],
@@ -458,15 +480,15 @@
         [mirrored, mirrored],
         [pltpu.VMEM(mirrored.shape, F32)],
     )
-    shared = lax.ppermute(sent, AXES, every)
+    shared_odd = lax.ppermute(sent, AXES, pairs_in_rows)
 
     offs = jax.ShapeDtypeStruct((2, 2 * width, width // 2), F32)
     diags = jax.ShapeDtypeStruct((2,) + quarter, F32)
-    off, diag = run(density_kernel, [], [weight, own, m_f0s, m_f0t, m_gs, m_gt, m_w], [offs, diags])
+    off, diag = run(density_kernel, [], [weight, own, m_f0s, m_f0t, m_gs, m_gt, m_w, shared_even], [offs, diags])
     off, us, ts = run(
         more_off_kernel,
         [],
-        [weight, shared, e_in, o_f0s, o_f0t, o_gs, o_w, off],
+        [weight, shared_even, shared_odd, e_in, o_f0s, o_f0t, o_gs, o_w, off],
         [offs, parts, parts],
     )
 

time: 68.4 us -> 70 us (1.023); the launches traced: 68.2 us -> 68.8 us
  starting transfers between devices: 19.5 us -> 23 us
  waiting for transfers between devices: 30.3 us -> 27.4 us
    ppermute x3 -> x5, starting transfers between devices: 2.54 us -> 7.06 us  [the longest x1 2.93 us: local(): shared_odd = lax.ppermute(sent, AXES, pairs_in_rows)]
    ppermute x3 -> x5, waiting for transfers between devices: 16.3 us -> 13.3 us  [the longest x2 11.9 us: local(): arrived = [lax.ppermute(wave, AXES, odd), lax.ppermute(wave, AXES, even)]]
    ppermute x6, starting transfers between devices: 10.9 us -> 9.8 us  [exchanged(): lax.ppermute(value, 'pole', [(p, p ^ distance) for p in range(poles)])]
    pallas_call x17 -> x18, Pallas kernels: 16.8 us -> 16.8 us  [run(): pl.pallas_call(kernel, out_shape=shapes, in_specs=[SCALAR] * len(scalars)...]
  transfers between devices with their start and end apart: 15 -> 17, of which waited for: 8 -> 9; matrix products, arithmetic and copies ran while one was open for 0% -> 0% of each run, Pallas kernels for 15% -> 17%
where the time goes in v10:
time: 70 us; the launch traced here: 68.8 us
  waiting for transfers between devices  27.4 us (39%)
  starting transfers between devices  23 us (33%)
  Pallas kernels  16.8 us (24%)
  between operations  0.94 us (1%)
    pallas_call x18, Pallas kernels, run(): pl.pallas_call(kernel, out_shape=shapes, in_specs=[SCALAR] * len(scalars)...  16.8 us
    ppermute x2, waiting for transfers between devices, local(): arrived = [lax.ppermute(wave, AXES, odd), lax.ppermute(wave, AXES, even)]  11.9 us
    ppermute x6, starting transfers between devices, exchanged(): lax.ppermute(value, 'pole', [(p, p ^ distance) for p in range(poles)])  9.8 us
    ppermute x6, waiting for transfers between devices, exchanged(): lax.ppermute(value, 'pole', [(p, p ^ distance) for p in range(poles)])  8.12 us
    ppermute x1, waiting for transfers between devices, local(): g_in = lax.ppermute(o_g, AXES, swaps)  5.92 us
    ppermute x1, starting transfers between devices, local(): shared_odd = lax.ppermute(sent, AXES, pairs_in_rows)  2.93 us
    ppermute x1, starting transfers between devices, local(): g_in = lax.ppermute(o_g, AXES, swaps)  2.16 us
    ppermute x2, starting transfers between devices, local(): arrived = [lax.ppermute(wave, AXES, odd), lax.ppermute(wave, AXES, even)]  1.97 us
  transfers between devices with their start and end apart: 17, of which 9 were waited for; matrix products, arithmetic and copies ran while one was open for 0% of the time, Pallas kernels for 17%

profile of v10, /device:TPU:29, one launch (start us, length us, event | category | flops | bytes accessed | tf_op | source)
XLA Modules:
  0.0 68.8 jit_solution(5319952905513226480)
XLA Ops:
  0.6 2.6 %shard_map.59 = (bf16[4,256,256]{2,1,0:T(8,128)(2,1)S(1)}, f32[2,264,128]{2,1,0:T(8,128)S(1)}, f32[4,264,128]{2,1,0:T(8,128)S(1)}, f32[2,256,256]{2,1,0:T(8,128)...) custom-call(s32[2]{0:T(128)} %live.11, ...), custom_call_target="tpu_custom_call" | custom-call | flops 1 | bytes 1 | tf_op jit(solution)/shard_map/pallas_call | solution.py:379
  3.3 1.3 %collective-permute-start.3 = (f32[2,264,128]{2,1,0:T(8,128)S(1)}, f32[2,264,128]{2,1,0:T(8,128)S(1)}, u32[]{:S(2)}, u32[]{:S(2)}) collective-permute-start(f32[2,264,128]{2,1,0:T(8,128)S(1)} %get-tuple-element.48.refs_1_), channel_id=1, source_target_pairs={{0,1},{1,0},{2,3},{3,2},{4,5},{5,4},{6,7},{7,6},{8,9},{9,8},{10,11... | collective-permute-start | bytes 811016 | tf_op jit(solution)/shard_map/ppermute | solution.py:423
  4.5 0.2 shard_map.60
  4.7 0.4 copy-done.3
  5.2 1.3 %shard_map.61 = (bf16[4,256,256]{2,1,0:T(8,128)(2,1)S(1)}, bf16[4,256,256]{2,1,0:T(8,128)(2,1)S(1)}, bf16[4,256,256]{2,1,0:T(8,128)(2,1)S(1)}, bf16[4,256,256]{2,1,0:T(8,128)(2,1)S(1)}, f32[2,256,256]{2,1,0:T(8,128)S(1)}) custom-call(s32[2]{0:T(128)S(1)} %copy-done.3, f32[2,256,256]{2,1,0:T(8,128)S(1)} %get-tuple-element.51.factor, ...), custom_call_target="tpu_custom_call" | custom-call | flops 1 | bytes 1 | tf_op jit(solution)/shard_map/pallas_call | solution.py:379
  6.5 2.2 %collective-permute-start.2 = (f32[2,256,256]{2,1,0:T(8,128)S(1)}, f32[2,256,256]{2,1,0:T(8,128)S(1)}, u32[]{:S(2)}, u32[]{:S(2)}) collective-permute-start(f32[2,256,256]{2,1,0:T(8,128)S(1)} %get-tuple-element.53._), channel_id=1, source_target_pairs={{2,3},{3,2},{4,5},{5,4},{6,7},{7,6},{10,11},{11,10},{12,13},{13,12... | collective-permute-start | bytes 1572872 | tf_op jit(solution)/shard_map/ppermute | solution.py:428
  8.7 1.8 %shard_map.62 = (bf16[4,256,256]{2,1,0:T(8,128)(2,1)S(1)}, f32[2,264,128]{2,1,0:T(8,128)S(1)}, f32[4,264,128]{2,1,0:T(8,128)S(1)}, f32[2,256,256]{2,1,0:T(8,128)S(1)}) custom-call(s32[2]{0:T(128)S(1)} %copy-done.3, f32[2,2,2,256,256]{4,3,2,1,0:T(8,128)S(1)} %copy-done, f32[2,2,2,256,256]{4,3,2,1,0:T(8,128)S(1)} %copy-done.1, f32[2,2]{1,0:T(2,128)S(1)} %copy-done.2, ...), custom_call_target="tpu_custom_call" | custom-call | flops 1 | bytes 1 | tf_op jit(solution)/shard_map/pallas_call | solution.py:379
  10.6 0.7 collective-permute-start
  11.2 0.0 collective-permute-done.3.e_in.refs_0_.x_first
  11.3 0.7 collective-permute-start.4
  12.0 0.7 shard_map.63
  12.6 1.3 %shard_map.64 = (bf16[4,256,256]{2,1,0:T(8,128)(2,1)S(1)}, bf16[4,256,256]{2,1,0:T(8,128)(2,1)S(1)}, bf16[4,256,256]{2,1,0:T(8,128)(2,1)S(1)}, bf16[4,256,256]{2,1,0:T(8,128)(2,1)S(1)}, f32[2,256,256]{2,1,0:T(8,128)S(1)}) custom-call(s32[2]{0:T(128)S(1)} %copy-done.3, f32[2,256,256]{2,1,0:T(8,128)S(1)} %get-tuple-element.62.factor, ...), custom_call_target="tpu_custom_call" | custom-call | flops 1 | bytes 1 | tf_op jit(solution)/shard_map/pallas_call | solution.py:379
  13.9 0.0 collective-permute-done.refs_0_.e_second
  14.0 0.7 collective-permute-start.1
  14.7 0.0 collective-permute-done.4
  14.7 0.7 collective-permute-start.5
  15.4 5.9 %collective-permute-done.2.g_in = f32[2,256,256]{2,1,0:T(8,128)S(1)} collective-permute-done((f32[2,256,256]{2,1,0:T(8,128)S(1)}, f32[2,256,256]{2,1,0:T(8,128)S(1)}, u32[]{:S(2)}, u32[]{:S(2)}) %collective-permute-start.2) | collective-permute-done | bytes 524320 | tf_op jit(solution)/shard_map/ppermute | solution.py:428
  21.3 1.7 %shard_map.66 = (bf16[4,256,256]{2,1,0:T(8,128)(2,1)S(1)}, bf16[4,256,256]{2,1,0:T(8,128)(2,1)S(1)}, f32[2,264,128]{2,1,0:T(8,128)S(1)}, bf16[4,256,256]{2,1,0:T...) custom-call(f32[2,256,256]{2,1,0:T(8,128)S(1)} %get-tuple-element.67.g, ...), custom_call_target="tpu_custom_call" | custom-call | flops 99999997952 | bytes 1 | tf_op jit(solution)/shard_map/pallas_call | solution.py:379
  23.0 0.0 collective-permute-done.1.refs_0_
  23.0 0.0 collective-permute-done.5.refs_1_
  23.0 0.9 %collective-permute-start.6 = (f32[2,264,128]{2,1,0:T(8,128)S(1)}, f32[2,264,128]{2,1,0:T(8,128)S(1)}, u32[]{:S(2)}, u32[]{:S(2)}) collective-permute-start(f32[2,264,128]{2,1,0:T(8,128)S(1)} %shard_map.68), channel_id=1, source_target_pairs={{3,5},{11,13},{19,21},{27,29},{2,4},{10,12},{18,20},{26,28}} | collective-permute-start | bytes 811016 | tf_op jit(solution)/shard_map/ppermute | solution.py:469
  23.9 0.7 collective-permute-start.7
  24.6 1.3 %collective-permute-start.9 = (f32[2,264,128]{2,1,0:T(8,128)S(1)}, f32[2,264,128]{2,1,0:T(8,128)S(1)}, u32[]{:S(2)}, u32[]{:S(2)}) collective-permute-start(f32[2,264,128]{2,1,0:T(8,128)S(1)} %shard_map.69), channel_id=1, source_target_pairs={{4,6},{12,14},{20,22},{28,30}} | collective-permute-start | bytes 811016 | tf_op jit(solution)/shard_map/ppermute | solution.py:471
  25.9 0.0 collective-permute-done.7.refs_2_.refs_3_
  25.9 0.1 shard_map.70
  26.0 1.3 %collective-permute-start.8 = (f32[2,264,128]{2,1,0:T(8,128)S(1)}, f32[2,264,128]{2,1,0:T(8,128)S(1)}, u32[]{:S(2)}, u32[]{:S(2)}) collective-permute-start(f32[2,264,128]{2,1,0:T(8,128)S(1)} %shard_map.70), channel_id=1, source_target_pairs={{3,2},{5,4},{7,6},{11,10},{13,12},{15,14},{19,18},{21,20},{23,22},... | collective-permute-start | bytes 811016 | tf_op jit(solution)/shard_map/ppermute | solution.py:475
  27.3 11.9 %collective-permute-done.9.refs_4_ = f32[2,264,128]{2,1,0:T(8,128)S(1)} collective-permute-done((f32[2,264,128]{2,1,0:T(8,128)S(1)}, f32[2,264,128]{2,1,0:T(8,128)S(1)}, u32[]{:S(2)}, u32[]{:S(2)}) %collective-permute-start.9) | collective-permute-done | bytes 270368 | tf_op jit(solution)/shard_map/ppermute | solution.py:471
  39.2 1.2 %shard_map.71 = (f32[2,264,128]{2,1,0:T(8,128)S(1)}, f32[2,264,128]{2,1,0:T(8,128)S(1)}) custom-call(bf16[4,256,256]{2,1,0:T(8,128)(2,1)S(1)} %get-tuple-element.74.fas, bf16[4,256,256]{2,1,0:T(8,128)(2,1)S(1)} %get-tuple-element.75.fat, f32[2,264,128]{2,1,0:T(8,128)S(1)} %get-tuple-element.76.ea, f32[2,264,128]{2,1,0:T(8,128)S(1)} %collective-permute-done.1.refs_0_, ...), custom_call_target="tpu_custom_call" | custom-call | flops 1 | bytes 1 | tf_op jit(solution)/shard_map/pallas_call | solution.py:379
  40.5 2.9 %collective-permute-start.10 = (f32[2,264,128]{2,1,0:T(8,128)S(1)}, f32[2,264,128]{2,1,0:T(8,128)S(1)}, u32[]{:S(2)}, u32[]{:S(2)}) collective-permute-start(f32[2,264,128]{2,1,0:T(8,128)S(1)} %get-tuple-element.77), channel_id=1, source_target_pairs={{2,3},{4,5},{6,7},{10,11},{12,13},{14,15},{18,19},{20,21},{22,23},... | collective-permute-start | bytes 811016 | tf_op jit(solution)/shard_map/ppermute | solution.py:483
  43.4 0.8 %collective-permute-done.8._.x_even = f32[2,264,128]{2,1,0:T(8,128)S(1)} collective-permute-done((f32[2,264,128]{2,1,0:T(8,128)S(1)}, f32[2,264,128]{2,1,0:T(8,128)S(1)}, u32[]{:S(2)}, u32[]{:S(2)}) %collective-permute-start.8) | collective-permute-done | bytes 270368 | tf_op jit(solution)/shard_map/ppermute | solution.py:475
  44.2 2.0 %shard_map.72 = (f32[2,512,128]{2,1,0:T(8,128)S(1)}, f32[2,264,128]{2,1,0:T(8,128)S(1)}) custom-call(f32[2,2]{1,0:T(2,128)S(1)} %copy-done.2, f32[2,264,128]{2,1,0:T(8,128)S(1)} %get-tuple-element.81.x, bf16[4,256,256]{2,1,0:T(8,128)(2,1)S(1)} %get-tuple-element.82.f0s, bf16[4,256,256]{2,1,0:T(8,128)(2,1)S(1)} %get-tuple-element.83.f0t, ...), custom_call_target="tpu_custom_call" | custom-call | flops 1 | bytes 1 | tf_op jit(solution)/shard_map/pallas_call | solution.py:379
  46.1 0.6 collective-permute-done.10.x_odd
  46.8 1.5 %shard_map.73 = (f32[2,512,128]{2,1,0:T(8,128)S(1)}, bf16[4,256,256]{2,1,0:T(8,128)(2,1)S(1)}, bf16[4,256,256]{2,1,0:T(8,128)(2,1)S(1)}) custom-call(f32[2,2]{1,0:T(2,128)S(1)} %copy-done.2, f32[2,264,128]{2,1,0:T(8,128)S(1)} %collective-permute-done.8._.x_even, f32[2,264,128]{2,1,0:T(8,128)S(1)} %collective-permute-done.10.x_odd, ...), custom_call_target="tpu_custom_call" | custom-call | flops 1 | bytes 1 | tf_op jit(solution)/shard_map/pallas_call | solution.py:379
  48.3 5.5 %collective-permute-start.14 = (f32[512,128]{1,0:T(8,128)S(1)}, f32[512,128]{1,0:T(8,128)S(1)}, u32[]{:S(2)}, u32[]{:S(2)}) collective-permute-start(f32[512,128]{1,0:T(8,128)S(1)} %slice_bitcast_fusion), channel_id=1, source_target_pairs={{0,8},{8,0},{16,24},{24,16},{1,9},{9,1},{17,25},{25,17},{2,10},{10... | collective-permute-start | bytes 786440 | tf_op jit(solution)/shard_map/ppermute | solution.py:496
  53.9 0.6 shard_map.74
  54.5 0.1 collective-permute-start.11
  54.6 0.5 collective-permute-done.14
  55.1 0.1 collective-permute-start.15
  55.2 0.8 %collective-permute-done.11 = f32[264,128]{1,0:T(8,128)S(1)} collective-permute-done((f32[264,128]{1,0:T(8,128)S(1)}, f32[264,128]{1,0:T(8,128)S(1)}, u32[]{:S(2)}, u32[]{:S(2)}) %collective-permute-start.11) | collective-permute-done | bytes 135200 | tf_op jit(solution)/shard_map/ppermute | solution.py:496
  55.9 0.8 %collective-permute-start.12 = (f32[264,128]{1,0:T(8,128)S(1)}, f32[264,128]{1,0:T(8,128)S(1)}, u32[]{:S(2)}, u32[]{:S(2)}) collective-permute-start(f32[264,128]{1,0:T(8,128)S(1)} %fusion), channel_id=1, source_target_pairs={{0,16},{8,24},{16,0},{24,8},{1,17},{9,25},{17,1},{25,9},{2,18},{10... | collective-permute-start | bytes 405512 | tf_op jit(solution)/shard_map/ppermute | solution.py:496
  56.7 6.0 %collective-permute-done.15 = f32[512,128]{1,0:T(8,128)S(1)} collective-permute-done((f32[512,128]{1,0:T(8,128)S(1)}, f32[512,128]{1,0:T(8,128)S(1)}, u32[]{:S(2)}, u32[]{:S(2)}) %collective-permute-start.15) | collective-permute-done | bytes 262176 | tf_op jit(solution)/shard_map/ppermute | solution.py:496
  62.7 2.1 %collective-permute-start.16 = (f32[512,128]{1,0:T(8,128)S(1)}, f32[512,128]{1,0:T(8,128)S(1)}, u32[]{:S(2)}, u32[]{:S(2)}) collective-permute-start(f32[512,128]{1,0:T(8,128)S(1)} %add.15.mine), channel_id=1, source_target_pairs={{0,8},{8,0},{16,24},{24,16},{1,9},{9,1},{17,25},{25,17},{2,10},{10... | collective-permute-start | bytes 786440 | tf_op jit(solution)/shard_map/ppermute | solution.py:496
  64.8 0.8 %collective-permute-done.12 = f32[264,128]{1,0:T(8,128)S(1)} collective-permute-done((f32[264,128]{1,0:T(8,128)S(1)}, f32[264,128]{1,0:T(8,128)S(1)}, u32[]{:S(2)}, u32[]{:S(2)}) %collective-permute-start.12) | collective-permute-done | bytes 135200 | tf_op jit(solution)/shard_map/ppermute | solution.py:496
  65.6 1.3 %collective-permute-start.13 = (f32[264,128]{1,0:T(8,128)S(1)}, f32[264,128]{1,0:T(8,128)S(1)}, u32[]{:S(2)}, u32[]{:S(2)}) collective-permute-start(f32[264,128]{1,0:T(8,128)S(1)} %add.13.mine), channel_id=1, source_target_pairs={{0,8},{8,0},{16,24},{24,16},{1,9},{9,1},{17,25},{25,17},{2,10},{10... | collective-permute-start | bytes 405512 | tf_op jit(solution)/shard_map/ppermute | solution.py:496
  66.8 0.0 collective-permute-done.16.theirs
  66.8 0.8 %shard_map.75 = (f32[2,256,256]{2,1,0:T(8,128)}, f32[8,128]{1,0:T(8,128)S(1)}) custom-call(f32[512,128]{1,0:T(8,128)S(1)} %add.15.mine, f32[512,128]{1,0:T(8,128)S(1)} %collective-permute-done.16.theirs), custom_call_target="tpu_custom_call" | custom-call | flops 1 | bytes 1 | tf_op jit(solution)/shard_map/pallas_call | solution.py:379
  67.7 0.1 collective-permute-done.13.theirs
  67.8 0.9 %shard_map.76 = f32[2,256,256]{2,1,0:T(8,128)} custom-call(f32[264,128]{1,0:T(8,128)S(1)} %add.13.mine, f32[264,128]{1,0:T(8,128)S(1)} %collective-permute-done.13.theirs, f32[8,128]{1,0:T(8,128)S(1)} %get-tuple-element.90._), custom_call_target="tpu_custom_call" | custom-call | flops 1 | bytes 1 | tf_op jit(solution)/shard_map/pallas_call | solution.py:379
  (18 shorter events, 0.2 us)
Async XLA Ops:
  3.3 8.0 %collective-permute-start.3 = (f32[2,264,128]{2,1,0:T(8,128)S(1)}, f32[2,264,128]{2,1,0:T(8,128)S(1)}, u32[]{:S(2)}, u32[]{:S(2)}) collective-permute-start(f32[2,264,128]{2,1,0:T(8,128)S(1)} %get-tuple-element.48.refs_1_), channel_id=1, source_target_pairs={{0,1},{1,0},{2,3},{3,2},{4,5},{5,4},{6,7},{7,6},{8,9},{9,8},{10,11... | collective-permute-start | bytes 811016 | tf_op jit(solution)/shard_map/ppermute | solution.py:423
  4.5 0.7 copy-start.3
  4.5 4.2 %copy-start = (f32[2,2,2,256,256]{4,3,2,1,0:T(8,128)S(1)}, f32[2,2,2,256,256]{4,3,2,1,0:T(8,128)}, u32[]{:S(2)}) copy-start(f32[2,2,2,256,256]{4,3,2,1,0:T(8,128)} %pivot.7) | copy-start | bytes 6291460
  4.5 4.2 %copy-start.1 = (f32[2,2,2,256,256]{4,3,2,1,0:T(8,128)S(1)}, f32[2,2,2,256,256]{4,3,2,1,0:T(8,128)}, u32[]{:S(2)}) copy-start(f32[2,2,2,256,256]{4,3,2,1,0:T(8,128)} %factor.7) | copy-start | bytes 6291460
  4.5 4.2 %copy-start.2 = (f32[2,2]{1,0:T(2,128)S(1)}, f32[2,2]{1,0:T(2,128)}, u32[]{:S(2)}) copy-start(f32[2,2]{1,0:T(2,128)} %weight.11) | copy-start | bytes 52
  6.5 14.8 %collective-permute-start.2 = (f32[2,256,256]{2,1,0:T(8,128)S(1)}, f32[2,256,256]{2,1,0:T(8,128)S(1)}, u32[]{:S(2)}, u32[]{:S(2)}) collective-permute-start(f32[2,256,256]{2,1,0:T(8,128)S(1)} %get-tuple-element.53._), channel_id=1, source_target_pairs={{2,3},{3,2},{4,5},{5,4},{6,7},{7,6},{10,11},{11,10},{12,13},{13,12... | collective-permute-start | bytes 1572872 | tf_op jit(solution)/shard_map/ppermute | solution.py:428
  10.6 3.4 %collective-permute-start = (f32[2,264,128]{2,1,0:T(8,128)S(1)}, f32[2,264,128]{2,1,0:T(8,128)S(1)}, u32[]{:S(2)}, u32[]{:S(2)}) collective-permute-start(f32[2,264,128]{2,1,0:T(8,128)S(1)} %get-tuple-element.59.refs_1_), channel_id=1, source_target_pairs={{0,1},{8,9},{16,17},{24,25}} | collective-permute-start | bytes 811016 | tf_op jit(solution)/shard_map/ppermute | solution.py:430
  11.3 3.4 %collective-permute-start.4 = (f32[2,264,128]{2,1,0:T(8,128)S(1)}, f32[2,264,128]{2,1,0:T(8,128)S(1)}, u32[]{:S(2)}, u32[]{:S(2)}) collective-permute-start(f32[2,264,128]{2,1,0:T(8,128)S(1)} %shard_map.67), channel_id=1, source_target_pairs={{1,0},{9,8},{17,16},{25,24}} | collective-permute-start | bytes 811016 | tf_op jit(solution)/shard_map/ppermute | solution.py:439
  14.0 9.0 %collective-permute-start.1 = (f32[2,264,128]{2,1,0:T(8,128)S(1)}, f32[2,264,128]{2,1,0:T(8,128)S(1)}, u32[]{:S(2)}, u32[]{:S(2)}) collective-permute-start(f32[2,264,128]{2,1,0:T(8,128)S(1)} %shard_map.65), channel_id=1, source_target_pairs={{1,3},{9,11},{17,19},{25,27}} | collective-permute-start | bytes 811016 | tf_op jit(solution)/shard_map/ppermute | solution.py:444
  14.7 8.3 %collective-permute-start.5 = (f32[2,264,128]{2,1,0:T(8,128)S(1)}, f32[2,264,128]{2,1,0:T(8,128)S(1)}, u32[]{:S(2)}, u32[]{:S(2)}) collective-permute-start(f32[2,264,128]{2,1,0:T(8,128)S(1)} %collective-permute-done.4), channel_id=1, source_target_pairs={{0,2},{8,10},{16,18},{24,26}} | collective-permute-start | bytes 811016 | tf_op jit(solution)/shard_map/ppermute | solution.py:445
  23.0 0.9 %collective-permute-start.6 = (f32[2,264,128]{2,1,0:T(8,128)S(1)}, f32[2,264,128]{2,1,0:T(8,128)S(1)}, u32[]{:S(2)}, u32[]{:S(2)}) collective-permute-start(f32[2,264,128]{2,1,0:T(8,128)S(1)} %shard_map.68), channel_id=1, source_target_pairs={{3,5},{11,13},{19,21},{27,29},{2,4},{10,12},{18,20},{26,28}} | collective-permute-start | bytes 811016 | tf_op jit(solution)/shard_map/ppermute | solution.py:469
  23.9 2.0 %collective-permute-start.7 = (f32[2,264,128]{2,1,0:T(8,128)S(1)}, f32[2,264,128]{2,1,0:T(8,128)S(1)}, u32[]{:S(2)}, u32[]{:S(2)}) collective-permute-start(f32[2,264,128]{2,1,0:T(8,128)S(1)} %shard_map.69), channel_id=1, source_target_pairs={{5,7},{13,15},{21,23},{29,31}} | collective-permute-start | bytes 811016 | tf_op jit(solution)/shard_map/ppermute | solution.py:471
  24.6 14.6 %collective-permute-start.9 = (f32[2,264,128]{2,1,0:T(8,128)S(1)}, f32[2,264,128]{2,1,0:T(8,128)S(1)}, u32[]{:S(2)}, u32[]{:S(2)}) collective-permute-start(f32[2,264,128]{2,1,0:T(8,128)S(1)} %shard_map.69), channel_id=1, source_target_pairs={{4,6},{12,14},{20,22},{28,30}} | collective-permute-start | bytes 811016 | tf_op jit(solution)/shard_map/ppermute | solution.py:471
  26.0 18.2 %collective-permute-start.8 = (f32[2,264,128]{2,1,0:T(8,128)S(1)}, f32[2,264,128]{2,1,0:T(8,128)S(1)}, u32[]{:S(2)}, u32[]{:S(2)}) collective-permute-start(f32[2,264,128]{2,1,0:T(8,128)S(1)} %shard_map.70), channel_id=1, source_target_pairs={{3,2},{5,4},{7,6},{11,10},{13,12},{15,14},{19,18},{21,20},{23,22},... | collective-permute-start | bytes 811016 | tf_op jit(solution)/shard_map/ppermute | solution.py:475
  40.5 6.3 %collective-permute-start.10 = (f32[2,264,128]{2,1,0:T(8,128)S(1)}, f32[2,264,128]{2,1,0:T(8,128)S(1)}, u32[]{:S(2)}, u32[]{:S(2)}) collective-permute-start(f32[2,264,128]{2,1,0:T(8,128)S(1)} %get-tuple-element.77), channel_id=1, source_target_pairs={{2,3},{4,5},{6,7},{10,11},{12,13},{14,15},{18,19},{20,21},{22,23},... | collective-permute-start | bytes 811016 | tf_op jit(solution)/shard_map/ppermute | solution.py:483
  48.3 6.7 %collective-permute-start.14 = (f32[512,128]{1,0:T(8,128)S(1)}, f32[512,128]{1,0:T(8,128)S(1)}, u32[]{:S(2)}, u32[]{:S(2)}) collective-permute-start(f32[512,128]{1,0:T(8,128)S(1)} %slice_bitcast_fusion), channel_id=1, source_target_pairs={{0,8},{8,0},{16,24},{24,16},{1,9},{9,1},{17,25},{25,17},{2,10},{10... | collective-permute-start | bytes 786440 | tf_op jit(solution)/shard_map/ppermute | solution.py:496
  54.5 1.4 %collective-permute-start.11 = (f32[264,128]{1,0:T(8,128)S(1)}, f32[264,128]{1,0:T(8,128)S(1)}, u32[]{:S(2)}, u32[]{:S(2)}) collective-permute-start(f32[264,128]{1,0:T(8,128)S(1)} %slice_bitcast_fusion.1), channel_id=1, source_target_pairs={{0,8},{8,0},{16,24},{24,16},{1,9},{9,1},{17,25},{25,17},{2,10},{10... | collective-permute-start | bytes 405512 | tf_op jit(solution)/shard_map/ppermute | solution.py:496
  55.1 7.6 %collective-permute-start.15 = (f32[512,128]{1,0:T(8,128)S(1)}, f32[512,128]{1,0:T(8,128)S(1)}, u32[]{:S(2)}, u32[]{:S(2)}) collective-permute-start(f32[512,128]{1,0:T(8,128)S(1)} %bitcast_add_fusion), channel_id=1, source_target_pairs={{0,16},{8,24},{16,0},{24,8},{1,17},{9,25},{17,1},{25,9},{2,18},{10... | collective-permute-start | bytes 786440 | tf_op jit(solution)/shard_map/ppermute | solution.py:496
  55.9 9.6 %collective-permute-start.12 = (f32[264,128]{1,0:T(8,128)S(1)}, f32[264,128]{1,0:T(8,128)S(1)}, u32[]{:S(2)}, u32[]{:S(2)}) collective-permute-start(f32[264,128]{1,0:T(8,128)S(1)} %fusion), channel_id=1, source_target_pairs={{0,16},{8,24},{16,0},{24,8},{1,17},{9,25},{17,1},{25,9},{2,18},{10... | collective-permute-start | bytes 405512 | tf_op jit(solution)/shard_map/ppermute | solution.py:496
  62.7 4.2 %collective-permute-start.16 = (f32[512,128]{1,0:T(8,128)S(1)}, f32[512,128]{1,0:T(8,128)S(1)}, u32[]{:S(2)}, u32[]{:S(2)}) collective-permute-start(f32[512,128]{1,0:T(8,128)S(1)} %add.15.mine), channel_id=1, source_target_pairs={{0,8},{8,0},{16,24},{24,16},{1,9},{9,1},{17,25},{25,17},{2,10},{10... | collective-permute-start | bytes 786440 | tf_op jit(solution)/shard_map/ppermute | solution.py:496
  65.6 2.3 %collective-permute-start.13 = (f32[264,128]{1,0:T(8,128)S(1)}, f32[264,128]{1,0:T(8,128)S(1)}, u32[]{:S(2)}, u32[]{:S(2)}) collective-permute-start(f32[264,128]{1,0:T(8,128)S(1)} %add.13.mine), channel_id=1, source_target_pairs={{0,8},{8,0},{16,24},{24,16},{1,9},{9,1},{17,25},{25,17},{2,10},{10... | collective-permute-start | bytes 405512 | tf_op jit(solution)/shard_map/ppermute | solution.py:496

commit v11 on v9

--- a/solution.py
+++ b/solution.py
@@ -250,6 +250,18 @@
         fold(split_pair(unpacked(value[0]), unpacked(value[1])), gs, gt, e, out)
 
 
+def cross_kernel(gs, gt, e, x, second, out):
+    place = whereabouts()[0]
+
+    @pl.when(place == 0)
+    def _():
+        out[...] = second[...]
+
+    @pl.when(place == 1)
+    def _():
+        fold(unpacked_split(x), gs, gt, e, out)
+
+
 def pair_kernel(g, e, g_in, e_in, e_second, fas, fat, ea, ps, pt, ep):
     upper = whereabouts()[0] > 1
     is_odd = whereabouts()[1] == 1
@@ -418,7 +430,10 @@
     )
     g_in = lax.ppermute(o_g, AXES, swaps)
     made = run(sent_second_kernel, [live], [pivot, factor, weight, o_g, *second], constants)
-    e_second = lax.ppermute(made[1], AXES, first)
+    (wave_even,) = run(cross_kernel, [], [o_gs, o_gt, o_e, e_in, made[1]], [mirrored])
+    crossed = lax.ppermute(
+        wave_even, AXES, first + [(at(p, 1), at(p, 0)) for p in range(poles)]
+    )
     m_f1s, m_e, m_w, m_f0 = run(
         second_constant_kernel, [live], [pivot, factor, weight, *made], constants
     )
@@ -426,21 +441,19 @@
         factor_kernel, [live], [m_f0, m_f1s], factors
     )
     starts = functools.partial(step_kernel, lambda place: place == 1)
-    (wave_even,) = run(starts, [], [o_gs, o_gt, o_e, e_in], [mirrored])
-    wave_even = lax.ppermute(wave_even, AXES, [(at(p, 1), at(p, 0)) for p in range(poles)])
-    (wave_odd,) = run(starts, [], [m_gs, m_gt, m_e, e_second], [mirrored])
+    (wave_odd,) = run(starts, [], [m_gs, m_gt, m_e, crossed], [mirrored])
     received = []
     if rows > 1:
         received = [
             lax.ppermute(wave_odd, AXES, [(at(p, 1), at(p, 3)) for p in range(poles)]),
-            lax.ppermute(wave_even, AXES, [(at(p, 0), at(p, 2)) for p in range(poles)]),
+            lax.ppermute(crossed, AXES, [(at(p, 0), at(p, 2)) for p in range(poles)]),
         ]
     else:
         received = [jnp.zeros(mirrored.shape, F32)]
     fas, fat, ea, ps, pt, ep = run(
         pair_kernel,
         [],
-        [m_g, m_e, g_in, e_in, e_second],
+        [m_g, m_e, g_in, e_in, crossed],
         [parts, parts, mirrored, parts, parts, mirrored],
         cost=LONG,
     )

time: 68.4 us -> 67.6 us (0.988)
  waiting for transfers between devices: 30.3 us -> 28.1 us
  starting transfers between devices: 19.5 us -> 20.5 us
    ppermute x2, waiting for transfers between devices: 13.3 us -> 11.5 us  [local(): arrived = [lax.ppermute(wave, AXES, up)]]
    ppermute x1, waiting for transfers between devices: 2.98 us -> 1.92 us  [local(): shared = lax.ppermute(sent, AXES, every)]
    ppermute x1, starting transfers between devices: 0.39 us -> 1.43 us  [local(): shared = lax.ppermute(sent, AXES, every)]
    ppermute x6, starting transfers between devices: 10.9 us -> 11.7 us  [exchanged(): lax.ppermute(value, 'pole', [(p, p ^ distance) for p in range(poles)])]
    ppermute x1, waiting for transfers between devices: 5.92 us -> 6.61 us  [local(): g_in = lax.ppermute(o_g, AXES, swaps)]
    ppermute x3 -> x2, starting transfers between devices: 2.03 us -> 1.36 us  [the longest x1 0.68 us: local(): lax.ppermute(crossed, AXES, [(at(p, 0), at(p, 2)) for p in range(poles)])]
  transfers between devices with their start and end apart: 15 -> 14, of which waited for: 8 -> 8; matrix products, arithmetic and copies ran while one was open for 0% -> 0% of each run, Pallas kernels for 15% -> 16%
where the time goes in v11:
time: 67.6 us; the launch traced here: 67.2 us
  waiting for transfers between devices  28.1 us (42%)
  starting transfers between devices  20.5 us (30%)
  Pallas kernels  17 us (25%)
  between operations  0.9 us (1%)
    pallas_call x17, Pallas kernels, run(): pl.pallas_call(kernel, out_shape=shapes, in_specs=[SCALAR] * len(scalars)...  17 us
    ppermute x6, starting transfers between devices, exchanged(): lax.ppermute(value, 'pole', [(p, p ^ distance) for p in range(poles)])  11.7 us
    ppermute x2, waiting for transfers between devices, local(): arrived = [lax.ppermute(wave, AXES, up)]  11.5 us
    ppermute x6, waiting for transfers between devices, exchanged(): lax.ppermute(value, 'pole', [(p, p ^ distance) for p in range(poles)])  8.13 us
    ppermute x1, waiting for transfers between devices, local(): g_in = lax.ppermute(o_g, AXES, swaps)  6.61 us
    ppermute x1, starting transfers between devices, local(): g_in = lax.ppermute(o_g, AXES, swaps)  2.16 us
    ppermute x2, starting transfers between devices, local(): arrived = [lax.ppermute(wave, AXES, up)]  1.97 us
    ppermute x1, waiting for transfers between devices, local(): shared = lax.ppermute(sent, AXES, every)  1.92 us
  transfers between devices with their start and end apart: 14, of which 8 were waited for; matrix products, arithmetic and copies ran while one was open for 0% of the time, Pallas kernels for 16%

profile of v11, /device:TPU:29, one launch (start us, length us, event | category | flops | bytes accessed | tf_op | source)
XLA Modules:
  0.0 67.2 jit_solution(2915475092188377193)
XLA Ops:
  0.6 2.6 %shard_map.59 = (bf16[4,256,256]{2,1,0:T(8,128)(2,1)S(1)}, f32[2,264,128]{2,1,0:T(8,128)S(1)}, f32[4,264,128]{2,1,0:T(8,128)S(1)}, f32[2,256,256]{2,1,0:T(8,128)...) custom-call(s32[2]{0:T(128)} %live.11, ...), custom_call_target="tpu_custom_call" | custom-call | flops 1 | bytes 1 | tf_op jit(solution)/shard_map/pallas_call | solution.py:382
  3.3 1.3 %collective-permute-start.1 = (f32[2,264,128]{2,1,0:T(8,128)S(1)}, f32[2,264,128]{2,1,0:T(8,128)S(1)}, u32[]{:S(2)}, u32[]{:S(2)}) collective-permute-start(f32[2,264,128]{2,1,0:T(8,128)S(1)} %get-tuple-element.48.refs_1_), channel_id=1, source_target_pairs={{0,1},{1,0},{2,3},{3,2},{4,5},{5,4},{6,7},{7,6},{8,9},{9,8},{10,11... | collective-permute-start | bytes 811016 | tf_op jit(solution)/shard_map/ppermute | solution.py:426
  4.5 0.0 copy-start.3
  4.5 0.0 copy-start
  4.5 0.2 shard_map.60
  4.7 0.4 copy-done.3
  5.2 1.3 %shard_map.61 = (bf16[4,256,256]{2,1,0:T(8,128)(2,1)S(1)}, bf16[4,256,256]{2,1,0:T(8,128)(2,1)S(1)}, bf16[4,256,256]{2,1,0:T(8,128)(2,1)S(1)}, bf16[4,256,256]{2,1,0:T(8,128)(2,1)S(1)}, f32[2,256,256]{2,1,0:T(8,128)S(1)}) custom-call(s32[2]{0:T(128)S(1)} %copy-done.3, f32[2,256,256]{2,1,0:T(8,128)S(1)} %get-tuple-element.51.factor, ...), custom_call_target="tpu_custom_call" | custom-call | flops 1 | bytes 1 | tf_op jit(solution)/shard_map/pallas_call | solution.py:382
  6.5 2.2 %collective-permute-start = (f32[2,256,256]{2,1,0:T(8,128)S(1)}, f32[2,256,256]{2,1,0:T(8,128)S(1)}, u32[]{:S(2)}, u32[]{:S(2)}) collective-permute-start(f32[2,256,256]{2,1,0:T(8,128)S(1)} %get-tuple-element.53._), channel_id=1, source_target_pairs={{2,3},{3,2},{4,5},{5,4},{6,7},{7,6},{10,11},{11,10},{12,13},{13,12... | collective-permute-start | bytes 1572872 | tf_op jit(solution)/shard_map/ppermute | solution.py:431
  8.7 0.0 copy-done
  8.7 0.0 copy-done.1
  8.7 0.0 copy-done.2
  8.7 1.8 %shard_map.62 = (bf16[4,256,256]{2,1,0:T(8,128)(2,1)S(1)}, f32[2,264,128]{2,1,0:T(8,128)S(1)}, f32[4,264,128]{2,1,0:T(8,128)S(1)}, f32[2,256,256]{2,1,0:T(8,128)S(1)}) custom-call(s32[2]{0:T(128)S(1)} %copy-done.3, f32[2,2,2,256,256]{4,3,2,1,0:T(8,128)S(1)} %copy-done, f32[2,2,2,256,256]{4,3,2,1,0:T(8,128)S(1)} %copy-done.1, f32[2,2]{1,0:T(2,128)S(1)} %copy-done.2, ...), custom_call_target="tpu_custom_call" | custom-call | flops 1 | bytes 1 | tf_op jit(solution)/shard_map/pallas_call | solution.py:382
  10.6 0.0 collective-permute-done.1.x.e_in.x_first
  10.6 0.7 %collective-permute-start.2 = (f32[2,264,128]{2,1,0:T(8,128)S(1)}, f32[2,264,128]{2,1,0:T(8,128)S(1)}, u32[]{:S(2)}, u32[]{:S(2)}) collective-permute-start(f32[2,264,128]{2,1,0:T(8,128)S(1)} %shard_map.65), channel_id=1, source_target_pairs={{0,1},{8,9},{16,17},{24,25},{1,0},{9,8},{17,16},{25,24}} | collective-permute-start | bytes 811016 | tf_op jit(solution)/shard_map/ppermute | solution.py:434
  11.3 0.7 %shard_map.63 = (bf16[4,256,256]{2,1,0:T(8,128)(2,1)S(1)}, f32[2,264,128]{2,1,0:T(8,128)S(1)}, f32[4,264,128]{2,1,0:T(8,128)S(1)}, f32[2,256,256]{2,1,0:T(8,128)S(1)}) custom-call(s32[2]{0:T(128)S(1)} %copy-done.3, f32[2,2,2,256,256]{4,3,2,1,0:T(8,128)S(1)} %copy-done, f32[2,2,2,256,256]{4,3,2,1,0:T(8,128)S(1)} %copy-done.1, f32[2,2]{1,0:T(2,128)S(1)} %copy-done.2, ...), custom_call_target="tpu_custom_call" | custom-call | flops 1 | bytes 1 | tf_op jit(solution)/shard_map/pallas_call | solution.py:382
  12.0 1.3 %shard_map.64 = (bf16[4,256,256]{2,1,0:T(8,128)(2,1)S(1)}, bf16[4,256,256]{2,1,0:T(8,128)(2,1)S(1)}, bf16[4,256,256]{2,1,0:T(8,128)(2,1)S(1)}, bf16[4,256,256]{2,1,0:T(8,128)(2,1)S(1)}, f32[2,256,256]{2,1,0:T(8,128)S(1)}) custom-call(s32[2]{0:T(128)S(1)} %copy-done.3, f32[2,256,256]{2,1,0:T(8,128)S(1)} %get-tuple-element.62.factor, ...), custom_call_target="tpu_custom_call" | custom-call | flops 1 | bytes 1 | tf_op jit(solution)/shard_map/pallas_call | solution.py:382
  13.3 0.0 collective-permute-done.2.e_second.refs_0_
  13.3 0.7 %collective-permute-start.3 = (f32[2,264,128]{2,1,0:T(8,128)S(1)}, f32[2,264,128]{2,1,0:T(8,128)S(1)}, u32[]{:S(2)}, u32[]{:S(2)}) collective-permute-start(f32[2,264,128]{2,1,0:T(8,128)S(1)} %shard_map.67), channel_id=1, source_target_pairs={{1,3},{9,11},{17,19},{25,27}} | collective-permute-start | bytes 811016 | tf_op jit(solution)/shard_map/ppermute | solution.py:448
  14.0 0.7 %collective-permute-start.4 = (f32[2,264,128]{2,1,0:T(8,128)S(1)}, f32[2,264,128]{2,1,0:T(8,128)S(1)}, u32[]{:S(2)}, u32[]{:S(2)}) collective-permute-start(f32[2,264,128]{2,1,0:T(8,128)S(1)} %collective-permute-done.2.e_second.refs_0_), channel_id=1, source_target_pairs={{0,2},{8,10},{16,18},{24,26}} | collective-permute-start | bytes 811016 | tf_op jit(solution)/shard_map/ppermute | solution.py:449
  14.7 6.6 %collective-permute-done.g_in = f32[2,256,256]{2,1,0:T(8,128)S(1)} collective-permute-done((f32[2,256,256]{2,1,0:T(8,128)S(1)}, f32[2,256,256]{2,1,0:T(8,128)S(1)}, u32[]{:S(2)}, u32[]{:S(2)}) %collective-permute-start) | collective-permute-done | bytes 524320 | tf_op jit(solution)/shard_map/ppermute | solution.py:431
  21.3 1.7 %shard_map.66 = (bf16[4,256,256]{2,1,0:T(8,128)(2,1)S(1)}, bf16[4,256,256]{2,1,0:T(8,128)(2,1)S(1)}, f32[2,264,128]{2,1,0:T(8,128)S(1)}, bf16[4,256,256]{2,1,0:T...) custom-call(f32[2,256,256]{2,1,0:T(8,128)S(1)} %get-tuple-element.64.g, ...), custom_call_target="tpu_custom_call" | custom-call | flops 99999997952 | bytes 1 | tf_op jit(solution)/shard_map/pallas_call | solution.py:382
  23.0 0.0 collective-permute-done.3.refs_0_
  23.0 0.0 collective-permute-done.4.refs_1_
  23.0 0.7 %collective-permute-start.5 = (f32[2,264,128]{2,1,0:T(8,128)S(1)}, f32[2,264,128]{2,1,0:T(8,128)S(1)}, u32[]{:S(2)}, u32[]{:S(2)}) collective-permute-start(f32[2,264,128]{2,1,0:T(8,128)S(1)} %shard_map.68), channel_id=1, source_target_pairs={{3,5},{2,4},{11,13},{10,12},{19,21},{18,20},{27,29},{26,28}} | collective-permute-start | bytes 811016 | tf_op jit(solution)/shard_map/ppermute | solution.py:465
  23.7 0.0 collective-permute-done.5.refs_0_.refs_2_
  23.7 0.2 shard_map.69
  23.9 1.3 %collective-permute-start.6 = (f32[2,264,128]{2,1,0:T(8,128)S(1)}, f32[2,264,128]{2,1,0:T(8,128)S(1)}, u32[]{:S(2)}, u32[]{:S(2)}) collective-permute-start(f32[2,264,128]{2,1,0:T(8,128)S(1)} %shard_map.69), channel_id=1, source_target_pairs={{5,7},{4,6},{13,15},{12,14},{21,23},{20,22},{29,31},{28,30}} | collective-permute-start | bytes 811016 | tf_op jit(solution)/shard_map/ppermute | solution.py:465
  25.2 11.5 %collective-permute-done.6.refs_3_ = f32[2,264,128]{2,1,0:T(8,128)S(1)} collective-permute-done((f32[2,264,128]{2,1,0:T(8,128)S(1)}, f32[2,264,128]{2,1,0:T(8,128)S(1)}, u32[]{:S(2)}, u32[]{:S(2)}) %collective-permute-start.6) | collective-permute-done | bytes 270368 | tf_op jit(solution)/shard_map/ppermute | solution.py:465
  36.7 1.2 %shard_map.70 = (f32[2,264,128]{2,1,0:T(8,128)S(1)}, f32[2,264,128]{2,1,0:T(8,128)S(1)}) custom-call(bf16[4,256,256]{2,1,0:T(8,128)(2,1)S(1)} %get-tuple-element.69.fas, bf16[4,256,256]{2,1,0:T(8,128)(2,1)S(1)} %get-tuple-element.70.fat, f32[2,264,128]{2,1,0:T(8,128)S(1)} %get-tuple-element.71.ea, f32[2,264,128]{2,1,0:T(8,128)S(1)} %collective-permute-done.3.refs_0_, ...), custom_call_target="tpu_custom_call" | custom-call | flops 1 | bytes 1 | tf_op jit(solution)/shard_map/pallas_call | solution.py:382
  37.9 1.4 %collective-permute-start.7 = (f32[2,264,128]{2,1,0:T(8,128)S(1)}, f32[2,264,128]{2,1,0:T(8,128)S(1)}, u32[]{:S(2)}, u32[]{:S(2)}) collective-permute-start(f32[2,264,128]{2,1,0:T(8,128)S(1)} %get-tuple-element.77), channel_id=1, source_target_pairs={{0,1},{1,0},{2,3},{3,2},{4,5},{5,4},{6,7},{7,6},{8,9},{9,8},{10,11... | collective-permute-start | bytes 811016 | tf_op jit(solution)/shard_map/ppermute | solution.py:474
  39.4 2.0 %shard_map.71 = (f32[2,512,128]{2,1,0:T(8,128)S(1)}, f32[2,264,128]{2,1,0:T(8,128)S(1)}) custom-call(f32[2,2]{1,0:T(2,128)S(1)} %copy-done.2, f32[2,264,128]{2,1,0:T(8,128)S(1)} %get-tuple-element.81.x, bf16[4,256,256]{2,1,0:T(8,128)(2,1)S(1)} %get-tuple-element.82.f0s, bf16[4,256,256]{2,1,0:T(8,128)(2,1)S(1)} %get-tuple-element.83.f0t, ...), custom_call_target="tpu_custom_call" | custom-call | flops 1 | bytes 1 | tf_op jit(solution)/shard_map/pallas_call | solution.py:382
  41.4 1.9 %collective-permute-done.7.x = f32[2,264,128]{2,1,0:T(8,128)S(1)} collective-permute-done((f32[2,264,128]{2,1,0:T(8,128)S(1)}, f32[2,264,128]{2,1,0:T(8,128)S(1)}, u32[]{:S(2)}, u32[]{:S(2)}) %collective-permute-start.7) | collective-permute-done | bytes 270368 | tf_op jit(solution)/shard_map/ppermute | solution.py:474
  43.3 1.6 %shard_map.72 = (f32[2,512,128]{2,1,0:T(8,128)S(1)}, bf16[4,256,256]{2,1,0:T(8,128)(2,1)S(1)}, bf16[4,256,256]{2,1,0:T(8,128)(2,1)S(1)}) custom-call(f32[2,2]{1,0:T(2,128)S(1)} %copy-done.2, f32[2,264,128]{2,1,0:T(8,128)S(1)} %collective-permute-done.7.x, f32[2,264,128]{2,1,0:T(8,128)S(1)} %collective-permute-done.1.x.e_in.x_first, ...), custom_call_target="tpu_custom_call" | custom-call | flops 1 | bytes 1 | tf_op jit(solution)/shard_map/pallas_call | solution.py:382
  44.9 7.4 %collective-permute-start.11 = (f32[512,128]{1,0:T(8,128)S(1)}, f32[512,128]{1,0:T(8,128)S(1)}, u32[]{:S(2)}, u32[]{:S(2)}) collective-permute-start(f32[512,128]{1,0:T(8,128)S(1)} %slice_bitcast_fusion), channel_id=1, source_target_pairs={{0,8},{8,0},{16,24},{24,16},{1,9},{9,1},{17,25},{25,17},{2,10},{10... | collective-permute-start | bytes 786440 | tf_op jit(solution)/shard_map/ppermute | solution.py:487
  52.3 0.6 shard_map.73
  52.9 0.1 collective-permute-start.8
  53.0 0.5 collective-permute-done.11
  53.5 0.1 collective-permute-start.12
  53.6 0.8 %collective-permute-done.8 = f32[264,128]{1,0:T(8,128)S(1)} collective-permute-done((f32[264,128]{1,0:T(8,128)S(1)}, f32[264,128]{1,0:T(8,128)S(1)}, u32[]{:S(2)}, u32[]{:S(2)}) %collective-permute-start.8) | collective-permute-done | bytes 135200 | tf_op jit(solution)/shard_map/ppermute | solution.py:487
  54.4 0.8 %collective-permute-start.9 = (f32[264,128]{1,0:T(8,128)S(1)}, f32[264,128]{1,0:T(8,128)S(1)}, u32[]{:S(2)}, u32[]{:S(2)}) collective-permute-start(f32[264,128]{1,0:T(8,128)S(1)} %fusion), channel_id=1, source_target_pairs={{0,16},{8,24},{16,0},{24,8},{1,17},{9,25},{17,1},{25,9},{2,18},{10... | collective-permute-start | bytes 405512 | tf_op jit(solution)/shard_map/ppermute | solution.py:487
  55.1 6.0 %collective-permute-done.12 = f32[512,128]{1,0:T(8,128)S(1)} collective-permute-done((f32[512,128]{1,0:T(8,128)S(1)}, f32[512,128]{1,0:T(8,128)S(1)}, u32[]{:S(2)}, u32[]{:S(2)}) %collective-permute-start.12) | collective-permute-done | bytes 262176 | tf_op jit(solution)/shard_map/ppermute | solution.py:487
  61.1 2.1 %collective-permute-start.13 = (f32[512,128]{1,0:T(8,128)S(1)}, f32[512,128]{1,0:T(8,128)S(1)}, u32[]{:S(2)}, u32[]{:S(2)}) collective-permute-start(f32[512,128]{1,0:T(8,128)S(1)} %add.15.mine), channel_id=1, source_target_pairs={{0,8},{8,0},{16,24},{24,16},{1,9},{9,1},{17,25},{25,17},{2,10},{10... | collective-permute-start | bytes 786440 | tf_op jit(solution)/shard_map/ppermute | solution.py:487
  63.2 0.8 %collective-permute-done.9 = f32[264,128]{1,0:T(8,128)S(1)} collective-permute-done((f32[264,128]{1,0:T(8,128)S(1)}, f32[264,128]{1,0:T(8,128)S(1)}, u32[]{:S(2)}, u32[]{:S(2)}) %collective-permute-start.9) | collective-permute-done | bytes 135200 | tf_op jit(solution)/shard_map/ppermute | solution.py:487
  64.0 1.3 %collective-permute-start.10 = (f32[264,128]{1,0:T(8,128)S(1)}, f32[264,128]{1,0:T(8,128)S(1)}, u32[]{:S(2)}, u32[]{:S(2)}) collective-permute-start(f32[264,128]{1,0:T(8,128)S(1)} %add.13.mine), channel_id=1, source_target_pairs={{0,8},{8,0},{16,24},{24,16},{1,9},{9,1},{17,25},{25,17},{2,10},{10... | collective-permute-start | bytes 405512 | tf_op jit(solution)/shard_map/ppermute | solution.py:487
  65.3 0.0 collective-permute-done.13.theirs
  65.3 0.8 %shard_map.74 = (f32[2,256,256]{2,1,0:T(8,128)}, f32[8,128]{1,0:T(8,128)S(1)}) custom-call(f32[512,128]{1,0:T(8,128)S(1)} %add.15.mine, f32[512,128]{1,0:T(8,128)S(1)} %collective-permute-done.13.theirs), custom_call_target="tpu_custom_call" | custom-call | flops 1 | bytes 1 | tf_op jit(solution)/shard_map/pallas_call | solution.py:382
  66.1 0.1 collective-permute-done.10.theirs
  66.3 0.9 %shard_map.75 = f32[2,256,256]{2,1,0:T(8,128)} custom-call(f32[264,128]{1,0:T(8,128)S(1)} %add.13.mine, f32[264,128]{1,0:T(8,128)S(1)} %collective-permute-done.10.theirs, f32[8,128]{1,0:T(8,128)S(1)} %get-tuple-element.90._), custom_call_target="tpu_custom_call" | custom-call | flops 1 | bytes 1 | tf_op jit(solution)/shard_map/pallas_call | solution.py:382
  (11 shorter events, 0.2 us)
Async XLA Ops:
  3.3 7.3 %collective-permute-start.1 = (f32[2,264,128]{2,1,0:T(8,128)S(1)}, f32[2,264,128]{2,1,0:T(8,128)S(1)}, u32[]{:S(2)}, u32[]{:S(2)}) collective-permute-start(f32[2,264,128]{2,1,0:T(8,128)S(1)} %get-tuple-element.48.refs_1_), channel_id=1, source_target_pairs={{0,1},{1,0},{2,3},{3,2},{4,5},{5,4},{6,7},{7,6},{8,9},{9,8},{10,11... | collective-permute-start | bytes 811016 | tf_op jit(solution)/shard_map/ppermute | solution.py:426
  4.5 0.7 copy-start.3
  4.5 4.2 %copy-start = (f32[2,2,2,256,256]{4,3,2,1,0:T(8,128)S(1)}, f32[2,2,2,256,256]{4,3,2,1,0:T(8,128)}, u32[]{:S(2)}) copy-start(f32[2,2,2,256,256]{4,3,2,1,0:T(8,128)} %pivot.7) | copy-start | bytes 6291460
  4.5 4.2 %copy-start.1 = (f32[2,2,2,256,256]{4,3,2,1,0:T(8,128)S(1)}, f32[2,2,2,256,256]{4,3,2,1,0:T(8,128)}, u32[]{:S(2)}) copy-start(f32[2,2,2,256,256]{4,3,2,1,0:T(8,128)} %factor.7) | copy-start | bytes 6291460
  4.5 4.2 %copy-start.2 = (f32[2,2]{1,0:T(2,128)S(1)}, f32[2,2]{1,0:T(2,128)}, u32[]{:S(2)}) copy-start(f32[2,2]{1,0:T(2,128)} %weight.11) | copy-start | bytes 52
  6.5 14.8 %collective-permute-start = (f32[2,256,256]{2,1,0:T(8,128)S(1)}, f32[2,256,256]{2,1,0:T(8,128)S(1)}, u32[]{:S(2)}, u32[]{:S(2)}) collective-permute-start(f32[2,256,256]{2,1,0:T(8,128)S(1)} %get-tuple-element.53._), channel_id=1, source_target_pairs={{2,3},{3,2},{4,5},{5,4},{6,7},{7,6},{10,11},{11,10},{12,13},{13,12... | collective-permute-start | bytes 1572872 | tf_op jit(solution)/shard_map/ppermute | solution.py:431
  10.6 2.7 %collective-permute-start.2 = (f32[2,264,128]{2,1,0:T(8,128)S(1)}, f32[2,264,128]{2,1,0:T(8,128)S(1)}, u32[]{:S(2)}, u32[]{:S(2)}) collective-permute-start(f32[2,264,128]{2,1,0:T(8,128)S(1)} %shard_map.65), channel_id=1, source_target_pairs={{0,1},{8,9},{16,17},{24,25},{1,0},{9,8},{17,16},{25,24}} | collective-permute-start | bytes 811016 | tf_op jit(solution)/shard_map/ppermute | solution.py:434
  13.3 9.7 %collective-permute-start.3 = (f32[2,264,128]{2,1,0:T(8,128)S(1)}, f32[2,264,128]{2,1,0:T(8,128)S(1)}, u32[]{:S(2)}, u32[]{:S(2)}) collective-permute-start(f32[2,264,128]{2,1,0:T(8,128)S(1)} %shard_map.67), channel_id=1, source_target_pairs={{1,3},{9,11},{17,19},{25,27}} | collective-permute-start | bytes 811016 | tf_op jit(solution)/shard_map/ppermute | solution.py:448
  14.0 9.0 %collective-permute-start.4 = (f32[2,264,128]{2,1,0:T(8,128)S(1)}, f32[2,264,128]{2,1,0:T(8,128)S(1)}, u32[]{:S(2)}, u32[]{:S(2)}) collective-permute-start(f32[2,264,128]{2,1,0:T(8,128)S(1)} %collective-permute-done.2.e_second.refs_0_), channel_id=1, source_target_pairs={{0,2},{8,10},{16,18},{24,26}} | collective-permute-start | bytes 811016 | tf_op jit(solution)/shard_map/ppermute | solution.py:449
  23.0 0.7 %collective-permute-start.5 = (f32[2,264,128]{2,1,0:T(8,128)S(1)}, f32[2,264,128]{2,1,0:T(8,128)S(1)}, u32[]{:S(2)}, u32[]{:S(2)}) collective-permute-start(f32[2,264,128]{2,1,0:T(8,128)S(1)} %shard_map.68), channel_id=1, source_target_pairs={{3,5},{2,4},{11,13},{10,12},{19,21},{18,20},{27,29},{26,28}} | collective-permute-start | bytes 811016 | tf_op jit(solution)/shard_map/ppermute | solution.py:465
  23.9 12.8 %collective-permute-start.6 = (f32[2,264,128]{2,1,0:T(8,128)S(1)}, f32[2,264,128]{2,1,0:T(8,128)S(1)}, u32[]{:S(2)}, u32[]{:S(2)}) collective-permute-start(f32[2,264,128]{2,1,0:T(8,128)S(1)} %shard_map.69), channel_id=1, source_target_pairs={{5,7},{4,6},{13,15},{12,14},{21,23},{20,22},{29,31},{28,30}} | collective-permute-start | bytes 811016 | tf_op jit(solution)/shard_map/ppermute | solution.py:465
  37.9 5.4 %collective-permute-start.7 = (f32[2,264,128]{2,1,0:T(8,128)S(1)}, f32[2,264,128]{2,1,0:T(8,128)S(1)}, u32[]{:S(2)}, u32[]{:S(2)}) collective-permute-start(f32[2,264,128]{2,1,0:T(8,128)S(1)} %get-tuple-element.77), channel_id=1, source_target_pairs={{0,1},{1,0},{2,3},{3,2},{4,5},{5,4},{6,7},{7,6},{8,9},{9,8},{10,11... | collective-permute-start | bytes 811016 | tf_op jit(solution)/shard_map/ppermute | solution.py:474
  44.9 8.6 %collective-permute-start.11 = (f32[512,128]{1,0:T(8,128)S(1)}, f32[512,128]{1,0:T(8,128)S(1)}, u32[]{:S(2)}, u32[]{:S(2)}) collective-permute-start(f32[512,128]{1,0:T(8,128)S(1)} %slice_bitcast_fusion), channel_id=1, source_target_pairs={{0,8},{8,0},{16,24},{24,16},{1,9},{9,1},{17,25},{25,17},{2,10},{10... | collective-permute-start | bytes 786440 | tf_op jit(solution)/shard_map/ppermute | solution.py:487
  52.9 1.4 %collective-permute-start.8 = (f32[264,128]{1,0:T(8,128)S(1)}, f32[264,128]{1,0:T(8,128)S(1)}, u32[]{:S(2)}, u32[]{:S(2)}) collective-permute-start(f32[264,128]{1,0:T(8,128)S(1)} %slice_bitcast_fusion.1), channel_id=1, source_target_pairs={{0,8},{8,0},{16,24},{24,16},{1,9},{9,1},{17,25},{25,17},{2,10},{10... | collective-permute-start | bytes 405512 | tf_op jit(solution)/shard_map/ppermute | solution.py:487
  53.5 7.6 %collective-permute-start.12 = (f32[512,128]{1,0:T(8,128)S(1)}, f32[512,128]{1,0:T(8,128)S(1)}, u32[]{:S(2)}, u32[]{:S(2)}) collective-permute-start(f32[512,128]{1,0:T(8,128)S(1)} %bitcast_add_fusion), channel_id=1, source_target_pairs={{0,16},{8,24},{16,0},{24,8},{1,17},{9,25},{17,1},{25,9},{2,18},{10... | collective-permute-start | bytes 786440 | tf_op jit(solution)/shard_map/ppermute | solution.py:487
  54.4 9.6 %collective-permute-start.9 = (f32[264,128]{1,0:T(8,128)S(1)}, f32[264,128]{1,0:T(8,128)S(1)}, u32[]{:S(2)}, u32[]{:S(2)}) collective-permute-start(f32[264,128]{1,0:T(8,128)S(1)} %fusion), channel_id=1, source_target_pairs={{0,16},{8,24},{16,0},{24,8},{1,17},{9,25},{17,1},{25,9},{2,18},{10... | collective-permute-start | bytes 405512 | tf_op jit(solution)/shard_map/ppermute | solution.py:487
  61.1 4.2 %collective-permute-start.13 = (f32[512,128]{1,0:T(8,128)S(1)}, f32[512,128]{1,0:T(8,128)S(1)}, u32[]{:S(2)}, u32[]{:S(2)}) collective-permute-start(f32[512,128]{1,0:T(8,128)S(1)} %add.15.mine), channel_id=1, source_target_pairs={{0,8},{8,0},{16,24},{24,16},{1,9},{9,1},{17,25},{25,17},{2,10},{10... | collective-permute-start | bytes 786440 | tf_op jit(solution)/shard_map/ppermute | solution.py:487
  64.0 2.3 %collective-permute-start.10 = (f32[264,128]{1,0:T(8,128)S(1)}, f32[264,128]{1,0:T(8,128)S(1)}, u32[]{:S(2)}, u32[]{:S(2)}) collective-permute-start(f32[264,128]{1,0:T(8,128)S(1)} %add.13.mine), channel_id=1, source_target_pairs={{0,8},{8,0},{16,24},{24,16},{1,9},{9,1},{17,25},{25,17},{2,10},{10... | collective-permute-start | bytes 405512 | tf_op jit(solution)/shard_map/ppermute | solution.py:487

commit v12 on v11

--- a/solution.py
+++ b/solution.py
@@ -304,17 +304,24 @@
     return dot3(left[0], left[2], right[0], right[2]) + dot3(left[1], left[3], right[1], right[3])
 
 
-def off_values(slot, weight, xs, f0s, f0t, gs, weighted):
-    width = f0s.shape[-1]
-    w0, w1 = weight[pl.ds(slot, 1), 0:1], weight[pl.ds(slot, 1), 1:2]
+def weights_of(wave_slot, weight):
+    return weight[pl.ds(wave_slot, 1), 0:1], weight[pl.ds(wave_slot, 1), 1:2]
+
+
+def first_off(weights, xs, f0s):
+    w0, w1 = weights
+    pr, pi = wide_dot(xs, load4(f0s))
+    u = w1 * pr + w0 * pi
+    return -flat(u), split_pair(u, w0 * pr - w1 * pi)
+
+
+def second_off(weights, xs, f0t, gs, weighted):
+    width = f0t.shape[-1]
+    w0, w1 = weights
     qr, qi = wide_dot(xs, load4(gs))
     ts = split_pair(w1 * qr + w0 * qi, w0 * qr - w1 * qi)
-    second = real_dot(load4(f0t), ts)
-    pr, pi = wide_dot(xs, load4(f0s))
-    u = w1 * pr + w0 * pi
-    us = split_pair(u, w0 * pr - w1 * pi)
     constant = jnp.concatenate([weighted[2], weighted[3, : width - 8]], axis=0)
-    return -flat(u), -(flat(second) + constant), us, ts
+    return -(flat(real_dot(load4(f0t), ts)) + constant), ts
 
 
 def diag_values(us, ts, f0t, gt, weighted):
@@ -326,30 +333,41 @@
 
 def density_kernel(weight, x, f0s, f0t, gs, gt, weighted, off, diag):
     core = whereabouts()[2]
-    first, second, us, ts = off_values(slot_of(True), weight, unpacked_split(x), f0s, f0t, gs, weighted)
+    xs, weights = unpacked_split(x), weights_of(slot_of(True), weight)
+    second, ts = second_off(weights, xs, f0t, gs, weighted)
+    first, us = first_off(weights, xs, f0s)
     off[core], off[1 - core] = first, second
     diag[core], diag[1 - core] = diag_values(us, ts, f0t, gt, weighted)
 
 
-def more_off_kernel(weight, x, x_first, f0s, f0t, gs, weighted, before, off, us_out, ts_out):
+def more_off_kernel(sent, weight, x, x_first, f0s, f0t, gs, weighted, before, out, split):
+    place, _, core = whereabouts()
+    for first in (False, True):
+
+        @pl.when(core == (1 if first == sent else 0))
+        def _():
+            value = [
+                jnp.where(place > 1, x[c], jnp.where(place == 1, x_first[c], 0.0)) for c in range(2)
+            ]
+            xs = split_pair(unpacked(value[0]), unpacked(value[1]))
+            weights = weights_of(slot_of(False), weight)
+            if first:
+                block, parts = first_off(weights, xs, f0s)
+            else:
+                block, parts = second_off(weights, xs, f0t, gs, weighted)
+            out[...] = block + before[1 if sent else 0]
+            store4(split, parts)
+
+
+def more_diag_kernel(kept, sent, f0t, gt, weighted, before, diag):
     core = whereabouts()[2]
-    place = whereabouts()[0]
-    x = [
-        jnp.where(place > 1, x[c], jnp.where(place == 1, x_first[c], 0.0)) for c in range(2)
-    ]
-    xs = split_pair(unpacked(x[0]), unpacked(x[1]))
-    first, second, us, ts = off_values(slot_of(False), weight, xs, f0s, f0t, gs, weighted)
-    off[core] = first + before[core]
-    off[1 - core] = second + before[1 - core]
-    store4(us_out, us)
-    store4(ts_out, ts)
-
-
-def more_diag_kernel(us, ts, f0t, gt, weighted, before, diag):
-    core = whereabouts()[2]
-    first, second = diag_values(load4(us), load4(ts), f0t, gt, weighted)
-    diag[core] = first + before[core]
-    diag[1 - core] = second + before[1 - core]
+    for here, us, ts in ((0, kept, sent), (1, sent, kept)):
+
+        @pl.when(core == here)
+        def _():
+            first, second = diag_values(load4(us), load4(ts), f0t, gt, weighted)
+            diag[here] = first + before[here]
+            diag[1 - here] = second + before[1 - here]
 
 
 def unpack_off_kernel(mine, theirs, off, done):
@@ -476,18 +494,20 @@
     offs = jax.ShapeDtypeStruct((2, 2 * width, width // 2), F32)
     diags = jax.ShapeDtypeStruct((2,) + quarter, F32)
     off, diag = run(density_kernel, [], [weight, own, m_f0s, m_f0t, m_gs, m_gt, m_w], [offs, diags])
-    off, us, ts = run(
-        more_off_kernel,
-        [],
-        [weight, shared, e_in, o_f0s, o_f0t, o_gs, o_w, off],
-        [offs, parts, parts],
+    flat_off = jax.ShapeDtypeStruct(offs.shape[1:], F32)
+    arrays = [weight, shared, e_in, o_f0s, o_f0t, o_gs, o_w, off]
+    off_sent, sent_split = run(
+        functools.partial(more_off_kernel, True), [], arrays, [flat_off, parts]
+    )
+    off_kept, kept_split = run(
+        functools.partial(more_off_kernel, False), [], arrays, [flat_off, parts]
     )
 
     def exchanged(value, distance):
         return lax.ppermute(value, "pole", [(p, p ^ distance) for p in range(poles)])
 
-    def summed(parts):
-        kept = parts[0] + exchanged(parts[1], 1)
+    def summed(kept, sent):
+        kept = kept + exchanged(sent, 1)
         distance = 2
         while distance < poles:
             kept = kept + exchanged(kept, distance)
@@ -495,9 +515,11 @@
         return kept, exchanged(kept, 1)
 
     full = jax.ShapeDtypeStruct((2, width, width), F32)
-    off_sums = summed(off)
-    (diag,) = run(more_diag_kernel, [], [us, ts, o_f0t, o_gt, o_w, diag], [diags])
-    diag_sums = summed(diag)
+    off_sums = summed(off_kept, off_sent)
+    (diag,) = run(
+        more_diag_kernel, [], [kept_split, sent_split, o_f0t, o_gt, o_w, diag], [diags]
+    )
+    diag_sums = summed(diag[0], diag[1])
     done = jax.ShapeDtypeStruct((8, 128), F32)
     density_off, done = run(unpack_off_kernel, [], list(off_sums), [full, done])
     (density_diag,) = run(unpack_diag_kernel, [], [*diag_sums, done], [full])

time: 67.6 us -> 68.4 us (1.012)
    pallas_call x17 -> x18, Pallas kernels: 17 us -> 17.6 us  [run(): pl.pallas_call(kernel, out_shape=shapes, in_specs=[SCALAR] * len(scalars)...]
  transfers between devices with their start and end apart: 14 -> 14, of which waited for: 8 -> 7; matrix products, arithmetic and copies ran while one was open for 0% -> 0% of each run, Pallas kernels for 16% -> 18%
where the time goes in v12:
time: 68.4 us; the launch traced here: 68 us
  waiting for transfers between devices  27.7 us (40%)
  starting transfers between devices  21.1 us (31%)
  Pallas kernels  17.6 us (26%)
  between operations  0.92 us (1%)
    pallas_call x18, Pallas kernels, run(): pl.pallas_call(kernel, out_shape=shapes, in_specs=[SCALAR] * len(scalars)...  17.6 us
    ppermute x6, starting transfers between devices, exchanged(): lax.ppermute(value, 'pole', [(p, p ^ distance) for p in range(poles)])  12.3 us
    ppermute x2, waiting for transfers between devices, local(): arrived = [lax.ppermute(wave, AXES, up)]  11.5 us
    ppermute x6, waiting for transfers between devices, exchanged(): lax.ppermute(value, 'pole', [(p, p ^ distance) for p in range(poles)])  7.73 us
    ppermute x1, waiting for transfers between devices, local(): g_in = lax.ppermute(o_g, AXES, swaps)  6.61 us
    ppermute x1, starting transfers between devices, local(): g_in = lax.ppermute(o_g, AXES, swaps)  2.16 us
    ppermute x2, starting transfers between devices, local(): arrived = [lax.ppermute(wave, AXES, up)]  1.97 us
    ppermute x1, waiting for transfers between devices, local(): shared = lax.ppermute(sent, AXES, every)  1.92 us
  transfers between devices with their start and end apart: 14, of which 7 were waited for; matrix products, arithmetic and copies ran while one was open for 0% of the time, Pallas kernels for 18%

profile of v12, /device:TPU:29, one launch (start us, length us, event | category | flops | bytes accessed | tf_op | source)
XLA Modules:
  0.0 68.0 jit_solution(6743805529009326141)
XLA Ops:
  0.6 2.6 %shard_map.59 = (bf16[4,256,256]{2,1,0:T(8,128)(2,1)S(1)}, f32[2,264,128]{2,1,0:T(8,128)S(1)}, f32[4,264,128]{2,1,0:T(8,128)S(1)}, f32[2,256,256]{2,1,0:T(8,128)...) custom-call(s32[2]{0:T(128)} %live.11, ...), custom_call_target="tpu_custom_call" | custom-call | flops 1 | bytes 1 | tf_op jit(solution)/shard_map/pallas_call | solution.py:400
  3.3 1.3 %collective-permute-start.1 = (f32[2,264,128]{2,1,0:T(8,128)S(1)}, f32[2,264,128]{2,1,0:T(8,128)S(1)}, u32[]{:S(2)}, u32[]{:S(2)}) collective-permute-start(f32[2,264,128]{2,1,0:T(8,128)S(1)} %get-tuple-element.49.refs_1_), channel_id=1, source_target_pairs={{0,1},{1,0},{2,3},{3,2},{4,5},{5,4},{6,7},{7,6},{8,9},{9,8},{10,11... | collective-permute-start | bytes 811016 | tf_op jit(solution)/shard_map/ppermute | solution.py:444
  4.5 0.0 copy-start.3
  4.5 0.2 shard_map.60
  4.7 0.4 copy-done.3
  5.2 1.3 %shard_map.61 = (bf16[4,256,256]{2,1,0:T(8,128)(2,1)S(1)}, bf16[4,256,256]{2,1,0:T(8,128)(2,1)S(1)}, bf16[4,256,256]{2,1,0:T(8,128)(2,1)S(1)}, bf16[4,256,256]{2,1,0:T(8,128)(2,1)S(1)}, f32[2,256,256]{2,1,0:T(8,128)S(1)}) custom-call(s32[2]{0:T(128)S(1)} %copy-done.3, f32[2,256,256]{2,1,0:T(8,128)S(1)} %get-tuple-element.52.factor, ...), custom_call_target="tpu_custom_call" | custom-call | flops 1 | bytes 1 | tf_op jit(solution)/shard_map/pallas_call | solution.py:400
  6.5 2.2 %collective-permute-start = (f32[2,256,256]{2,1,0:T(8,128)S(1)}, f32[2,256,256]{2,1,0:T(8,128)S(1)}, u32[]{:S(2)}, u32[]{:S(2)}) collective-permute-start(f32[2,256,256]{2,1,0:T(8,128)S(1)} %get-tuple-element.54._), channel_id=1, source_target_pairs={{2,3},{3,2},{4,5},{5,4},{6,7},{7,6},{10,11},{11,10},{12,13},{13,12... | collective-permute-start | bytes 1572872 | tf_op jit(solution)/shard_map/ppermute | solution.py:449
  8.7 0.0 copy-done
  8.7 0.0 copy-done.1
  8.7 0.0 copy-done.2
  8.7 1.8 %shard_map.62 = (bf16[4,256,256]{2,1,0:T(8,128)(2,1)S(1)}, f32[2,264,128]{2,1,0:T(8,128)S(1)}, f32[4,264,128]{2,1,0:T(8,128)S(1)}, f32[2,256,256]{2,1,0:T(8,128)S(1)}) custom-call(s32[2]{0:T(128)S(1)} %copy-done.3, f32[2,2,2,256,256]{4,3,2,1,0:T(8,128)S(1)} %copy-done, f32[2,2,2,256,256]{4,3,2,1,0:T(8,128)S(1)} %copy-done.1, f32[2,2]{1,0:T(2,128)S(1)} %copy-done.2, ...), custom_call_target="tpu_custom_call" | custom-call | flops 1 | bytes 1 | tf_op jit(solution)/shard_map/pallas_call | solution.py:400
  10.6 0.0 collective-permute-done.1.x.e_in.x_first
  10.6 0.7 collective-permute-start.2
  11.3 0.7 shard_map.63
  12.0 1.3 %shard_map.64 = (bf16[4,256,256]{2,1,0:T(8,128)(2,1)S(1)}, bf16[4,256,256]{2,1,0:T(8,128)(2,1)S(1)}, bf16[4,256,256]{2,1,0:T(8,128)(2,1)S(1)}, bf16[4,256,256]{2,1,0:T(8,128)(2,1)S(1)}, f32[2,256,256]{2,1,0:T(8,128)S(1)}) custom-call(s32[2]{0:T(128)S(1)} %copy-done.3, f32[2,256,256]{2,1,0:T(8,128)S(1)} %get-tuple-element.63.factor, ...), custom_call_target="tpu_custom_call" | custom-call | flops 1 | bytes 1 | tf_op jit(solution)/shard_map/pallas_call | solution.py:400
  13.3 0.0 collective-permute-done.2.e_second.refs_0_
  13.3 0.7 collective-permute-start.3
  14.0 0.7 collective-permute-start.4
  14.7 6.6 %collective-permute-done.g_in = f32[2,256,256]{2,1,0:T(8,128)S(1)} collective-permute-done((f32[2,256,256]{2,1,0:T(8,128)S(1)}, f32[2,256,256]{2,1,0:T(8,128)S(1)}, u32[]{:S(2)}, u32[]{:S(2)}) %collective-permute-start) | collective-permute-done | bytes 524320 | tf_op jit(solution)/shard_map/ppermute | solution.py:449
  21.3 1.7 %shard_map.66 = (bf16[4,256,256]{2,1,0:T(8,128)(2,1)S(1)}, bf16[4,256,256]{2,1,0:T(8,128)(2,1)S(1)}, f32[2,264,128]{2,1,0:T(8,128)S(1)}, bf16[4,256,256]{2,1,0:T...) custom-call(f32[2,256,256]{2,1,0:T(8,128)S(1)} %get-tuple-element.65.g, ...), custom_call_target="tpu_custom_call" | custom-call | flops 99999997952 | bytes 1 | tf_op jit(solution)/shard_map/pallas_call | solution.py:400
  23.0 0.0 collective-permute-done.3.refs_0_
  23.0 0.0 collective-permute-done.4.refs_1_
  23.0 0.7 collective-permute-start.5
  23.7 0.0 collective-permute-done.5.refs_0_.refs_2_
  23.7 0.2 shard_map.69
  23.9 1.3 %collective-permute-start.6 = (f32[2,264,128]{2,1,0:T(8,128)S(1)}, f32[2,264,128]{2,1,0:T(8,128)S(1)}, u32[]{:S(2)}, u32[]{:S(2)}) collective-permute-start(f32[2,264,128]{2,1,0:T(8,128)S(1)} %shard_map.69), channel_id=1, source_target_pairs={{5,7},{4,6},{13,15},{12,14},{21,23},{20,22},{29,31},{28,30}} | collective-permute-start | bytes 811016 | tf_op jit(solution)/shard_map/ppermute | solution.py:483
  25.2 11.5 %collective-permute-done.6.refs_3_ = f32[2,264,128]{2,1,0:T(8,128)S(1)} collective-permute-done((f32[2,264,128]{2,1,0:T(8,128)S(1)}, f32[2,264,128]{2,1,0:T(8,128)S(1)}, u32[]{:S(2)}, u32[]{:S(2)}) %collective-permute-start.6) | collective-permute-done | bytes 270368 | tf_op jit(solution)/shard_map/ppermute | solution.py:483
  36.7 1.2 %shard_map.70 = (f32[2,264,128]{2,1,0:T(8,128)S(1)}, f32[2,264,128]{2,1,0:T(8,128)S(1)}) custom-call(bf16[4,256,256]{2,1,0:T(8,128)(2,1)S(1)} %get-tuple-element.70.fas, bf16[4,256,256]{2,1,0:T(8,128)(2,1)S(1)} %get-tuple-element.71.fat, f32[2,264,128]{2,1,0:T(8,128)S(1)} %get-tuple-element.72.ea, f32[2,264,128]{2,1,0:T(8,128)S(1)} %collective-permute-done.3.refs_0_, ...), custom_call_target="tpu_custom_call" | custom-call | flops 1 | bytes 1 | tf_op jit(solution)/shard_map/pallas_call | solution.py:400
  37.9 1.4 %collective-permute-start.7 = (f32[2,264,128]{2,1,0:T(8,128)S(1)}, f32[2,264,128]{2,1,0:T(8,128)S(1)}, u32[]{:S(2)}, u32[]{:S(2)}) collective-permute-start(f32[2,264,128]{2,1,0:T(8,128)S(1)} %get-tuple-element.78), channel_id=1, source_target_pairs={{0,1},{1,0},{2,3},{3,2},{4,5},{5,4},{6,7},{7,6},{8,9},{9,8},{10,11... | collective-permute-start | bytes 811016 | tf_op jit(solution)/shard_map/ppermute | solution.py:492
  39.3 2.0 %shard_map.71 = (f32[2,512,128]{2,1,0:T(8,128)S(1)}, f32[2,264,128]{2,1,0:T(8,128)S(1)}) custom-call(f32[2,2]{1,0:T(2,128)S(1)} %copy-done.2, f32[2,264,128]{2,1,0:T(8,128)S(1)} %get-tuple-element.82.x, bf16[4,256,256]{2,1,0:T(8,128)(2,1)S(1)} %get-tuple-element.83.f0s, bf16[4,256,256]{2,1,0:T(8,128)(2,1)S(1)} %get-tuple-element.84.f0t, ...), custom_call_target="tpu_custom_call" | custom-call | flops 1 | bytes 1 | tf_op jit(solution)/shard_map/pallas_call | solution.py:400
  41.4 1.9 %collective-permute-done.7.x = f32[2,264,128]{2,1,0:T(8,128)S(1)} collective-permute-done((f32[2,264,128]{2,1,0:T(8,128)S(1)}, f32[2,264,128]{2,1,0:T(8,128)S(1)}, u32[]{:S(2)}, u32[]{:S(2)}) %collective-permute-start.7) | collective-permute-done | bytes 270368 | tf_op jit(solution)/shard_map/ppermute | solution.py:492
  43.3 0.7 %shard_map.73 = (f32[512,128]{1,0:T(8,128)S(1)}, bf16[4,256,256]{2,1,0:T(8,128)(2,1)S(1)}) custom-call(f32[2,2]{1,0:T(2,128)S(1)} %copy-done.2, f32[2,264,128]{2,1,0:T(8,128)S(1)} %collective-permute-done.7.x, f32[2,264,128]{2,1,0:T(8,128)S(1)} %collective-permute-done.1.x.e_in.x_first, bf16[4,256,256]{2,1,0:T(8,128)(2,1)S(1)} %get-tuple-element.79.f0s, ...), custom_call_target="tpu_custom_call" | custom-call | flops 1 | bytes 1 | tf_op jit(solution)/shard_map/pallas_call | solution.py:400
  44.0 8.1 %collective-permute-start.11 = (f32[512,128]{1,0:T(8,128)S(1)}, f32[512,128]{1,0:T(8,128)S(1)}, u32[]{:S(2)}, u32[]{:S(2)}) collective-permute-start(f32[512,128]{1,0:T(8,128)S(1)} %get-tuple-element.91), channel_id=1, source_target_pairs={{0,8},{8,0},{16,24},{24,16},{1,9},{9,1},{17,25},{25,17},{2,10},{10... | collective-permute-start | bytes 786440 | tf_op jit(solution)/shard_map/ppermute | solution.py:507
  52.1 1.4 %shard_map.72 = (f32[512,128]{1,0:T(8,128)S(1)}, bf16[4,256,256]{2,1,0:T(8,128)(2,1)S(1)}) custom-call(f32[2,2]{1,0:T(2,128)S(1)} %copy-done.2, f32[2,264,128]{2,1,0:T(8,128)S(1)} %collective-permute-done.7.x, f32[2,264,128]{2,1,0:T(8,128)S(1)} %collective-permute-done.1.x.e_in.x_first, bf16[4,256,256]{2,1,0:T(8,128)(2,1)S(1)} %get-tuple-element.79.f0s, ...), custom_call_target="tpu_custom_call" | custom-call | flops 1 | bytes 1 | tf_op jit(solution)/shard_map/pallas_call | solution.py:400
  53.5 0.6 shard_map.74
  54.1 0.1 collective-permute-start.8
  54.2 0.0 collective-permute-done.11
  54.3 0.1 collective-permute-start.12
  54.3 1.2 %collective-permute-done.8 = f32[264,128]{1,0:T(8,128)S(1)} collective-permute-done((f32[264,128]{1,0:T(8,128)S(1)}, f32[264,128]{1,0:T(8,128)S(1)}, u32[]{:S(2)}, u32[]{:S(2)}) %collective-permute-start.8) | collective-permute-done | bytes 135200 | tf_op jit(solution)/shard_map/ppermute | solution.py:507
  55.6 0.3 collective-permute-start.9
  55.9 5.8 %collective-permute-done.12 = f32[512,128]{1,0:T(8,128)S(1)} collective-permute-done((f32[512,128]{1,0:T(8,128)S(1)}, f32[512,128]{1,0:T(8,128)S(1)}, u32[]{:S(2)}, u32[]{:S(2)}) %collective-permute-start.12) | collective-permute-done | bytes 262176 | tf_op jit(solution)/shard_map/ppermute | solution.py:507
  61.8 2.3 %collective-permute-start.13 = (f32[512,128]{1,0:T(8,128)S(1)}, f32[512,128]{1,0:T(8,128)S(1)}, u32[]{:S(2)}, u32[]{:S(2)}) collective-permute-start(f32[512,128]{1,0:T(8,128)S(1)} %add.15.mine), channel_id=1, source_target_pairs={{0,8},{8,0},{16,24},{24,16},{1,9},{9,1},{17,25},{25,17},{2,10},{10... | collective-permute-start | bytes 786440 | tf_op jit(solution)/shard_map/ppermute | solution.py:507
  64.1 0.5 collective-permute-done.9
  64.6 1.4 %collective-permute-start.10 = (f32[264,128]{1,0:T(8,128)S(1)}, f32[264,128]{1,0:T(8,128)S(1)}, u32[]{:S(2)}, u32[]{:S(2)}) collective-permute-start(f32[264,128]{1,0:T(8,128)S(1)} %add.13.mine), channel_id=1, source_target_pairs={{0,8},{8,0},{16,24},{24,16},{1,9},{9,1},{17,25},{25,17},{2,10},{10... | collective-permute-start | bytes 405512 | tf_op jit(solution)/shard_map/ppermute | solution.py:507
  66.0 0.0 collective-permute-done.13.theirs
  66.0 0.8 %shard_map.75 = (f32[2,256,256]{2,1,0:T(8,128)}, f32[8,128]{1,0:T(8,128)S(1)}) custom-call(f32[512,128]{1,0:T(8,128)S(1)} %add.15.mine, f32[512,128]{1,0:T(8,128)S(1)} %collective-permute-done.13.theirs), custom_call_target="tpu_custom_call" | custom-call | flops 1 | bytes 1 | tf_op jit(solution)/shard_map/pallas_call | solution.py:400
  66.9 0.1 collective-permute-done.10.theirs
  67.0 0.9 %shard_map.76 = f32[2,256,256]{2,1,0:T(8,128)} custom-call(f32[264,128]{1,0:T(8,128)S(1)} %add.13.mine, f32[264,128]{1,0:T(8,128)S(1)} %collective-permute-done.10.theirs, f32[8,128]{1,0:T(8,128)S(1)} %get-tuple-element.92._), custom_call_target="tpu_custom_call" | custom-call | flops 1 | bytes 1 | tf_op jit(solution)/shard_map/pallas_call | solution.py:400
  (11 shorter events, 0.2 us)
Async XLA Ops:
  3.3 7.3 %collective-permute-start.1 = (f32[2,264,128]{2,1,0:T(8,128)S(1)}, f32[2,264,128]{2,1,0:T(8,128)S(1)}, u32[]{:S(2)}, u32[]{:S(2)}) collective-permute-start(f32[2,264,128]{2,1,0:T(8,128)S(1)} %get-tuple-element.49.refs_1_), channel_id=1, source_target_pairs={{0,1},{1,0},{2,3},{3,2},{4,5},{5,4},{6,7},{7,6},{8,9},{9,8},{10,11... | collective-permute-start | bytes 811016 | tf_op jit(solution)/shard_map/ppermute | solution.py:444
  4.5 0.7 copy-start.3
  4.5 4.2 %copy-start = (f32[2,2,2,256,256]{4,3,2,1,0:T(8,128)S(1)}, f32[2,2,2,256,256]{4,3,2,1,0:T(8,128)}, u32[]{:S(2)}) copy-start(f32[2,2,2,256,256]{4,3,2,1,0:T(8,128)} %pivot.7) | copy-start | bytes 6291460
  4.5 4.2 %copy-start.1 = (f32[2,2,2,256,256]{4,3,2,1,0:T(8,128)S(1)}, f32[2,2,2,256,256]{4,3,2,1,0:T(8,128)}, u32[]{:S(2)}) copy-start(f32[2,2,2,256,256]{4,3,2,1,0:T(8,128)} %factor.7) | copy-start | bytes 6291460
  4.5 4.2 %copy-start.2 = (f32[2,2]{1,0:T(2,128)S(1)}, f32[2,2]{1,0:T(2,128)}, u32[]{:S(2)}) copy-start(f32[2,2]{1,0:T(2,128)} %weight.13) | copy-start | bytes 52
  6.5 14.8 %collective-permute-start = (f32[2,256,256]{2,1,0:T(8,128)S(1)}, f32[2,256,256]{2,1,0:T(8,128)S(1)}, u32[]{:S(2)}, u32[]{:S(2)}) collective-permute-start(f32[2,256,256]{2,1,0:T(8,128)S(1)} %get-tuple-element.54._), channel_id=1, source_target_pairs={{2,3},{3,2},{4,5},{5,4},{6,7},{7,6},{10,11},{11,10},{12,13},{13,12... | collective-permute-start | bytes 1572872 | tf_op jit(solution)/shard_map/ppermute | solution.py:449
  10.6 2.7 %collective-permute-start.2 = (f32[2,264,128]{2,1,0:T(8,128)S(1)}, f32[2,264,128]{2,1,0:T(8,128)S(1)}, u32[]{:S(2)}, u32[]{:S(2)}) collective-permute-start(f32[2,264,128]{2,1,0:T(8,128)S(1)} %shard_map.65), channel_id=1, source_target_pairs={{0,1},{8,9},{16,17},{24,25},{1,0},{9,8},{17,16},{25,24}} | collective-permute-start | bytes 811016 | tf_op jit(solution)/shard_map/ppermute | solution.py:452
  13.3 9.7 %collective-permute-start.3 = (f32[2,264,128]{2,1,0:T(8,128)S(1)}, f32[2,264,128]{2,1,0:T(8,128)S(1)}, u32[]{:S(2)}, u32[]{:S(2)}) collective-permute-start(f32[2,264,128]{2,1,0:T(8,128)S(1)} %shard_map.67), channel_id=1, source_target_pairs={{1,3},{9,11},{17,19},{25,27}} | collective-permute-start | bytes 811016 | tf_op jit(solution)/shard_map/ppermute | solution.py:466
  14.0 9.0 %collective-permute-start.4 = (f32[2,264,128]{2,1,0:T(8,128)S(1)}, f32[2,264,128]{2,1,0:T(8,128)S(1)}, u32[]{:S(2)}, u32[]{:S(2)}) collective-permute-start(f32[2,264,128]{2,1,0:T(8,128)S(1)} %collective-permute-done.2.e_second.refs_0_), channel_id=1, source_target_pairs={{0,2},{8,10},{16,18},{24,26}} | collective-permute-start | bytes 811016 | tf_op jit(solution)/shard_map/ppermute | solution.py:467
  23.0 0.7 %collective-permute-start.5 = (f32[2,264,128]{2,1,0:T(8,128)S(1)}, f32[2,264,128]{2,1,0:T(8,128)S(1)}, u32[]{:S(2)}, u32[]{:S(2)}) collective-permute-start(f32[2,264,128]{2,1,0:T(8,128)S(1)} %shard_map.68), channel_id=1, source_target_pairs={{3,5},{2,4},{11,13},{10,12},{19,21},{18,20},{27,29},{26,28}} | collective-permute-start | bytes 811016 | tf_op jit(solution)/shard_map/ppermute | solution.py:483
  23.9 12.8 %collective-permute-start.6 = (f32[2,264,128]{2,1,0:T(8,128)S(1)}, f32[2,264,128]{2,1,0:T(8,128)S(1)}, u32[]{:S(2)}, u32[]{:S(2)}) collective-permute-start(f32[2,264,128]{2,1,0:T(8,128)S(1)} %shard_map.69), channel_id=1, source_target_pairs={{5,7},{4,6},{13,15},{12,14},{21,23},{20,22},{29,31},{28,30}} | collective-permute-start | bytes 811016 | tf_op jit(solution)/shard_map/ppermute | solution.py:483
  37.9 5.4 %collective-permute-start.7 = (f32[2,264,128]{2,1,0:T(8,128)S(1)}, f32[2,264,128]{2,1,0:T(8,128)S(1)}, u32[]{:S(2)}, u32[]{:S(2)}) collective-permute-start(f32[2,264,128]{2,1,0:T(8,128)S(1)} %get-tuple-element.78), channel_id=1, source_target_pairs={{0,1},{1,0},{2,3},{3,2},{4,5},{5,4},{6,7},{7,6},{8,9},{9,8},{10,11... | collective-permute-start | bytes 811016 | tf_op jit(solution)/shard_map/ppermute | solution.py:492
  44.0 10.2 %collective-permute-start.11 = (f32[512,128]{1,0:T(8,128)S(1)}, f32[512,128]{1,0:T(8,128)S(1)}, u32[]{:S(2)}, u32[]{:S(2)}) collective-permute-start(f32[512,128]{1,0:T(8,128)S(1)} %get-tuple-element.91), channel_id=1, source_target_pairs={{0,8},{8,0},{16,24},{24,16},{1,9},{9,1},{17,25},{25,17},{2,10},{10... | collective-permute-start | bytes 786440 | tf_op jit(solution)/shard_map/ppermute | solution.py:507
  54.1 1.4 %collective-permute-start.8 = (f32[264,128]{1,0:T(8,128)S(1)}, f32[264,128]{1,0:T(8,128)S(1)}, u32[]{:S(2)}, u32[]{:S(2)}) collective-permute-start(f32[264,128]{1,0:T(8,128)S(1)} %slice_bitcast_fusion), channel_id=1, source_target_pairs={{0,8},{8,0},{16,24},{24,16},{1,9},{9,1},{17,25},{25,17},{2,10},{10... | collective-permute-start | bytes 405512 | tf_op jit(solution)/shard_map/ppermute | solution.py:507
  54.3 7.5 %collective-permute-start.12 = (f32[512,128]{1,0:T(8,128)S(1)}, f32[512,128]{1,0:T(8,128)S(1)}, u32[]{:S(2)}, u32[]{:S(2)}) collective-permute-start(f32[512,128]{1,0:T(8,128)S(1)} %add.14), channel_id=1, source_target_pairs={{0,16},{8,24},{16,0},{24,8},{1,17},{9,25},{17,1},{25,9},{2,18},{10... | collective-permute-start | bytes 786440 | tf_op jit(solution)/shard_map/ppermute | solution.py:507
  55.6 9.0 %collective-permute-start.9 = (f32[264,128]{1,0:T(8,128)S(1)}, f32[264,128]{1,0:T(8,128)S(1)}, u32[]{:S(2)}, u32[]{:S(2)}) collective-permute-start(f32[264,128]{1,0:T(8,128)S(1)} %fusion), channel_id=1, source_target_pairs={{0,16},{8,24},{16,0},{24,8},{1,17},{9,25},{17,1},{25,9},{2,18},{10... | collective-permute-start | bytes 405512 | tf_op jit(solution)/shard_map/ppermute | solution.py:507
  61.8 4.3 %collective-permute-start.13 = (f32[512,128]{1,0:T(8,128)S(1)}, f32[512,128]{1,0:T(8,128)S(1)}, u32[]{:S(2)}, u32[]{:S(2)}) collective-permute-start(f32[512,128]{1,0:T(8,128)S(1)} %add.15.mine), channel_id=1, source_target_pairs={{0,8},{8,0},{16,24},{24,16},{1,9},{9,1},{17,25},{25,17},{2,10},{10... | collective-permute-start | bytes 786440 | tf_op jit(solution)/shard_map/ppermute | solution.py:507
  64.6 2.4 %collective-permute-start.10 = (f32[264,128]{1,0:T(8,128)S(1)}, f32[264,128]{1,0:T(8,128)S(1)}, u32[]{:S(2)}, u32[]{:S(2)}) collective-permute-start(f32[264,128]{1,0:T(8,128)S(1)} %add.13.mine), channel_id=1, source_target_pairs={{0,8},{8,0},{16,24},{24,16},{1,9},{9,1},{17,25},{25,17},{2,10},{10... | collective-permute-start | bytes 405512 | tf_op jit(solution)/shard_map/ppermute | solution.py:507

commit v13 on v11

--- a/solution.py
+++ b/solution.py
@@ -134,19 +134,21 @@
     weighted[3, : width - 8] = weighted_b[width + 8 :]
 
 
-def fetched_constants(slot, live, pivot, factor, weight, outs, scratch):
+def fetches(slot, live, pivot, factor, weight, outs, scratch):
     blocks, link, widths, weights, sems = scratch
-    first_factor = pltpu.make_async_copy(factor.at[slot, 0], outs[3], sems.at[5])
-    copies = [
+    return [
         pltpu.make_async_copy(live, widths, sems.at[0]),
         pltpu.make_async_copy(factor.at[slot, 1], link, sems.at[1]),
         pltpu.make_async_copy(pivot.at[slot, 0], blocks.at[0], sems.at[2]),
         pltpu.make_async_copy(pivot.at[slot, 1], blocks.at[1], sems.at[3]),
         pltpu.make_async_copy(weight, weights, sems.at[4]),
+        pltpu.make_async_copy(factor.at[slot, 0], outs[3], sems.at[5]),
     ]
-    for copy in copies:
-        copy.start()
-    first_factor.start()
+
+
+def fetched_constants(slot, live, pivot, factor, weight, outs, scratch):
+    blocks, link, widths, weights, _ = scratch
+    copies = fetches(slot, live, pivot, factor, weight, outs, scratch)
     copies[0].wait()
     copies[1].wait()
 
@@ -155,20 +157,32 @@
             copy.wait()
 
     constants_of(slot, blocks, link, widths, weights, *outs, wait=wait)
-    first_factor.wait()
 
 
 def sent_constant_kernel(live, pivot, factor, weight, *refs):
-    outs, second, scratch = refs[:4], refs[4:8], refs[8:]
+    outs, second, scratch, second_scratch = refs[:4], refs[4:8], refs[8:13], refs[13:]
     place, _, core = whereabouts()
-
-    @pl.when(jnp.logical_and(place != 1, core == 0))
-    def _():
-        fetched_constants(slot_of(True), live, pivot, factor, weight, second, scratch)
-
-    @pl.when(jnp.logical_or(place != 1, core == 0))
-    def _():
-        fetched_constants(slot_of(False), live, pivot, factor, weight, outs, scratch)
+    makes = jnp.logical_or(place != 1, core == 0)
+    makes_second = jnp.logical_and(place != 1, core == 0)
+    sources = live, pivot, factor, weight
+
+    @pl.when(makes_second)
+    def _():
+        for copy in fetches(slot_of(True), *sources, second, second_scratch):
+            copy.start()
+
+    @pl.when(makes)
+    def _():
+        for copy in fetches(slot_of(False), *sources, outs, scratch):
+            copy.start()
+
+    @pl.when(makes_second)
+    def _():
+        fetched_constants(slot_of(True), *sources, second, second_scratch)
+
+    @pl.when(makes)
+    def _():
+        fetched_constants(slot_of(False), *sources, outs, scratch)
 
 
 def first_constant_kernel(live, pivot, factor, weight, *refs):
@@ -183,6 +197,8 @@
 
     @pl.when(late)
     def _():
+        for copy in fetches(slot_of(False), live, pivot, factor, weight, outs, scratch):
+            copy.start()
         fetched_constants(slot_of(False), live, pivot, factor, weight, outs, scratch)
 
 
@@ -421,7 +437,7 @@
         pltpu.SemaphoreType.DMA((6,)),
     ]
     far = [pltpu.with_memory_space_constraint(a, pltpu.HBM) for a in (live, pivot, factor, weight)]
-    made = run(sent_constant_kernel, [], [], constants * 2, scratch, far=far)
+    made = run(sent_constant_kernel, [], [], constants * 2, scratch * 2, far=far)
     made, second = made[:4], made[4:]
     e_in = lax.ppermute(made[1], AXES, every)
     o_f1s, o_e, o_w, o_f0 = run(first_constant_kernel, [], made, constants, scratch, far=far)

time: 67.6 us -> 68 us (level)
    ppermute x6, starting transfers between devices: 11.7 us -> 10.5 us  [exchanged(): lax.ppermute(value, 'pole', [(p, p ^ distance) for p in range(poles)])]
    ppermute x1, starting transfers between devices: 1.43 us -> 2.51 us  [local(): shared = lax.ppermute(sent, AXES, every)]
where the time goes in v13:
time: 68 us; the launch traced here: 67.2 us
  waiting for transfers between devices  28 us (41%)
  starting transfers between devices  20.5 us (30%)
  Pallas kernels  17.2 us (25%)
  between operations  0.9 us (1%)
    pallas_call x17, Pallas kernels, run(): pl.pallas_call(kernel, out_shape=shapes, in_specs=[SCALAR] * len(scalars)...  17.2 us
    ppermute x2, waiting for transfers between devices, local(): arrived = [lax.ppermute(wave, AXES, up)]  12 us
    ppermute x6, starting transfers between devices, exchanged(): lax.ppermute(value, 'pole', [(p, p ^ distance) for p in range(poles)])  10.5 us
    ppermute x6, waiting for transfers between devices, exchanged(): lax.ppermute(value, 'pole', [(p, p ^ distance) for p in range(poles)])  8.12 us
    ppermute x1, waiting for transfers between devices, local(): g_in = lax.ppermute(o_g, AXES, swaps)  6.02 us
    ppermute x1, starting transfers between devices, local(): shared = lax.ppermute(sent, AXES, every)  2.51 us
    ppermute x1, starting transfers between devices, local(): g_in = lax.ppermute(o_g, AXES, swaps)  2.17 us
    ppermute x2, starting transfers between devices, local(): arrived = [lax.ppermute(wave, AXES, up)]  1.97 us
  transfers between devices with their start and end apart: 14, of which 8 were waited for; matrix products, arithmetic and copies ran while one was open for 0% of the time, Pallas kernels for 16%

profile of v13, /device:TPU:29, one launch (start us, length us, event | category | flops | bytes accessed | tf_op | source)
XLA Modules:
  0.0 67.2 jit_solution(7513344466407435658)
XLA Ops:
  0.6 2.8 %shard_map.59 = (bf16[4,256,256]{2,1,0:T(8,128)(2,1)S(1)}, f32[2,264,128]{2,1,0:T(8,128)S(1)}, f32[4,264,128]{2,1,0:T(8,128)S(1)}, f32[2,256,256]{2,1,0:T(8,128)...) custom-call(s32[2]{0:T(128)} %live.11, ...), custom_call_target="tpu_custom_call" | custom-call | flops 1 | bytes 1 | tf_op jit(solution)/shard_map/pallas_call | solution.py:398
  3.5 1.3 %collective-permute-start.1 = (f32[2,264,128]{2,1,0:T(8,128)S(1)}, f32[2,264,128]{2,1,0:T(8,128)S(1)}, u32[]{:S(2)}, u32[]{:S(2)}) collective-permute-start(f32[2,264,128]{2,1,0:T(8,128)S(1)} %get-tuple-element.48.refs_1_), channel_id=1, source_target_pairs={{0,1},{1,0},{2,3},{3,2},{4,5},{5,4},{6,7},{7,6},{8,9},{9,8},{10,11... | collective-permute-start | bytes 811016 | tf_op jit(solution)/shard_map/ppermute | solution.py:442
  4.7 0.0 copy-start.3
  4.7 0.0 copy-start
  4.8 0.2 shard_map.60
  5.0 0.4 copy-done.3
  5.4 1.3 %shard_map.61 = (bf16[4,256,256]{2,1,0:T(8,128)(2,1)S(1)}, bf16[4,256,256]{2,1,0:T(8,128)(2,1)S(1)}, bf16[4,256,256]{2,1,0:T(8,128)(2,1)S(1)}, bf16[4,256,256]{2,1,0:T(8,128)(2,1)S(1)}, f32[2,256,256]{2,1,0:T(8,128)S(1)}) custom-call(s32[2]{0:T(128)S(1)} %copy-done.3, f32[2,256,256]{2,1,0:T(8,128)S(1)} %get-tuple-element.51.factor, ...), custom_call_target="tpu_custom_call" | custom-call | flops 1 | bytes 1 | tf_op jit(solution)/shard_map/pallas_call | solution.py:398
  6.7 2.2 %collective-permute-start = (f32[2,256,256]{2,1,0:T(8,128)S(1)}, f32[2,256,256]{2,1,0:T(8,128)S(1)}, u32[]{:S(2)}, u32[]{:S(2)}) collective-permute-start(f32[2,256,256]{2,1,0:T(8,128)S(1)} %get-tuple-element.53._), channel_id=1, source_target_pairs={{2,3},{3,2},{4,5},{5,4},{6,7},{7,6},{10,11},{11,10},{12,13},{13,12... | collective-permute-start | bytes 1572872 | tf_op jit(solution)/shard_map/ppermute | solution.py:447
  8.9 0.0 copy-done
  8.9 0.0 copy-done.1
  8.9 0.0 copy-done.2
  8.9 1.8 %shard_map.62 = (bf16[4,256,256]{2,1,0:T(8,128)(2,1)S(1)}, f32[2,264,128]{2,1,0:T(8,128)S(1)}, f32[4,264,128]{2,1,0:T(8,128)S(1)}, f32[2,256,256]{2,1,0:T(8,128)S(1)}) custom-call(s32[2]{0:T(128)S(1)} %copy-done.3, f32[2,2,2,256,256]{4,3,2,1,0:T(8,128)S(1)} %copy-done, f32[2,2,2,256,256]{4,3,2,1,0:T(8,128)S(1)} %copy-done.1, f32[2,2]{1,0:T(2,128)S(1)} %copy-done.2, ...), custom_call_target="tpu_custom_call" | custom-call | flops 1 | bytes 1 | tf_op jit(solution)/shard_map/pallas_call | solution.py:398
  10.8 0.0 collective-permute-done.1.x.e_in.x_first
  10.8 0.7 %collective-permute-start.2 = (f32[2,264,128]{2,1,0:T(8,128)S(1)}, f32[2,264,128]{2,1,0:T(8,128)S(1)}, u32[]{:S(2)}, u32[]{:S(2)}) collective-permute-start(f32[2,264,128]{2,1,0:T(8,128)S(1)} %shard_map.65), channel_id=1, source_target_pairs={{0,1},{8,9},{16,17},{24,25},{1,0},{9,8},{17,16},{25,24}} | collective-permute-start | bytes 811016 | tf_op jit(solution)/shard_map/ppermute | solution.py:450
  11.5 0.7 %shard_map.63 = (bf16[4,256,256]{2,1,0:T(8,128)(2,1)S(1)}, f32[2,264,128]{2,1,0:T(8,128)S(1)}, f32[4,264,128]{2,1,0:T(8,128)S(1)}, f32[2,256,256]{2,1,0:T(8,128)S(1)}) custom-call(s32[2]{0:T(128)S(1)} %copy-done.3, f32[2,2,2,256,256]{4,3,2,1,0:T(8,128)S(1)} %copy-done, f32[2,2,2,256,256]{4,3,2,1,0:T(8,128)S(1)} %copy-done.1, f32[2,2]{1,0:T(2,128)S(1)} %copy-done.2, ...), custom_call_target="tpu_custom_call" | custom-call | flops 1 | bytes 1 | tf_op jit(solution)/shard_map/pallas_call | solution.py:398
  12.2 1.3 %shard_map.64 = (bf16[4,256,256]{2,1,0:T(8,128)(2,1)S(1)}, bf16[4,256,256]{2,1,0:T(8,128)(2,1)S(1)}, bf16[4,256,256]{2,1,0:T(8,128)(2,1)S(1)}, bf16[4,256,256]{2,1,0:T(8,128)(2,1)S(1)}, f32[2,256,256]{2,1,0:T(8,128)S(1)}) custom-call(s32[2]{0:T(128)S(1)} %copy-done.3, f32[2,256,256]{2,1,0:T(8,128)S(1)} %get-tuple-element.62.factor, ...), custom_call_target="tpu_custom_call" | custom-call | flops 1 | bytes 1 | tf_op jit(solution)/shard_map/pallas_call | solution.py:398
  13.5 0.0 collective-permute-done.2.e_second.refs_0_
  13.5 0.7 %collective-permute-start.3 = (f32[2,264,128]{2,1,0:T(8,128)S(1)}, f32[2,264,128]{2,1,0:T(8,128)S(1)}, u32[]{:S(2)}, u32[]{:S(2)}) collective-permute-start(f32[2,264,128]{2,1,0:T(8,128)S(1)} %shard_map.67), channel_id=1, source_target_pairs={{1,3},{9,11},{17,19},{25,27}} | collective-permute-start | bytes 811016 | tf_op jit(solution)/shard_map/ppermute | solution.py:464
  14.2 0.7 %collective-permute-start.4 = (f32[2,264,128]{2,1,0:T(8,128)S(1)}, f32[2,264,128]{2,1,0:T(8,128)S(1)}, u32[]{:S(2)}, u32[]{:S(2)}) collective-permute-start(f32[2,264,128]{2,1,0:T(8,128)S(1)} %collective-permute-done.2.e_second.refs_0_), channel_id=1, source_target_pairs={{0,2},{8,10},{16,18},{24,26}} | collective-permute-start | bytes 811016 | tf_op jit(solution)/shard_map/ppermute | solution.py:465
  14.9 6.0 %collective-permute-done.g_in = f32[2,256,256]{2,1,0:T(8,128)S(1)} collective-permute-done((f32[2,256,256]{2,1,0:T(8,128)S(1)}, f32[2,256,256]{2,1,0:T(8,128)S(1)}, u32[]{:S(2)}, u32[]{:S(2)}) %collective-permute-start) | collective-permute-done | bytes 524320 | tf_op jit(solution)/shard_map/ppermute | solution.py:447
  20.9 1.7 %shard_map.66 = (bf16[4,256,256]{2,1,0:T(8,128)(2,1)S(1)}, bf16[4,256,256]{2,1,0:T(8,128)(2,1)S(1)}, f32[2,264,128]{2,1,0:T(8,128)S(1)}, bf16[4,256,256]{2,1,0:T...) custom-call(f32[2,256,256]{2,1,0:T(8,128)S(1)} %get-tuple-element.64.g, ...), custom_call_target="tpu_custom_call" | custom-call | flops 99999997952 | bytes 1 | tf_op jit(solution)/shard_map/pallas_call | solution.py:398
  22.6 0.0 collective-permute-done.3.refs_0_
  22.6 0.0 collective-permute-done.4.refs_1_
  22.6 0.7 %collective-permute-start.5 = (f32[2,264,128]{2,1,0:T(8,128)S(1)}, f32[2,264,128]{2,1,0:T(8,128)S(1)}, u32[]{:S(2)}, u32[]{:S(2)}) collective-permute-start(f32[2,264,128]{2,1,0:T(8,128)S(1)} %shard_map.68), channel_id=1, source_target_pairs={{3,5},{2,4},{11,13},{10,12},{19,21},{18,20},{27,29},{26,28}} | collective-permute-start | bytes 811016 | tf_op jit(solution)/shard_map/ppermute | solution.py:481
  23.3 0.0 collective-permute-done.5.refs_0_.refs_2_
  23.3 0.2 shard_map.69
  23.5 1.3 %collective-permute-start.6 = (f32[2,264,128]{2,1,0:T(8,128)S(1)}, f32[2,264,128]{2,1,0:T(8,128)S(1)}, u32[]{:S(2)}, u32[]{:S(2)}) collective-permute-start(f32[2,264,128]{2,1,0:T(8,128)S(1)} %shard_map.69), channel_id=1, source_target_pairs={{5,7},{4,6},{13,15},{12,14},{21,23},{20,22},{29,31},{28,30}} | collective-permute-start | bytes 811016 | tf_op jit(solution)/shard_map/ppermute | solution.py:481
  24.8 12.0 %collective-permute-done.6.refs_3_ = f32[2,264,128]{2,1,0:T(8,128)S(1)} collective-permute-done((f32[2,264,128]{2,1,0:T(8,128)S(1)}, f32[2,264,128]{2,1,0:T(8,128)S(1)}, u32[]{:S(2)}, u32[]{:S(2)}) %collective-permute-start.6) | collective-permute-done | bytes 270368 | tf_op jit(solution)/shard_map/ppermute | solution.py:481
  36.8 1.2 %shard_map.70 = (f32[2,264,128]{2,1,0:T(8,128)S(1)}, f32[2,264,128]{2,1,0:T(8,128)S(1)}) custom-call(bf16[4,256,256]{2,1,0:T(8,128)(2,1)S(1)} %get-tuple-element.69.fas, bf16[4,256,256]{2,1,0:T(8,128)(2,1)S(1)} %get-tuple-element.70.fat, f32[2,264,128]{2,1,0:T(8,128)S(1)} %get-tuple-element.71.ea, f32[2,264,128]{2,1,0:T(8,128)S(1)} %collective-permute-done.3.refs_0_, ...), custom_call_target="tpu_custom_call" | custom-call | flops 1 | bytes 1 | tf_op jit(solution)/shard_map/pallas_call | solution.py:398
  38.1 2.5 %collective-permute-start.7 = (f32[2,264,128]{2,1,0:T(8,128)S(1)}, f32[2,264,128]{2,1,0:T(8,128)S(1)}, u32[]{:S(2)}, u32[]{:S(2)}) collective-permute-start(f32[2,264,128]{2,1,0:T(8,128)S(1)} %get-tuple-element.77), channel_id=1, source_target_pairs={{0,1},{1,0},{2,3},{3,2},{4,5},{5,4},{6,7},{7,6},{8,9},{9,8},{10,11... | collective-permute-start | bytes 811016 | tf_op jit(solution)/shard_map/ppermute | solution.py:490
  40.6 2.0 %shard_map.71 = (f32[2,512,128]{2,1,0:T(8,128)S(1)}, f32[2,264,128]{2,1,0:T(8,128)S(1)}) custom-call(f32[2,2]{1,0:T(2,128)S(1)} %copy-done.2, f32[2,264,128]{2,1,0:T(8,128)S(1)} %get-tuple-element.81.x, bf16[4,256,256]{2,1,0:T(8,128)(2,1)S(1)} %get-tuple-element.82.f0s, bf16[4,256,256]{2,1,0:T(8,128)(2,1)S(1)} %get-tuple-element.83.f0t, ...), custom_call_target="tpu_custom_call" | custom-call | flops 1 | bytes 1 | tf_op jit(solution)/shard_map/pallas_call | solution.py:398
  42.6 1.8 %collective-permute-done.7.x = f32[2,264,128]{2,1,0:T(8,128)S(1)} collective-permute-done((f32[2,264,128]{2,1,0:T(8,128)S(1)}, f32[2,264,128]{2,1,0:T(8,128)S(1)}, u32[]{:S(2)}, u32[]{:S(2)}) %collective-permute-start.7) | collective-permute-done | bytes 270368 | tf_op jit(solution)/shard_map/ppermute | solution.py:490
  44.4 1.6 %shard_map.72 = (f32[2,512,128]{2,1,0:T(8,128)S(1)}, bf16[4,256,256]{2,1,0:T(8,128)(2,1)S(1)}, bf16[4,256,256]{2,1,0:T(8,128)(2,1)S(1)}) custom-call(f32[2,2]{1,0:T(2,128)S(1)} %copy-done.2, f32[2,264,128]{2,1,0:T(8,128)S(1)} %collective-permute-done.7.x, f32[2,264,128]{2,1,0:T(8,128)S(1)} %collective-permute-done.1.x.e_in.x_first, ...), custom_call_target="tpu_custom_call" | custom-call | flops 1 | bytes 1 | tf_op jit(solution)/shard_map/pallas_call | solution.py:398
  46.0 6.3 %collective-permute-start.11 = (f32[512,128]{1,0:T(8,128)S(1)}, f32[512,128]{1,0:T(8,128)S(1)}, u32[]{:S(2)}, u32[]{:S(2)}) collective-permute-start(f32[512,128]{1,0:T(8,128)S(1)} %slice_bitcast_fusion), channel_id=1, source_target_pairs={{0,8},{8,0},{16,24},{24,16},{1,9},{9,1},{17,25},{25,17},{2,10},{10... | collective-permute-start | bytes 786440 | tf_op jit(solution)/shard_map/ppermute | solution.py:503
  52.3 0.6 shard_map.73
  52.9 0.1 collective-permute-start.8
  53.0 0.5 collective-permute-done.11
  53.5 0.1 collective-permute-start.12
  53.6 0.8 %collective-permute-done.8 = f32[264,128]{1,0:T(8,128)S(1)} collective-permute-done((f32[264,128]{1,0:T(8,128)S(1)}, f32[264,128]{1,0:T(8,128)S(1)}, u32[]{:S(2)}, u32[]{:S(2)}) %collective-permute-start.8) | collective-permute-done | bytes 135200 | tf_op jit(solution)/shard_map/ppermute | solution.py:503
  54.4 0.8 %collective-permute-start.9 = (f32[264,128]{1,0:T(8,128)S(1)}, f32[264,128]{1,0:T(8,128)S(1)}, u32[]{:S(2)}, u32[]{:S(2)}) collective-permute-start(f32[264,128]{1,0:T(8,128)S(1)} %fusion), channel_id=1, source_target_pairs={{0,16},{8,24},{16,0},{24,8},{1,17},{9,25},{17,1},{25,9},{2,18},{10... | collective-permute-start | bytes 405512 | tf_op jit(solution)/shard_map/ppermute | solution.py:503
  55.1 6.0 %collective-permute-done.12 = f32[512,128]{1,0:T(8,128)S(1)} collective-permute-done((f32[512,128]{1,0:T(8,128)S(1)}, f32[512,128]{1,0:T(8,128)S(1)}, u32[]{:S(2)}, u32[]{:S(2)}) %collective-permute-start.12) | collective-permute-done | bytes 262176 | tf_op jit(solution)/shard_map/ppermute | solution.py:503
  61.1 2.1 %collective-permute-start.13 = (f32[512,128]{1,0:T(8,128)S(1)}, f32[512,128]{1,0:T(8,128)S(1)}, u32[]{:S(2)}, u32[]{:S(2)}) collective-permute-start(f32[512,128]{1,0:T(8,128)S(1)} %add.15.mine), channel_id=1, source_target_pairs={{0,8},{8,0},{16,24},{24,16},{1,9},{9,1},{17,25},{25,17},{2,10},{10... | collective-permute-start | bytes 786440 | tf_op jit(solution)/shard_map/ppermute | solution.py:503
  63.2 0.8 %collective-permute-done.9 = f32[264,128]{1,0:T(8,128)S(1)} collective-permute-done((f32[264,128]{1,0:T(8,128)S(1)}, f32[264,128]{1,0:T(8,128)S(1)}, u32[]{:S(2)}, u32[]{:S(2)}) %collective-permute-start.9) | collective-permute-done | bytes 135200 | tf_op jit(solution)/shard_map/ppermute | solution.py:503
  64.0 1.3 %collective-permute-start.10 = (f32[264,128]{1,0:T(8,128)S(1)}, f32[264,128]{1,0:T(8,128)S(1)}, u32[]{:S(2)}, u32[]{:S(2)}) collective-permute-start(f32[264,128]{1,0:T(8,128)S(1)} %add.13.mine), channel_id=1, source_target_pairs={{0,8},{8,0},{16,24},{24,16},{1,9},{9,1},{17,25},{25,17},{2,10},{10... | collective-permute-start | bytes 405512 | tf_op jit(solution)/shard_map/ppermute | solution.py:503
  65.3 0.0 collective-permute-done.13.theirs
  65.3 0.8 %shard_map.74 = (f32[2,256,256]{2,1,0:T(8,128)}, f32[8,128]{1,0:T(8,128)S(1)}) custom-call(f32[512,128]{1,0:T(8,128)S(1)} %add.15.mine, f32[512,128]{1,0:T(8,128)S(1)} %collective-permute-done.13.theirs), custom_call_target="tpu_custom_call" | custom-call | flops 1 | bytes 1 | tf_op jit(solution)/shard_map/pallas_call | solution.py:398
  66.1 0.1 collective-permute-done.10.theirs
  66.3 0.9 %shard_map.75 = f32[2,256,256]{2,1,0:T(8,128)} custom-call(f32[264,128]{1,0:T(8,128)S(1)} %add.13.mine, f32[264,128]{1,0:T(8,128)S(1)} %collective-permute-done.10.theirs, f32[8,128]{1,0:T(8,128)S(1)} %get-tuple-element.90._), custom_call_target="tpu_custom_call" | custom-call | flops 1 | bytes 1 | tf_op jit(solution)/shard_map/pallas_call | solution.py:398
  (11 shorter events, 0.2 us)
Async XLA Ops:
  3.5 7.3 %collective-permute-start.1 = (f32[2,264,128]{2,1,0:T(8,128)S(1)}, f32[2,264,128]{2,1,0:T(8,128)S(1)}, u32[]{:S(2)}, u32[]{:S(2)}) collective-permute-start(f32[2,264,128]{2,1,0:T(8,128)S(1)} %get-tuple-element.48.refs_1_), channel_id=1, source_target_pairs={{0,1},{1,0},{2,3},{3,2},{4,5},{5,4},{6,7},{7,6},{8,9},{9,8},{10,11... | collective-permute-start | bytes 811016 | tf_op jit(solution)/shard_map/ppermute | solution.py:442
  4.7 0.7 copy-start.3
  4.7 4.2 %copy-start = (f32[2,2,2,256,256]{4,3,2,1,0:T(8,128)S(1)}, f32[2,2,2,256,256]{4,3,2,1,0:T(8,128)}, u32[]{:S(2)}) copy-start(f32[2,2,2,256,256]{4,3,2,1,0:T(8,128)} %pivot.7) | copy-start | bytes 6291460
  4.7 4.2 %copy-start.1 = (f32[2,2,2,256,256]{4,3,2,1,0:T(8,128)S(1)}, f32[2,2,2,256,256]{4,3,2,1,0:T(8,128)}, u32[]{:S(2)}) copy-start(f32[2,2,2,256,256]{4,3,2,1,0:T(8,128)} %factor.7) | copy-start | bytes 6291460
  4.7 4.2 %copy-start.2 = (f32[2,2]{1,0:T(2,128)S(1)}, f32[2,2]{1,0:T(2,128)}, u32[]{:S(2)}) copy-start(f32[2,2]{1,0:T(2,128)} %weight.11) | copy-start | bytes 52
  6.7 14.2 %collective-permute-start = (f32[2,256,256]{2,1,0:T(8,128)S(1)}, f32[2,256,256]{2,1,0:T(8,128)S(1)}, u32[]{:S(2)}, u32[]{:S(2)}) collective-permute-start(f32[2,256,256]{2,1,0:T(8,128)S(1)} %get-tuple-element.53._), channel_id=1, source_target_pairs={{2,3},{3,2},{4,5},{5,4},{6,7},{7,6},{10,11},{11,10},{12,13},{13,12... | collective-permute-start | bytes 1572872 | tf_op jit(solution)/shard_map/ppermute | solution.py:447
  10.8 2.7 %collective-permute-start.2 = (f32[2,264,128]{2,1,0:T(8,128)S(1)}, f32[2,264,128]{2,1,0:T(8,128)S(1)}, u32[]{:S(2)}, u32[]{:S(2)}) collective-permute-start(f32[2,264,128]{2,1,0:T(8,128)S(1)} %shard_map.65), channel_id=1, source_target_pairs={{0,1},{8,9},{16,17},{24,25},{1,0},{9,8},{17,16},{25,24}} | collective-permute-start | bytes 811016 | tf_op jit(solution)/shard_map/ppermute | solution.py:450
  13.5 9.1 %collective-permute-start.3 = (f32[2,264,128]{2,1,0:T(8,128)S(1)}, f32[2,264,128]{2,1,0:T(8,128)S(1)}, u32[]{:S(2)}, u32[]{:S(2)}) collective-permute-start(f32[2,264,128]{2,1,0:T(8,128)S(1)} %shard_map.67), channel_id=1, source_target_pairs={{1,3},{9,11},{17,19},{25,27}} | collective-permute-start | bytes 811016 | tf_op jit(solution)/shard_map/ppermute | solution.py:464
  14.2 8.4 %collective-permute-start.4 = (f32[2,264,128]{2,1,0:T(8,128)S(1)}, f32[2,264,128]{2,1,0:T(8,128)S(1)}, u32[]{:S(2)}, u32[]{:S(2)}) collective-permute-start(f32[2,264,128]{2,1,0:T(8,128)S(1)} %collective-permute-done.2.e_second.refs_0_), channel_id=1, source_target_pairs={{0,2},{8,10},{16,18},{24,26}} | collective-permute-start | bytes 811016 | tf_op jit(solution)/shard_map/ppermute | solution.py:465
  22.6 0.7 %collective-permute-start.5 = (f32[2,264,128]{2,1,0:T(8,128)S(1)}, f32[2,264,128]{2,1,0:T(8,128)S(1)}, u32[]{:S(2)}, u32[]{:S(2)}) collective-permute-start(f32[2,264,128]{2,1,0:T(8,128)S(1)} %shard_map.68), channel_id=1, source_target_pairs={{3,5},{2,4},{11,13},{10,12},{19,21},{18,20},{27,29},{26,28}} | collective-permute-start | bytes 811016 | tf_op jit(solution)/shard_map/ppermute | solution.py:481
  23.5 13.3 %collective-permute-start.6 = (f32[2,264,128]{2,1,0:T(8,128)S(1)}, f32[2,264,128]{2,1,0:T(8,128)S(1)}, u32[]{:S(2)}, u32[]{:S(2)}) collective-permute-start(f32[2,264,128]{2,1,0:T(8,128)S(1)} %shard_map.69), channel_id=1, source_target_pairs={{5,7},{4,6},{13,15},{12,14},{21,23},{20,22},{29,31},{28,30}} | collective-permute-start | bytes 811016 | tf_op jit(solution)/shard_map/ppermute | solution.py:481
  38.1 6.4 %collective-permute-start.7 = (f32[2,264,128]{2,1,0:T(8,128)S(1)}, f32[2,264,128]{2,1,0:T(8,128)S(1)}, u32[]{:S(2)}, u32[]{:S(2)}) collective-permute-start(f32[2,264,128]{2,1,0:T(8,128)S(1)} %get-tuple-element.77), channel_id=1, source_target_pairs={{0,1},{1,0},{2,3},{3,2},{4,5},{5,4},{6,7},{7,6},{8,9},{9,8},{10,11... | collective-permute-start | bytes 811016 | tf_op jit(solution)/shard_map/ppermute | solution.py:490
  46.0 7.4 %collective-permute-start.11 = (f32[512,128]{1,0:T(8,128)S(1)}, f32[512,128]{1,0:T(8,128)S(1)}, u32[]{:S(2)}, u32[]{:S(2)}) collective-permute-start(f32[512,128]{1,0:T(8,128)S(1)} %slice_bitcast_fusion), channel_id=1, source_target_pairs={{0,8},{8,0},{16,24},{24,16},{1,9},{9,1},{17,25},{25,17},{2,10},{10... | collective-permute-start | bytes 786440 | tf_op jit(solution)/shard_map/ppermute | solution.py:503
  52.9 1.4 %collective-permute-start.8 = (f32[264,128]{1,0:T(8,128)S(1)}, f32[264,128]{1,0:T(8,128)S(1)}, u32[]{:S(2)}, u32[]{:S(2)}) collective-permute-start(f32[264,128]{1,0:T(8,128)S(1)} %slice_bitcast_fusion.1), channel_id=1, source_target_pairs={{0,8},{8,0},{16,24},{24,16},{1,9},{9,1},{17,25},{25,17},{2,10},{10... | collective-permute-start | bytes 405512 | tf_op jit(solution)/shard_map/ppermute | solution.py:503
  53.5 7.6 %collective-permute-start.12 = (f32[512,128]{1,0:T(8,128)S(1)}, f32[512,128]{1,0:T(8,128)S(1)}, u32[]{:S(2)}, u32[]{:S(2)}) collective-permute-start(f32[512,128]{1,0:T(8,128)S(1)} %bitcast_add_fusion), channel_id=1, source_target_pairs={{0,16},{8,24},{16,0},{24,8},{1,17},{9,25},{17,1},{25,9},{2,18},{10... | collective-permute-start | bytes 786440 | tf_op jit(solution)/shard_map/ppermute | solution.py:503
  54.4 9.6 %collective-permute-start.9 = (f32[264,128]{1,0:T(8,128)S(1)}, f32[264,128]{1,0:T(8,128)S(1)}, u32[]{:S(2)}, u32[]{:S(2)}) collective-permute-start(f32[264,128]{1,0:T(8,128)S(1)} %fusion), channel_id=1, source_target_pairs={{0,16},{8,24},{16,0},{24,8},{1,17},{9,25},{17,1},{25,9},{2,18},{10... | collective-permute-start | bytes 405512 | tf_op jit(solution)/shard_map/ppermute | solution.py:503
  61.1 4.2 %collective-permute-start.13 = (f32[512,128]{1,0:T(8,128)S(1)}, f32[512,128]{1,0:T(8,128)S(1)}, u32[]{:S(2)}, u32[]{:S(2)}) collective-permute-start(f32[512,128]{1,0:T(8,128)S(1)} %add.15.mine), channel_id=1, source_target_pairs={{0,8},{8,0},{16,24},{24,16},{1,9},{9,1},{17,25},{25,17},{2,10},{10... | collective-permute-start | bytes 786440 | tf_op jit(solution)/shard_map/ppermute | solution.py:503
  64.0 2.3 %collective-permute-start.10 = (f32[264,128]{1,0:T(8,128)S(1)}, f32[264,128]{1,0:T(8,128)S(1)}, u32[]{:S(2)}, u32[]{:S(2)}) collective-permute-start(f32[264,128]{1,0:T(8,128)S(1)} %add.13.mine), channel_id=1, source_target_pairs={{0,8},{8,0},{16,24},{24,16},{1,9},{9,1},{17,25},{25,17},{2,10},{10... | collective-permute-start | bytes 405512 | tf_op jit(solution)/shard_map/ppermute | solution.py:503

commit v14 on v11

--- a/solution.py
+++ b/solution.py
@@ -162,11 +162,11 @@
     outs, second, scratch = refs[:4], refs[4:8], refs[8:]
     place, _, core = whereabouts()
 
-    @pl.when(jnp.logical_and(place != 1, core == 0))
+    @pl.when(jnp.logical_and(place != 1, core == 1))
     def _():
         fetched_constants(slot_of(True), live, pivot, factor, weight, second, scratch)
 
-    @pl.when(jnp.logical_or(place != 1, core == 0))
+    @pl.when(jnp.logical_or(place != 1, core == 1))
     def _():
         fetched_constants(slot_of(False), live, pivot, factor, weight, outs, scratch)
 
@@ -174,7 +174,7 @@
 def first_constant_kernel(live, pivot, factor, weight, *refs):
     made, outs, scratch = refs[:4], refs[4:8], refs[8:]
     place, _, core = whereabouts()
-    late = jnp.logical_and(place == 1, core == 1)
+    late = jnp.logical_and(place == 1, core == 0)
 
     @pl.when(jnp.logical_not(late))
     def _():
@@ -196,12 +196,12 @@
     made, outs = refs[:4], refs[4:]
     place, _, core = whereabouts()
 
-    @pl.when(core == 0)
+    @pl.when(core == 1)
     def _():
         for source, target in zip(made, outs):
             target[...] = source[...]
 
-    @pl.when(jnp.logical_and(place != 1, core == 1))
+    @pl.when(jnp.logical_and(place != 1, core == 0))
     def _():
         second_constants(live, pivot, factor, weight, *outs)
 

time: 67.6 us -> 75.4 us (1.12)
  waiting for transfers between devices: 28.1 us -> 38.7 us
  starting transfers between devices: 20.5 us -> 16.3 us
  Pallas kernels: 17 us -> 18.4 us
    ppermute x2, waiting for transfers between devices: 11.5 us -> 19.8 us  [local(): arrived = [lax.ppermute(wave, AXES, up)]]
    ppermute x6, starting transfers between devices: 11.7 us -> 6.86 us  [exchanged(): lax.ppermute(value, 'pole', [(p, p ^ distance) for p in range(poles)])]
    ppermute x1, waiting for transfers between devices: 0.01 us -> 1.39 us  [local(): e_in = lax.ppermute(made[1], AXES, every)]
    pallas_call x17, Pallas kernels: 17 us -> 18.4 us  [run(): pl.pallas_call(kernel, out_shape=shapes, in_specs=[SCALAR] * len(scalars)...]
    ppermute x1, waiting for transfers between devices: 1.92 us -> 2.86 us  [local(): shared = lax.ppermute(sent, AXES, every)]
  transfers between devices with their start and end apart: 14 -> 14, of which waited for: 8 -> 9; matrix products, arithmetic and copies ran while one was open for 0% -> 0% of each run, Pallas kernels for 16% -> 12%
where the time goes in v14:
time: 75.4 us; the launch traced here: 74.9 us
  waiting for transfers between devices  38.7 us (51%)
  Pallas kernels  18.4 us (24%)
  starting transfers between devices  16.3 us (22%)
  between operations  0.88 us (1%)
    ppermute x2, waiting for transfers between devices, local(): arrived = [lax.ppermute(wave, AXES, up)]  19.8 us
    pallas_call x17, Pallas kernels, run(): pl.pallas_call(kernel, out_shape=shapes, in_specs=[SCALAR] * len(scalars)...  18.4 us
    ppermute x6, waiting for transfers between devices, exchanged(): lax.ppermute(value, 'pole', [(p, p ^ distance) for p in range(poles)])  8.12 us
    ppermute x6, starting transfers between devices, exchanged(): lax.ppermute(value, 'pole', [(p, p ^ distance) for p in range(poles)])  6.86 us
    ppermute x1, waiting for transfers between devices, local(): g_in = lax.ppermute(o_g, AXES, swaps)  6.5 us
    ppermute x1, waiting for transfers between devices, local(): shared = lax.ppermute(sent, AXES, every)  2.86 us
    ppermute x1, starting transfers between devices, local(): g_in = lax.ppermute(o_g, AXES, swaps)  2.16 us
    ppermute x1, starting transfers between devices, local(): shared = lax.ppermute(sent, AXES, every)  2.04 us
  transfers between devices with their start and end apart: 14, of which 9 were waited for; matrix products, arithmetic and copies ran while one was open for 0% of the time, Pallas kernels for 12%

profile of v14, /device:TPU:29, one launch (start us, length us, event | category | flops | bytes accessed | tf_op | source)
XLA Modules:
  0.0 74.9 jit_solution(3943704263695449623)
XLA Ops:
  0.6 5.1 %shard_map.59 = (bf16[4,256,256]{2,1,0:T(8,128)(2,1)S(1)}, f32[2,264,128]{2,1,0:T(8,128)S(1)}, f32[4,264,128]{2,1,0:T(8,128)S(1)}, f32[2,256,256]{2,1,0:T(8,128)...) custom-call(s32[2]{0:T(128)} %live.11, ...), custom_call_target="tpu_custom_call" | custom-call | flops 1 | bytes 1 | tf_op jit(solution)/shard_map/pallas_call | solution.py:382
  5.8 1.3 %collective-permute-start.1 = (f32[2,264,128]{2,1,0:T(8,128)S(1)}, f32[2,264,128]{2,1,0:T(8,128)S(1)}, u32[]{:S(2)}, u32[]{:S(2)}) collective-permute-start(f32[2,264,128]{2,1,0:T(8,128)S(1)} %get-tuple-element.48.refs_1_), channel_id=1, source_target_pairs={{0,1},{1,0},{2,3},{3,2},{4,5},{5,4},{6,7},{7,6},{8,9},{9,8},{10,11... | collective-permute-start | bytes 811016 | tf_op jit(solution)/shard_map/ppermute | solution.py:426
  7.1 0.0 copy-start.3
  7.1 0.0 copy-start
  7.1 0.2 shard_map.60
  7.3 0.4 copy-done.3
  7.7 1.3 %shard_map.61 = (bf16[4,256,256]{2,1,0:T(8,128)(2,1)S(1)}, bf16[4,256,256]{2,1,0:T(8,128)(2,1)S(1)}, bf16[4,256,256]{2,1,0:T(8,128)(2,1)S(1)}, bf16[4,256,256]{2,1,0:T(8,128)(2,1)S(1)}, f32[2,256,256]{2,1,0:T(8,128)S(1)}) custom-call(s32[2]{0:T(128)S(1)} %copy-done.3, f32[2,256,256]{2,1,0:T(8,128)S(1)} %get-tuple-element.51.factor, ...), custom_call_target="tpu_custom_call" | custom-call | flops 1 | bytes 1 | tf_op jit(solution)/shard_map/pallas_call | solution.py:382
  9.0 2.2 %collective-permute-start = (f32[2,256,256]{2,1,0:T(8,128)S(1)}, f32[2,256,256]{2,1,0:T(8,128)S(1)}, u32[]{:S(2)}, u32[]{:S(2)}) collective-permute-start(f32[2,256,256]{2,1,0:T(8,128)S(1)} %get-tuple-element.53._), channel_id=1, source_target_pairs={{2,3},{3,2},{4,5},{5,4},{6,7},{7,6},{10,11},{11,10},{12,13},{13,12... | collective-permute-start | bytes 1572872 | tf_op jit(solution)/shard_map/ppermute | solution.py:431
  11.2 0.0 copy-done
  11.2 0.0 copy-done.1
  11.2 0.0 copy-done.2
  11.2 0.7 shard_map.62
  11.9 1.4 %collective-permute-done.1.x.e_in.x_first = f32[2,264,128]{2,1,0:T(8,128)S(1)} collective-permute-done((f32[2,264,128]{2,1,0:T(8,128)S(1)}, f32[2,264,128]{2,1,0:T(8,128)S(1)}, u32[]{:S(2)}, u32[]{:S(2)}) %collective-permute-start.1) | collective-permute-done | bytes 270368 | tf_op jit(solution)/shard_map/ppermute | solution.py:426
  13.3 0.7 collective-permute-start.2
  14.0 0.7 shard_map.63
  14.7 1.3 %shard_map.64 = (bf16[4,256,256]{2,1,0:T(8,128)(2,1)S(1)}, bf16[4,256,256]{2,1,0:T(8,128)(2,1)S(1)}, bf16[4,256,256]{2,1,0:T(8,128)(2,1)S(1)}, bf16[4,256,256]{2,1,0:T(8,128)(2,1)S(1)}, f32[2,256,256]{2,1,0:T(8,128)S(1)}) custom-call(s32[2]{0:T(128)S(1)} %copy-done.3, f32[2,256,256]{2,1,0:T(8,128)S(1)} %get-tuple-element.62.factor, ...), custom_call_target="tpu_custom_call" | custom-call | flops 1 | bytes 1 | tf_op jit(solution)/shard_map/pallas_call | solution.py:382
  16.0 0.0 collective-permute-done.2.e_second.refs_0_
  16.0 0.7 collective-permute-start.3
  16.7 0.7 collective-permute-start.4
  17.4 6.5 %collective-permute-done.g_in = f32[2,256,256]{2,1,0:T(8,128)S(1)} collective-permute-done((f32[2,256,256]{2,1,0:T(8,128)S(1)}, f32[2,256,256]{2,1,0:T(8,128)S(1)}, u32[]{:S(2)}, u32[]{:S(2)}) %collective-permute-start) | collective-permute-done | bytes 524320 | tf_op jit(solution)/shard_map/ppermute | solution.py:431
  23.9 1.7 %shard_map.66 = (bf16[4,256,256]{2,1,0:T(8,128)(2,1)S(1)}, bf16[4,256,256]{2,1,0:T(8,128)(2,1)S(1)}, f32[2,264,128]{2,1,0:T(8,128)S(1)}, bf16[4,256,256]{2,1,0:T...) custom-call(f32[2,256,256]{2,1,0:T(8,128)S(1)} %get-tuple-element.64.g, ...), custom_call_target="tpu_custom_call" | custom-call | flops 99999997952 | bytes 1 | tf_op jit(solution)/shard_map/pallas_call | solution.py:382
  25.6 0.0 collective-permute-done.3.refs_0_
  25.6 0.0 collective-permute-done.4.refs_1_
  25.6 0.7 collective-permute-start.5
  26.3 0.0 collective-permute-done.5.refs_0_.refs_2_
  26.3 0.2 shard_map.69
  26.5 1.3 %collective-permute-start.6 = (f32[2,264,128]{2,1,0:T(8,128)S(1)}, f32[2,264,128]{2,1,0:T(8,128)S(1)}, u32[]{:S(2)}, u32[]{:S(2)}) collective-permute-start(f32[2,264,128]{2,1,0:T(8,128)S(1)} %shard_map.69), channel_id=1, source_target_pairs={{5,7},{4,6},{13,15},{12,14},{21,23},{20,22},{29,31},{28,30}} | collective-permute-start | bytes 811016 | tf_op jit(solution)/shard_map/ppermute | solution.py:465
  27.8 19.8 %collective-permute-done.6.refs_3_ = f32[2,264,128]{2,1,0:T(8,128)S(1)} collective-permute-done((f32[2,264,128]{2,1,0:T(8,128)S(1)}, f32[2,264,128]{2,1,0:T(8,128)S(1)}, u32[]{:S(2)}, u32[]{:S(2)}) %collective-permute-start.6) | collective-permute-done | bytes 270368 | tf_op jit(solution)/shard_map/ppermute | solution.py:465
  47.6 1.2 %shard_map.70 = (f32[2,264,128]{2,1,0:T(8,128)S(1)}, f32[2,264,128]{2,1,0:T(8,128)S(1)}) custom-call(bf16[4,256,256]{2,1,0:T(8,128)(2,1)S(1)} %get-tuple-element.69.fas, bf16[4,256,256]{2,1,0:T(8,128)(2,1)S(1)} %get-tuple-element.70.fat, f32[2,264,128]{2,1,0:T(8,128)S(1)} %get-tuple-element.71.ea, f32[2,264,128]{2,1,0:T(8,128)S(1)} %collective-permute-done.3.refs_0_, ...), custom_call_target="tpu_custom_call" | custom-call | flops 1 | bytes 1 | tf_op jit(solution)/shard_map/pallas_call | solution.py:382
  48.9 2.0 %collective-permute-start.7 = (f32[2,264,128]{2,1,0:T(8,128)S(1)}, f32[2,264,128]{2,1,0:T(8,128)S(1)}, u32[]{:S(2)}, u32[]{:S(2)}) collective-permute-start(f32[2,264,128]{2,1,0:T(8,128)S(1)} %get-tuple-element.77), channel_id=1, source_target_pairs={{0,1},{1,0},{2,3},{3,2},{4,5},{5,4},{6,7},{7,6},{8,9},{9,8},{10,11... | collective-permute-start | bytes 811016 | tf_op jit(solution)/shard_map/ppermute | solution.py:474
  50.9 2.0 %shard_map.71 = (f32[2,512,128]{2,1,0:T(8,128)S(1)}, f32[2,264,128]{2,1,0:T(8,128)S(1)}) custom-call(f32[2,2]{1,0:T(2,128)S(1)} %copy-done.2, f32[2,264,128]{2,1,0:T(8,128)S(1)} %get-tuple-element.81.x, bf16[4,256,256]{2,1,0:T(8,128)(2,1)S(1)} %get-tuple-element.82.f0s, bf16[4,256,256]{2,1,0:T(8,128)(2,1)S(1)} %get-tuple-element.83.f0t, ...), custom_call_target="tpu_custom_call" | custom-call | flops 1 | bytes 1 | tf_op jit(solution)/shard_map/pallas_call | solution.py:382
  52.9 2.9 %collective-permute-done.7.x = f32[2,264,128]{2,1,0:T(8,128)S(1)} collective-permute-done((f32[2,264,128]{2,1,0:T(8,128)S(1)}, f32[2,264,128]{2,1,0:T(8,128)S(1)}, u32[]{:S(2)}, u32[]{:S(2)}) %collective-permute-start.7) | collective-permute-done | bytes 270368 | tf_op jit(solution)/shard_map/ppermute | solution.py:474
  55.8 1.6 %shard_map.72 = (f32[2,512,128]{2,1,0:T(8,128)S(1)}, bf16[4,256,256]{2,1,0:T(8,128)(2,1)S(1)}, bf16[4,256,256]{2,1,0:T(8,128)(2,1)S(1)}) custom-call(f32[2,2]{1,0:T(2,128)S(1)} %copy-done.2, f32[2,264,128]{2,1,0:T(8,128)S(1)} %collective-permute-done.7.x, f32[2,264,128]{2,1,0:T(8,128)S(1)} %collective-permute-done.1.x.e_in.x_first, ...), custom_call_target="tpu_custom_call" | custom-call | flops 1 | bytes 1 | tf_op jit(solution)/shard_map/pallas_call | solution.py:382
  57.4 2.6 %collective-permute-start.11 = (f32[512,128]{1,0:T(8,128)S(1)}, f32[512,128]{1,0:T(8,128)S(1)}, u32[]{:S(2)}, u32[]{:S(2)}) collective-permute-start(f32[512,128]{1,0:T(8,128)S(1)} %slice_bitcast_fusion), channel_id=1, source_target_pairs={{0,8},{8,0},{16,24},{24,16},{1,9},{9,1},{17,25},{25,17},{2,10},{10... | collective-permute-start | bytes 786440 | tf_op jit(solution)/shard_map/ppermute | solution.py:487
  60.0 0.6 shard_map.73
  60.6 0.1 collective-permute-start.8
  60.7 0.5 collective-permute-done.11
  61.2 0.1 collective-permute-start.12
  61.3 0.8 %collective-permute-done.8 = f32[264,128]{1,0:T(8,128)S(1)} collective-permute-done((f32[264,128]{1,0:T(8,128)S(1)}, f32[264,128]{1,0:T(8,128)S(1)}, u32[]{:S(2)}, u32[]{:S(2)}) %collective-permute-start.8) | collective-permute-done | bytes 135200 | tf_op jit(solution)/shard_map/ppermute | solution.py:487
  62.0 0.8 %collective-permute-start.9 = (f32[264,128]{1,0:T(8,128)S(1)}, f32[264,128]{1,0:T(8,128)S(1)}, u32[]{:S(2)}, u32[]{:S(2)}) collective-permute-start(f32[264,128]{1,0:T(8,128)S(1)} %fusion), channel_id=1, source_target_pairs={{0,16},{8,24},{16,0},{24,8},{1,17},{9,25},{17,1},{25,9},{2,18},{10... | collective-permute-start | bytes 405512 | tf_op jit(solution)/shard_map/ppermute | solution.py:487
  62.8 6.0 %collective-permute-done.12 = f32[512,128]{1,0:T(8,128)S(1)} collective-permute-done((f32[512,128]{1,0:T(8,128)S(1)}, f32[512,128]{1,0:T(8,128)S(1)}, u32[]{:S(2)}, u32[]{:S(2)}) %collective-permute-start.12) | collective-permute-done | bytes 262176 | tf_op jit(solution)/shard_map/ppermute | solution.py:487
  68.8 2.1 %collective-permute-start.13 = (f32[512,128]{1,0:T(8,128)S(1)}, f32[512,128]{1,0:T(8,128)S(1)}, u32[]{:S(2)}, u32[]{:S(2)}) collective-permute-start(f32[512,128]{1,0:T(8,128)S(1)} %add.15.mine), channel_id=1, source_target_pairs={{0,8},{8,0},{16,24},{24,16},{1,9},{9,1},{17,25},{25,17},{2,10},{10... | collective-permute-start | bytes 786440 | tf_op jit(solution)/shard_map/ppermute | solution.py:487
  70.9 0.8 %collective-permute-done.9 = f32[264,128]{1,0:T(8,128)S(1)} collective-permute-done((f32[264,128]{1,0:T(8,128)S(1)}, f32[264,128]{1,0:T(8,128)S(1)}, u32[]{:S(2)}, u32[]{:S(2)}) %collective-permute-start.9) | collective-permute-done | bytes 135200 | tf_op jit(solution)/shard_map/ppermute | solution.py:487
  71.7 1.3 %collective-permute-start.10 = (f32[264,128]{1,0:T(8,128)S(1)}, f32[264,128]{1,0:T(8,128)S(1)}, u32[]{:S(2)}, u32[]{:S(2)}) collective-permute-start(f32[264,128]{1,0:T(8,128)S(1)} %add.13.mine), channel_id=1, source_target_pairs={{0,8},{8,0},{16,24},{24,16},{1,9},{9,1},{17,25},{25,17},{2,10},{10... | collective-permute-start | bytes 405512 | tf_op jit(solution)/shard_map/ppermute | solution.py:487
  73.0 0.0 collective-permute-done.13.theirs
  73.0 0.8 %shard_map.74 = (f32[2,256,256]{2,1,0:T(8,128)}, f32[8,128]{1,0:T(8,128)S(1)}) custom-call(f32[512,128]{1,0:T(8,128)S(1)} %add.15.mine, f32[512,128]{1,0:T(8,128)S(1)} %collective-permute-done.13.theirs), custom_call_target="tpu_custom_call" | custom-call | flops 1 | bytes 1 | tf_op jit(solution)/shard_map/pallas_call | solution.py:382
  73.8 0.1 collective-permute-done.10.theirs
  74.0 0.9 %shard_map.75 = f32[2,256,256]{2,1,0:T(8,128)} custom-call(f32[264,128]{1,0:T(8,128)S(1)} %add.13.mine, f32[264,128]{1,0:T(8,128)S(1)} %collective-permute-done.10.theirs, f32[8,128]{1,0:T(8,128)S(1)} %get-tuple-element.90._), custom_call_target="tpu_custom_call" | custom-call | flops 1 | bytes 1 | tf_op jit(solution)/shard_map/pallas_call | solution.py:382
  (11 shorter events, 0.2 us)
Async XLA Ops:
  5.8 7.5 %collective-permute-start.1 = (f32[2,264,128]{2,1,0:T(8,128)S(1)}, f32[2,264,128]{2,1,0:T(8,128)S(1)}, u32[]{:S(2)}, u32[]{:S(2)}) collective-permute-start(f32[2,264,128]{2,1,0:T(8,128)S(1)} %get-tuple-element.48.refs_1_), channel_id=1, source_target_pairs={{0,1},{1,0},{2,3},{3,2},{4,5},{5,4},{6,7},{7,6},{8,9},{9,8},{10,11... | collective-permute-start | bytes 811016 | tf_op jit(solution)/shard_map/ppermute | solution.py:426
  7.1 0.7 copy-start.3
  7.1 4.1 %copy-start = (f32[2,2,2,256,256]{4,3,2,1,0:T(8,128)S(1)}, f32[2,2,2,256,256]{4,3,2,1,0:T(8,128)}, u32[]{:S(2)}) copy-start(f32[2,2,2,256,256]{4,3,2,1,0:T(8,128)} %pivot.7) | copy-start | bytes 6291460
  7.1 4.2 %copy-start.1 = (f32[2,2,2,256,256]{4,3,2,1,0:T(8,128)S(1)}, f32[2,2,2,256,256]{4,3,2,1,0:T(8,128)}, u32[]{:S(2)}) copy-start(f32[2,2,2,256,256]{4,3,2,1,0:T(8,128)} %factor.7) | copy-start | bytes 6291460
  7.1 4.2 %copy-start.2 = (f32[2,2]{1,0:T(2,128)S(1)}, f32[2,2]{1,0:T(2,128)}, u32[]{:S(2)}) copy-start(f32[2,2]{1,0:T(2,128)} %weight.11) | copy-start | bytes 52
  9.0 14.9 %collective-permute-start = (f32[2,256,256]{2,1,0:T(8,128)S(1)}, f32[2,256,256]{2,1,0:T(8,128)S(1)}, u32[]{:S(2)}, u32[]{:S(2)}) collective-permute-start(f32[2,256,256]{2,1,0:T(8,128)S(1)} %get-tuple-element.53._), channel_id=1, source_target_pairs={{2,3},{3,2},{4,5},{5,4},{6,7},{7,6},{10,11},{11,10},{12,13},{13,12... | collective-permute-start | bytes 1572872 | tf_op jit(solution)/shard_map/ppermute | solution.py:431
  13.3 2.7 %collective-permute-start.2 = (f32[2,264,128]{2,1,0:T(8,128)S(1)}, f32[2,264,128]{2,1,0:T(8,128)S(1)}, u32[]{:S(2)}, u32[]{:S(2)}) collective-permute-start(f32[2,264,128]{2,1,0:T(8,128)S(1)} %shard_map.65), channel_id=1, source_target_pairs={{0,1},{8,9},{16,17},{24,25},{1,0},{9,8},{17,16},{25,24}} | collective-permute-start | bytes 811016 | tf_op jit(solution)/shard_map/ppermute | solution.py:434
  16.0 9.6 %collective-permute-start.3 = (f32[2,264,128]{2,1,0:T(8,128)S(1)}, f32[2,264,128]{2,1,0:T(8,128)S(1)}, u32[]{:S(2)}, u32[]{:S(2)}) collective-permute-start(f32[2,264,128]{2,1,0:T(8,128)S(1)} %shard_map.67), channel_id=1, source_target_pairs={{1,3},{9,11},{17,19},{25,27}} | collective-permute-start | bytes 811016 | tf_op jit(solution)/shard_map/ppermute | solution.py:448
  16.7 8.9 %collective-permute-start.4 = (f32[2,264,128]{2,1,0:T(8,128)S(1)}, f32[2,264,128]{2,1,0:T(8,128)S(1)}, u32[]{:S(2)}, u32[]{:S(2)}) collective-permute-start(f32[2,264,128]{2,1,0:T(8,128)S(1)} %collective-permute-done.2.e_second.refs_0_), channel_id=1, source_target_pairs={{0,2},{8,10},{16,18},{24,26}} | collective-permute-start | bytes 811016 | tf_op jit(solution)/shard_map/ppermute | solution.py:449
  25.6 0.7 collective-permute-start.5
  26.5 21.1 %collective-permute-start.6 = (f32[2,264,128]{2,1,0:T(8,128)S(1)}, f32[2,264,128]{2,1,0:T(8,128)S(1)}, u32[]{:S(2)}, u32[]{:S(2)}) collective-permute-start(f32[2,264,128]{2,1,0:T(8,128)S(1)} %shard_map.69), channel_id=1, source_target_pairs={{5,7},{4,6},{13,15},{12,14},{21,23},{20,22},{29,31},{28,30}} | collective-permute-start | bytes 811016 | tf_op jit(solution)/shard_map/ppermute | solution.py:465
  48.9 6.9 %collective-permute-start.7 = (f32[2,264,128]{2,1,0:T(8,128)S(1)}, f32[2,264,128]{2,1,0:T(8,128)S(1)}, u32[]{:S(2)}, u32[]{:S(2)}) collective-permute-start(f32[2,264,128]{2,1,0:T(8,128)S(1)} %get-tuple-element.77), channel_id=1, source_target_pairs={{0,1},{1,0},{2,3},{3,2},{4,5},{5,4},{6,7},{7,6},{8,9},{9,8},{10,11... | collective-permute-start | bytes 811016 | tf_op jit(solution)/shard_map/ppermute | solution.py:474
  57.4 3.8 %collective-permute-start.11 = (f32[512,128]{1,0:T(8,128)S(1)}, f32[512,128]{1,0:T(8,128)S(1)}, u32[]{:S(2)}, u32[]{:S(2)}) collective-permute-start(f32[512,128]{1,0:T(8,128)S(1)} %slice_bitcast_fusion), channel_id=1, source_target_pairs={{0,8},{8,0},{16,24},{24,16},{1,9},{9,1},{17,25},{25,17},{2,10},{10... | collective-permute-start | bytes 786440 | tf_op jit(solution)/shard_map/ppermute | solution.py:487
  60.6 1.4 %collective-permute-start.8 = (f32[264,128]{1,0:T(8,128)S(1)}, f32[264,128]{1,0:T(8,128)S(1)}, u32[]{:S(2)}, u32[]{:S(2)}) collective-permute-start(f32[264,128]{1,0:T(8,128)S(1)} %slice_bitcast_fusion.1), channel_id=1, source_target_pairs={{0,8},{8,0},{16,24},{24,16},{1,9},{9,1},{17,25},{25,17},{2,10},{10... | collective-permute-start | bytes 405512 | tf_op jit(solution)/shard_map/ppermute | solution.py:487
  61.2 7.6 %collective-permute-start.12 = (f32[512,128]{1,0:T(8,128)S(1)}, f32[512,128]{1,0:T(8,128)S(1)}, u32[]{:S(2)}, u32[]{:S(2)}) collective-permute-start(f32[512,128]{1,0:T(8,128)S(1)} %bitcast_add_fusion), channel_id=1, source_target_pairs={{0,16},{8,24},{16,0},{24,8},{1,17},{9,25},{17,1},{25,9},{2,18},{10... | collective-permute-start | bytes 786440 | tf_op jit(solution)/shard_map/ppermute | solution.py:487
  62.0 9.6 %collective-permute-start.9 = (f32[264,128]{1,0:T(8,128)S(1)}, f32[264,128]{1,0:T(8,128)S(1)}, u32[]{:S(2)}, u32[]{:S(2)}) collective-permute-start(f32[264,128]{1,0:T(8,128)S(1)} %fusion), channel_id=1, source_target_pairs={{0,16},{8,24},{16,0},{24,8},{1,17},{9,25},{17,1},{25,9},{2,18},{10... | collective-permute-start | bytes 405512 | tf_op jit(solution)/shard_map/ppermute | solution.py:487
  68.8 4.2 %collective-permute-start.13 = (f32[512,128]{1,0:T(8,128)S(1)}, f32[512,128]{1,0:T(8,128)S(1)}, u32[]{:S(2)}, u32[]{:S(2)}) collective-permute-start(f32[512,128]{1,0:T(8,128)S(1)} %add.15.mine), channel_id=1, source_target_pairs={{0,8},{8,0},{16,24},{24,16},{1,9},{9,1},{17,25},{25,17},{2,10},{10... | collective-permute-start | bytes 786440 | tf_op jit(solution)/shard_map/ppermute | solution.py:487
  71.7 2.3 %collective-permute-start.10 = (f32[264,128]{1,0:T(8,128)S(1)}, f32[264,128]{1,0:T(8,128)S(1)}, u32[]{:S(2)}, u32[]{:S(2)}) collective-permute-start(f32[264,128]{1,0:T(8,128)S(1)} %add.13.mine), channel_id=1, source_target_pairs={{0,8},{8,0},{16,24},{24,16},{1,9},{9,1},{17,25},{25,17},{2,10},{10... | collective-permute-start | bytes 405512 | tf_op jit(solution)/shard_map/ppermute | solution.py:487

commit v15 on v11

--- a/solution.py
+++ b/solution.py
@@ -345,7 +345,7 @@
     store4(ts_out, ts)
 
 
-def more_diag_kernel(us, ts, f0t, gt, weighted, before, diag):
+def more_diag_kernel(us, ts, f0t, gt, weighted, _, before, diag):
     core = whereabouts()[2]
     first, second = diag_values(load4(us), load4(ts), f0t, gt, weighted)
     diag[core] = first + before[core]
@@ -486,8 +486,10 @@
     def exchanged(value, distance):
         return lax.ppermute(value, "pole", [(p, p ^ distance) for p in range(poles)])
 
-    def summed(parts):
-        kept = parts[0] + exchanged(parts[1], 1)
+    def over_cores(parts):
+        return parts[0] + exchanged(parts[1], 1)
+
+    def over_chips(kept):
         distance = 2
         while distance < poles:
             kept = kept + exchanged(kept, distance)
@@ -495,9 +497,10 @@
         return kept, exchanged(kept, 1)
 
     full = jax.ShapeDtypeStruct((2, width, width), F32)
-    off_sums = summed(off)
-    (diag,) = run(more_diag_kernel, [], [us, ts, o_f0t, o_gt, o_w, diag], [diags])
-    diag_sums = summed(diag)
+    off = over_cores(off)
+    (diag,) = run(more_diag_kernel, [], [us, ts, o_f0t, o_gt, o_w, off, diag], [diags])
+    off_sums = over_chips(off)
+    diag_sums = over_chips(over_cores(diag))
     done = jax.ShapeDtypeStruct((8, 128), F32)
     density_off, done = run(unpack_off_kernel, [], list(off_sums), [full, done])
     (density_diag,) = run(unpack_diag_kernel, [], [*diag_sums, done], [full])

time: 67.6 us -> 68.6 us (1.015)
  waiting for transfers between devices: 28.1 us -> 29.8 us
    ppermute x6, waiting for transfers between devices: 8.13 us -> 9.81 us  [exchanged(): lax.ppermute(value, 'pole', [(p, p ^ distance) for p in range(poles)])]
  transfers between devices with their start and end apart: 14 -> 14, of which waited for: 8 -> 8; matrix products, arithmetic and copies ran while one was open for 0% -> 0% of each run, Pallas kernels for 16% -> 15%
where the time goes in v15:
time: 68.6 us; the launch traced here: 68.2 us
  waiting for transfers between devices  29.8 us (43%)
  starting transfers between devices  19.9 us (29%)
  Pallas kernels  17 us (25%)
  between operations  0.89 us (1%)
    pallas_call x17, Pallas kernels, run(): pl.pallas_call(kernel, out_shape=shapes, in_specs=[SCALAR] * len(scalars)...  17 us
    ppermute x2, waiting for transfers between devices, local(): arrived = [lax.ppermute(wave, AXES, up)]  11.5 us
    ppermute x6, starting transfers between devices, exchanged(): lax.ppermute(value, 'pole', [(p, p ^ distance) for p in range(poles)])  11 us
    ppermute x6, waiting for transfers between devices, exchanged(): lax.ppermute(value, 'pole', [(p, p ^ distance) for p in range(poles)])  9.81 us
    ppermute x1, waiting for transfers between devices, local(): g_in = lax.ppermute(o_g, AXES, swaps)  6.61 us
    ppermute x1, starting transfers between devices, local(): g_in = lax.ppermute(o_g, AXES, swaps)  2.16 us
    ppermute x2, starting transfers between devices, local(): arrived = [lax.ppermute(wave, AXES, up)]  1.97 us
    ppermute x1, waiting for transfers between devices, local(): shared = lax.ppermute(sent, AXES, every)  1.91 us
  transfers between devices with their start and end apart: 14, of which 8 were waited for; matrix products, arithmetic and copies ran while one was open for 0% of the time, Pallas kernels for 15%

profile of v15, /device:TPU:29, one launch (start us, length us, event | category | flops | bytes accessed | tf_op | source)
XLA Modules:
  0.0 68.2 jit_solution(13453735295575367154)
XLA Ops:
  0.6 2.6 %shard_map.59 = (bf16[4,256,256]{2,1,0:T(8,128)(2,1)S(1)}, f32[2,264,128]{2,1,0:T(8,128)S(1)}, f32[4,264,128]{2,1,0:T(8,128)S(1)}, f32[2,256,256]{2,1,0:T(8,128)...) custom-call(s32[2]{0:T(128)} %live.11, ...), custom_call_target="tpu_custom_call" | custom-call | flops 1 | bytes 1 | tf_op jit(solution)/shard_map/pallas_call | solution.py:382
  3.3 1.3 %collective-permute-start.1 = (f32[2,264,128]{2,1,0:T(8,128)S(1)}, f32[2,264,128]{2,1,0:T(8,128)S(1)}, u32[]{:S(2)}, u32[]{:S(2)}) collective-permute-start(f32[2,264,128]{2,1,0:T(8,128)S(1)} %get-tuple-element.48.refs_1_), channel_id=1, source_target_pairs={{0,1},{1,0},{2,3},{3,2},{4,5},{5,4},{6,7},{7,6},{8,9},{9,8},{10,11... | collective-permute-start | bytes 811016 | tf_op jit(solution)/shard_map/ppermute | solution.py:426
  4.5 0.0 copy-start.3
  4.5 0.0 copy-start
  4.5 0.2 shard_map.60
  4.7 0.4 copy-done.3
  5.2 1.3 %shard_map.61 = (bf16[4,256,256]{2,1,0:T(8,128)(2,1)S(1)}, bf16[4,256,256]{2,1,0:T(8,128)(2,1)S(1)}, bf16[4,256,256]{2,1,0:T(8,128)(2,1)S(1)}, bf16[4,256,256]{2,1,0:T(8,128)(2,1)S(1)}, f32[2,256,256]{2,1,0:T(8,128)S(1)}) custom-call(s32[2]{0:T(128)S(1)} %copy-done.3, f32[2,256,256]{2,1,0:T(8,128)S(1)} %get-tuple-element.51.factor, ...), custom_call_target="tpu_custom_call" | custom-call | flops 1 | bytes 1 | tf_op jit(solution)/shard_map/pallas_call | solution.py:382
  6.5 2.2 %collective-permute-start = (f32[2,256,256]{2,1,0:T(8,128)S(1)}, f32[2,256,256]{2,1,0:T(8,128)S(1)}, u32[]{:S(2)}, u32[]{:S(2)}) collective-permute-start(f32[2,256,256]{2,1,0:T(8,128)S(1)} %get-tuple-element.53._), channel_id=1, source_target_pairs={{2,3},{3,2},{4,5},{5,4},{6,7},{7,6},{10,11},{11,10},{12,13},{13,12... | collective-permute-start | bytes 1572872 | tf_op jit(solution)/shard_map/ppermute | solution.py:431
  8.7 0.0 copy-done
  8.7 0.0 copy-done.1
  8.7 0.0 copy-done.2
  8.7 1.8 %shard_map.62 = (bf16[4,256,256]{2,1,0:T(8,128)(2,1)S(1)}, f32[2,264,128]{2,1,0:T(8,128)S(1)}, f32[4,264,128]{2,1,0:T(8,128)S(1)}, f32[2,256,256]{2,1,0:T(8,128)S(1)}) custom-call(s32[2]{0:T(128)S(1)} %copy-done.3, f32[2,2,2,256,256]{4,3,2,1,0:T(8,128)S(1)} %copy-done, f32[2,2,2,256,256]{4,3,2,1,0:T(8,128)S(1)} %copy-done.1, f32[2,2]{1,0:T(2,128)S(1)} %copy-done.2, ...), custom_call_target="tpu_custom_call" | custom-call | flops 1 | bytes 1 | tf_op jit(solution)/shard_map/pallas_call | solution.py:382
  10.6 0.0 collective-permute-done.1.x.e_in.x_first
  10.6 0.7 collective-permute-start.2
  11.3 0.7 shard_map.63
  12.0 1.3 %shard_map.64 = (bf16[4,256,256]{2,1,0:T(8,128)(2,1)S(1)}, bf16[4,256,256]{2,1,0:T(8,128)(2,1)S(1)}, bf16[4,256,256]{2,1,0:T(8,128)(2,1)S(1)}, bf16[4,256,256]{2,1,0:T(8,128)(2,1)S(1)}, f32[2,256,256]{2,1,0:T(8,128)S(1)}) custom-call(s32[2]{0:T(128)S(1)} %copy-done.3, f32[2,256,256]{2,1,0:T(8,128)S(1)} %get-tuple-element.62.factor, ...), custom_call_target="tpu_custom_call" | custom-call | flops 1 | bytes 1 | tf_op jit(solution)/shard_map/pallas_call | solution.py:382
  13.3 0.0 collective-permute-done.2.e_second.refs_0_
  13.3 0.7 collective-permute-start.3
  14.0 0.7 collective-permute-start.4
  14.7 6.6 %collective-permute-done.g_in = f32[2,256,256]{2,1,0:T(8,128)S(1)} collective-permute-done((f32[2,256,256]{2,1,0:T(8,128)S(1)}, f32[2,256,256]{2,1,0:T(8,128)S(1)}, u32[]{:S(2)}, u32[]{:S(2)}) %collective-permute-start) | collective-permute-done | bytes 524320 | tf_op jit(solution)/shard_map/ppermute | solution.py:431
  21.3 1.7 %shard_map.66 = (bf16[4,256,256]{2,1,0:T(8,128)(2,1)S(1)}, bf16[4,256,256]{2,1,0:T(8,128)(2,1)S(1)}, f32[2,264,128]{2,1,0:T(8,128)S(1)}, bf16[4,256,256]{2,1,0:T...) custom-call(f32[2,256,256]{2,1,0:T(8,128)S(1)} %get-tuple-element.64.g, ...), custom_call_target="tpu_custom_call" | custom-call | flops 99999997952 | bytes 1 | tf_op jit(solution)/shard_map/pallas_call | solution.py:382
  23.0 0.0 collective-permute-done.3.refs_0_
  23.0 0.0 collective-permute-done.4.refs_1_
  23.0 0.7 collective-permute-start.5
  23.7 0.0 collective-permute-done.5.refs_0_.refs_2_
  23.7 0.2 shard_map.69
  23.9 1.3 %collective-permute-start.6 = (f32[2,264,128]{2,1,0:T(8,128)S(1)}, f32[2,264,128]{2,1,0:T(8,128)S(1)}, u32[]{:S(2)}, u32[]{:S(2)}) collective-permute-start(f32[2,264,128]{2,1,0:T(8,128)S(1)} %shard_map.69), channel_id=1, source_target_pairs={{5,7},{4,6},{13,15},{12,14},{21,23},{20,22},{29,31},{28,30}} | collective-permute-start | bytes 811016 | tf_op jit(solution)/shard_map/ppermute | solution.py:465
  25.2 11.5 %collective-permute-done.6.refs_3_ = f32[2,264,128]{2,1,0:T(8,128)S(1)} collective-permute-done((f32[2,264,128]{2,1,0:T(8,128)S(1)}, f32[2,264,128]{2,1,0:T(8,128)S(1)}, u32[]{:S(2)}, u32[]{:S(2)}) %collective-permute-start.6) | collective-permute-done | bytes 270368 | tf_op jit(solution)/shard_map/ppermute | solution.py:465
  36.7 1.2 %shard_map.70 = (f32[2,264,128]{2,1,0:T(8,128)S(1)}, f32[2,264,128]{2,1,0:T(8,128)S(1)}) custom-call(bf16[4,256,256]{2,1,0:T(8,128)(2,1)S(1)} %get-tuple-element.69.fas, bf16[4,256,256]{2,1,0:T(8,128)(2,1)S(1)} %get-tuple-element.70.fat, f32[2,264,128]{2,1,0:T(8,128)S(1)} %get-tuple-element.71.ea, f32[2,264,128]{2,1,0:T(8,128)S(1)} %collective-permute-done.3.refs_0_, ...), custom_call_target="tpu_custom_call" | custom-call | flops 1 | bytes 1 | tf_op jit(solution)/shard_map/pallas_call | solution.py:382
  37.9 1.4 %collective-permute-start.7 = (f32[2,264,128]{2,1,0:T(8,128)S(1)}, f32[2,264,128]{2,1,0:T(8,128)S(1)}, u32[]{:S(2)}, u32[]{:S(2)}) collective-permute-start(f32[2,264,128]{2,1,0:T(8,128)S(1)} %get-tuple-element.77), channel_id=1, source_target_pairs={{0,1},{1,0},{2,3},{3,2},{4,5},{5,4},{6,7},{7,6},{8,9},{9,8},{10,11... | collective-permute-start | bytes 811016 | tf_op jit(solution)/shard_map/ppermute | solution.py:474
  39.4 2.0 %shard_map.71 = (f32[2,512,128]{2,1,0:T(8,128)S(1)}, f32[2,264,128]{2,1,0:T(8,128)S(1)}) custom-call(f32[2,2]{1,0:T(2,128)S(1)} %copy-done.2, f32[2,264,128]{2,1,0:T(8,128)S(1)} %get-tuple-element.81.x, bf16[4,256,256]{2,1,0:T(8,128)(2,1)S(1)} %get-tuple-element.82.f0s, bf16[4,256,256]{2,1,0:T(8,128)(2,1)S(1)} %get-tuple-element.83.f0t, ...), custom_call_target="tpu_custom_call" | custom-call | flops 1 | bytes 1 | tf_op jit(solution)/shard_map/pallas_call | solution.py:382
  41.4 1.9 %collective-permute-done.7.x = f32[2,264,128]{2,1,0:T(8,128)S(1)} collective-permute-done((f32[2,264,128]{2,1,0:T(8,128)S(1)}, f32[2,264,128]{2,1,0:T(8,128)S(1)}, u32[]{:S(2)}, u32[]{:S(2)}) %collective-permute-start.7) | collective-permute-done | bytes 270368 | tf_op jit(solution)/shard_map/ppermute | solution.py:474
  43.3 1.5 %shard_map.72 = (f32[2,512,128]{2,1,0:T(8,128)S(1)}, bf16[4,256,256]{2,1,0:T(8,128)(2,1)S(1)}, bf16[4,256,256]{2,1,0:T(8,128)(2,1)S(1)}) custom-call(f32[2,2]{1,0:T(2,128)S(1)} %copy-done.2, f32[2,264,128]{2,1,0:T(8,128)S(1)} %collective-permute-done.7.x, f32[2,264,128]{2,1,0:T(8,128)S(1)} %collective-permute-done.1.x.e_in.x_first, ...), custom_call_target="tpu_custom_call" | custom-call | flops 1 | bytes 1 | tf_op jit(solution)/shard_map/pallas_call | solution.py:382
  44.9 7.4 %collective-permute-start.8 = (f32[512,128]{1,0:T(8,128)S(1)}, f32[512,128]{1,0:T(8,128)S(1)}, u32[]{:S(2)}, u32[]{:S(2)}) collective-permute-start(f32[512,128]{1,0:T(8,128)S(1)} %slice_bitcast_fusion), channel_id=1, source_target_pairs={{0,8},{8,0},{16,24},{24,16},{1,9},{9,1},{17,25},{25,17},{2,10},{10... | collective-permute-start | bytes 786440 | tf_op jit(solution)/shard_map/ppermute | solution.py:487
  52.3 1.2 %collective-permute-done.8 = f32[512,128]{1,0:T(8,128)S(1)} collective-permute-done((f32[512,128]{1,0:T(8,128)S(1)}, f32[512,128]{1,0:T(8,128)S(1)}, u32[]{:S(2)}, u32[]{:S(2)}) %collective-permute-start.8) | collective-permute-done | bytes 262176 | tf_op jit(solution)/shard_map/ppermute | solution.py:487
  53.5 0.6 shard_map.73
  54.1 0.4 collective-permute-start.9
  54.5 0.0 collective-permute-start.12
  54.5 1.0 %collective-permute-done.9 = f32[264,128]{1,0:T(8,128)S(1)} collective-permute-done((f32[264,128]{1,0:T(8,128)S(1)}, f32[264,128]{1,0:T(8,128)S(1)}, u32[]{:S(2)}, u32[]{:S(2)}) %collective-permute-start.9) | collective-permute-done | bytes 135200 | tf_op jit(solution)/shard_map/ppermute | solution.py:487
  55.6 0.5 collective-permute-start.10
  56.1 6.2 %collective-permute-done.12 = f32[512,128]{1,0:T(8,128)S(1)} collective-permute-done((f32[512,128]{1,0:T(8,128)S(1)}, f32[512,128]{1,0:T(8,128)S(1)}, u32[]{:S(2)}, u32[]{:S(2)}) %collective-permute-start.12) | collective-permute-done | bytes 262176 | tf_op jit(solution)/shard_map/ppermute | solution.py:487
  62.3 1.6 %collective-permute-start.13 = (f32[512,128]{1,0:T(8,128)S(1)}, f32[512,128]{1,0:T(8,128)S(1)}, u32[]{:S(2)}, u32[]{:S(2)}) collective-permute-start(f32[512,128]{1,0:T(8,128)S(1)} %add.15.mine), channel_id=1, source_target_pairs={{0,8},{8,0},{16,24},{24,16},{1,9},{9,1},{17,25},{25,17},{2,10},{10... | collective-permute-start | bytes 786440 | tf_op jit(solution)/shard_map/ppermute | solution.py:487
  63.9 1.3 %collective-permute-done.10 = f32[264,128]{1,0:T(8,128)S(1)} collective-permute-done((f32[264,128]{1,0:T(8,128)S(1)}, f32[264,128]{1,0:T(8,128)S(1)}, u32[]{:S(2)}, u32[]{:S(2)}) %collective-permute-start.10) | collective-permute-done | bytes 135200 | tf_op jit(solution)/shard_map/ppermute | solution.py:487
  65.2 1.0 %collective-permute-start.11 = (f32[264,128]{1,0:T(8,128)S(1)}, f32[264,128]{1,0:T(8,128)S(1)}, u32[]{:S(2)}, u32[]{:S(2)}) collective-permute-start(f32[264,128]{1,0:T(8,128)S(1)} %add.14.mine), channel_id=1, source_target_pairs={{0,8},{8,0},{16,24},{24,16},{1,9},{9,1},{17,25},{25,17},{2,10},{10... | collective-permute-start | bytes 405512 | tf_op jit(solution)/shard_map/ppermute | solution.py:487
  66.2 0.0 collective-permute-done.13.theirs
  66.2 0.8 %shard_map.74 = (f32[2,256,256]{2,1,0:T(8,128)}, f32[8,128]{1,0:T(8,128)S(1)}) custom-call(f32[512,128]{1,0:T(8,128)S(1)} %add.15.mine, f32[512,128]{1,0:T(8,128)S(1)} %collective-permute-done.13.theirs), custom_call_target="tpu_custom_call" | custom-call | flops 1 | bytes 1 | tf_op jit(solution)/shard_map/pallas_call | solution.py:382
  67.1 0.1 collective-permute-done.11.theirs
  67.2 0.9 %shard_map.75 = f32[2,256,256]{2,1,0:T(8,128)} custom-call(f32[264,128]{1,0:T(8,128)S(1)} %add.14.mine, f32[264,128]{1,0:T(8,128)S(1)} %collective-permute-done.11.theirs, f32[8,128]{1,0:T(8,128)S(1)} %get-tuple-element.90._), custom_call_target="tpu_custom_call" | custom-call | flops 1 | bytes 1 | tf_op jit(solution)/shard_map/pallas_call | solution.py:382
  (11 shorter events, 0.2 us)
Async XLA Ops:
  3.3 7.3 %collective-permute-start.1 = (f32[2,264,128]{2,1,0:T(8,128)S(1)}, f32[2,264,128]{2,1,0:T(8,128)S(1)}, u32[]{:S(2)}, u32[]{:S(2)}) collective-permute-start(f32[2,264,128]{2,1,0:T(8,128)S(1)} %get-tuple-element.48.refs_1_), channel_id=1, source_target_pairs={{0,1},{1,0},{2,3},{3,2},{4,5},{5,4},{6,7},{7,6},{8,9},{9,8},{10,11... | collective-permute-start | bytes 811016 | tf_op jit(solution)/shard_map/ppermute | solution.py:426
  4.5 0.7 copy-start.3
  4.5 4.2 %copy-start = (f32[2,2,2,256,256]{4,3,2,1,0:T(8,128)S(1)}, f32[2,2,2,256,256]{4,3,2,1,0:T(8,128)}, u32[]{:S(2)}) copy-start(f32[2,2,2,256,256]{4,3,2,1,0:T(8,128)} %pivot.7) | copy-start | bytes 6291460
  4.5 4.2 %copy-start.1 = (f32[2,2,2,256,256]{4,3,2,1,0:T(8,128)S(1)}, f32[2,2,2,256,256]{4,3,2,1,0:T(8,128)}, u32[]{:S(2)}) copy-start(f32[2,2,2,256,256]{4,3,2,1,0:T(8,128)} %factor.7) | copy-start | bytes 6291460
  4.5 4.2 %copy-start.2 = (f32[2,2]{1,0:T(2,128)S(1)}, f32[2,2]{1,0:T(2,128)}, u32[]{:S(2)}) copy-start(f32[2,2]{1,0:T(2,128)} %weight.11) | copy-start | bytes 52
  6.5 14.8 %collective-permute-start = (f32[2,256,256]{2,1,0:T(8,128)S(1)}, f32[2,256,256]{2,1,0:T(8,128)S(1)}, u32[]{:S(2)}, u32[]{:S(2)}) collective-permute-start(f32[2,256,256]{2,1,0:T(8,128)S(1)} %get-tuple-element.53._), channel_id=1, source_target_pairs={{2,3},{3,2},{4,5},{5,4},{6,7},{7,6},{10,11},{11,10},{12,13},{13,12... | collective-permute-start | bytes 1572872 | tf_op jit(solution)/shard_map/ppermute | solution.py:431
  10.6 2.7 %collective-permute-start.2 = (f32[2,264,128]{2,1,0:T(8,128)S(1)}, f32[2,264,128]{2,1,0:T(8,128)S(1)}, u32[]{:S(2)}, u32[]{:S(2)}) collective-permute-start(f32[2,264,128]{2,1,0:T(8,128)S(1)} %shard_map.65), channel_id=1, source_target_pairs={{0,1},{8,9},{16,17},{24,25},{1,0},{9,8},{17,16},{25,24}} | collective-permute-start | bytes 811016 | tf_op jit(solution)/shard_map/ppermute | solution.py:434
  13.3 9.7 %collective-permute-start.3 = (f32[2,264,128]{2,1,0:T(8,128)S(1)}, f32[2,264,128]{2,1,0:T(8,128)S(1)}, u32[]{:S(2)}, u32[]{:S(2)}) collective-permute-start(f32[2,264,128]{2,1,0:T(8,128)S(1)} %shard_map.67), channel_id=1, source_target_pairs={{1,3},{9,11},{17,19},{25,27}} | collective-permute-start | bytes 811016 | tf_op jit(solution)/shard_map/ppermute | solution.py:448
  14.0 9.0 %collective-permute-start.4 = (f32[2,264,128]{2,1,0:T(8,128)S(1)}, f32[2,264,128]{2,1,0:T(8,128)S(1)}, u32[]{:S(2)}, u32[]{:S(2)}) collective-permute-start(f32[2,264,128]{2,1,0:T(8,128)S(1)} %collective-permute-done.2.e_second.refs_0_), channel_id=1, source_target_pairs={{0,2},{8,10},{16,18},{24,26}} | collective-permute-start | bytes 811016 | tf_op jit(solution)/shard_map/ppermute | solution.py:449
  23.0 0.7 %collective-permute-start.5 = (f32[2,264,128]{2,1,0:T(8,128)S(1)}, f32[2,264,128]{2,1,0:T(8,128)S(1)}, u32[]{:S(2)}, u32[]{:S(2)}) collective-permute-start(f32[2,264,128]{2,1,0:T(8,128)S(1)} %shard_map.68), channel_id=1, source_target_pairs={{3,5},{2,4},{11,13},{10,12},{19,21},{18,20},{27,29},{26,28}} | collective-permute-start | bytes 811016 | tf_op jit(solution)/shard_map/ppermute | solution.py:465
  23.9 12.8 %collective-permute-start.6 = (f32[2,264,128]{2,1,0:T(8,128)S(1)}, f32[2,264,128]{2,1,0:T(8,128)S(1)}, u32[]{:S(2)}, u32[]{:S(2)}) collective-permute-start(f32[2,264,128]{2,1,0:T(8,128)S(1)} %shard_map.69), channel_id=1, source_target_pairs={{5,7},{4,6},{13,15},{12,14},{21,23},{20,22},{29,31},{28,30}} | collective-permute-start | bytes 811016 | tf_op jit(solution)/shard_map/ppermute | solution.py:465
  37.9 5.4 %collective-permute-start.7 = (f32[2,264,128]{2,1,0:T(8,128)S(1)}, f32[2,264,128]{2,1,0:T(8,128)S(1)}, u32[]{:S(2)}, u32[]{:S(2)}) collective-permute-start(f32[2,264,128]{2,1,0:T(8,128)S(1)} %get-tuple-element.77), channel_id=1, source_target_pairs={{0,1},{1,0},{2,3},{3,2},{4,5},{5,4},{6,7},{7,6},{8,9},{9,8},{10,11... | collective-permute-start | bytes 811016 | tf_op jit(solution)/shard_map/ppermute | solution.py:474
  44.9 8.6 %collective-permute-start.8 = (f32[512,128]{1,0:T(8,128)S(1)}, f32[512,128]{1,0:T(8,128)S(1)}, u32[]{:S(2)}, u32[]{:S(2)}) collective-permute-start(f32[512,128]{1,0:T(8,128)S(1)} %slice_bitcast_fusion), channel_id=1, source_target_pairs={{0,8},{8,0},{16,24},{24,16},{1,9},{9,1},{17,25},{25,17},{2,10},{10... | collective-permute-start | bytes 786440 | tf_op jit(solution)/shard_map/ppermute | solution.py:487
  54.1 1.4 %collective-permute-start.9 = (f32[264,128]{1,0:T(8,128)S(1)}, f32[264,128]{1,0:T(8,128)S(1)}, u32[]{:S(2)}, u32[]{:S(2)}) collective-permute-start(f32[264,128]{1,0:T(8,128)S(1)} %slice_bitcast_fusion.1), channel_id=1, source_target_pairs={{0,8},{8,0},{16,24},{24,16},{1,9},{9,1},{17,25},{25,17},{2,10},{10... | collective-permute-start | bytes 405512 | tf_op jit(solution)/shard_map/ppermute | solution.py:487
  54.5 7.8 %collective-permute-start.12 = (f32[512,128]{1,0:T(8,128)S(1)}, f32[512,128]{1,0:T(8,128)S(1)}, u32[]{:S(2)}, u32[]{:S(2)}) collective-permute-start(f32[512,128]{1,0:T(8,128)S(1)} %bitcast_add_fusion._), channel_id=1, source_target_pairs={{0,16},{8,24},{16,0},{24,8},{1,17},{9,25},{17,1},{25,9},{2,18},{10... | collective-permute-start | bytes 786440 | tf_op jit(solution)/shard_map/ppermute | solution.py:487
  55.6 9.7 %collective-permute-start.10 = (f32[264,128]{1,0:T(8,128)S(1)}, f32[264,128]{1,0:T(8,128)S(1)}, u32[]{:S(2)}, u32[]{:S(2)}) collective-permute-start(f32[264,128]{1,0:T(8,128)S(1)} %fusion), channel_id=1, source_target_pairs={{0,16},{8,24},{16,0},{24,8},{1,17},{9,25},{17,1},{25,9},{2,18},{10... | collective-permute-start | bytes 405512 | tf_op jit(solution)/shard_map/ppermute | solution.py:487
  62.3 3.9 %collective-permute-start.13 = (f32[512,128]{1,0:T(8,128)S(1)}, f32[512,128]{1,0:T(8,128)S(1)}, u32[]{:S(2)}, u32[]{:S(2)}) collective-permute-start(f32[512,128]{1,0:T(8,128)S(1)} %add.15.mine), channel_id=1, source_target_pairs={{0,8},{8,0},{16,24},{24,16},{1,9},{9,1},{17,25},{25,17},{2,10},{10... | collective-permute-start | bytes 786440 | tf_op jit(solution)/shard_map/ppermute | solution.py:487
  65.2 2.0 %collective-permute-start.11 = (f32[264,128]{1,0:T(8,128)S(1)}, f32[264,128]{1,0:T(8,128)S(1)}, u32[]{:S(2)}, u32[]{:S(2)}) collective-permute-start(f32[264,128]{1,0:T(8,128)S(1)} %add.14.mine), channel_id=1, source_target_pairs={{0,8},{8,0},{16,24},{24,16},{1,9},{9,1},{17,25},{25,17},{2,10},{10... | collective-permute-start | bytes 405512 | tf_op jit(solution)/shard_map/ppermute | solution.py:487

commit v16 on v11

--- a/solution.py
+++ b/solution.py
@@ -156,6 +156,9 @@
 
     constants_of(slot, blocks, link, widths, weights, *outs, wait=wait)
     first_factor.wait()
+    _, column = rows_columns(blocks.shape[-1])
+    for c in range(2):
+        outs[3][c] = jnp.where(column < widths[0], outs[3][c], 0.0)
 
 
 def sent_constant_kernel(live, pivot, factor, weight, *refs):
@@ -188,7 +191,9 @@
 
 def second_constants(live, pivot, factor, weight, f1s, e, weighted, first_factor):
     slot = slot_of(True)
-    first_factor[...] = factor[slot, 0]
+    _, column = rows_columns(factor.shape[-1])
+    for c in range(2):
+        first_factor[c] = jnp.where(column < live[0], factor[slot, 0, c], 0.0)
     constants_of(slot, pivot.at[slot], factor.at[slot, 1], live, weight, f1s, e, weighted)
 
 
@@ -220,9 +225,8 @@
         second_constants(live, pivot, factor, weight, *outs)
 
 
-def factor_kernel(live, factor, f1s, f0s, f0t, gs, gt, g):
-    _, column = rows_columns(factor.shape[-1])
-    f0 = [jnp.where(column < live[0], factor[c], 0.0) for c in range(2)]
+def factor_kernel(factor, f1s, f0s, f0t, gs, gt, g):
+    f0 = [factor[c] for c in range(2)]
     s0 = split_pair(*f0)
     gr, gi = complex_dot(s0, load4(f1s))
     g[0], g[1] = gr, gi
@@ -426,7 +430,7 @@
     e_in = lax.ppermute(made[1], AXES, every)
     o_f1s, o_e, o_w, o_f0 = run(first_constant_kernel, [], made, constants, scratch, far=far)
     o_f0s, o_f0t, o_gs, o_gt, o_g = run(
-        factor_kernel, [live], [o_f0, o_f1s], factors
+        factor_kernel, [], [o_f0, o_f1s], factors
     )
     g_in = lax.ppermute(o_g, AXES, swaps)
     made = run(sent_second_kernel, [live], [pivot, factor, weight, o_g, *second], constants)
@@ -438,7 +442,7 @@
         second_constant_kernel, [live], [pivot, factor, weight, *made], constants
     )
     m_f0s, m_f0t, m_gs, m_gt, m_g = run(
-        factor_kernel, [live], [m_f0, m_f1s], factors
+        factor_kernel, [], [m_f0, m_f1s], factors
     )
     starts = functools.partial(step_kernel, lambda place: place == 1)
     (wave_odd,) = run(starts, [], [m_gs, m_gt, m_e, crossed], [mirrored])

time: 67.6 us -> 67.7 us (level)
  waiting for transfers between devices: 28.1 us -> 30.2 us
  Pallas kernels: 17 us -> 15.8 us
    ppermute x1, waiting for transfers between devices: 6.61 us -> 8.13 us  [local(): g_in = lax.ppermute(o_g, AXES, swaps)]
    pallas_call x17, Pallas kernels: 17 us -> 15.8 us  [run(): pl.pallas_call(kernel, out_shape=shapes, in_specs=[SCALAR] * len(scalars)...]
  transfers between devices with their start and end apart: 14 -> 14, of which waited for: 8 -> 8; matrix products, arithmetic and copies ran while one was open for 0% -> 0% of each run, Pallas kernels for 16% -> 14%
where the time goes in v16:
time: 67.7 us; the launch traced here: 67.3 us
  waiting for transfers between devices  30.2 us (45%)
  starting transfers between devices  20.2 us (30%)
  Pallas kernels  15.8 us (23%)
  between operations  0.91 us (1%)
    pallas_call x17, Pallas kernels, run(): pl.pallas_call(kernel, out_shape=shapes, in_specs=[SCALAR] * len(scalars)...  15.8 us
    ppermute x6, starting transfers between devices, exchanged(): lax.ppermute(value, 'pole', [(p, p ^ distance) for p in range(poles)])  11.6 us
    ppermute x2, waiting for transfers between devices, local(): arrived = [lax.ppermute(wave, AXES, up)]  11.5 us
    ppermute x1, waiting for transfers between devices, local(): g_in = lax.ppermute(o_g, AXES, swaps)  8.13 us
    ppermute x6, waiting for transfers between devices, exchanged(): lax.ppermute(value, 'pole', [(p, p ^ distance) for p in range(poles)])  8.12 us
    ppermute x1, waiting for transfers between devices, local(): shared = lax.ppermute(sent, AXES, every)  2.5 us
    ppermute x1, starting transfers between devices, local(): g_in = lax.ppermute(o_g, AXES, swaps)  2.3 us
    ppermute x2, starting transfers between devices, local(): arrived = [lax.ppermute(wave, AXES, up)]  2.15 us
  transfers between devices with their start and end apart: 14, of which 8 were waited for; matrix products, arithmetic and copies ran while one was open for 0% of the time, Pallas kernels for 14%

profile of v16, /device:TPU:29, one launch (start us, length us, event | category | flops | bytes accessed | tf_op | source)
XLA Modules:
  0.0 67.3 jit_solution(18318549611218548333)
XLA Ops:
  0.6 2.7 %shard_map.59 = (bf16[4,256,256]{2,1,0:T(8,128)(2,1)S(1)}, f32[2,264,128]{2,1,0:T(8,128)S(1)}, f32[4,264,128]{2,1,0:T(8,128)S(1)}, f32[2,256,256]{2,1,0:T(8,128)...) custom-call(s32[2]{0:T(128)} %live.7, ...), custom_call_target="tpu_custom_call" | custom-call | flops 1 | bytes 1 | tf_op jit(solution)/shard_map/pallas_call | solution.py:386
  3.3 1.3 %collective-permute-start.1 = (f32[2,264,128]{2,1,0:T(8,128)S(1)}, f32[2,264,128]{2,1,0:T(8,128)S(1)}, u32[]{:S(2)}, u32[]{:S(2)}) collective-permute-start(f32[2,264,128]{2,1,0:T(8,128)S(1)} %get-tuple-element.48.refs_1_), channel_id=1, source_target_pairs={{0,1},{1,0},{2,3},{3,2},{4,5},{5,4},{6,7},{7,6},{8,9},{9,8},{10,11... | collective-permute-start | bytes 811016 | tf_op jit(solution)/shard_map/ppermute | solution.py:430
  4.6 0.0 copy-start
  4.6 0.0 copy-start.1
  4.6 0.0 copy-start.2
  4.6 0.2 shard_map.60
  4.8 0.8 %shard_map.61 = (bf16[4,256,256]{2,1,0:T(8,128)(2,1)S(1)}, bf16[4,256,256]{2,1,0:T(8,128)(2,1)S(1)}, bf16[4,256,256]{2,1,0:T(8,128)(2,1)S(1)}, bf16[4,256,256]{2,1,0:T(8,128)(2,1)S(1)}, f32[2,256,256]{2,1,0:T(8,128)S(1)}) custom-call(f32[2,256,256]{2,1,0:T(8,128)S(1)} %get-tuple-element.51.factor, bf16[4,256,256]{2,1,0:T(8,128)(2,1)S(1)} %get-tuple-element.52.f1s), custom_call_target="tpu_custom_call" | custom-call | flops 1 | bytes 1 | tf_op jit(solution)/shard_map/pallas_call | solution.py:386
  5.6 2.3 %collective-permute-start = (f32[2,256,256]{2,1,0:T(8,128)S(1)}, f32[2,256,256]{2,1,0:T(8,128)S(1)}, u32[]{:S(2)}, u32[]{:S(2)}) collective-permute-start(f32[2,256,256]{2,1,0:T(8,128)S(1)} %get-tuple-element.53._), channel_id=1, source_target_pairs={{2,3},{3,2},{4,5},{5,4},{6,7},{7,6},{10,11},{11,10},{12,13},{13,12... | collective-permute-start | bytes 1572872 | tf_op jit(solution)/shard_map/ppermute | solution.py:435
  7.9 0.0 copy-done
  7.9 0.0 copy-done.1
  7.9 0.0 copy-done.2
  7.9 0.0 copy-done.3
  7.9 1.9 %shard_map.62 = (bf16[4,256,256]{2,1,0:T(8,128)(2,1)S(1)}, f32[2,264,128]{2,1,0:T(8,128)S(1)}, f32[4,264,128]{2,1,0:T(8,128)S(1)}, f32[2,256,256]{2,1,0:T(8,128)S(1)}) custom-call(s32[2]{0:T(128)S(1)} %copy-done.3, f32[2,2,2,256,256]{4,3,2,1,0:T(8,128)S(1)} %copy-done, f32[2,2,2,256,256]{4,3,2,1,0:T(8,128)S(1)} %copy-done.1, f32[2,2]{1,0:T(2,128)S(1)} %copy-done.2, ...), custom_call_target="tpu_custom_call" | custom-call | flops 1 | bytes 1 | tf_op jit(solution)/shard_map/pallas_call | solution.py:386
  9.8 0.0 collective-permute-done.1.x.e_in.x_first
  9.8 0.7 %collective-permute-start.2 = (f32[2,264,128]{2,1,0:T(8,128)S(1)}, f32[2,264,128]{2,1,0:T(8,128)S(1)}, u32[]{:S(2)}, u32[]{:S(2)}) collective-permute-start(f32[2,264,128]{2,1,0:T(8,128)S(1)} %shard_map.65), channel_id=1, source_target_pairs={{0,1},{8,9},{16,17},{24,25},{1,0},{9,8},{17,16},{25,24}} | collective-permute-start | bytes 811016 | tf_op jit(solution)/shard_map/ppermute | solution.py:438
  10.5 0.7 %shard_map.63 = (bf16[4,256,256]{2,1,0:T(8,128)(2,1)S(1)}, f32[2,264,128]{2,1,0:T(8,128)S(1)}, f32[4,264,128]{2,1,0:T(8,128)S(1)}, f32[2,256,256]{2,1,0:T(8,128)S(1)}) custom-call(s32[2]{0:T(128)S(1)} %copy-done.3, f32[2,2,2,256,256]{4,3,2,1,0:T(8,128)S(1)} %copy-done, f32[2,2,2,256,256]{4,3,2,1,0:T(8,128)S(1)} %copy-done.1, f32[2,2]{1,0:T(2,128)S(1)} %copy-done.2, ...), custom_call_target="tpu_custom_call" | custom-call | flops 1 | bytes 1 | tf_op jit(solution)/shard_map/pallas_call | solution.py:386
  11.2 0.8 %shard_map.64 = (bf16[4,256,256]{2,1,0:T(8,128)(2,1)S(1)}, bf16[4,256,256]{2,1,0:T(8,128)(2,1)S(1)}, bf16[4,256,256]{2,1,0:T(8,128)(2,1)S(1)}, bf16[4,256,256]{2,1,0:T(8,128)(2,1)S(1)}, f32[2,256,256]{2,1,0:T(8,128)S(1)}) custom-call(f32[2,256,256]{2,1,0:T(8,128)S(1)} %get-tuple-element.62.factor, bf16[4,256,256]{2,1,0:T(8,128)(2,1)S(1)} %get-tuple-element.63.f1s), custom_call_target="tpu_custom_call" | custom-call | flops 1 | bytes 1 | tf_op jit(solution)/shard_map/pallas_call | solution.py:386
  11.9 0.0 collective-permute-done.2.e_second.refs_0_
  12.0 0.7 %collective-permute-start.3 = (f32[2,264,128]{2,1,0:T(8,128)S(1)}, f32[2,264,128]{2,1,0:T(8,128)S(1)}, u32[]{:S(2)}, u32[]{:S(2)}) collective-permute-start(f32[2,264,128]{2,1,0:T(8,128)S(1)} %shard_map.67), channel_id=1, source_target_pairs={{1,3},{9,11},{17,19},{25,27}} | collective-permute-start | bytes 811016 | tf_op jit(solution)/shard_map/ppermute | solution.py:452
  12.6 0.7 %collective-permute-start.4 = (f32[2,264,128]{2,1,0:T(8,128)S(1)}, f32[2,264,128]{2,1,0:T(8,128)S(1)}, u32[]{:S(2)}, u32[]{:S(2)}) collective-permute-start(f32[2,264,128]{2,1,0:T(8,128)S(1)} %collective-permute-done.2.e_second.refs_0_), channel_id=1, source_target_pairs={{0,2},{8,10},{16,18},{24,26}} | collective-permute-start | bytes 811016 | tf_op jit(solution)/shard_map/ppermute | solution.py:453
  13.3 8.1 %collective-permute-done.g_in = f32[2,256,256]{2,1,0:T(8,128)S(1)} collective-permute-done((f32[2,256,256]{2,1,0:T(8,128)S(1)}, f32[2,256,256]{2,1,0:T(8,128)S(1)}, u32[]{:S(2)}, u32[]{:S(2)}) %collective-permute-start) | collective-permute-done | bytes 524320 | tf_op jit(solution)/shard_map/ppermute | solution.py:435
  21.5 1.7 %shard_map.66 = (bf16[4,256,256]{2,1,0:T(8,128)(2,1)S(1)}, bf16[4,256,256]{2,1,0:T(8,128)(2,1)S(1)}, f32[2,264,128]{2,1,0:T(8,128)S(1)}, bf16[4,256,256]{2,1,0:T...) custom-call(f32[2,256,256]{2,1,0:T(8,128)S(1)} %get-tuple-element.64.g, ...), custom_call_target="tpu_custom_call" | custom-call | flops 99999997952 | bytes 1 | tf_op jit(solution)/shard_map/pallas_call | solution.py:386
  23.1 0.0 collective-permute-done.3.refs_0_
  23.2 0.0 collective-permute-done.4.refs_1_
  23.2 0.9 %collective-permute-start.5 = (f32[2,264,128]{2,1,0:T(8,128)S(1)}, f32[2,264,128]{2,1,0:T(8,128)S(1)}, u32[]{:S(2)}, u32[]{:S(2)}) collective-permute-start(f32[2,264,128]{2,1,0:T(8,128)S(1)} %shard_map.68), channel_id=1, source_target_pairs={{3,5},{2,4},{11,13},{10,12},{19,21},{18,20},{27,29},{26,28}} | collective-permute-start | bytes 811016 | tf_op jit(solution)/shard_map/ppermute | solution.py:469
  24.1 0.0 collective-permute-done.5.refs_0_.refs_2_
  24.1 1.3 %collective-permute-start.6 = (f32[2,264,128]{2,1,0:T(8,128)S(1)}, f32[2,264,128]{2,1,0:T(8,128)S(1)}, u32[]{:S(2)}, u32[]{:S(2)}) collective-permute-start(f32[2,264,128]{2,1,0:T(8,128)S(1)} %shard_map.69), channel_id=1, source_target_pairs={{5,7},{4,6},{13,15},{12,14},{21,23},{20,22},{29,31},{28,30}} | collective-permute-start | bytes 811016 | tf_op jit(solution)/shard_map/ppermute | solution.py:469
  25.4 11.5 %collective-permute-done.6.refs_3_ = f32[2,264,128]{2,1,0:T(8,128)S(1)} collective-permute-done((f32[2,264,128]{2,1,0:T(8,128)S(1)}, f32[2,264,128]{2,1,0:T(8,128)S(1)}, u32[]{:S(2)}, u32[]{:S(2)}) %collective-permute-start.6) | collective-permute-done | bytes 270368 | tf_op jit(solution)/shard_map/ppermute | solution.py:469
  36.9 1.2 %shard_map.70 = (f32[2,264,128]{2,1,0:T(8,128)S(1)}, f32[2,264,128]{2,1,0:T(8,128)S(1)}) custom-call(bf16[4,256,256]{2,1,0:T(8,128)(2,1)S(1)} %get-tuple-element.69.fas, bf16[4,256,256]{2,1,0:T(8,128)(2,1)S(1)} %get-tuple-element.70.fat, f32[2,264,128]{2,1,0:T(8,128)S(1)} %get-tuple-element.71.ea, f32[2,264,128]{2,1,0:T(8,128)S(1)} %collective-permute-done.3.refs_0_, ...), custom_call_target="tpu_custom_call" | custom-call | flops 1 | bytes 1 | tf_op jit(solution)/shard_map/pallas_call | solution.py:386
  38.1 0.8 %collective-permute-start.7 = (f32[2,264,128]{2,1,0:T(8,128)S(1)}, f32[2,264,128]{2,1,0:T(8,128)S(1)}, u32[]{:S(2)}, u32[]{:S(2)}) collective-permute-start(f32[2,264,128]{2,1,0:T(8,128)S(1)} %get-tuple-element.77), channel_id=1, source_target_pairs={{0,1},{1,0},{2,3},{3,2},{4,5},{5,4},{6,7},{7,6},{8,9},{9,8},{10,11... | collective-permute-start | bytes 811016 | tf_op jit(solution)/shard_map/ppermute | solution.py:478
  38.9 2.0 %shard_map.71 = (f32[2,512,128]{2,1,0:T(8,128)S(1)}, f32[2,264,128]{2,1,0:T(8,128)S(1)}) custom-call(f32[2,2]{1,0:T(2,128)S(1)} %copy-done.2, f32[2,264,128]{2,1,0:T(8,128)S(1)} %get-tuple-element.81.x, bf16[4,256,256]{2,1,0:T(8,128)(2,1)S(1)} %get-tuple-element.82.f0s, bf16[4,256,256]{2,1,0:T(8,128)(2,1)S(1)} %get-tuple-element.83.f0t, ...), custom_call_target="tpu_custom_call" | custom-call | flops 1 | bytes 1 | tf_op jit(solution)/shard_map/pallas_call | solution.py:386
  41.0 2.5 %collective-permute-done.7.x = f32[2,264,128]{2,1,0:T(8,128)S(1)} collective-permute-done((f32[2,264,128]{2,1,0:T(8,128)S(1)}, f32[2,264,128]{2,1,0:T(8,128)S(1)}, u32[]{:S(2)}, u32[]{:S(2)}) %collective-permute-start.7) | collective-permute-done | bytes 270368 | tf_op jit(solution)/shard_map/ppermute | solution.py:478
  43.5 1.6 %shard_map.72 = (f32[2,512,128]{2,1,0:T(8,128)S(1)}, bf16[4,256,256]{2,1,0:T(8,128)(2,1)S(1)}, bf16[4,256,256]{2,1,0:T(8,128)(2,1)S(1)}) custom-call(f32[2,2]{1,0:T(2,128)S(1)} %copy-done.2, f32[2,264,128]{2,1,0:T(8,128)S(1)} %collective-permute-done.7.x, f32[2,264,128]{2,1,0:T(8,128)S(1)} %collective-permute-done.1.x.e_in.x_first, ...), custom_call_target="tpu_custom_call" | custom-call | flops 1 | bytes 1 | tf_op jit(solution)/shard_map/pallas_call | solution.py:386
  45.0 7.3 %collective-permute-start.11 = (f32[512,128]{1,0:T(8,128)S(1)}, f32[512,128]{1,0:T(8,128)S(1)}, u32[]{:S(2)}, u32[]{:S(2)}) collective-permute-start(f32[512,128]{1,0:T(8,128)S(1)} %slice_bitcast_fusion), channel_id=1, source_target_pairs={{0,8},{8,0},{16,24},{24,16},{1,9},{9,1},{17,25},{25,17},{2,10},{10... | collective-permute-start | bytes 786440 | tf_op jit(solution)/shard_map/ppermute | solution.py:491
  52.4 0.6 shard_map.73
  53.0 0.1 collective-permute-start.8
  53.1 0.5 collective-permute-done.11
  53.6 0.1 collective-permute-start.12
  53.7 0.8 %collective-permute-done.8 = f32[264,128]{1,0:T(8,128)S(1)} collective-permute-done((f32[264,128]{1,0:T(8,128)S(1)}, f32[264,128]{1,0:T(8,128)S(1)}, u32[]{:S(2)}, u32[]{:S(2)}) %collective-permute-start.8) | collective-permute-done | bytes 135200 | tf_op jit(solution)/shard_map/ppermute | solution.py:491
  54.4 0.8 %collective-permute-start.9 = (f32[264,128]{1,0:T(8,128)S(1)}, f32[264,128]{1,0:T(8,128)S(1)}, u32[]{:S(2)}, u32[]{:S(2)}) collective-permute-start(f32[264,128]{1,0:T(8,128)S(1)} %fusion), channel_id=1, source_target_pairs={{0,16},{8,24},{16,0},{24,8},{1,17},{9,25},{17,1},{25,9},{2,18},{10... | collective-permute-start | bytes 405512 | tf_op jit(solution)/shard_map/ppermute | solution.py:491
  55.2 6.0 %collective-permute-done.12 = f32[512,128]{1,0:T(8,128)S(1)} collective-permute-done((f32[512,128]{1,0:T(8,128)S(1)}, f32[512,128]{1,0:T(8,128)S(1)}, u32[]{:S(2)}, u32[]{:S(2)}) %collective-permute-start.12) | collective-permute-done | bytes 262176 | tf_op jit(solution)/shard_map/ppermute | solution.py:491
  61.2 2.1 %collective-permute-start.13 = (f32[512,128]{1,0:T(8,128)S(1)}, f32[512,128]{1,0:T(8,128)S(1)}, u32[]{:S(2)}, u32[]{:S(2)}) collective-permute-start(f32[512,128]{1,0:T(8,128)S(1)} %add.15.mine), channel_id=1, source_target_pairs={{0,8},{8,0},{16,24},{24,16},{1,9},{9,1},{17,25},{25,17},{2,10},{10... | collective-permute-start | bytes 786440 | tf_op jit(solution)/shard_map/ppermute | solution.py:491
  63.3 0.8 %collective-permute-done.9 = f32[264,128]{1,0:T(8,128)S(1)} collective-permute-done((f32[264,128]{1,0:T(8,128)S(1)}, f32[264,128]{1,0:T(8,128)S(1)}, u32[]{:S(2)}, u32[]{:S(2)}) %collective-permute-start.9) | collective-permute-done | bytes 135200 | tf_op jit(solution)/shard_map/ppermute | solution.py:491
  64.1 1.3 %collective-permute-start.10 = (f32[264,128]{1,0:T(8,128)S(1)}, f32[264,128]{1,0:T(8,128)S(1)}, u32[]{:S(2)}, u32[]{:S(2)}) collective-permute-start(f32[264,128]{1,0:T(8,128)S(1)} %add.13.mine), channel_id=1, source_target_pairs={{0,8},{8,0},{16,24},{24,16},{1,9},{9,1},{17,25},{25,17},{2,10},{10... | collective-permute-start | bytes 405512 | tf_op jit(solution)/shard_map/ppermute | solution.py:491
  65.4 0.0 collective-permute-done.13.theirs
  65.4 0.8 %shard_map.74 = (f32[2,256,256]{2,1,0:T(8,128)}, f32[8,128]{1,0:T(8,128)S(1)}) custom-call(f32[512,128]{1,0:T(8,128)S(1)} %add.15.mine, f32[512,128]{1,0:T(8,128)S(1)} %collective-permute-done.13.theirs), custom_call_target="tpu_custom_call" | custom-call | flops 1 | bytes 1 | tf_op jit(solution)/shard_map/pallas_call | solution.py:386
  66.2 0.1 collective-permute-done.10.theirs
  66.3 0.9 %shard_map.75 = f32[2,256,256]{2,1,0:T(8,128)} custom-call(f32[264,128]{1,0:T(8,128)S(1)} %add.13.mine, f32[264,128]{1,0:T(8,128)S(1)} %collective-permute-done.10.theirs, f32[8,128]{1,0:T(8,128)S(1)} %get-tuple-element.90._), custom_call_target="tpu_custom_call" | custom-call | flops 1 | bytes 1 | tf_op jit(solution)/shard_map/pallas_call | solution.py:386
  (11 shorter events, 0.2 us)
Async XLA Ops:
  3.3 6.5 %collective-permute-start.1 = (f32[2,264,128]{2,1,0:T(8,128)S(1)}, f32[2,264,128]{2,1,0:T(8,128)S(1)}, u32[]{:S(2)}, u32[]{:S(2)}) collective-permute-start(f32[2,264,128]{2,1,0:T(8,128)S(1)} %get-tuple-element.48.refs_1_), channel_id=1, source_target_pairs={{0,1},{1,0},{2,3},{3,2},{4,5},{5,4},{6,7},{7,6},{8,9},{9,8},{10,11... | collective-permute-start | bytes 811016 | tf_op jit(solution)/shard_map/ppermute | solution.py:430
  4.6 3.3 %copy-start = (f32[2,2,2,256,256]{4,3,2,1,0:T(8,128)S(1)}, f32[2,2,2,256,256]{4,3,2,1,0:T(8,128)}, u32[]{:S(2)}) copy-start(f32[2,2,2,256,256]{4,3,2,1,0:T(8,128)} %pivot.7) | copy-start | bytes 6291460
  4.6 3.3 %copy-start.1 = (f32[2,2,2,256,256]{4,3,2,1,0:T(8,128)S(1)}, f32[2,2,2,256,256]{4,3,2,1,0:T(8,128)}, u32[]{:S(2)}) copy-start(f32[2,2,2,256,256]{4,3,2,1,0:T(8,128)} %factor.7) | copy-start | bytes 6291460
  4.6 3.3 %copy-start.2 = (f32[2,2]{1,0:T(2,128)S(1)}, f32[2,2]{1,0:T(2,128)}, u32[]{:S(2)}) copy-start(f32[2,2]{1,0:T(2,128)} %weight.11) | copy-start | bytes 52
  4.6 3.3 %copy-start.3 = (s32[2]{0:T(128)S(1)}, s32[2]{0:T(128)}, u32[]{:S(2)}) copy-start(s32[2]{0:T(128)} %live.7) | copy-start | bytes 28
  5.6 15.9 %collective-permute-start = (f32[2,256,256]{2,1,0:T(8,128)S(1)}, f32[2,256,256]{2,1,0:T(8,128)S(1)}, u32[]{:S(2)}, u32[]{:S(2)}) collective-permute-start(f32[2,256,256]{2,1,0:T(8,128)S(1)} %get-tuple-element.53._), channel_id=1, source_target_pairs={{2,3},{3,2},{4,5},{5,4},{6,7},{7,6},{10,11},{11,10},{12,13},{13,12... | collective-permute-start | bytes 1572872 | tf_op jit(solution)/shard_map/ppermute | solution.py:435
  9.8 2.1 %collective-permute-start.2 = (f32[2,264,128]{2,1,0:T(8,128)S(1)}, f32[2,264,128]{2,1,0:T(8,128)S(1)}, u32[]{:S(2)}, u32[]{:S(2)}) collective-permute-start(f32[2,264,128]{2,1,0:T(8,128)S(1)} %shard_map.65), channel_id=1, source_target_pairs={{0,1},{8,9},{16,17},{24,25},{1,0},{9,8},{17,16},{25,24}} | collective-permute-start | bytes 811016 | tf_op jit(solution)/shard_map/ppermute | solution.py:438
  12.0 11.2 %collective-permute-start.3 = (f32[2,264,128]{2,1,0:T(8,128)S(1)}, f32[2,264,128]{2,1,0:T(8,128)S(1)}, u32[]{:S(2)}, u32[]{:S(2)}) collective-permute-start(f32[2,264,128]{2,1,0:T(8,128)S(1)} %shard_map.67), channel_id=1, source_target_pairs={{1,3},{9,11},{17,19},{25,27}} | collective-permute-start | bytes 811016 | tf_op jit(solution)/shard_map/ppermute | solution.py:452
  12.6 10.5 %collective-permute-start.4 = (f32[2,264,128]{2,1,0:T(8,128)S(1)}, f32[2,264,128]{2,1,0:T(8,128)S(1)}, u32[]{:S(2)}, u32[]{:S(2)}) collective-permute-start(f32[2,264,128]{2,1,0:T(8,128)S(1)} %collective-permute-done.2.e_second.refs_0_), channel_id=1, source_target_pairs={{0,2},{8,10},{16,18},{24,26}} | collective-permute-start | bytes 811016 | tf_op jit(solution)/shard_map/ppermute | solution.py:453
  23.2 0.9 %collective-permute-start.5 = (f32[2,264,128]{2,1,0:T(8,128)S(1)}, f32[2,264,128]{2,1,0:T(8,128)S(1)}, u32[]{:S(2)}, u32[]{:S(2)}) collective-permute-start(f32[2,264,128]{2,1,0:T(8,128)S(1)} %shard_map.68), channel_id=1, source_target_pairs={{3,5},{2,4},{11,13},{10,12},{19,21},{18,20},{27,29},{26,28}} | collective-permute-start | bytes 811016 | tf_op jit(solution)/shard_map/ppermute | solution.py:469
  24.1 12.8 %collective-permute-start.6 = (f32[2,264,128]{2,1,0:T(8,128)S(1)}, f32[2,264,128]{2,1,0:T(8,128)S(1)}, u32[]{:S(2)}, u32[]{:S(2)}) collective-permute-start(f32[2,264,128]{2,1,0:T(8,128)S(1)} %shard_map.69), channel_id=1, source_target_pairs={{5,7},{4,6},{13,15},{12,14},{21,23},{20,22},{29,31},{28,30}} | collective-permute-start | bytes 811016 | tf_op jit(solution)/shard_map/ppermute | solution.py:469
  38.1 5.4 %collective-permute-start.7 = (f32[2,264,128]{2,1,0:T(8,128)S(1)}, f32[2,264,128]{2,1,0:T(8,128)S(1)}, u32[]{:S(2)}, u32[]{:S(2)}) collective-permute-start(f32[2,264,128]{2,1,0:T(8,128)S(1)} %get-tuple-element.77), channel_id=1, source_target_pairs={{0,1},{1,0},{2,3},{3,2},{4,5},{5,4},{6,7},{7,6},{8,9},{9,8},{10,11... | collective-permute-start | bytes 811016 | tf_op jit(solution)/shard_map/ppermute | solution.py:478
  45.0 8.5 %collective-permute-start.11 = (f32[512,128]{1,0:T(8,128)S(1)}, f32[512,128]{1,0:T(8,128)S(1)}, u32[]{:S(2)}, u32[]{:S(2)}) collective-permute-start(f32[512,128]{1,0:T(8,128)S(1)} %slice_bitcast_fusion), channel_id=1, source_target_pairs={{0,8},{8,0},{16,24},{24,16},{1,9},{9,1},{17,25},{25,17},{2,10},{10... | collective-permute-start | bytes 786440 | tf_op jit(solution)/shard_map/ppermute | solution.py:491
  53.0 1.4 %collective-permute-start.8 = (f32[264,128]{1,0:T(8,128)S(1)}, f32[264,128]{1,0:T(8,128)S(1)}, u32[]{:S(2)}, u32[]{:S(2)}) collective-permute-start(f32[264,128]{1,0:T(8,128)S(1)} %slice_bitcast_fusion.1), channel_id=1, source_target_pairs={{0,8},{8,0},{16,24},{24,16},{1,9},{9,1},{17,25},{25,17},{2,10},{10... | collective-permute-start | bytes 405512 | tf_op jit(solution)/shard_map/ppermute | solution.py:491
  53.6 7.6 %collective-permute-start.12 = (f32[512,128]{1,0:T(8,128)S(1)}, f32[512,128]{1,0:T(8,128)S(1)}, u32[]{:S(2)}, u32[]{:S(2)}) collective-permute-start(f32[512,128]{1,0:T(8,128)S(1)} %bitcast_add_fusion), channel_id=1, source_target_pairs={{0,16},{8,24},{16,0},{24,8},{1,17},{9,25},{17,1},{25,9},{2,18},{10... | collective-permute-start | bytes 786440 | tf_op jit(solution)/shard_map/ppermute | solution.py:491
  54.4 9.6 %collective-permute-start.9 = (f32[264,128]{1,0:T(8,128)S(1)}, f32[264,128]{1,0:T(8,128)S(1)}, u32[]{:S(2)}, u32[]{:S(2)}) collective-permute-start(f32[264,128]{1,0:T(8,128)S(1)} %fusion), channel_id=1, source_target_pairs={{0,16},{8,24},{16,0},{24,8},{1,17},{9,25},{17,1},{25,9},{2,18},{10... | collective-permute-start | bytes 405512 | tf_op jit(solution)/shard_map/ppermute | solution.py:491
  61.2 4.2 %collective-permute-start.13 = (f32[512,128]{1,0:T(8,128)S(1)}, f32[512,128]{1,0:T(8,128)S(1)}, u32[]{:S(2)}, u32[]{:S(2)}) collective-permute-start(f32[512,128]{1,0:T(8,128)S(1)} %add.15.mine), channel_id=1, source_target_pairs={{0,8},{8,0},{16,24},{24,16},{1,9},{9,1},{17,25},{25,17},{2,10},{10... | collective-permute-start | bytes 786440 | tf_op jit(solution)/shard_map/ppermute | solution.py:491
  64.1 2.3 %collective-permute-start.10 = (f32[264,128]{1,0:T(8,128)S(1)}, f32[264,128]{1,0:T(8,128)S(1)}, u32[]{:S(2)}, u32[]{:S(2)}) collective-permute-start(f32[264,128]{1,0:T(8,128)S(1)} %add.13.mine), channel_id=1, source_target_pairs={{0,8},{8,0},{16,24},{24,16},{1,9},{9,1},{17,25},{25,17},{2,10},{10... | collective-permute-start | bytes 405512 | tf_op jit(solution)/shard_map/ppermute | solution.py:491
